TPU v7x, 32 devices: a whole 2x2x4 slice. The times are simulated.
32 devices in a mesh: dp: 8 (over y, x, core), tsp: 4 (over z).
Axes of the slice: x: 2, y: 2, z: 4, core: 2. Of those that a mesh axis runs over, the one named last changes fastest.
Arguments:
- tokens: bfloat16 [16384, 8192], P('dp', 'tsp'), may hold values from -6 to 6
- cotangent: bfloat16 [16384, 1024], P('dp', 'tsp'), may hold values from -6 to 6
- frozen_key_weight: bfloat16 [8192, 1024], P('tsp'), may hold values from -0.1875 to 0.1875
- adapter_down_weight: bfloat16 [16, 64, 8192], P('dp', None, 'tsp'), may hold values from -0.0625 to 0.0625
- adapter_up_weight: bfloat16 [16, 64, 1024], P('dp', None, 'tsp'), may hold values from -0.1875 to 0.1875
- adapter_place_table: int32 [16], replicated, may hold values from 0 to 15, as said below
- segment_adapter: int32 [128], P('dp'), may hold values from 0 to 15, as said below
- segment_live_count: int32 [128], P('dp'), may hold values from 1 to 128, as said below
Outputs:
- token_gradient: bfloat16 [16384, 8192], P('dp', 'tsp')
- down_grad: float32 [16, 64, 8192], P('dp', None, 'tsp')
- up_grad: float32 [16, 64, 1024], P('dp', None, 'tsp')
Inputs may be any that keep to these rules, and one draw needn't show every extreme that they name: A permutation: adapter a is held at place adapter_place_table[a], that is by the dp index adapter_place_table[a] // 2 as its entry adapter_place_table[a] % 2; the adapters' arrays and gradients are indexed by place. `segment_adapter`: the 16 segments of one dp index name at most one adapter held by any one dp index; an adapter may be named by several of them. `segment_live_count`: the live rows stand at the start of each segment; on every dp index some segment is full.
All inputs are finite; a program needn't handle non-finite values.
Results may differ from a plain program's by a relative error of at most 0.0034.
Values may be sent and summed in bfloat16 or wider, within the bound.
No kernel may reach another device: no remote copies, remote signals or barrier semaphores. Data moves between devices by JAX's collectives and lax.ppermute only.
A program may use at most 128 MiB of HBM per device.

v0:
```python
import jax
import jax.numpy as jnp
from jax import lax
from jax.sharding import PartitionSpec as P

ADAPTER_SCALE = 2.0


def lookup(idents, mapping):
    matches = idents[:, None] == jnp.arange(mapping.shape[0], dtype=jnp.int32)[None, :]
    return jnp.sum(jnp.where(matches, mapping[None, :], 0), axis=1)


def on_device(
    tokens,
    cotangent,
    frozen_key_weight,
    adapter_down_weight,
    adapter_up_weight,
    adapter_place_table,
    segment_adapter,
    segment_live_count,
):
    dp_count = lax.axis_size("dp")
    places_per_device = adapter_down_weight.shape[0]
    rank_of_adapter = adapter_down_weight.shape[1]
    width_per_device = tokens.shape[1]
    key_dev = cotangent.shape[1]
    segments_per_device = segment_adapter.shape[0]
    segment_token_rows = tokens.shape[0] // segments_per_device
    adapter_places = lookup(segment_adapter, adapter_place_table)
    seg_owner = adapter_places // places_per_device
    seg_entry = adapter_places % places_per_device
    owner_hit = seg_owner[:, None] == jnp.arange(dp_count, dtype=jnp.int32)[None, :]
    wanted = jnp.max(jnp.where(owner_hit, seg_entry[:, None], -1), axis=0)
    incoming = lax.all_to_all(wanted[:, None], "dp", split_axis=0, concat_axis=0, tiled=True)[:, 0]
    serving_mesh = (
        incoming[:, None] == jnp.arange(places_per_device, dtype=jnp.int32)[None, :]
    ).astype(jnp.bfloat16)
    reply_down = jnp.einsum(
        "ap,phc->ahc", serving_mesh, adapter_down_weight, preferred_element_type=jnp.float32
    ).astype(jnp.bfloat16)
    reply_up = jnp.einsum(
        "hv,vun->hun", serving_mesh, adapter_up_weight, preferred_element_type=jnp.float32
    ).astype(jnp.bfloat16)
    fetched_down, fetched_up = (
        lax.all_to_all(reply_down, "dp", split_axis=0, concat_axis=0, tiled=True),
        lax.all_to_all(reply_up, "dp", split_axis=0, concat_axis=0, tiled=True),
    )
    picker = owner_hit.astype(jnp.bfloat16)
    segment_down_weight = jnp.einsum(
        "go,ord->grd", picker, fetched_down, preferred_element_type=jnp.float32
    ).astype(jnp.bfloat16)
    segment_up_weight = jnp.einsum(
        "go,ork->grk", picker, fetched_up, preferred_element_type=jnp.float32
    ).astype(jnp.bfloat16)
    seg_tokens = tokens.reshape(segments_per_device, segment_token_rows, width_per_device)
    seg_cotangent = cotangent.reshape(segments_per_device, segment_token_rows, key_dev)
    live_rows = (
        jnp.arange(segment_token_rows, dtype=jnp.int32)[None, :] < segment_live_count[:, None]
    ).astype(jnp.float32)
    partial_terms = jnp.concatenate(
        [
            jnp.einsum(
                "gtd,grd->gtr", seg_tokens, segment_down_weight, preferred_element_type=jnp.float32
            ),
            jnp.einsum(
                "gtk,grk->gtr", seg_cotangent, segment_up_weight, preferred_element_type=jnp.float32
            ),
        ],
        axis=2,
    )
    summed = lax.psum(partial_terms, "tsp")
    reduced_rows = (summed[:, :, :rank_of_adapter] * live_rows[:, :, None]).astype(jnp.bfloat16)
    gathered_weights = (summed[:, :, rank_of_adapter:] * live_rows[:, :, None]).astype(jnp.bfloat16)
    frozen_output = lax.dot_general(
        lax.all_gather(cotangent, "tsp", axis=1, tiled=True),
        frozen_key_weight,
        (((1,), (1,)), ((), ())),
        preferred_element_type=jnp.float32,
    )
    adapter_output = jnp.einsum(
        "wks,wsx->wkx", gathered_weights, segment_down_weight, preferred_element_type=jnp.float32
    )
    token_gradient = (
        frozen_output.reshape(segments_per_device, segment_token_rows, width_per_device)
        + ADAPTER_SCALE * adapter_output
    ) * live_rows[:, :, None]
    token_gradient = token_gradient.reshape(
        segments_per_device * segment_token_rows, width_per_device
    ).astype(jnp.bfloat16)
    gradient_scale = ADAPTER_SCALE / segment_token_rows
    segment_down_gradient = jnp.einsum(
        "upf,upb->ufb", gathered_weights, seg_tokens, preferred_element_type=jnp.float32
    )
    segment_up_gradient = jnp.einsum(
        "ija,ijn->ian", reduced_rows, seg_cotangent, preferred_element_type=jnp.float32
    )
    picker_f = owner_hit.astype(jnp.float32)
    slot_dgrad = (
        jnp.einsum("go,grd->ord", picker_f, segment_down_gradient, precision=lax.Precision.HIGHEST)
        * gradient_scale
    )
    slot_ugrad = (
        jnp.einsum("go,grk->ork", picker_f, segment_up_gradient, precision=lax.Precision.HIGHEST)
        * gradient_scale
    )
    slot_match = (wanted[:, None] == jnp.arange(places_per_device, dtype=jnp.int32)[None, :])[
        :, :, None, None
    ]
    dense_down = jnp.where(slot_match, slot_dgrad[:, None], 0.0).reshape(
        dp_count * places_per_device, rank_of_adapter, width_per_device
    )
    dense_up = jnp.where(slot_match, slot_ugrad[:, None], 0.0).reshape(
        dp_count * places_per_device, rank_of_adapter, key_dev
    )
    down_grad, up_grad = (
        lax.psum_scatter(dense_down, "dp", scatter_dimension=0, tiled=True),
        lax.psum_scatter(dense_up, "dp", scatter_dimension=0, tiled=True),
    )
    return (token_gradient, down_grad, up_grad)


def solution(mesh):
    placed = (
        P("dp", "tsp"),
        P("dp", "tsp"),
        P("tsp", None),
        P("dp", None, "tsp"),
        P("dp", None, "tsp"),
        P(),
        P("dp"),
        P("dp"),
    )
    return jax.shard_map(
        on_device,
        mesh=mesh,
        in_specs=placed,
        out_specs=(P("dp", "tsp"), P("dp", None, "tsp"), P("dp", None, "tsp")),
        check_vma=False,
    )
```

profile of v0, /device:TPU:0, one launch (start us, length us, event | category | flops | bytes accessed | tf_op | source)
XLA Modules:
  0.0 328.3 jit_solution(18069655823959307340)
XLA Ops:
  7.2 0.0 copy-start
  7.2 0.9 select_reduce_fusion
  8.1 0.1 select_reduce_fusion.1
  8.2 0.1 copy.57
  8.3 9.6 %all_to_all.19 = s32[8,1,1]{2,1,0:T(1,128)S(1)} all-to-all(s32[8,1,1]{2,1,0:T(1,128)S(1)} %copy.57), channel_id=1, replica_groups=mesh['dp'=8,'tsp'=4] {'dp'}, dimensions={0} | all-to-all | bytes 64 | tf_op jit(solution)/shard_map/all_to_all | solution.py:36
  17.9 0.2 reduce
  18.2 1.1 convolution_convert_fusion.3
  19.3 0.8 copy.63
  20.1 3.4 %all-to-all-start.2 = ((bf16[8,64,256]{2,1,0:T(8,128)(2,1)}), bf16[8,64,256]{2,1,0:T(8,128)(2,1)S(1)}, u32[]{:S(2)}, u32[]{:S(2)}) async-start(bf16[8,64,256]{2,1,0:T(8,128)(2,1)} %copy.63), calls=%async_computation.2 | async-start | bytes 524288 | tf_op jit(solution)/shard_map/all_to_all | solution.py:48
  23.5 0.0 copy-done
  23.5 1.1 convolution_convert_fusion.1
  24.6 0.0 copy-start.3
  24.6 2.5 copy.59
  27.0 3.3 %all-to-all-done.2 = bf16[8,64,256]{2,1,0:T(8,128)(2,1)S(1)} async-done(((bf16[8,64,256]{2,1,0:T(8,128)(2,1)}), bf16[8,64,256]{2,1,0:T(8,128)(2,1)S(1)}, u32[]{:S(2)}, u32[]{:S(2)}) %all-to-all-start.2) | async-done | bytes 262176 | tf_op jit(solution)/shard_map/all_to_all | solution.py:48
  30.3 4.4 %all-to-all-start.1 = ((bf16[8,64,2048]{2,1,0:T(8,128)(2,1)}), bf16[8,64,2048]{2,1,0:T(8,128)(2,1)}, u32[]{:S(2)}, u32[]{:S(2)}) async-start(bf16[8,64,2048]{2,1,0:T(8,128)(2,1)} %copy.59), calls=%async_computation.1 | async-start | bytes 4194304 | tf_op jit(solution)/shard_map/all_to_all | solution.py:47
  34.7 0.0 all-reduce.2.cloned.1.call-start
  34.7 0.4 convolution_convert_fusion.2
  35.1 0.0 copy-done.3
  35.1 0.5 convolution_bitcast_fusion
  35.6 25.8 %all-to-all-done.1 = bf16[8,64,2048]{2,1,0:T(8,128)(2,1)} async-done(((bf16[8,64,2048]{2,1,0:T(8,128)(2,1)}), bf16[8,64,2048]{2,1,0:T(8,128)(2,1)}, u32[]{:S(2)}, u32[]{:S(2)}) %all-to-all-start.1) | async-done | bytes 2097184 | tf_op jit(solution)/shard_map/all_to_all | solution.py:47
  61.3 3.2 convolution_convert_fusion
  64.5 0.0 copy-start.2
  64.5 9.2 %fusion.9 = f32[16,128,64]{1,2,0:T(8,128)S(1)} fusion(bf16[16,128,2048]{2,1,0:T(8,128)(2,1)} %bitcast.30, bf16[16,64,2048]{2,0,1:T(8,128)(2,1)S(1)} %convolution_convert_fusion), kind=kOutput, calls=%fused_computation.12 | convolution fusion | flops 536870912 | bytes 13107200 | tf_op jit(solution)/shard_map/gtd,grd->gtr/dot_general | solution.py:64
  73.8 0.0 copy-done.2
  73.8 0.0 copy-start.6
  73.8 0.0 copy-start.4
  73.8 1.1 pad_maximum_fusion
  74.8 0.0 all-reduce.2.cloned.1.call-update
  74.9 0.0 all-gather.2.cloned.1.call-start
  74.9 0.7 all-gather.2.cloned.1.call-update
  75.6 0.0 reduce-scatter.5.cloned.1.call-start
  75.7 0.1 iota_compare_fusion.2
  75.7 0.1 eq.76
  75.8 0.0 copy-done.6
  75.8 0.1 fusion.25
  75.9 50.3 %all-reduce.2.cloned.1.call-done = f32[16,128,128]{1,2,0:T(8,128)} async-done(((f32[16,128,128]{1,2,0:T(8,128)}), f32[16,128,128]{1,2,0:T(8,128)}) %all-reduce.2.cloned.1.call-update) | async-done | bytes 1048592 | tf_op jit(solution)/shard_map/psum | solution.py:73
  126.2 0.0 copy-done.4
  126.2 0.0 copy-start.5
  126.2 1.4 fusion.17
  127.7 1.1 convolution_multiply_fusion
  128.7 0.2 copy.70
  128.9 1.1 bitcast_select_fusion.1
  130.0 0.0 reduce-scatter.5.cloned.1.call-update
  130.1 0.2 reduce-scatter.3.cloned.1.call-start
  130.3 0.0 copy-done.5
  130.3 4.6 %fusion.21 = f32[16,64,2048]{2,1,0:T(8,128)S(1)} fusion(bf16[16,128,2048]{2,1,0:T(8,128)(2,1)} %bitcast.31, f32[16,128,128]{1,2,0:T(8,128)S(1)} %copy-done.5, f32[16,128]{1,0:T(8,128)S(1)} %fusion.25), kind=kOutput, calls=%fused_computation.28 | convolution fusion | flops 537133056 | bytes 17309696 | tf_op jit(solution)/shard_map/upf,upb->ufb/dot_general | solution.py:93
  135.0 8.1 %fusion.5 = f32[8,64,2048]{2,0,1:T(8,128)S(1)} fusion(f32[16,64,2048]{2,1,0:T(8,128)S(1)} %fusion.21, s32[16]{0:T(128)S(1)} %get-tuple-element.3), kind=kOutput, calls=%fused_computation.8 | convolution fusion | flops 202375296 | bytes 12582976 | tf_op jit(solution)/shard_map/go,grd->ord/dot_general | solution.py:101
  143.0 2.7 copy.68
  145.7 4.6 %bitcast_select_fusion = f32[16,64,2048]{2,1,0:T(8,128)} fusion(f32[8,64,2048]{2,1,0:T(8,128)S(1)} %copy.68, pred[16]{0:T(512)(128)(4,1)S(1)} %eq.76), kind=kLoop, calls=%fused_computation.1 | loop fusion | flops 2097152 | bytes 12582928 | tf_op jit(solution)/shard_map/jit(_where)/select_n | solution.py:111
  150.3 0.0 reduce-scatter.3.cloned.1.call-update
  150.3 57.5 %all-gather.2.cloned.1.call-done = bf16[2048,1024]{1,0:T(8,128)(2,1)} async-done(((bf16[2048,256]{1,0:T(8,128)(2,1)}), bf16[2048,1024]{1,0:T(8,128)(2,1)}) %all-gather.2.cloned.1.call-update) | async-done | bytes 4194320 | tf_op jit(solution)/shard_map/all_gather | solution.py:77
  207.9 15.3 %fusion.39 = f32[2048,2048]{1,0:T(8,128)} fusion(bf16[2048,1024]{1,0:T(8,128)(2,1)} %all-gather.2.cloned.1.call-done, bf16[2048,1024]{1,0:T(8,128)(2,1)} %param.10), kind=kOutput, calls=%fused_computation.52 | convolution fusion | flops 8589934592 | bytes 25165824 | tf_op jit(solution)/shard_map/dot_general | solution.py:76
  223.1 0.0 copy-start.1
  223.1 14.2 %multiply_convert_fusion = bf16[16,128,2048]{2,1,0:T(8,128)(2,1)} fusion(f32[16,128,2048]{2,1,0:T(8,128)} %bitcast.32, f32[16,128]{1,0:T(8,128)S(1)} %fusion.25, bf16[16,64,2048]{2,0,1:T(8,128)(2,1)} %copy-done.2, f32[16,128,128]{1,2,0:T(8,128)S(1)} %copy-done.5), kind=kOutput, calls=%fused_computation | convolution fusion | flops 553910272 | bytes 29900800 | tf_op jit(solution)/shard_map/wks,wsx->wkx/dot_general | solution.py:82
  237.3 8.9 %reduce-scatter.5.cloned.1.call-done = f32[2,64,256]{2,1,0:T(8,128)} async-done(((f32[16,64,256]{2,1,0:T(8,128)}), f32[2,64,256]{2,1,0:T(8,128)}) %reduce-scatter.5.cloned.1.call-update) | async-done | bytes 131088 | tf_op jit(solution)/shard_map/reduce_scatter | solution.py:119
  246.2 75.6 %reduce-scatter.3.cloned.1.call-done = f32[2,64,2048]{2,1,0:T(8,128)} async-done(((f32[16,64,2048]{2,1,0:T(8,128)}), f32[2,64,2048]{2,1,0:T(8,128)}) %reduce-scatter.3.cloned.1.call-update) | async-done | bytes 1048592 | tf_op jit(solution)/shard_map/reduce_scatter | solution.py:118
  321.8 0.0 copy-done.1
  (1 shorter events, 0.0 us)
Async XLA Ops:
  7.2 16.3 %copy-start = (bf16[2,64,2048]{2,1,0:T(8,128)(2,1)S(1)}, bf16[2,64,2048]{2,1,0:T(8,128)(2,1)}, u32[]{:S(2)}) copy-start(bf16[2,64,2048]{2,1,0:T(8,128)(2,1)} %param.11) | copy-start | bytes 1572868
  20.1 10.3 %all-to-all-start.2 = ((bf16[8,64,256]{2,1,0:T(8,128)(2,1)}), bf16[8,64,256]{2,1,0:T(8,128)(2,1)S(1)}, u32[]{:S(2)}, u32[]{:S(2)}) async-start(bf16[8,64,256]{2,1,0:T(8,128)(2,1)} %copy.63), calls=%async_computation.2 | async-start | bytes 524288 | tf_op jit(solution)/shard_map/all_to_all | solution.py:48
  24.6 10.5 %copy-start.3 = (bf16[2048,256]{1,0:T(8,128)(2,1)S(1)}, bf16[2048,256]{1,0:T(8,128)(2,1)}, u32[]{:S(2)}) copy-start(bf16[2048,256]{1,0:T(8,128)(2,1)} %param.9) | copy-start | bytes 3145732
  30.3 31.0 %all-to-all-start.1 = ((bf16[8,64,2048]{2,1,0:T(8,128)(2,1)}), bf16[8,64,2048]{2,1,0:T(8,128)(2,1)}, u32[]{:S(2)}, u32[]{:S(2)}) async-start(bf16[8,64,2048]{2,1,0:T(8,128)(2,1)} %copy.59), calls=%async_computation.1 | async-start | bytes 4194304 | tf_op jit(solution)/shard_map/all_to_all | solution.py:47
  34.7 91.5 %all-reduce.2.cloned.1.call-start = ((), (), s32[]{:S(2)}) async-start(), calls=%async_computation.6 | async-start | bytes 2097152 | tf_op jit(solution)/shard_map/psum | solution.py:73
  64.5 9.2 %copy-start.2 = (bf16[16,64,2048]{2,0,1:T(8,128)(2,1)}, bf16[16,64,2048]{2,0,1:T(8,128)(2,1)S(1)}, u32[]{:S(2)}) copy-start(bf16[16,64,2048]{2,0,1:T(8,128)(2,1)S(1)} %convolution_convert_fusion) | copy-start | bytes 12582916
  73.8 2.1 copy-start.6
  73.8 52.5 %copy-start.4 = (bf16[2048,256]{1,0:T(8,128)(2,1)S(1)}, bf16[2048,256]{1,0:T(8,128)(2,1)}, u32[]{:S(2)}) copy-start(bf16[2048,256]{1,0:T(8,128)(2,1)} %param.9) | copy-start | bytes 3145732
  74.9 133.0 %all-gather.2.cloned.1.call-start = ((), (), s32[]{:S(2)}) async-start(), calls=%async_computation.5 | async-start | bytes 5242880 | tf_op jit(solution)/shard_map/all_gather | solution.py:77
  75.6 170.6 %reduce-scatter.5.cloned.1.call-start = ((), (), s32[]{:S(2)}) async-start(), calls=%async_computation.8 | async-start | bytes 1179648 | tf_op jit(solution)/shard_map/reduce_scatter | solution.py:119
  126.2 4.1 %copy-start.5 = (f32[16,128,128]{1,2,0:T(8,128)S(1)}, f32[16,128,128]{1,2,0:T(8,128)}, u32[]{:S(2)}) copy-start(f32[16,128,128]{1,2,0:T(8,128)} %all-reduce.2.cloned.1.call-done) | copy-start | bytes 3145732
  130.1 191.7 %reduce-scatter.3.cloned.1.call-start = ((), (), s32[]{:S(2)}) async-start(), calls=%async_computation.7 | async-start | bytes 9437184 | tf_op jit(solution)/shard_map/reduce_scatter | solution.py:118
  223.1 98.7 %copy-start.1 = (bf16[2,64,2048]{2,1,0:T(8,128)(2,1)S(1)}, bf16[2,64,2048]{2,1,0:T(8,128)(2,1)}, u32[]{:S(2)}) copy-start(bf16[2,64,2048]{2,1,0:T(8,128)(2,1)} %param.11) | copy-start | bytes 1572868
Sparse Core Ops, SparseCore 0:
  75.0 51.2 all-reduce.1
  127.9 79.9 all-gather.1
  211.9 34.2 reduce-scatter.4
  250.5 71.2 reduce-scatter.2
where the time goes:
time: 329 us; the launch traced here: 328 us
  waiting for transfers between devices  222 us (67%)
  matrix products  60.1 us (18%)
  between operations  13.9 us (4%)
  blocking collectives  9.62 us (3%)
  other arithmetic  8.2 us (2%)
  starting transfers between devices  8.11 us (2%)
  local copies, waits for them, and re-layouts  6.27 us (2%)
    reduce_scatter x1, waiting for transfers between devices, on_device(): lax.psum_scatter(dense_down, 'dp', scatter_dimension=0, tiled=True)  75.6 us
    all_gather x1, waiting for transfers between devices, on_device(): lax.all_gather(cotangent, 'tsp', axis=1, tiled=True)  57.5 us
    psum x1, waiting for transfers between devices, on_device(): summed = lax.psum(partial_terms, 'tsp')  50.3 us
    all_to_all x1, waiting for transfers between devices, on_device(): lax.all_to_all(reply_down, 'dp', split_axis=0, concat_axis=0, tiled=True)  25.8 us
    dot_general x1, matrix products, on_device(): lax.dot_general(lax.all_gather(cotangent, 'tsp', axis=1, tiled=True), fro...  15.3 us
    dot_general x1, matrix products, on_device(): jnp.einsum('wks,wsx->wkx', gathered_weights, segment_down_weight, preferr...  14.2 us
    all_to_all x1, blocking collectives, on_device(): lax.all_to_all(wanted[:, None], 'dp', split_axis=0, concat_axis=0, tiled=...  9.62 us
    dot_general x1, matrix products, on_device(): jnp.einsum('gtd,grd->gtr', seg_tokens, segment_down_weight, preferred_ele...  9.23 us
  transfers between devices with their start and end apart: 6, of which 6 were waited for; matrix products, arithmetic and copies ran while one was open for 18% of the time, Pallas kernels for 0%

commit v1 on v0

v1 whole, which is shorter than its diff:
```python
import functools

import jax
import jax.numpy as jnp
from jax import lax
from jax.experimental import pallas as pl
from jax.experimental.pallas import tpu as pltpu
from jax.sharding import PartitionSpec as P

ADAPTER_SCALE = 2.0
ANY = pl.BlockSpec(memory_space=pl.ANY)
SMEM = pl.BlockSpec(memory_space=pltpu.SMEM)
VMEM = pl.BlockSpec(memory_space=pltpu.VMEM)
NT = (((1,), (1,)), ((), ()))
TN = (((0,), (0,)), ((), ()))
NN = (((1,), (0,)), ((), ()))
LIMIT = 56 * 1024 * 1024


def lookup(idents, mapping):
    matches = idents[:, None] == jnp.arange(mapping.shape[0], dtype=jnp.int32)[None, :]
    return jnp.sum(jnp.where(matches, mapping[None, :], 0), axis=1)


def params():
    return pltpu.CompilerParams(vmem_limit_bytes=LIMIT)


def load_all(pairs, sem):
    copies = [pltpu.make_async_copy(src, dst, sem.at[i]) for i, (src, dst) in enumerate(pairs)]
    for copy in copies:
        copy.start()
    for copy in copies:
        copy.wait()


def load_line(z, n, own, ups, downs, dst, sem):
    def each(act):
        act(pltpu.make_async_copy(own, dst(z), sem.at[0]))
        for s in range(1, n):

            @pl.when(z >= s)
            def _():
                act(pltpu.make_async_copy(ups[s - 1], dst(z - s), sem.at[s]))

            @pl.when(z + s < n)
            def _():
                act(pltpu.make_async_copy(downs[s - 1], dst(z + s), sem.at[n - 1 + s]))

    each(lambda copy: copy.start())
    each(lambda copy: copy.wait())


def live_mask(count, rows, width):
    return lax.broadcasted_iota(jnp.int32, (rows, width), 0) < count


def pack_kernel(segs, rows, packed, off, cot, *refs):
    outs, buf = refs[:-1], refs[-1]
    buf[...] = jnp.zeros_like(buf)
    for g in range(segs):
        start = pl.multiple_of(off[g], 16)
        buf[pl.ds(start, rows), :] = cot[g * rows : (g + 1) * rows, :]
    part = packed // len(outs)
    for c, out in enumerate(outs):
        out[...] = buf[c * part : (c + 1) * part, :]


def pack(cot, off, segs, packed, chunks):
    rows, width = cot.shape[0] // segs, cot.shape[1]
    return pl.pallas_call(
        functools.partial(pack_kernel, segs, rows, packed),
        out_shape=[jax.ShapeDtypeStruct((packed // chunks, width), cot.dtype)] * chunks,
        in_specs=[SMEM, VMEM],
        out_specs=[VMEM] * chunks,
        scratch_shapes=[pltpu.VMEM((packed + rows, width), cot.dtype)],
        compiler_params=params(),
        name="pack",
    )(off, cot)


def project_kernel(n, per, rows, packed, n_maps, z, idx, off, count, x, *refs):
    maps, refs = refs[:n_maps], refs[n_maps:]
    outs, (table, buf, sem) = refs[: 2 * n - 1], refs[2 * n - 1 :]
    step = pl.program_id(0)

    @pl.when(step == 0)
    def _():
        each = maps[0].shape[0]
        load_all([(m, table.at[pl.ds(i * each, each)]) for i, m in enumerate(maps)], sem)
        buf[...] = jnp.zeros_like(buf)

    for i in range(per):
        g = step * per + i
        term = lax.dot_general(
            x[i * rows : (i + 1) * rows, :], table[idx[g]], NT, preferred_element_type=jnp.float32
        )
        term = jnp.where(live_mask(count[g], *term.shape), term, 0.0)
        buf[pl.ds(pl.multiple_of(off[g], 16), rows), :] = term

    @pl.when(step == pl.num_programs(0) - 1)
    def _():
        block = packed // n
        half = block // 2

        def paired(j):
            start = pl.multiple_of(j * block, 16)
            return jnp.concatenate(
                [buf[pl.ds(start, half), :], buf[pl.ds(start + half, half), :]], axis=1
            )

        outs[0][...] = paired(z[0])
        for s in range(1, n):
            outs[s][...] = paired(jnp.minimum(z[0] + s, n - 1))
            outs[n - 1 + s][...] = paired(jnp.maximum(z[0] - s, 0))


def project(z, idx, off, count, x, maps, n, packed, per):
    segs = idx.shape[0]
    rows, width = x.shape[0] // segs, x.shape[1]
    ranks = maps[0].shape[1]
    total = sum(m.shape[0] for m in maps)
    block = jax.ShapeDtypeStruct((packed // n // 2, 2 * ranks), jnp.float32)
    return pl.pallas_call(
        functools.partial(project_kernel, n, per, rows, packed, len(maps)),
        grid=(segs // per,),
        out_shape=[block] * (2 * n - 1),
        in_specs=[SMEM] * 4
        + [pl.BlockSpec((per * rows, width), lambda i: (i, 0))]
        + [ANY] * len(maps),
        out_specs=[pl.BlockSpec(block.shape, lambda i: (0, 0))] * (2 * n - 1),
        scratch_shapes=[
            pltpu.VMEM((total, ranks, width), x.dtype),
            pltpu.VMEM((packed + rows, ranks), jnp.float32),
            pltpu.SemaphoreType.DMA((len(maps),)),
        ],
        compiler_params=params(),
        name="project",
    )(z, idx, off, count, x, *maps)


def unpair(n, raw, buf):
    half, ranks = raw.shape[1], raw.shape[2] // 2
    for j in range(n):
        buf[pl.ds(2 * j * half, half), :] = raw[j][:, :ranks]
        buf[pl.ds((2 * j + 1) * half, half), :] = raw[j][:, ranks:]
    tail = buf.shape[0] - 2 * n * half
    buf[pl.ds(2 * n * half, tail), :] = jnp.zeros((tail, ranks), buf.dtype)


def sums_kernel(n, per, rows, scale, z, slot, off, count, x, *refs):
    line, refs = refs[: 2 * n - 1], refs[2 * n - 1 :]
    outs, (raw, buf, total, sem) = refs[:-4], refs[-4:]
    step = pl.program_id(0)

    @pl.when(step == 0)
    def _():
        load_line(z[0], n, line[0], line[1:n], line[n:], lambda j: raw.at[j], sem)
        unpair(n, raw, buf)
        total[...] = jnp.zeros_like(total)

    for i in range(per):
        g = step * per + i
        terms = buf[pl.ds(pl.multiple_of(off[g], 16), rows), :]
        terms = jnp.where(live_mask(count[g], *terms.shape), terms, jnp.zeros_like(terms))
        total[slot[g]] += lax.dot_general(
            terms, x[i * rows : (i + 1) * rows, :], TN, preferred_element_type=jnp.float32
        )

    @pl.when(step == pl.num_programs(0) - 1)
    def _():
        for k, out in enumerate(outs):
            out[...] = (total[k] * scale).astype(out.dtype)


def sums(z, slot, off, count, x, line, n, slots, packed, per):
    segs = slot.shape[0]
    rows, width = x.shape[0] // segs, x.shape[1]
    half, ranks = line[0].shape[0], line[0].shape[1] // 2
    outs = [jax.ShapeDtypeStruct((ranks, width), jnp.float32 if k == 0 else jnp.bfloat16) for k in range(slots)]
    return pl.pallas_call(
        functools.partial(sums_kernel, n, per, rows, ADAPTER_SCALE / rows),
        grid=(segs // per,),
        out_shape=outs,
        in_specs=[SMEM] * 4
        + [pl.BlockSpec((per * rows, width), lambda i: (i, 0))]
        + [ANY] * (2 * n - 1),
        out_specs=[pl.BlockSpec((ranks, width), lambda i: (0, 0))] * slots,
        scratch_shapes=[
            pltpu.VMEM((n, half, 2 * ranks), jnp.bfloat16),
            pltpu.VMEM((packed + rows, ranks), jnp.bfloat16),
            pltpu.VMEM((slots, ranks, width), jnp.float32),
            pltpu.SemaphoreType.DMA((2 * n - 1,)),
        ],
        compiler_params=params(),
        name="sums",
    )(z, slot, off, count, x, *line)


def token_kernel(n, per, rows, packed, chunks, n_maps, z, idx, off, count, weight, *refs):
    line = 2 * n - 1
    maps, refs = refs[:n_maps], refs[n_maps:]
    pulled, refs = refs[:line], refs[line:]
    cots, refs = refs[: chunks * line], refs[chunks * line :]
    out, table, raw, ranks_buf, cot, map_sem, line_sem = refs
    part = packed // chunks
    step = pl.program_id(0)

    @pl.when(step == 0)
    def _():
        each = maps[0].shape[0]
        load_all([(m, table.at[pl.ds(i * each, each)]) for i, m in enumerate(maps)], map_sem)
        load_line(z[0], n, pulled[0], pulled[1:n], pulled[n:], lambda j: raw.at[j], line_sem)
        for c in range(chunks):
            got = cots[c * line : (c + 1) * line]
            load_line(
                z[0], n, got[0], got[1:n], got[n:], lambda j: cot.at[j, pl.ds(c * part, part)], line_sem
            )
        cot[:, pl.ds(packed, rows), :] = jnp.zeros((n, rows, cot.shape[2]), cot.dtype)
        unpair(n, raw, ranks_buf)

    key = cot.shape[2]
    width = weight.shape[0]
    tile = min(512, width)
    starts = [pl.multiple_of(off[step * per + i], 16) for i in range(per)]
    counts = [count[step * per + i] for i in range(per)]
    shards = [
        jnp.concatenate([cot[j, pl.ds(start, rows), :] for start in starts], axis=0) for j in range(n)
    ]
    for d in range(0, width, tile):
        total = lax.dot_general(
            shards[0], weight[d : d + tile, :key], NT, preferred_element_type=jnp.float32
        )
        for j in range(1, n):
            total += lax.dot_general(
                shards[j],
                weight[d : d + tile, j * key : (j + 1) * key],
                NT,
                preferred_element_type=jnp.float32,
            )
        for i in range(per):
            terms = ranks_buf[pl.ds(starts[i], rows), :]
            adapter = lax.dot_general(
                terms, table[idx[step * per + i], :, d : d + tile], NN, preferred_element_type=jnp.float32
            )
            both = total[i * rows : (i + 1) * rows, :] + ADAPTER_SCALE * adapter
            both = jnp.where(live_mask(counts[i], rows, tile), both, 0.0)
            out[i * rows : (i + 1) * rows, d : d + tile] = both.astype(out.dtype)


def token_gradients(z, idx, off, count, weight, maps, pulled, cots, n, packed, rows, per):
    segs = idx.shape[0]
    width = weight.shape[0]
    chunks = len(cots)
    key = cots[0][0].shape[1]
    ranks = maps[0].shape[1]
    total = sum(m.shape[0] for m in maps)
    half = pulled[0].shape[0]
    return pl.pallas_call(
        functools.partial(token_kernel, n, per, rows, packed, chunks, len(maps)),
        grid=(segs // per,),
        out_shape=jax.ShapeDtypeStruct((segs * rows, width), jnp.bfloat16),
        in_specs=[SMEM] * 4
        + [pl.BlockSpec(weight.shape, lambda i: (0, 0), pipeline_mode=pl.Buffered(1))]
        + [ANY] * (len(maps) + (chunks + 1) * (2 * n - 1)),
        out_specs=pl.BlockSpec((per * rows, width), lambda i: (i, 0)),
        scratch_shapes=[
            pltpu.VMEM((total, ranks, width), jnp.bfloat16),
            pltpu.VMEM((n, half, 2 * ranks), jnp.bfloat16),
            pltpu.VMEM((packed + rows, ranks), jnp.bfloat16),
            pltpu.VMEM((n, packed + rows, key), jnp.bfloat16),
            pltpu.SemaphoreType.DMA((len(maps),)),
            pltpu.SemaphoreType.DMA((2 * n - 1,)),
        ],
        compiler_params=params(),
        name="token_gradient",
    )(z, idx, off, count, weight, *maps, *pulled, *[a for got in cots for a in got])


def shift(x, n, by):
    return lax.ppermute(x, "tsp", [(i, i + by) for i in range(n) if 0 <= i + by < n])


def gather_line(x, n):
    ups, downs = [x], [x]
    for _ in range(n - 1):
        ups.append(shift(ups[-1], n, 1))
        downs.append(shift(downs[-1], n, -1))
    return [x] + ups[1:] + downs[1:]


def gather_direct(x, n):
    return [x] + [shift(x, n, s) for s in range(1, n)] + [shift(x, n, -s) for s in range(1, n)]


def reduce_blocks(blocks, n):
    total = blocks[0]
    for s in range(1, n):
        total = total + shift(blocks[s], n, s) + shift(blocks[n - 1 + s], n, -s)
    return total.astype(jnp.bfloat16)


def flip(x, n, by):
    return lax.ppermute(x, "dp", [(i, i ^ by) for i in range(n)])


def gather_maps_small(maps, n):
    same = [maps] + [flip(maps, n, k) for k in (2, 4, 6)]
    other = [flip(m, n, 1) for m in same]
    return [m for pair in zip(same, other) for m in pair]


def gather_maps(maps, n):
    half = maps.shape[0] // 2
    low, high = maps[:half], maps[half:]
    over_x, over_y = [flip(m, n, 2) for m in (low, high)], [flip(m, n, 4) for m in (low, high)]
    corner = [flip(over_x[0], n, 4), flip(over_y[1], n, 2)]
    same = [[low, high], over_x, over_y, corner]
    other = [[flip(m, n, 1) for m in pair] for pair in same]
    return [m for a, b in zip(same, other) for m in a + b]


def on_device(
    tokens,
    cotangent,
    frozen_key_weight,
    adapter_down_weight,
    adapter_up_weight,
    adapter_place_table,
    segment_adapter,
    segment_live_count,
):
    n_dp = lax.axis_size("dp")
    n = lax.axis_size("tsp")
    me = lax.axis_index("dp").astype(jnp.int32)
    z = lax.axis_index("tsp").astype(jnp.int32)[None]
    held = adapter_down_weight.shape[0]
    segs = segment_adapter.shape[0]
    rows = tokens.shape[0] // segs
    packed = segs * rows
    cube = n_dp == 8 and held % 2 == 0

    places = lookup(segment_adapter, adapter_place_table)
    owner, entry = places // held, places % held
    peers = jnp.arange(n_dp, dtype=jnp.int32)
    wanted = jnp.max(jnp.where(owner[:, None] == peers[None, :], entry[:, None], -1), axis=0)
    asked = lax.all_gather(wanted, "dp", axis=0, tiled=False)[:, me]
    slot = owner ^ me
    if cube:
        idx = slot * held + entry
        ups = gather_maps_small(adapter_up_weight, n_dp)
        downs = gather_maps(adapter_down_weight, n_dp)
    else:
        idx = places
        ups = [lax.all_gather(adapter_up_weight, "dp", axis=0, tiled=True)]
        downs = [lax.all_gather(adapter_down_weight, "dp", axis=0, tiled=True)]
    count = segment_live_count
    padded = (count + 15) // 16 * 16
    off = jnp.cumsum(padded) - padded

    chunks = pack(cotangent, off, segs, packed, 2)
    cots = [gather_line(chunk, n) for chunk in chunks]

    pulled = reduce_blocks(project(z, idx, off, count, cotangent, ups, n, packed, segs), n)
    pulled = gather_direct(pulled, n)
    lowered = reduce_blocks(project(z, idx, off, count, tokens, downs, n, packed, 2), n)
    lowered = gather_direct(lowered, n)

    token_gradient = token_gradients(
        z, idx, off, count, frozen_key_weight, downs, pulled, cots, n, packed, rows, 2
    )

    def owned(terms, x, per):
        sent = sums(z, slot, off, count, x, terms, n, n_dp, packed, per)
        if n_dp == 8:
            got = [sent[0]] + [flip(sent[k], n_dp, k) for k in range(1, n_dp)]
        else:
            others = jnp.stack([sent[0].astype(jnp.bfloat16)] + list(sent[1:]))
            others = others[peers ^ me]
            others = lax.all_to_all(others, "dp", 0, 0, tiled=True)
            got = [others[k] for k in range(n_dp)]
        grads = []
        for e in range(held):
            total = 0.0
            for k, term in enumerate(got):
                hit = asked[(me ^ k) if n_dp == 8 else k] == e
                total = total + jnp.where(hit, term.astype(jnp.float32), 0.0)
            grads.append(total)
        return jnp.stack(grads)

    down_grad = owned(pulled, tokens, 2)
    up_grad = owned(lowered, cotangent, segs)
    return (token_gradient, down_grad, up_grad)


def solution(mesh):
    placed = (
        P("dp", "tsp"),
        P("dp", "tsp"),
        P("tsp", None),
        P("dp", None, "tsp"),
        P("dp", None, "tsp"),
        P(),
        P("dp"),
        P("dp"),
    )
    return jax.shard_map(
        on_device,
        mesh=mesh,
        in_specs=placed,
        out_specs=(P("dp", "tsp"), P("dp", None, "tsp"), P("dp", None, "tsp")),
        check_vma=False,
    )
```

time: 329 us -> 260 us (0.79)
  waiting for transfers between devices: 222 us -> 45.3 us
  starting transfers between devices: 8.11 us -> 114 us
  matrix products: 60.1 us -> 0 us
  Pallas kernels: 0 us -> 55.4 us
  blocking collectives: 9.62 us -> 17.4 us
    ppermute x0 -> x71, starting transfers between devices: none -> 114 us  [the longest x36 88.9 us: shift(): lax.ppermute(x, 'tsp', [(i, i + by) for i in range(n) if 0 <= i + by < n])]
    reduce_scatter x2 -> x0, waiting for transfers between devices: 84.5 us -> none  [the longest x1 75.6 us: on_device(): lax.psum_scatter(dense_down, 'dp', scatter_dimension=0, tiled=True)]
    dot_general x12 -> x0, matrix products: 60.1 us -> none  [the longest x1 15.3 us: on_device(): lax.dot_general(lax.all_gather(cotangent, 'tsp', axis=1, tiled=True), fro...]
    all_gather x1 -> x0, waiting for transfers between devices: 57.5 us -> none  [on_device(): lax.all_gather(cotangent, 'tsp', axis=1, tiled=True)]
    pallas_call x0 -> x6, Pallas kernels: none -> 55.4 us  [the longest x1 24.2 us: token_gradients(): pl.pallas_call(functools.partial(token_kernel, n, per, rows, packed, chun...]
    psum x1 -> x0, waiting for transfers between devices: 50.3 us -> none  [on_device(): summed = lax.psum(partial_terms, 'tsp')]
    ppermute x0 -> x71, waiting for transfers between devices: none -> 45.3 us  [the longest x36 38.7 us: shift(): lax.ppermute(x, 'tsp', [(i, i + by) for i in range(n) if 0 <= i + by < n])]
    all_to_all x2 -> x0, waiting for transfers between devices: 29.1 us -> none  [the longest x1 25.8 us: on_device(): lax.all_to_all(reply_down, 'dp', split_axis=0, concat_axis=0, tiled=True)]
  transfers between devices with their start and end apart: 6 -> 71, of which waited for: 6 -> 17; matrix products, arithmetic and copies ran while one was open for 18% -> 5% of each run, Pallas kernels for 0% -> 12%
where the time goes in v1:
time: 260 us; the launch traced here: 258 us
  starting transfers between devices  114 us (44%)
  Pallas kernels  55.4 us (21%)
  waiting for transfers between devices  45.3 us (17%)
  blocking collectives  17.4 us (7%)
  between operations  12.6 us (5%)
  other arithmetic  9.16 us (4%)
  local copies, waits for them, and re-layouts  4.46 us (2%)
    ppermute x36, starting transfers between devices, shift(): lax.ppermute(x, 'tsp', [(i, i + by) for i in range(n) if 0 <= i + by < n])  88.9 us
    ppermute x36, waiting for transfers between devices, shift(): lax.ppermute(x, 'tsp', [(i, i + by) for i in range(n) if 0 <= i + by < n])  38.7 us
    ppermute x35, starting transfers between devices, flip(): return lax.ppermute(x, 'dp', [(i, i ^ by) for i in range(n)])  25 us
    pallas_call x1, Pallas kernels, token_gradients(): pl.pallas_call(functools.partial(token_kernel, n, per, rows, packed, chun...  24.2 us
    unnamed x1, blocking collectives  17.4 us
    pallas_call x2, Pallas kernels, project(): pl.pallas_call(functools.partial(project_kernel, n, per, rows, packed, le...  15 us
    pallas_call x2, Pallas kernels, sums(): pl.pallas_call(functools.partial(sums_kernel, n, per, rows, ADAPTER_SCALE...  13.8 us
    ppermute x35, waiting for transfers between devices, flip(): return lax.ppermute(x, 'dp', [(i, i ^ by) for i in range(n)])  6.57 us
  transfers between devices with their start and end apart: 71, of which 17 were waited for; matrix products, arithmetic and copies ran while one was open for 5% of the time, Pallas kernels for 12%

profile of v1, /device:TPU:0, one launch (start us, length us, event | category | flops | bytes accessed | tf_op | source)
XLA Modules:
  0.0 258.2 jit_solution(11914919361143279648)
XLA Ops:
  1.1 2.6 collective-permute-start.15
  3.7 1.5 collective-permute-start.17
  8.2 2.4 collective-permute-done.19.refs_6_
  10.6 1.3 fusion.35.off
  12.6 1.5 collective-permute-start.3
  14.6 1.5 collective-permute-start.7
  17.7 3.9 %project.2 = (f32[256,128]{1,0:T(8,128)}, f32[256,128]{1,0:T(8,128)}, f32[256,128]{1,0:T(8,128)}, f32[256,128]{1,0:T(8,128)}, f32[256,128]{1,0:T(8,128)}, /*index=5*/f32[256,128]{1,0:T(8,128)}, f32[256,128]{1,0:T(8,128)}) custom-call(s32[1]{0:T(128)} %bitcast.z, s32[16]{0:T(128)} %get-tuple-element.67.idx, s32[16]{0:T(128)} %fusion.35.off, s32[16]{0:T(128)} %count.9, ...), custom_call_target="tpu_custom_call" | custom-call | tf_op jit(solution)/shard_map/project/pallas_call | solution.py:124
  21.6 1.3 collective-permute-start.26
  22.9 6.4 %collective-permute-start.25 = (f32[256,128]{1,0:T(8,128)}, f32[256,128]{1,0:T(8,128)S(1)}, u32[]{:S(2)}, u32[]{:S(2)}) collective-permute-start(f32[256,128]{1,0:T(8,128)} %get-tuple-element.40), channel_id=1, source_target_pairs={{0,3},{4,7},{8,11},{12,15},{16,19},{20,23},{24,27},{28,31}} | collective-permute-start | bytes 393224 | tf_op jit(solution)/shard_map/ppermute | solution.py:281
  29.3 1.3 collective-permute-start.24
  30.6 5.5 %collective-permute-start.23 = (f32[256,128]{1,0:T(8,128)}, f32[256,128]{1,0:T(8,128)S(1)}, u32[]{:S(2)}, u32[]{:S(2)}) collective-permute-start(f32[256,128]{1,0:T(8,128)} %get-tuple-element.38), channel_id=1, source_target_pairs={{0,2},{1,3},{4,6},{5,7},{8,10},{9,11},{12,14},{13,15},{16,18},{17,... | collective-permute-start | bytes 393224 | tf_op jit(solution)/shard_map/ppermute | solution.py:281
  36.1 1.3 collective-permute-start.22
  39.4 3.7 %collective-permute-done.22 = f32[256,128]{1,0:T(8,128)S(1)} collective-permute-done((f32[256,128]{1,0:T(8,128)}, f32[256,128]{1,0:T(8,128)S(1)}, u32[]{:S(2)}, u32[]{:S(2)}) %collective-permute-start.22) | collective-permute-done | bytes 131104 | tf_op jit(solution)/shard_map/ppermute | solution.py:281
  43.1 1.6 collective-permute-start.21
  44.7 2.4 pack.1
  47.5 4.3 %collective-permute-start.33 = (bf16[1024,256]{1,0:T(8,128)(2,1)}, bf16[1024,256]{1,0:T(8,128)(2,1)S(1)}, u32[]{:S(2)}, u32[]{:S(2)}) collective-permute-start(bf16[1024,256]{1,0:T(8,128)(2,1)} %get-tuple-element.42.refs_23_), channel_id=1, source_target_pairs={{0,1},{1,2},{2,3},{4,5},{5,6},{6,7},{8,9},{9,10},{10,11},{12,13},{... | collective-permute-start | bytes 1572872 | tf_op jit(solution)/shard_map/ppermute | solution.py:281
  53.9 2.3 collective-permute-start.27
  56.2 1.4 collective-permute-start.28
  57.6 1.3 collective-permute-start.29
  58.9 1.3 collective-permute-start.30
  60.4 11.1 %project.3 = (f32[256,128]{1,0:T(8,128)}, f32[256,128]{1,0:T(8,128)}, f32[256,128]{1,0:T(8,128)}, f32[256,128]{1,0:T(8,128)}, f32[256,128]{1,0:T(8,128)}, /*index=5*/f32[256,128]{1,0:T(8,128)}, f32[256,128]{1,0:T(8,128)}) custom-call(s32[1]{0:T(128)} %bitcast.z, s32[16]{0:T(128)} %get-tuple-element.67.idx, s32[16]{0:T(128)} %fusion.35.off, s32[16]{0:T(128)} %count.9, ...), custom_call_target="tpu_custom_call" | custom-call | tf_op jit(solution)/shard_map/project/pallas_call | solution.py:124
  71.6 1.4 collective-permute-start.57
  73.0 6.4 %collective-permute-start.56 = (f32[256,128]{1,0:T(8,128)}, f32[256,128]{1,0:T(8,128)S(1)}, u32[]{:S(2)}, u32[]{:S(2)}) collective-permute-start(f32[256,128]{1,0:T(8,128)} %get-tuple-element.57), channel_id=1, source_target_pairs={{0,3},{4,7},{8,11},{12,15},{16,19},{20,23},{24,27},{28,31}} | collective-permute-start | bytes 393224 | tf_op jit(solution)/shard_map/ppermute | solution.py:281
  79.4 1.3 collective-permute-start.31
  80.7 1.3 collective-permute-start.32
  82.0 5.1 %collective-permute-done.31.refs_21_.refs_5_ = bf16[256,128]{1,0:T(8,128)(2,1)S(1)} collective-permute-done((bf16[256,128]{1,0:T(8,128)(2,1)S(1)}, bf16[256,128]{1,0:T(8,128)(2,1)S(1)}, u32[]{:S(2)}, u32[]{:S(2)}) %collective-permute-start.31) | collective-permute-done | bytes 65568 | tf_op jit(solution)/shard_map/ppermute | solution.py:281
  87.2 1.3 collective-permute-start.36
  89.0 1.3 collective-permute-start.55
  90.3 5.5 %collective-permute-start.54 = (f32[256,128]{1,0:T(8,128)}, f32[256,128]{1,0:T(8,128)S(1)}, u32[]{:S(2)}, u32[]{:S(2)}) collective-permute-start(f32[256,128]{1,0:T(8,128)} %get-tuple-element.55), channel_id=1, source_target_pairs={{0,2},{1,3},{4,6},{5,7},{8,10},{9,11},{12,14},{13,15},{16,18},{17,... | collective-permute-start | bytes 393224 | tf_op jit(solution)/shard_map/ppermute | solution.py:281
  95.8 4.1 %collective-permute-start.39 = (bf16[1024,256]{1,0:T(8,128)(2,1)S(1)}, bf16[1024,256]{1,0:T(8,128)(2,1)S(1)}, u32[]{:S(2)}, u32[]{:S(2)}) collective-permute-start(bf16[1024,256]{1,0:T(8,128)(2,1)S(1)} %copy-done.18), channel_id=1, source_target_pairs={{0,1},{1,2},{2,3},{4,5},{5,6},{6,7},{8,9},{9,10},{10,11},{12,13},{... | collective-permute-start | bytes 1572872 | tf_op jit(solution)/shard_map/ppermute | solution.py:281
  99.9 1.3 collective-permute-start.42
  101.2 5.3 %collective-permute-done.55 = f32[256,128]{1,0:T(8,128)S(1)} collective-permute-done((f32[256,128]{1,0:T(8,128)}, f32[256,128]{1,0:T(8,128)S(1)}, u32[]{:S(2)}, u32[]{:S(2)}) %collective-permute-start.55) | collective-permute-done | bytes 131104 | tf_op jit(solution)/shard_map/ppermute | solution.py:281
  106.5 1.3 collective-permute-start.53
  107.8 4.6 %collective-permute-start.52 = (f32[256,128]{1,0:T(8,128)}, f32[256,128]{1,0:T(8,128)S(1)}, u32[]{:S(2)}, u32[]{:S(2)}) collective-permute-start(f32[256,128]{1,0:T(8,128)} %get-tuple-element.53), channel_id=1, source_target_pairs={{0,1},{1,2},{2,3},{4,5},{5,6},{6,7},{8,9},{9,10},{10,11},{12,13},{... | collective-permute-start | bytes 393224 | tf_op jit(solution)/shard_map/ppermute | solution.py:281
  112.4 10.2 %sums.2 = (f32[64,2048]{1,0:T(8,128)}, bf16[64,2048]{1,0:T(8,128)(2,1)}, bf16[64,2048]{1,0:T(8,128)(2,1)}, bf16[64,2048]{1,0:T(8,128)(2,1)}, bf16[64,2048]{1,0:T...) custom-call(s32[1]{0:T(128)} %bitcast.z, s32[16]{0:T(128)} %get-tuple-element.68.slot, ...), custom_call_target="tpu_custom_call" | custom-call | tf_op jit(solution)/shard_map/sums/pallas_call | solution.py:181
  122.8 1.5 collective-permute-start.46
  124.4 1.9 collective-permute-start.58
  126.3 1.6 collective-permute-start.59
  127.9 1.3 collective-permute-start.60
  129.2 1.3 collective-permute-start.61
  131.7 1.3 collective-permute-start.62
  133.0 1.3 collective-permute-start.63
  135.6 1.7 collective-permute-start.49
  137.3 1.7 collective-permute-done.62.refs_5_
  139.0 2.6 %collective-permute-start.50 = (bf16[64,2048]{1,0:T(8,128)(2,1)}, bf16[64,2048]{1,0:T(8,128)(2,1)S(1)}, u32[]{:S(2)}, u32[]{:S(2)}) collective-permute-start(bf16[64,2048]{1,0:T(8,128)(2,1)} %get-tuple-element.50), channel_id=1, source_target_pairs={{0,24},{4,28},{8,16},{12,20},{16,8},{20,12},{24,0},{28,4},{1,25},{... | collective-permute-start | bytes 786440 | tf_op jit(solution)/shard_map/ppermute | solution.py:304
  144.0 17.4 %all-reduce = s32[64]{0:T(128)S(1)} all-reduce(s32[64]{0:T(128)S(1)} %dynamic-update-slice), channel_id=2, replica_groups=mesh['dp'=8,'tsp'=4] {'dp'}, use_global_device_ids=true, to_apply=%add | all-reduce | flops 64 | bytes 512
  172.2 3.6 %sums.3 = (f32[64,256]{1,0:T(8,128)}, bf16[64,256]{1,0:T(8,128)(2,1)}, bf16[64,256]{1,0:T(8,128)(2,1)}, bf16[64,256]{1,0:T(8,128)(2,1)}, bf16[64,256]{1,0:T(8,12...) custom-call(s32[1]{0:T(128)} %bitcast.z, s32[16]{0:T(128)} %get-tuple-element.68.slot, ...), custom_call_target="tpu_custom_call" | custom-call | tf_op jit(solution)/shard_map/sums/pallas_call | solution.py:181
  176.5 1.2 collective-permute-start.66
  179.8 1.9 collective-permute-start.34
  181.7 1.3 collective-permute-start.37
  183.0 5.9 %collective-permute-start.40 = (bf16[1024,256]{1,0:T(8,128)(2,1)S(1)}, bf16[1024,256]{1,0:T(8,128)(2,1)S(1)}, u32[]{:S(2)}, u32[]{:S(2)}) collective-permute-start(bf16[1024,256]{1,0:T(8,128)(2,1)S(1)} %collective-permute-done.39.refs_31_), channel_id=1, source_target_pairs={{0,1},{1,2},{2,3},{4,5},{5,6},{6,7},{8,9},{9,10},{10,11},{12,13},{... | collective-permute-start | bytes 1572872 | tf_op jit(solution)/shard_map/ppermute | solution.py:281
  188.9 1.3 collective-permute-start.43
  191.4 1.4 fusion.7
  192.8 2.7 %collective-permute-done.69 = bf16[64,256]{1,0:T(8,128)(2,1)S(1)} collective-permute-done((bf16[64,256]{1,0:T(8,128)(2,1)}, bf16[64,256]{1,0:T(8,128)(2,1)S(1)}, u32[]{:S(2)}, u32[]{:S(2)}) %collective-permute-start.69) | collective-permute-done | bytes 32800 | tf_op jit(solution)/shard_map/ppermute | solution.py:304
  197.4 4.6 %collective-permute-start.35 = (bf16[1024,256]{1,0:T(8,128)(2,1)S(1)}, bf16[1024,256]{1,0:T(8,128)(2,1)S(1)}, u32[]{:S(2)}, u32[]{:S(2)}) collective-permute-start(bf16[1024,256]{1,0:T(8,128)(2,1)S(1)} %collective-permute-done.34.refs_25_), channel_id=1, source_target_pairs={{0,1},{1,2},{2,3},{4,5},{5,6},{6,7},{8,9},{9,10},{10,11},{12,13},{... | collective-permute-start | bytes 1572872 | tf_op jit(solution)/shard_map/ppermute | solution.py:281
  202.0 1.3 collective-permute-start.38
  203.3 1.4 collective-permute-done.40.refs_32_
  204.8 5.4 %collective-permute-start.41 = (bf16[1024,256]{1,0:T(8,128)(2,1)S(1)}, bf16[1024,256]{1,0:T(8,128)(2,1)S(1)}, u32[]{:S(2)}, u32[]{:S(2)}) collective-permute-start(bf16[1024,256]{1,0:T(8,128)(2,1)S(1)} %collective-permute-done.40.refs_32_), channel_id=1, source_target_pairs={{0,1},{1,2},{2,3},{4,5},{5,6},{6,7},{8,9},{9,10},{10,11},{12,13},{... | collective-permute-start | bytes 1572872 | tf_op jit(solution)/shard_map/ppermute | solution.py:281
  210.6 1.3 collective-permute-start.44
  213.6 2.4 collective-permute-done.35.refs_26_
  216.0 5.9 %collective-permute-done.38.refs_29_ = bf16[1024,256]{1,0:T(8,128)(2,1)S(1)} collective-permute-done((bf16[1024,256]{1,0:T(8,128)(2,1)S(1)}, bf16[1024,256]{1,0:T(8,128)(2,1)S(1)}, u32[]{:S(2)}, u32[]{:S(2)}) %collective-permute-start.38) | collective-permute-done | bytes 524320 | tf_op jit(solution)/shard_map/ppermute | solution.py:281
  221.9 5.4 %collective-permute-done.41.refs_33_ = bf16[1024,256]{1,0:T(8,128)(2,1)S(1)} collective-permute-done((bf16[1024,256]{1,0:T(8,128)(2,1)S(1)}, bf16[1024,256]{1,0:T(8,128)(2,1)S(1)}, u32[]{:S(2)}, u32[]{:S(2)}) %collective-permute-start.41) | collective-permute-done | bytes 524320 | tf_op jit(solution)/shard_map/ppermute | solution.py:281
  227.3 5.9 %collective-permute-done.44.refs_36_ = bf16[1024,256]{1,0:T(8,128)(2,1)S(1)} collective-permute-done((bf16[1024,256]{1,0:T(8,128)(2,1)S(1)}, bf16[1024,256]{1,0:T(8,128)(2,1)S(1)}, u32[]{:S(2)}, u32[]{:S(2)}) %collective-permute-start.44) | collective-permute-done | bytes 524320 | tf_op jit(solution)/shard_map/ppermute | solution.py:281
  234.0 24.2 %token_gradient.1 = bf16[2048,2048]{1,0:T(8,128)(2,1)} custom-call(s32[1]{0:T(128)} %bitcast.z, s32[16]{0:T(128)} %get-tuple-element.67.idx, s32[16]{0:T(128)} %fusion.35.off, s32[16]{0:T(128)} %count.9, bf16[2048,1024]{1,0:T(8,128)(2,1)} %weight.1, bf16[1,64,2048]{2,1,0:T(8,128)(2,1)} %copy-done.1, bf16[1,64,2048]{2,1,0:T(8,128)(2,1)} %copy-done, ...), custom_call_target="tpu_custom_call" | custom-call | tf_op jit(solution)/shard_map/token_gradient/pallas_call | solution.py:259
  (213 shorter events, 25.2 us)
Async XLA Ops:
  0.6 11.2 %collective-permute-start.14 = (bf16[2,64,256]{2,1,0:T(8,128)(2,1)}, bf16[2,64,256]{2,1,0:T(8,128)(2,1)S(1)}, u32[]{:S(2)}, u32[]{:S(2)}) collective-permute-start(bf16[2,64,256]{2,1,0:T(8,128)(2,1)} %refs_0_.1), channel_id=1, source_target_pairs={{0,4},{4,0},{8,12},{12,8},{16,20},{20,16},{24,28},{28,24},{1,5},{5... | collective-permute-start | bytes 196616 | tf_op jit(solution)/shard_map/ppermute | solution.py:304
  1.1 6.2 %collective-permute-start.15 = (bf16[2,64,256]{2,1,0:T(8,128)(2,1)}, bf16[2,64,256]{2,1,0:T(8,128)(2,1)S(1)}, u32[]{:S(2)}, u32[]{:S(2)}) collective-permute-start(bf16[2,64,256]{2,1,0:T(8,128)(2,1)} %refs_0_.1), channel_id=1, source_target_pairs={{0,8},{4,12},{8,0},{12,4},{16,24},{20,28},{24,16},{28,20},{1,9},{5... | collective-permute-start | bytes 196616 | tf_op jit(solution)/shard_map/ppermute | solution.py:304
  5.2 5.4 %collective-permute-start.19 = (bf16[2,64,256]{2,1,0:T(8,128)(2,1)}, bf16[2,64,256]{2,1,0:T(8,128)(2,1)S(1)}, u32[]{:S(2)}, u32[]{:S(2)}) collective-permute-start(bf16[2,64,256]{2,1,0:T(8,128)(2,1)} %refs_0_.1), channel_id=1, source_target_pairs={{0,24},{4,28},{8,16},{12,20},{16,8},{20,12},{24,0},{28,4},{1,25},{... | collective-permute-start | bytes 196616 | tf_op jit(solution)/shard_map/ppermute | solution.py:304
  6.4 8.3 %collective-permute-start = (bf16[1,64,2048]{2,1,0:T(8,128)(2,1)S(1)}, bf16[1,64,2048]{2,1,0:T(8,128)(2,1)S(1)}, u32[]{:S(2)}, u32[]{:S(2)}) collective-permute-start(bf16[1,64,2048]{2,1,0:T(8,128)(2,1)S(1)} %get-tuple-element.72.refs_0_), channel_id=1, source_target_pairs={{0,4},{4,0},{8,12},{12,8},{16,20},{20,16},{24,28},{28,24},{1,5},{5... | collective-permute-start | bytes 786440 | tf_op jit(solution)/shard_map/ppermute | solution.py:304
  7.4 5.0 %collective-permute-start.16 = (bf16[2,64,256]{2,1,0:T(8,128)(2,1)S(1)}, bf16[2,64,256]{2,1,0:T(8,128)(2,1)S(1)}, u32[]{:S(2)}, u32[]{:S(2)}) collective-permute-start(bf16[2,64,256]{2,1,0:T(8,128)(2,1)S(1)} %collective-permute-done.15.refs_2_), channel_id=1, source_target_pairs={{0,4},{4,0},{8,12},{12,8},{16,20},{20,16},{24,28},{28,24},{1,5},{5... | collective-permute-start | bytes 196616 | tf_op jit(solution)/shard_map/ppermute | solution.py:304
  11.9 11.0 %collective-permute-start.2 = (bf16[1,64,2048]{2,1,0:T(8,128)(2,1)S(1)}, bf16[1,64,2048]{2,1,0:T(8,128)(2,1)S(1)}, u32[]{:S(2)}, u32[]{:S(2)}) collective-permute-start(bf16[1,64,2048]{2,1,0:T(8,128)(2,1)S(1)} %get-tuple-element.72.refs_0_), channel_id=1, source_target_pairs={{0,8},{4,12},{8,0},{12,4},{16,24},{20,28},{24,16},{28,20},{1,9},{5... | collective-permute-start | bytes 786440 | tf_op jit(solution)/shard_map/ppermute | solution.py:304
  12.4 9.1 %collective-permute-start.1 = (bf16[1,64,2048]{2,1,0:T(8,128)(2,1)S(1)}, bf16[1,64,2048]{2,1,0:T(8,128)(2,1)S(1)}, u32[]{:S(2)}, u32[]{:S(2)}) collective-permute-start(bf16[1,64,2048]{2,1,0:T(8,128)(2,1)S(1)} %get-tuple-element.71.refs_1_), channel_id=1, source_target_pairs={{0,4},{4,0},{8,12},{12,8},{16,20},{20,16},{24,28},{28,24},{1,5},{5... | collective-permute-start | bytes 786440 | tf_op jit(solution)/shard_map/ppermute | solution.py:304
  12.6 16.6 %collective-permute-start.3 = (bf16[1,64,2048]{2,1,0:T(8,128)(2,1)S(1)}, bf16[1,64,2048]{2,1,0:T(8,128)(2,1)S(1)}, u32[]{:S(2)}, u32[]{:S(2)}) collective-permute-start(bf16[1,64,2048]{2,1,0:T(8,128)(2,1)S(1)} %get-tuple-element.71.refs_1_), channel_id=1, source_target_pairs={{0,8},{4,12},{8,0},{12,4},{16,24},{20,28},{24,16},{28,20},{1,9},{5... | collective-permute-start | bytes 786440 | tf_op jit(solution)/shard_map/ppermute | solution.py:304
  14.1 16.4 %collective-permute-start.6 = (bf16[1,64,2048]{2,1,0:T(8,128)(2,1)S(1)}, bf16[1,64,2048]{2,1,0:T(8,128)(2,1)S(1)}, u32[]{:S(2)}, u32[]{:S(2)}) collective-permute-start(bf16[1,64,2048]{2,1,0:T(8,128)(2,1)S(1)} %get-tuple-element.72.refs_0_), channel_id=1, source_target_pairs={{0,16},{4,20},{8,24},{12,28},{16,0},{20,4},{24,8},{28,12},{1,17},{... | collective-permute-start | bytes 786440 | tf_op jit(solution)/shard_map/ppermute | solution.py:304
  14.6 21.4 %collective-permute-start.7 = (bf16[1,64,2048]{2,1,0:T(8,128)(2,1)S(1)}, bf16[1,64,2048]{2,1,0:T(8,128)(2,1)S(1)}, u32[]{:S(2)}, u32[]{:S(2)}) collective-permute-start(bf16[1,64,2048]{2,1,0:T(8,128)(2,1)S(1)} %get-tuple-element.71.refs_1_), channel_id=1, source_target_pairs={{0,16},{4,20},{8,24},{12,28},{16,0},{20,4},{24,8},{28,12},{1,17},{... | collective-permute-start | bytes 786440 | tf_op jit(solution)/shard_map/ppermute | solution.py:304
  21.6 15.8 %collective-permute-start.26 = (f32[256,128]{1,0:T(8,128)}, f32[256,128]{1,0:T(8,128)S(1)}, u32[]{:S(2)}, u32[]{:S(2)}) collective-permute-start(f32[256,128]{1,0:T(8,128)} %get-tuple-element.41), channel_id=1, source_target_pairs={{3,0},{7,4},{11,8},{15,12},{19,16},{23,20},{27,24},{31,28}} | collective-permute-start | bytes 393224 | tf_op jit(solution)/shard_map/ppermute | solution.py:281
  22.9 14.6 %collective-permute-start.25 = (f32[256,128]{1,0:T(8,128)}, f32[256,128]{1,0:T(8,128)S(1)}, u32[]{:S(2)}, u32[]{:S(2)}) collective-permute-start(f32[256,128]{1,0:T(8,128)} %get-tuple-element.40), channel_id=1, source_target_pairs={{0,3},{4,7},{8,11},{12,15},{16,19},{20,23},{24,27},{28,31}} | collective-permute-start | bytes 393224 | tf_op jit(solution)/shard_map/ppermute | solution.py:281
  29.3 9.1 %collective-permute-start.24 = (f32[256,128]{1,0:T(8,128)}, f32[256,128]{1,0:T(8,128)S(1)}, u32[]{:S(2)}, u32[]{:S(2)}) collective-permute-start(f32[256,128]{1,0:T(8,128)} %get-tuple-element.39), channel_id=1, source_target_pairs={{2,0},{3,1},{6,4},{7,5},{10,8},{11,9},{14,12},{15,13},{18,16},{19,... | collective-permute-start | bytes 393224 | tf_op jit(solution)/shard_map/ppermute | solution.py:281
  30.6 8.3 %collective-permute-start.23 = (f32[256,128]{1,0:T(8,128)}, f32[256,128]{1,0:T(8,128)S(1)}, u32[]{:S(2)}, u32[]{:S(2)}) collective-permute-start(f32[256,128]{1,0:T(8,128)} %get-tuple-element.38), channel_id=1, source_target_pairs={{0,2},{1,3},{4,6},{5,7},{8,10},{9,11},{12,14},{13,15},{16,18},{17,... | collective-permute-start | bytes 393224 | tf_op jit(solution)/shard_map/ppermute | solution.py:281
  36.1 7.1 %collective-permute-start.22 = (f32[256,128]{1,0:T(8,128)}, f32[256,128]{1,0:T(8,128)S(1)}, u32[]{:S(2)}, u32[]{:S(2)}) collective-permute-start(f32[256,128]{1,0:T(8,128)} %get-tuple-element.37), channel_id=1, source_target_pairs={{1,0},{2,1},{3,2},{5,4},{6,5},{7,6},{9,8},{10,9},{11,10},{13,12},{... | collective-permute-start | bytes 393224 | tf_op jit(solution)/shard_map/ppermute | solution.py:281
  37.4 14.4 %collective-permute-start.4 = (bf16[1,64,2048]{2,1,0:T(8,128)(2,1)S(1)}, bf16[1,64,2048]{2,1,0:T(8,128)(2,1)S(1)}, u32[]{:S(2)}, u32[]{:S(2)}) collective-permute-start(bf16[1,64,2048]{2,1,0:T(8,128)(2,1)S(1)} %collective-permute-done.2.refs_4_), channel_id=1, source_target_pairs={{0,4},{4,0},{8,12},{12,8},{16,20},{20,16},{24,28},{28,24},{1,5},{5... | collective-permute-start | bytes 786440 | tf_op jit(solution)/shard_map/ppermute | solution.py:304
  37.5 14.5 %collective-permute-start.5 = (bf16[1,64,2048]{2,1,0:T(8,128)(2,1)S(1)}, bf16[1,64,2048]{2,1,0:T(8,128)(2,1)S(1)}, u32[]{:S(2)}, u32[]{:S(2)}) collective-permute-start(bf16[1,64,2048]{2,1,0:T(8,128)(2,1)S(1)} %collective-permute-done.3.refs_5_), channel_id=1, source_target_pairs={{0,4},{4,0},{8,12},{12,8},{16,20},{20,16},{24,28},{28,24},{1,5},{5... | collective-permute-start | bytes 786440 | tf_op jit(solution)/shard_map/ppermute | solution.py:304
  38.3 14.1 %collective-permute-start.10 = (bf16[1,64,2048]{2,1,0:T(8,128)(2,1)S(1)}, bf16[1,64,2048]{2,1,0:T(8,128)(2,1)S(1)}, u32[]{:S(2)}, u32[]{:S(2)}) collective-permute-start(bf16[1,64,2048]{2,1,0:T(8,128)(2,1)S(1)} %collective-permute-done.2.refs_4_), channel_id=1, source_target_pairs={{0,16},{4,20},{8,24},{12,28},{16,0},{20,4},{24,8},{28,12},{1,17},{... | collective-permute-start | bytes 786440 | tf_op jit(solution)/shard_map/ppermute | solution.py:304
  38.9 13.7 %collective-permute-start.11 = (bf16[1,64,2048]{2,1,0:T(8,128)(2,1)S(1)}, bf16[1,64,2048]{2,1,0:T(8,128)(2,1)S(1)}, u32[]{:S(2)}, u32[]{:S(2)}) collective-permute-start(bf16[1,64,2048]{2,1,0:T(8,128)(2,1)S(1)} %collective-permute-done.7.refs_9_), channel_id=1, source_target_pairs={{0,8},{4,12},{8,0},{12,4},{16,24},{20,28},{24,16},{28,20},{1,9},{5... | collective-permute-start | bytes 786440 | tf_op jit(solution)/shard_map/ppermute | solution.py:304
  47.5 42.8 %collective-permute-start.33 = (bf16[1024,256]{1,0:T(8,128)(2,1)}, bf16[1024,256]{1,0:T(8,128)(2,1)S(1)}, u32[]{:S(2)}, u32[]{:S(2)}) collective-permute-start(bf16[1024,256]{1,0:T(8,128)(2,1)} %get-tuple-element.42.refs_23_), channel_id=1, source_target_pairs={{0,1},{1,2},{2,3},{4,5},{5,6},{6,7},{8,9},{9,10},{10,11},{12,13},{... | collective-permute-start | bytes 1572872 | tf_op jit(solution)/shard_map/ppermute | solution.py:281
  52.4 5.2 %collective-permute-start.12 = (bf16[1,64,2048]{2,1,0:T(8,128)(2,1)S(1)}, bf16[1,64,2048]{2,1,0:T(8,128)(2,1)S(1)}, u32[]{:S(2)}, u32[]{:S(2)}) collective-permute-start(bf16[1,64,2048]{2,1,0:T(8,128)(2,1)S(1)} %collective-permute-done.10.refs_12_), channel_id=1, source_target_pairs={{0,4},{4,0},{8,12},{12,8},{16,20},{20,16},{24,28},{28,24},{1,5},{5... | collective-permute-start | bytes 786440 | tf_op jit(solution)/shard_map/ppermute | solution.py:304
  52.5 6.4 %collective-permute-start.13 = (bf16[1,64,2048]{2,1,0:T(8,128)(2,1)S(1)}, bf16[1,64,2048]{2,1,0:T(8,128)(2,1)S(1)}, u32[]{:S(2)}, u32[]{:S(2)}) collective-permute-start(bf16[1,64,2048]{2,1,0:T(8,128)(2,1)S(1)} %collective-permute-done.11.refs_13_), channel_id=1, source_target_pairs={{0,4},{4,0},{8,12},{12,8},{16,20},{20,16},{24,28},{28,24},{1,5},{5... | collective-permute-start | bytes 786440 | tf_op jit(solution)/shard_map/ppermute | solution.py:304
  53.9 17.6 %collective-permute-start.27 = (bf16[256,128]{1,0:T(8,128)(2,1)S(1)}, bf16[256,128]{1,0:T(8,128)(2,1)S(1)}, u32[]{:S(2)}, u32[]{:S(2)}) collective-permute-start(bf16[256,128]{1,0:T(8,128)(2,1)S(1)} %add_convert_fusion.1.refs_16_.refs_0_), channel_id=1, source_target_pairs={{0,1},{1,2},{2,3},{4,5},{5,6},{6,7},{8,9},{9,10},{10,11},{12,13},{... | collective-permute-start | bytes 196616 | tf_op jit(solution)/shard_map/ppermute | solution.py:281
  56.2 16.8 %collective-permute-start.28 = (bf16[256,128]{1,0:T(8,128)(2,1)S(1)}, bf16[256,128]{1,0:T(8,128)(2,1)S(1)}, u32[]{:S(2)}, u32[]{:S(2)}) collective-permute-start(bf16[256,128]{1,0:T(8,128)(2,1)S(1)} %add_convert_fusion.1.refs_16_.refs_0_), channel_id=1, source_target_pairs={{0,2},{1,3},{4,6},{5,7},{8,10},{9,11},{12,14},{13,15},{16,18},{17,... | collective-permute-start | bytes 196616 | tf_op jit(solution)/shard_map/ppermute | solution.py:281
  57.6 21.8 %collective-permute-start.29 = (bf16[256,128]{1,0:T(8,128)(2,1)S(1)}, bf16[256,128]{1,0:T(8,128)(2,1)S(1)}, u32[]{:S(2)}, u32[]{:S(2)}) collective-permute-start(bf16[256,128]{1,0:T(8,128)(2,1)S(1)} %add_convert_fusion.1.refs_16_.refs_0_), channel_id=1, source_target_pairs={{0,3},{4,7},{8,11},{12,15},{16,19},{20,23},{24,27},{28,31}} | collective-permute-start | bytes 196616 | tf_op jit(solution)/shard_map/ppermute | solution.py:281
  58.9 21.8 %collective-permute-start.30 = (bf16[256,128]{1,0:T(8,128)(2,1)S(1)}, bf16[256,128]{1,0:T(8,128)(2,1)S(1)}, u32[]{:S(2)}, u32[]{:S(2)}) collective-permute-start(bf16[256,128]{1,0:T(8,128)(2,1)S(1)} %add_convert_fusion.1.refs_16_.refs_0_), channel_id=1, source_target_pairs={{1,0},{2,1},{3,2},{5,4},{6,5},{7,6},{9,8},{10,9},{11,10},{13,12},{... | collective-permute-start | bytes 196616 | tf_op jit(solution)/shard_map/ppermute | solution.py:281
  71.6 24.2 %collective-permute-start.57 = (f32[256,128]{1,0:T(8,128)}, f32[256,128]{1,0:T(8,128)S(1)}, u32[]{:S(2)}, u32[]{:S(2)}) collective-permute-start(f32[256,128]{1,0:T(8,128)} %get-tuple-element.58), channel_id=1, source_target_pairs={{3,0},{7,4},{11,8},{15,12},{19,16},{23,20},{27,24},{31,28}} | collective-permute-start | bytes 393224 | tf_op jit(solution)/shard_map/ppermute | solution.py:281
  73.0 26.9 %collective-permute-start.56 = (f32[256,128]{1,0:T(8,128)}, f32[256,128]{1,0:T(8,128)S(1)}, u32[]{:S(2)}, u32[]{:S(2)}) collective-permute-start(f32[256,128]{1,0:T(8,128)} %get-tuple-element.57), channel_id=1, source_target_pairs={{0,3},{4,7},{8,11},{12,15},{16,19},{20,23},{24,27},{28,31}} | collective-permute-start | bytes 393224 | tf_op jit(solution)/shard_map/ppermute | solution.py:281
  79.4 7.8 %collective-permute-start.31 = (bf16[256,128]{1,0:T(8,128)(2,1)S(1)}, bf16[256,128]{1,0:T(8,128)(2,1)S(1)}, u32[]{:S(2)}, u32[]{:S(2)}) collective-permute-start(bf16[256,128]{1,0:T(8,128)(2,1)S(1)} %add_convert_fusion.1.refs_16_.refs_0_), channel_id=1, source_target_pairs={{2,0},{3,1},{6,4},{7,5},{10,8},{11,9},{14,12},{15,13},{18,16},{19,... | collective-permute-start | bytes 196616 | tf_op jit(solution)/shard_map/ppermute | solution.py:281
  80.7 8.3 %collective-permute-start.32 = (bf16[256,128]{1,0:T(8,128)(2,1)S(1)}, bf16[256,128]{1,0:T(8,128)(2,1)S(1)}, u32[]{:S(2)}, u32[]{:S(2)}) collective-permute-start(bf16[256,128]{1,0:T(8,128)(2,1)S(1)} %add_convert_fusion.1.refs_16_.refs_0_), channel_id=1, source_target_pairs={{3,0},{7,4},{11,8},{15,12},{19,16},{23,20},{27,24},{31,28}} | collective-permute-start | bytes 196616 | tf_op jit(solution)/shard_map/ppermute | solution.py:281
  87.2 37.2 %collective-permute-start.36 = (bf16[1024,256]{1,0:T(8,128)(2,1)S(1)}, bf16[1024,256]{1,0:T(8,128)(2,1)S(1)}, u32[]{:S(2)}, u32[]{:S(2)}) collective-permute-start(bf16[1024,256]{1,0:T(8,128)(2,1)S(1)} %copy-done.17), channel_id=1, source_target_pairs={{1,0},{2,1},{3,2},{5,4},{6,5},{7,6},{9,8},{10,9},{11,10},{13,12},{... | collective-permute-start | bytes 1572872 | tf_op jit(solution)/shard_map/ppermute | solution.py:281
  89.0 17.5 %collective-permute-start.55 = (f32[256,128]{1,0:T(8,128)}, f32[256,128]{1,0:T(8,128)S(1)}, u32[]{:S(2)}, u32[]{:S(2)}) collective-permute-start(f32[256,128]{1,0:T(8,128)} %get-tuple-element.56), channel_id=1, source_target_pairs={{2,0},{3,1},{6,4},{7,5},{10,8},{11,9},{14,12},{15,13},{18,16},{19,... | collective-permute-start | bytes 393224 | tf_op jit(solution)/shard_map/ppermute | solution.py:281
  90.3 17.5 %collective-permute-start.54 = (f32[256,128]{1,0:T(8,128)}, f32[256,128]{1,0:T(8,128)S(1)}, u32[]{:S(2)}, u32[]{:S(2)}) collective-permute-start(f32[256,128]{1,0:T(8,128)} %get-tuple-element.55), channel_id=1, source_target_pairs={{0,2},{1,3},{4,6},{5,7},{8,10},{9,11},{12,14},{13,15},{16,18},{17,... | collective-permute-start | bytes 393224 | tf_op jit(solution)/shard_map/ppermute | solution.py:281
  95.8 30.5 %collective-permute-start.39 = (bf16[1024,256]{1,0:T(8,128)(2,1)S(1)}, bf16[1024,256]{1,0:T(8,128)(2,1)S(1)}, u32[]{:S(2)}, u32[]{:S(2)}) collective-permute-start(bf16[1024,256]{1,0:T(8,128)(2,1)S(1)} %copy-done.18), channel_id=1, source_target_pairs={{0,1},{1,2},{2,3},{4,5},{5,6},{6,7},{8,9},{9,10},{10,11},{12,13},{... | collective-permute-start | bytes 1572872 | tf_op jit(solution)/shard_map/ppermute | solution.py:281
  99.9 28.0 %collective-permute-start.42 = (bf16[1024,256]{1,0:T(8,128)(2,1)S(1)}, bf16[1024,256]{1,0:T(8,128)(2,1)S(1)}, u32[]{:S(2)}, u32[]{:S(2)}) collective-permute-start(bf16[1024,256]{1,0:T(8,128)(2,1)S(1)} %copy-done.18), channel_id=1, source_target_pairs={{1,0},{2,1},{3,2},{5,4},{6,5},{7,6},{9,8},{10,9},{11,10},{13,12},{... | collective-permute-start | bytes 1572872 | tf_op jit(solution)/shard_map/ppermute | solution.py:281
  106.5 16.2 %collective-permute-start.53 = (f32[256,128]{1,0:T(8,128)}, f32[256,128]{1,0:T(8,128)S(1)}, u32[]{:S(2)}, u32[]{:S(2)}) collective-permute-start(f32[256,128]{1,0:T(8,128)} %get-tuple-element.54), channel_id=1, source_target_pairs={{1,0},{2,1},{3,2},{5,4},{6,5},{7,6},{9,8},{10,9},{11,10},{13,12},{... | collective-permute-start | bytes 393224 | tf_op jit(solution)/shard_map/ppermute | solution.py:281
  107.8 15.0 %collective-permute-start.52 = (f32[256,128]{1,0:T(8,128)}, f32[256,128]{1,0:T(8,128)S(1)}, u32[]{:S(2)}, u32[]{:S(2)}) collective-permute-start(f32[256,128]{1,0:T(8,128)} %get-tuple-element.53), channel_id=1, source_target_pairs={{0,1},{1,2},{2,3},{4,5},{5,6},{6,7},{8,9},{9,10},{10,11},{12,13},{... | collective-permute-start | bytes 393224 | tf_op jit(solution)/shard_map/ppermute | solution.py:281
  122.7 6.6 %collective-permute-start.45 = (bf16[64,2048]{1,0:T(8,128)(2,1)}, bf16[64,2048]{1,0:T(8,128)(2,1)S(1)}, u32[]{:S(2)}, u32[]{:S(2)}) collective-permute-start(bf16[64,2048]{1,0:T(8,128)(2,1)} %get-tuple-element.45), channel_id=1, source_target_pairs={{0,4},{4,0},{8,12},{12,8},{16,20},{20,16},{24,28},{28,24},{1,5},{5... | collective-permute-start | bytes 786440 | tf_op jit(solution)/shard_map/ppermute | solution.py:304
  122.8 8.9 %collective-permute-start.46 = (bf16[64,2048]{1,0:T(8,128)(2,1)}, bf16[64,2048]{1,0:T(8,128)(2,1)S(1)}, u32[]{:S(2)}, u32[]{:S(2)}) collective-permute-start(bf16[64,2048]{1,0:T(8,128)(2,1)} %get-tuple-element.46), channel_id=1, source_target_pairs={{0,8},{4,12},{8,0},{12,4},{16,24},{20,28},{24,16},{28,20},{1,9},{5... | collective-permute-start | bytes 786440 | tf_op jit(solution)/shard_map/ppermute | solution.py:304
  124.4 8.6 %collective-permute-start.58 = (bf16[256,128]{1,0:T(8,128)(2,1)S(1)}, bf16[256,128]{1,0:T(8,128)(2,1)S(1)}, u32[]{:S(2)}, u32[]{:S(2)}) collective-permute-start(bf16[256,128]{1,0:T(8,128)(2,1)S(1)} %add_convert_fusion.refs_0_), channel_id=1, source_target_pairs={{0,1},{1,2},{2,3},{4,5},{5,6},{6,7},{8,9},{9,10},{10,11},{12,13},{... | collective-permute-start | bytes 196616 | tf_op jit(solution)/shard_map/ppermute | solution.py:281
  126.3 8.0 %collective-permute-start.59 = (bf16[256,128]{1,0:T(8,128)(2,1)S(1)}, bf16[256,128]{1,0:T(8,128)(2,1)S(1)}, u32[]{:S(2)}, u32[]{:S(2)}) collective-permute-start(bf16[256,128]{1,0:T(8,128)(2,1)S(1)} %add_convert_fusion.refs_0_), channel_id=1, source_target_pairs={{0,2},{1,3},{4,6},{5,7},{8,10},{9,11},{12,14},{13,15},{16,18},{17,... | collective-permute-start | bytes 196616 | tf_op jit(solution)/shard_map/ppermute | solution.py:281
  127.9 7.2 %collective-permute-start.60 = (bf16[256,128]{1,0:T(8,128)(2,1)S(1)}, bf16[256,128]{1,0:T(8,128)(2,1)S(1)}, u32[]{:S(2)}, u32[]{:S(2)}) collective-permute-start(bf16[256,128]{1,0:T(8,128)(2,1)S(1)} %add_convert_fusion.refs_0_), channel_id=1, source_target_pairs={{0,3},{4,7},{8,11},{12,15},{16,19},{20,23},{24,27},{28,31}} | collective-permute-start | bytes 196616 | tf_op jit(solution)/shard_map/ppermute | solution.py:281
  129.2 6.4 %collective-permute-start.61 = (bf16[256,128]{1,0:T(8,128)(2,1)S(1)}, bf16[256,128]{1,0:T(8,128)(2,1)S(1)}, u32[]{:S(2)}, u32[]{:S(2)}) collective-permute-start(bf16[256,128]{1,0:T(8,128)(2,1)S(1)} %add_convert_fusion.refs_0_), channel_id=1, source_target_pairs={{1,0},{2,1},{3,2},{5,4},{6,5},{7,6},{9,8},{10,9},{11,10},{13,12},{... | collective-permute-start | bytes 196616 | tf_op jit(solution)/shard_map/ppermute | solution.py:281
  131.7 7.3 %collective-permute-start.62 = (bf16[256,128]{1,0:T(8,128)(2,1)S(1)}, bf16[256,128]{1,0:T(8,128)(2,1)S(1)}, u32[]{:S(2)}, u32[]{:S(2)}) collective-permute-start(bf16[256,128]{1,0:T(8,128)(2,1)S(1)} %add_convert_fusion.refs_0_), channel_id=1, source_target_pairs={{2,0},{3,1},{6,4},{7,5},{10,8},{11,9},{14,12},{15,13},{18,16},{19,... | collective-permute-start | bytes 196616 | tf_op jit(solution)/shard_map/ppermute | solution.py:281
  133.0 8.6 %collective-permute-start.63 = (bf16[256,128]{1,0:T(8,128)(2,1)S(1)}, bf16[256,128]{1,0:T(8,128)(2,1)S(1)}, u32[]{:S(2)}, u32[]{:S(2)}) collective-permute-start(bf16[256,128]{1,0:T(8,128)(2,1)S(1)} %add_convert_fusion.refs_0_), channel_id=1, source_target_pairs={{3,0},{7,4},{11,8},{15,12},{19,16},{23,20},{27,24},{31,28}} | collective-permute-start | bytes 196616 | tf_op jit(solution)/shard_map/ppermute | solution.py:281
  134.3 41.4 %collective-permute-start.47 = (bf16[64,2048]{1,0:T(8,128)(2,1)}, bf16[64,2048]{1,0:T(8,128)(2,1)S(1)}, u32[]{:S(2)}, u32[]{:S(2)}) collective-permute-start(bf16[64,2048]{1,0:T(8,128)(2,1)} %get-tuple-element.47), channel_id=1, source_target_pairs={{0,12},{4,8},{8,4},{12,0},{16,28},{20,24},{24,20},{28,16},{1,13},{... | collective-permute-start | bytes 786440 | tf_op jit(solution)/shard_map/ppermute | solution.py:304
  135.1 40.7 %collective-permute-start.48 = (bf16[64,2048]{1,0:T(8,128)(2,1)}, bf16[64,2048]{1,0:T(8,128)(2,1)S(1)}, u32[]{:S(2)}, u32[]{:S(2)}) collective-permute-start(bf16[64,2048]{1,0:T(8,128)(2,1)} %get-tuple-element.48), channel_id=1, source_target_pairs={{0,16},{4,20},{8,24},{12,28},{16,0},{20,4},{24,8},{28,12},{1,17},{... | collective-permute-start | bytes 786440 | tf_op jit(solution)/shard_map/ppermute | solution.py:304
  135.6 40.8 %collective-permute-start.49 = (bf16[64,2048]{1,0:T(8,128)(2,1)}, bf16[64,2048]{1,0:T(8,128)(2,1)S(1)}, u32[]{:S(2)}, u32[]{:S(2)}) collective-permute-start(bf16[64,2048]{1,0:T(8,128)(2,1)} %get-tuple-element.49), channel_id=1, source_target_pairs={{0,20},{4,16},{8,28},{12,24},{16,4},{20,0},{24,12},{28,8},{1,21},{... | collective-permute-start | bytes 786440 | tf_op jit(solution)/shard_map/ppermute | solution.py:304
  139.0 38.7 %collective-permute-start.50 = (bf16[64,2048]{1,0:T(8,128)(2,1)}, bf16[64,2048]{1,0:T(8,128)(2,1)S(1)}, u32[]{:S(2)}, u32[]{:S(2)}) collective-permute-start(bf16[64,2048]{1,0:T(8,128)(2,1)} %get-tuple-element.50), channel_id=1, source_target_pairs={{0,24},{4,28},{8,16},{12,20},{16,8},{20,12},{24,0},{28,4},{1,25},{... | collective-permute-start | bytes 786440 | tf_op jit(solution)/shard_map/ppermute | solution.py:304
  142.3 35.9 %collective-permute-start.51 = (bf16[64,2048]{1,0:T(8,128)(2,1)}, bf16[64,2048]{1,0:T(8,128)(2,1)S(1)}, u32[]{:S(2)}, u32[]{:S(2)}) collective-permute-start(bf16[64,2048]{1,0:T(8,128)(2,1)} %get-tuple-element.51), channel_id=1, source_target_pairs={{0,28},{4,24},{8,20},{12,16},{16,12},{20,8},{24,4},{28,0},{1,29},{... | collective-permute-start | bytes 786440 | tf_op jit(solution)/shard_map/ppermute | solution.py:304
  175.8 5.9 %collective-permute-start.65 = (bf16[64,256]{1,0:T(8,128)(2,1)}, bf16[64,256]{1,0:T(8,128)(2,1)S(1)}, u32[]{:S(2)}, u32[]{:S(2)}) collective-permute-start(bf16[64,256]{1,0:T(8,128)(2,1)} %get-tuple-element.61), channel_id=1, source_target_pairs={{0,8},{4,12},{8,0},{12,4},{16,24},{20,28},{24,16},{28,20},{1,9},{5... | collective-permute-start | bytes 98312 | tf_op jit(solution)/shard_map/ppermute | solution.py:304
  176.5 6.6 %collective-permute-start.66 = (bf16[64,256]{1,0:T(8,128)(2,1)}, bf16[64,256]{1,0:T(8,128)(2,1)S(1)}, u32[]{:S(2)}, u32[]{:S(2)}) collective-permute-start(bf16[64,256]{1,0:T(8,128)(2,1)} %get-tuple-element.62), channel_id=1, source_target_pairs={{0,12},{4,8},{8,4},{12,0},{16,28},{20,24},{24,20},{28,16},{1,13},{... | collective-permute-start | bytes 98312 | tf_op jit(solution)/shard_map/ppermute | solution.py:304
  177.7 11.2 %collective-permute-start.67 = (bf16[64,256]{1,0:T(8,128)(2,1)}, bf16[64,256]{1,0:T(8,128)(2,1)S(1)}, u32[]{:S(2)}, u32[]{:S(2)}) collective-permute-start(bf16[64,256]{1,0:T(8,128)(2,1)} %get-tuple-element.63), channel_id=1, source_target_pairs={{0,16},{4,20},{8,24},{12,28},{16,0},{20,4},{24,8},{28,12},{1,17},{... | collective-permute-start | bytes 98312 | tf_op jit(solution)/shard_map/ppermute | solution.py:304
  178.2 12.0 %collective-permute-start.68 = (bf16[64,256]{1,0:T(8,128)(2,1)}, bf16[64,256]{1,0:T(8,128)(2,1)S(1)}, u32[]{:S(2)}, u32[]{:S(2)}) collective-permute-start(bf16[64,256]{1,0:T(8,128)(2,1)} %get-tuple-element.64), channel_id=1, source_target_pairs={{0,20},{4,16},{8,28},{12,24},{16,4},{20,0},{24,12},{28,8},{1,21},{... | collective-permute-start | bytes 98312 | tf_op jit(solution)/shard_map/ppermute | solution.py:304
  179.8 17.6 %collective-permute-start.34 = (bf16[1024,256]{1,0:T(8,128)(2,1)S(1)}, bf16[1024,256]{1,0:T(8,128)(2,1)S(1)}, u32[]{:S(2)}, u32[]{:S(2)}) collective-permute-start(bf16[1024,256]{1,0:T(8,128)(2,1)S(1)} %collective-permute-done.33.refs_24_), channel_id=1, source_target_pairs={{0,1},{1,2},{2,3},{4,5},{5,6},{6,7},{8,9},{9,10},{10,11},{12,13},{... | collective-permute-start | bytes 1572872 | tf_op jit(solution)/shard_map/ppermute | solution.py:281
  181.7 20.3 %collective-permute-start.37 = (bf16[1024,256]{1,0:T(8,128)(2,1)S(1)}, bf16[1024,256]{1,0:T(8,128)(2,1)S(1)}, u32[]{:S(2)}, u32[]{:S(2)}) collective-permute-start(bf16[1024,256]{1,0:T(8,128)(2,1)S(1)} %collective-permute-done.36.refs_27_), channel_id=1, source_target_pairs={{1,0},{2,1},{3,2},{5,4},{6,5},{7,6},{9,8},{10,9},{11,10},{13,12},{... | collective-permute-start | bytes 1572872 | tf_op jit(solution)/shard_map/ppermute | solution.py:281
  183.0 21.7 %collective-permute-start.40 = (bf16[1024,256]{1,0:T(8,128)(2,1)S(1)}, bf16[1024,256]{1,0:T(8,128)(2,1)S(1)}, u32[]{:S(2)}, u32[]{:S(2)}) collective-permute-start(bf16[1024,256]{1,0:T(8,128)(2,1)S(1)} %collective-permute-done.39.refs_31_), channel_id=1, source_target_pairs={{0,1},{1,2},{2,3},{4,5},{5,6},{6,7},{8,9},{9,10},{10,11},{12,13},{... | collective-permute-start | bytes 1572872 | tf_op jit(solution)/shard_map/ppermute | solution.py:281
  188.9 21.7 %collective-permute-start.43 = (bf16[1024,256]{1,0:T(8,128)(2,1)}, bf16[1024,256]{1,0:T(8,128)(2,1)S(1)}, u32[]{:S(2)}, u32[]{:S(2)}) collective-permute-start(bf16[1024,256]{1,0:T(8,128)(2,1)} %copy-done.22), channel_id=1, source_target_pairs={{1,0},{2,1},{3,2},{5,4},{6,5},{7,6},{9,8},{10,9},{11,10},{13,12},{... | collective-permute-start | bytes 1572872 | tf_op jit(solution)/shard_map/ppermute | solution.py:281
  190.2 5.2 %collective-permute-start.69 = (bf16[64,256]{1,0:T(8,128)(2,1)}, bf16[64,256]{1,0:T(8,128)(2,1)S(1)}, u32[]{:S(2)}, u32[]{:S(2)}) collective-permute-start(bf16[64,256]{1,0:T(8,128)(2,1)} %get-tuple-element.65), channel_id=1, source_target_pairs={{0,24},{4,28},{8,16},{12,20},{16,8},{20,12},{24,0},{28,4},{1,25},{... | collective-permute-start | bytes 98312 | tf_op jit(solution)/shard_map/ppermute | solution.py:304
  195.4 16.5 %collective-permute-start.70 = (bf16[64,256]{1,0:T(8,128)(2,1)}, bf16[64,256]{1,0:T(8,128)(2,1)S(1)}, u32[]{:S(2)}, u32[]{:S(2)}) collective-permute-start(bf16[64,256]{1,0:T(8,128)(2,1)} %get-tuple-element.66), channel_id=1, source_target_pairs={{0,28},{4,24},{8,20},{12,16},{16,12},{20,8},{24,4},{28,0},{1,29},{... | collective-permute-start | bytes 98312 | tf_op jit(solution)/shard_map/ppermute | solution.py:304
  197.4 18.6 %collective-permute-start.35 = (bf16[1024,256]{1,0:T(8,128)(2,1)S(1)}, bf16[1024,256]{1,0:T(8,128)(2,1)S(1)}, u32[]{:S(2)}, u32[]{:S(2)}) collective-permute-start(bf16[1024,256]{1,0:T(8,128)(2,1)S(1)} %collective-permute-done.34.refs_25_), channel_id=1, source_target_pairs={{0,1},{1,2},{2,3},{4,5},{5,6},{6,7},{8,9},{9,10},{10,11},{12,13},{... | collective-permute-start | bytes 1572872 | tf_op jit(solution)/shard_map/ppermute | solution.py:281
  202.0 19.8 %collective-permute-start.38 = (bf16[1024,256]{1,0:T(8,128)(2,1)S(1)}, bf16[1024,256]{1,0:T(8,128)(2,1)S(1)}, u32[]{:S(2)}, u32[]{:S(2)}) collective-permute-start(bf16[1024,256]{1,0:T(8,128)(2,1)S(1)} %collective-permute-done.37.refs_28_), channel_id=1, source_target_pairs={{1,0},{2,1},{3,2},{5,4},{6,5},{7,6},{9,8},{10,9},{11,10},{13,12},{... | collective-permute-start | bytes 1572872 | tf_op jit(solution)/shard_map/ppermute | solution.py:281
  204.8 22.5 %collective-permute-start.41 = (bf16[1024,256]{1,0:T(8,128)(2,1)S(1)}, bf16[1024,256]{1,0:T(8,128)(2,1)S(1)}, u32[]{:S(2)}, u32[]{:S(2)}) collective-permute-start(bf16[1024,256]{1,0:T(8,128)(2,1)S(1)} %collective-permute-done.40.refs_32_), channel_id=1, source_target_pairs={{0,1},{1,2},{2,3},{4,5},{5,6},{6,7},{8,9},{9,10},{10,11},{12,13},{... | collective-permute-start | bytes 1572872 | tf_op jit(solution)/shard_map/ppermute | solution.py:281
  210.6 22.5 %collective-permute-start.44 = (bf16[1024,256]{1,0:T(8,128)(2,1)S(1)}, bf16[1024,256]{1,0:T(8,128)(2,1)S(1)}, u32[]{:S(2)}, u32[]{:S(2)}) collective-permute-start(bf16[1024,256]{1,0:T(8,128)(2,1)S(1)} %collective-permute-done.43.refs_35_), channel_id=1, source_target_pairs={{1,0},{2,1},{3,2},{5,4},{6,5},{7,6},{9,8},{10,9},{11,10},{13,12},{... | collective-permute-start | bytes 1572872 | tf_op jit(solution)/shard_map/ppermute | solution.py:281
  (60 other events, 1514.5 us)

commit v2 on v1

v2 whole, which is shorter than its diff:
```python
import functools

import jax
import jax.numpy as jnp
from jax import lax
from jax.experimental import pallas as pl
from jax.experimental.pallas import tpu as pltpu
from jax.sharding import PartitionSpec as P

ADAPTER_SCALE = 2.0
ANY = pl.BlockSpec(memory_space=pl.ANY)
SMEM = pl.BlockSpec(memory_space=pltpu.SMEM)
VMEM = pl.BlockSpec(memory_space=pltpu.VMEM)
NT = (((1,), (1,)), ((), ()))
TN = (((0,), (0,)), ((), ()))
NN = (((1,), (0,)), ((), ()))
MIB = 1024 * 1024


def lookup(idents, mapping):
    matches = idents[:, None] == jnp.arange(mapping.shape[0], dtype=jnp.int32)[None, :]
    return jnp.sum(jnp.where(matches, mapping[None, :], 0), axis=1)


def params(mib):
    return pltpu.CompilerParams(vmem_limit_bytes=mib * MIB)


def cost(us):
    return pl.CostEstimate(flops=0, bytes_accessed=int(us * 3e5), transcendentals=0)


def load_all(pairs, sem):
    copies = [pltpu.make_async_copy(src, dst, sem.at[i]) for i, (src, dst) in enumerate(pairs)]
    for copy in copies:
        copy.start()
    for copy in copies:
        copy.wait()


def live_mask(count, rows, width):
    return lax.broadcasted_iota(jnp.int32, (rows, width), 0) < count


def pack_kernel(segs, rows, sizes, off, cot, *refs):
    outs, buf = refs[-1 - len(sizes) : -1], refs[-1]
    buf[...] = jnp.zeros_like(buf)
    for g in range(segs):
        start = pl.multiple_of(off[g], 16)
        buf[pl.ds(start, rows), :] = cot[g * rows : (g + 1) * rows, :]
    first = 0
    for out, size in zip(outs, sizes):
        out[...] = buf[first : first + size, :]
        first += size


def pack(cot, off, segs, sizes, after=()):
    rows, width = cot.shape[0] // segs, cot.shape[1]
    return pl.pallas_call(
        functools.partial(pack_kernel, segs, rows, sizes),
        out_shape=[jax.ShapeDtypeStruct((size, width), cot.dtype) for size in sizes],
        in_specs=[SMEM, VMEM] + [ANY] * len(after),
        out_specs=[VMEM] * len(sizes),
        scratch_shapes=[pltpu.VMEM((segs * rows + rows, width), cot.dtype)],
        compiler_params=params(8),
        cost_estimate=cost(1),
        name="pack",
    )(off, cot, *after)


def project_kernel(n, per, rows, packed, n_maps, idx, off, count, x, *refs):
    maps, (out, table, buf, sem) = refs[:n_maps], refs[-4:]
    step = pl.program_id(0)

    @pl.when(step == 0)
    def _():
        each = maps[0].shape[0]
        load_all([(m, table.at[pl.ds(i * each, each)]) for i, m in enumerate(maps)], sem)
        buf[...] = jnp.zeros_like(buf)

    for i in range(per):
        g = step * per + i
        term = lax.dot_general(
            table[idx[g]], x[i * rows : (i + 1) * rows, :], NT, preferred_element_type=jnp.float32
        ).T
        term = jnp.where(live_mask(count[g], *term.shape), term, 0.0)
        buf[pl.ds(pl.multiple_of(off[g], 16), rows), :] = term

    @pl.when(step == pl.num_programs(0) - 1)
    def _():
        half = packed // n // 2
        for j in range(n):
            start = 2 * j * half
            out[j] = jnp.concatenate(
                [buf[start : start + half, :], buf[start + half : start + 2 * half, :]], axis=1
            )


def project(idx, off, count, x, maps, n, packed, per, us, after=()):
    segs = idx.shape[0]
    rows, width = x.shape[0] // segs, x.shape[1]
    ranks = maps[0].shape[1]
    total = sum(m.shape[0] for m in maps)
    shape = (n, packed // n // 2, 2 * ranks)
    return pl.pallas_call(
        functools.partial(project_kernel, n, per, rows, packed, len(maps)),
        grid=(segs // per,),
        out_shape=jax.ShapeDtypeStruct(shape, jnp.float32),
        in_specs=[SMEM] * 3
        + [pl.BlockSpec((per * rows, width), lambda i: (i, 0))]
        + [ANY] * (len(maps) + len(after)),
        out_specs=pl.BlockSpec(shape, lambda i: (0, 0, 0)),
        scratch_shapes=[
            pltpu.VMEM((total, ranks, width), x.dtype),
            pltpu.VMEM((segs * rows + rows, ranks), jnp.float32),
            pltpu.SemaphoreType.DMA((len(maps),)),
        ],
        compiler_params=params(60),
        cost_estimate=cost(us),
        name="project",
    )(idx, off, count, x, *maps, *after)


def cot_copies(n, z, sizes, cots, cot, sem):
    key = cots[0].shape[1]
    copies, first = [], 0
    for c, size in enumerate(sizes):
        for s in range(n):
            column = pl.multiple_of(lax.rem(z - s + n, n) * key, key)
            dst = cot.at[pl.ds(first, size), pl.ds(column, key)]
            copies.append(pltpu.make_async_copy(cots[c * n + s], dst, sem.at[c * n + s]))
        first += size
    return copies


def add_terms(total, owner, terms, x):
    total[owner] += lax.dot_general(terms, x, TN, preferred_element_type=jnp.float32)


def up_sums_kernel(rows, scale, owner, off, count, x, raw, sent, out, buf, total):
    del sent
    n, half, ranks = raw.shape[0], raw.shape[1], raw.shape[2] // 2
    packed = 2 * n * half
    for j in range(n):
        start = 2 * j * half
        buf[start : start + half, :] = raw[j][:, :ranks]
        buf[start + half : start + 2 * half, :] = raw[j][:, ranks:]
    buf[packed : packed + rows, :] = jnp.zeros((rows, ranks), buf.dtype)
    total[...] = jnp.zeros_like(total)
    for g in range(x.shape[0] // rows):
        terms = buf[pl.ds(pl.multiple_of(off[g], 16), rows), :]
        terms = jnp.where(live_mask(count[g], *terms.shape), terms, jnp.zeros_like(terms))
        add_terms(total, owner[g], terms, x[g * rows : (g + 1) * rows, :])
    out[...] = (total[...] * scale).astype(out.dtype)


def up_sums(owner, off, count, x, lowered, sent, us):
    segs = owner.shape[0]
    rows, width = x.shape[0] // segs, x.shape[1]
    packed, ranks = 2 * lowered.shape[0] * lowered.shape[1], lowered.shape[2] // 2
    owners, last = sent.shape[0], sent.shape[2] // width - 1
    return pl.pallas_call(
        functools.partial(up_sums_kernel, rows, ADAPTER_SCALE / rows),
        grid=(1,),
        out_shape=jax.ShapeDtypeStruct(sent.shape, sent.dtype),
        in_specs=[SMEM] * 3 + [VMEM] * 2 + [ANY],
        out_specs=pl.BlockSpec((owners, ranks, width), lambda i: (0, 0, last)),
        scratch_shapes=[
            pltpu.VMEM((packed + rows, ranks), jnp.bfloat16),
            pltpu.VMEM((owners, ranks, width), jnp.float32),
        ],
        input_output_aliases={5: 0},
        compiler_params=params(12),
        cost_estimate=cost(us),
        name="up_sums",
    )(owner, off, count, x, lowered, sent)


def down_sums_kernel(n, per, rows, sizes, n_maps, scale, z, idx, owner, off, count, x, *refs):
    maps, refs = refs[:n_maps], refs[n_maps:]
    cots, refs = refs[: n * len(sizes)], refs[n * len(sizes) :]
    out, pulled, table, cot, total, map_sem, cot_sem = refs[-7:]
    step = pl.program_id(0)
    packed = sum(sizes)

    @pl.when(step == 0)
    def _():
        copies = cot_copies(n, z[0], sizes, cots, cot, cot_sem)
        parts, held, _, key = maps[0].shape
        for i, m in enumerate(maps):
            for j in range(parts):
                column = pl.multiple_of(lax.rem(z[0] - j + n, n) * key, key)
                dst = table.at[pl.ds(i * held, held), :, pl.ds(column, key)]
                copies.append(pltpu.make_async_copy(m.at[j], dst, map_sem.at[i * parts + j]))
        for copy in copies:
            copy.start()
        total[...] = jnp.zeros_like(total)
        cot[packed : packed + rows, :] = jnp.zeros((rows, cot.shape[1]), cot.dtype)
        for copy in copies:
            copy.wait()

    for i in range(per):
        g = step * per + i
        terms = lax.dot_general(
            cot[pl.ds(pl.multiple_of(off[g], 16), rows), :],
            table[idx[g]],
            NT,
            preferred_element_type=jnp.float32,
        )
        terms = jnp.where(live_mask(count[g], *terms.shape), terms, 0.0).astype(pulled.dtype)
        pulled[i * rows : (i + 1) * rows, :] = terms
        add_terms(total, owner[g], terms, x[i * rows : (i + 1) * rows, :])

    @pl.when(step == pl.num_programs(0) - 1)
    def _():
        out[:, :, : x.shape[1]] = (total[...] * scale).astype(out.dtype)


def down_sums(z, idx, owner, off, count, x, maps, cots, owners, n, per, us, extra):
    segs = owner.shape[0]
    rows, width = x.shape[0] // segs, x.shape[1]
    sizes = [got[0].shape[0] for got in cots]
    parts, held, ranks, key = maps[0].shape
    shape = (owners, ranks, width)
    wide = (owners, ranks, width + extra)
    return pl.pallas_call(
        functools.partial(down_sums_kernel, n, per, rows, sizes, len(maps), ADAPTER_SCALE / rows),
        grid=(segs // per,),
        out_shape=[
            jax.ShapeDtypeStruct(wide, jnp.bfloat16),
            jax.ShapeDtypeStruct((segs * rows, ranks), jnp.bfloat16),
        ],
        in_specs=[SMEM] * 5
        + [pl.BlockSpec((per * rows, width), lambda i: (i, 0))]
        + [ANY] * (len(maps) + n * len(sizes)),
        out_specs=[
            pl.BlockSpec(wide, lambda i: (0, 0, 0)),
            pl.BlockSpec((per * rows, ranks), lambda i: (i, 0)),
        ],
        scratch_shapes=[
            pltpu.VMEM((held * len(maps), ranks, parts * key), jnp.bfloat16),
            pltpu.VMEM((sum(sizes) + rows, n * key), jnp.bfloat16),
            pltpu.VMEM(shape, jnp.float32),
            pltpu.SemaphoreType.DMA((parts * len(maps),)),
            pltpu.SemaphoreType.DMA((n * len(sizes),)),
        ],
        compiler_params=params(60),
        cost_estimate=cost(us),
        name="down_sums",
    )(z, idx, owner, off, count, x, *maps, *[a for got in cots for a in got])


def token_kernel(n, per, rows, sizes, n_maps, z, idx, off, count, weight, pulled, *refs):
    maps, refs = refs[:n_maps], refs[n_maps:]
    cots, (out, table, cot, map_sem, cot_sem) = refs[:-5], refs[-5:]
    packed = sum(sizes)
    step = pl.program_id(0)

    @pl.when(step == 0)
    def _():
        each = maps[0].shape[0]
        copies = cot_copies(n, z[0], sizes, cots, cot, cot_sem)
        for i, m in enumerate(maps):
            copies.append(pltpu.make_async_copy(m, table.at[pl.ds(i * each, each)], map_sem.at[i]))
        for copy in copies:
            copy.start()
        cot[packed : packed + rows, :] = jnp.zeros((rows, cot.shape[1]), cot.dtype)
        for copy in copies:
            copy.wait()

    width = weight.shape[0]
    tile = min(512, width)
    starts = [pl.multiple_of(off[step * per + i], 16) for i in range(per)]
    counts = [count[step * per + i] for i in range(per)]
    x = jnp.concatenate([cot[pl.ds(start, rows), :] for start in starts], axis=0)
    for d in range(0, width, tile):
        total = lax.dot_general(x, weight[d : d + tile, :], NT, preferred_element_type=jnp.float32)
        for i in range(per):
            adapter = lax.dot_general(
                pulled[i * rows : (i + 1) * rows, :],
                table[idx[step * per + i], :, d : d + tile],
                NN,
                preferred_element_type=jnp.float32,
            )
            both = total[i * rows : (i + 1) * rows, :] + ADAPTER_SCALE * adapter
            both = jnp.where(live_mask(counts[i], rows, tile), both, 0.0)
            out[i * rows : (i + 1) * rows, d : d + tile] = both.astype(out.dtype)


def token_gradients(z, idx, off, count, weight, pulled, maps, cots, n, rows, per):
    segs = idx.shape[0]
    width, keys = weight.shape
    sizes = [got[0].shape[0] for got in cots]
    ranks = maps[0].shape[1]
    total = sum(m.shape[0] for m in maps)
    return pl.pallas_call(
        functools.partial(token_kernel, n, per, rows, sizes, len(maps)),
        grid=(segs // per,),
        out_shape=jax.ShapeDtypeStruct((segs * rows, width), jnp.bfloat16),
        in_specs=[SMEM] * 4
        + [pl.BlockSpec(weight.shape, lambda i: (0, 0), pipeline_mode=pl.Buffered(1))]
        + [pl.BlockSpec((per * rows, ranks), lambda i: (i, 0))]
        + [ANY] * (len(maps) + n * len(sizes)),
        out_specs=pl.BlockSpec((per * rows, width), lambda i: (i, 0)),
        scratch_shapes=[
            pltpu.VMEM((total, ranks, width), jnp.bfloat16),
            pltpu.VMEM((sum(sizes) + rows, keys), jnp.bfloat16),
            pltpu.SemaphoreType.DMA((len(maps),)),
            pltpu.SemaphoreType.DMA((n * len(sizes),)),
        ],
        compiler_params=params(60),
        cost_estimate=cost(16),
        name="token_gradient",
    )(z, idx, off, count, weight, pulled, *maps, *[a for got in cots for a in got])


def gate_kernel(*refs):
    del refs


def gate(*arrays):
    return pl.pallas_call(
        gate_kernel,
        out_shape=[jax.ShapeDtypeStruct(a.shape, a.dtype) for a in arrays],
        in_specs=[ANY] * len(arrays),
        out_specs=[ANY] * len(arrays),
        input_output_aliases={i: i for i in range(len(arrays))},
        compiler_params=params(1),
        cost_estimate=cost(0),
        name="gate",
    )(*arrays)


def ring(x, n):
    return lax.ppermute(x, "tsp", [(i, (i + 1) % n) for i in range(n)])


def flip(x, n, by):
    return lax.ppermute(x, "dp", [(i, i ^ by) for i in range(n)])


def on_device(
    tokens,
    cotangent,
    frozen_key_weight,
    adapter_down_weight,
    adapter_up_weight,
    adapter_place_table,
    segment_adapter,
    segment_live_count,
):
    n_dp = lax.axis_size("dp")
    n = lax.axis_size("tsp")
    me = lax.axis_index("dp").astype(jnp.int32)
    z = lax.axis_index("tsp").astype(jnp.int32)[None]
    held = adapter_down_weight.shape[0]
    segs = segment_adapter.shape[0]
    rows = tokens.shape[0] // segs
    full = segs * rows
    cube = n_dp == 8 and held == 2

    places = lookup(segment_adapter, adapter_place_table)
    owner, entry = places // held, places % held
    peers = jnp.arange(n_dp, dtype=jnp.int32)
    wanted = jnp.max(jnp.where(owner[:, None] == peers[None, :], entry[:, None], -1), axis=0)
    count = segment_live_count
    padded = (count + 15) // 16 * 16
    off = jnp.cumsum(padded) - padded

    up_line = [
        lax.ppermute(adapter_up_weight, "tsp", [(i, (i + s) % n) for i in range(n)]) for s in range(1, n)
    ]
    whole = pack(cotangent, off, segs, [full], after=up_line)[0]
    up_line = jnp.stack([adapter_up_weight, *up_line])
    first = ring(whole, n)
    if cube:
        idx = (owner ^ me) * held + entry
        over_x, over_y = flip(adapter_down_weight, n_dp, 2), flip(adapter_down_weight, n_dp, 4)
        first, over_x, over_y = gate(first, over_x, over_y)
    else:
        idx = places

    def main(packed):
        cots = [whole, first]
        cots.append(ring(cots[-1], n))
        if cube:
            corner = [flip(over_x[:1], n_dp, 4), flip(over_y[1:], n_dp, 2)]
            same = [adapter_down_weight, over_x, over_y]
            other = [flip(m, n_dp, 1) for m in same]
            up_same = [flip(up_line, n_dp, k) for k in (2, 4, 6)]
            told = wanted[None]
            told = jnp.concatenate([told, flip(told, n_dp, 1)])
            *corner, ux, uy, ud, told = gate(*corner, *up_same, told)
            up_same = [up_line, ux, uy, ud]
            ups = [m for u in up_same for m in (u, flip(u, n_dp, 1))]
            far = [flip(m, n_dp, 1) for m in corner]
            downs = [m for pair in zip(same, other) for m in pair]
            downs += [jnp.concatenate(corner), jnp.concatenate(far)]
            told = jnp.concatenate([told] + [flip(told, n_dp, k) for k in (2, 4, 6)])
            asked = jnp.sum(jnp.where(peers[None, :] == me, told, 0), axis=1)[peers ^ me]
        else:
            ups = [lax.all_gather(up_line, "dp", axis=1, tiled=True)]
            downs = [lax.all_gather(adapter_down_weight, "dp", axis=0, tiled=True)]
            asked = lax.all_gather(wanted, "dp", axis=0, tiled=False)[:, me]
        lowered = project(idx, off, count, tokens, downs, n, packed, 4, 4)
        cots[2], lowered, asked = gate(cots[2], lowered, asked)
        parts = lax.all_to_all(lowered, "tsp", 0, 0, tiled=True)
        while len(cots) < n:
            cots.append(ring(cots[-1], n))
        cots[-1], parts = gate(cots[-1], parts)
        lowered = jnp.sum(parts, axis=0).astype(jnp.bfloat16)
        lowered = lax.all_to_all(jnp.broadcast_to(lowered, parts.shape), "tsp", 0, 0, tiled=True)

        sent, pulled = down_sums(
            z, idx, owner, off, count, tokens, ups, [cots], n_dp, n, 4, 7, cotangent.shape[1]
        )
        sent = up_sums(owner, off, count, cotangent, lowered, sent, 2)
        got = lax.all_to_all(sent, "dp", 0, 0, tiled=True)
        token_gradient = token_gradients(
            z, idx, off, count, frozen_key_weight, pulled, downs, [cots], n, rows, 2
        )
        hits = asked[None, :] == jnp.arange(held, dtype=jnp.int32)[:, None]
        grads = jnp.sum(jnp.where(hits[:, :, None, None], got.astype(jnp.float32)[None], 0.0), axis=1)
        width = tokens.shape[1]
        return token_gradient, grads[:, :, :width], grads[:, :, width:]

    return main(full)


def solution(mesh):
    placed = (
        P("dp", "tsp"),
        P("dp", "tsp"),
        P("tsp", None),
        P("dp", None, "tsp"),
        P("dp", None, "tsp"),
        P(),
        P("dp"),
        P("dp"),
    )
    return jax.shard_map(
        on_device,
        mesh=mesh,
        in_specs=placed,
        out_specs=(P("dp", "tsp"), P("dp", None, "tsp"), P("dp", None, "tsp")),
        check_vma=False,
    )
```

time: 260 us -> 173 us (0.67)
  starting transfers between devices: 114 us -> 30.7 us
  blocking collectives: 17.4 us -> 37.5 us
  local copies, waits for them, and re-layouts: 4.46 us -> 16.3 us
  between operations: 12.6 us -> 0.99 us
  Pallas kernels: 55.4 us -> 44.9 us
  waiting for transfers between devices: 45.3 us -> 36.5 us
  other arithmetic: 9.16 us -> 5.18 us
    ppermute x36 -> x6, starting transfers between devices: 88.9 us -> 10.3 us  [the longest x3 7.01 us: on_device(): lax.ppermute(adapter_up_weight, 'tsp', [(i, (i + s) % n) for i in range(n)])]
    all_to_all x0 -> x1, blocking collectives: none -> 37.5 us  [main(): parts = lax.all_to_all(lowered, 'tsp', 0, 0, tiled=True)]
    ppermute x36 -> x6, waiting for transfers between devices: 38.7 us -> 6.36 us  [the longest x3 4.37 us: ring(): return lax.ppermute(x, 'tsp', [(i, (i + 1) % n) for i in range(n)])]
    unnamed x1 -> x0, blocking collectives: 17.4 us -> none
    ppermute x35 -> x20, waiting for transfers between devices: 6.57 us -> 22 us  [flip(): return lax.ppermute(x, 'dp', [(i, i ^ by) for i in range(n)])]
    ppermute x35 -> x20, starting transfers between devices: 25 us -> 13.4 us  [flip(): return lax.ppermute(x, 'dp', [(i, i ^ by) for i in range(n)])]
    unnamed x109 -> x60, local copies, waits for them, and re-layouts: 2.55 us -> 11.1 us
    all_to_all x0 -> x2, waiting for transfers between devices: none -> 8.16 us  [the longest x1 8.16 us: main(): got = lax.all_to_all(sent, 'dp', 0, 0, tiled=True)]
  transfers between devices with their start and end apart: 71 -> 28, of which waited for: 17 -> 16; matrix products, arithmetic and copies ran while one was open for 5% -> 4% of each run, Pallas kernels for 12% -> 25%
where the time goes in v2:
time: 173 us; the launch traced here: 172 us
  Pallas kernels  44.9 us (26%)
  blocking collectives  37.5 us (22%)
  waiting for transfers between devices  36.5 us (21%)
  starting transfers between devices  30.7 us (18%)
  local copies, waits for them, and re-layouts  16.3 us (9%)
  other arithmetic  5.18 us (3%)
    all_to_all x1, blocking collectives, main(): parts = lax.all_to_all(lowered, 'tsp', 0, 0, tiled=True)  37.5 us
    ppermute x20, waiting for transfers between devices, flip(): return lax.ppermute(x, 'dp', [(i, i ^ by) for i in range(n)])  22 us
    pallas_call x1, Pallas kernels, token_gradients(): pl.pallas_call(functools.partial(token_kernel, n, per, rows, sizes, len(m...  21.2 us
    ppermute x20, starting transfers between devices, flip(): return lax.ppermute(x, 'dp', [(i, i ^ by) for i in range(n)])  13.4 us
    pallas_call x1, Pallas kernels, down_sums(): pl.pallas_call(functools.partial(down_sums_kernel, n, per, rows, sizes, l...  11.4 us
    unnamed x60, local copies, waits for them, and re-layouts  11.1 us
    pallas_call x1, Pallas kernels, project(): pl.pallas_call(functools.partial(project_kernel, n, per, rows, packed, le...  9.61 us
    all_to_all x1, waiting for transfers between devices, main(): got = lax.all_to_all(sent, 'dp', 0, 0, tiled=True)  8.16 us
  transfers between devices with their start and end apart: 28, of which 16 were waited for; matrix products, arithmetic and copies ran while one was open for 4% of the time, Pallas kernels for 25%

profile of v2, /device:TPU:0, one launch (start us, length us, event | category | flops | bytes accessed | tf_op | source)
XLA Modules:
  0.0 172.0 jit_solution(5406439463842747554)
XLA Ops:
  0.6 3.1 %collective-permute-start = (bf16[2,64,256]{2,1,0:T(8,128)(2,1)}, bf16[2,64,256]{2,1,0:T(8,128)(2,1)S(1)}, u32[]{:S(2)}, u32[]{:S(2)}) collective-permute-start(bf16[2,64,256]{2,1,0:T(8,128)(2,1)} %param.12), channel_id=1, source_target_pairs={{0,1},{1,2},{2,3},{3,0},{4,5},{5,6},{6,7},{7,4},{8,9},{9,10},{10,1... | collective-permute-start | bytes 196616 | tf_op jit(solution)/shard_map/ppermute | solution.py:371
  3.7 2.6 %collective-permute-start.1 = (bf16[2,64,256]{2,1,0:T(8,128)(2,1)}, bf16[2,64,256]{2,1,0:T(8,128)(2,1)S(1)}, u32[]{:S(2)}, u32[]{:S(2)}) collective-permute-start(bf16[2,64,256]{2,1,0:T(8,128)(2,1)} %param.12), channel_id=1, source_target_pairs={{0,2},{1,3},{2,0},{3,1},{4,6},{5,7},{6,4},{7,5},{8,10},{9,11},{10,... | collective-permute-start | bytes 196616 | tf_op jit(solution)/shard_map/ppermute | solution.py:371
  6.3 1.3 collective-permute-start.2
  7.6 0.7 fusion.4
  8.6 0.7 fusion.3.off
  9.2 1.8 %collective-permute-done.1.refs_1_ = bf16[2,64,256]{2,1,0:T(8,128)(2,1)S(1)} collective-permute-done((bf16[2,64,256]{2,1,0:T(8,128)(2,1)}, bf16[2,64,256]{2,1,0:T(8,128)(2,1)S(1)}, u32[]{:S(2)}, u32[]{:S(2)}) %collective-permute-start.1) | collective-permute-done | bytes 65568 | tf_op jit(solution)/shard_map/ppermute | solution.py:371
  11.2 1.2 copy-done.10
  12.4 0.7 pack.1.refs_8_
  13.2 1.6 collective-permute-start.4
  14.9 1.5 collective-permute-start.5
  16.3 1.5 collective-permute-start.6
  17.9 0.9 select_reduce_fusion.1
  18.7 0.5 multiply_add_fusion
  19.4 0.9 pad_maximum_fusion.refs_0_
  20.3 0.6 collective-permute-start.10
  20.9 7.7 %collective-permute-done.5.refs_1_ = bf16[2,64,2048]{2,1,0:T(8,128)(2,1)S(1)} collective-permute-done((bf16[2,64,2048]{2,1,0:T(8,128)(2,1)}, bf16[2,64,2048]{2,1,0:T(8,128)(2,1)S(1)}, u32[]{:S(2)}, u32[]{:S(2)}) %collective-permute-start.5) | collective-permute-done | bytes 524320 | tf_op jit(solution)/shard_map/ppermute | solution.py:339
  28.6 2.2 %collective-permute-start.11 = (bf16[4,2,64,256]{3,2,1,0:T(8,128)(2,1)S(1)}, bf16[4,2,64,256]{3,2,1,0:T(8,128)(2,1)S(1)}, u32[]{:S(2)}, u32[]{:S(2)}) collective-permute-start(bf16[4,2,64,256]{3,2,1,0:T(8,128)(2,1)S(1)} %pad_maximum_fusion.refs_0_), channel_id=1, source_target_pairs={{0,24},{4,28},{8,16},{12,20},{16,8},{20,12},{24,0},{28,4},{1,25},{... | collective-permute-start | bytes 786440 | tf_op jit(solution)/shard_map/ppermute | solution.py:339
  30.8 4.6 %collective-permute-done.6.refs_2_ = bf16[2,64,2048]{2,1,0:T(8,128)(2,1)S(1)} collective-permute-done((bf16[2,64,2048]{2,1,0:T(8,128)(2,1)}, bf16[2,64,2048]{2,1,0:T(8,128)(2,1)S(1)}, u32[]{:S(2)}, u32[]{:S(2)}) %collective-permute-start.6) | collective-permute-done | bytes 524320 | tf_op jit(solution)/shard_map/ppermute | solution.py:339
  35.3 4.4 %collective-permute-done.4.refs_0_ = bf16[2048,256]{1,0:T(8,128)(2,1)S(1)} collective-permute-done((bf16[2048,256]{1,0:T(8,128)(2,1)S(1)}, bf16[2048,256]{1,0:T(8,128)(2,1)S(1)}, u32[]{:S(2)}, u32[]{:S(2)}) %collective-permute-start.4) | collective-permute-done | bytes 1048608 | tf_op jit(solution)/shard_map/ppermute | solution.py:335
  39.7 1.0 copy-done.5
  40.8 0.9 collective-permute-start.7
  41.7 1.6 collective-permute-start.8
  43.3 0.7 collective-permute-start.16
  44.1 3.7 %collective-permute-done.7.refs_0_ = bf16[1,64,2048]{2,1,0:T(8,128)(2,1)S(1)} collective-permute-done((bf16[1,64,2048]{2,1,0:T(8,128)(2,1)S(1)}, bf16[1,64,2048]{2,1,0:T(8,128)(2,1)S(1)}, u32[]{:S(2)}, u32[]{:S(2)}) %collective-permute-start.7) | collective-permute-done | bytes 262176 | tf_op jit(solution)/shard_map/ppermute | solution.py:339
  47.7 0.5 collective-permute-done.8.refs_1_
  48.2 0.7 copy-done.13
  49.0 0.7 copy-done.15
  49.7 1.5 collective-permute-start.22
  51.2 0.5 collective-permute-start.23
  51.7 1.0 constant_dynamic-update-slice_fusion.refs_6_
  52.7 0.6 collective-permute-done.22
  53.2 1.4 collective-permute-start.24
  54.7 3.0 %collective-permute-done.24 = s32[2,8]{1,0:T(2,128)S(1)} collective-permute-done((s32[2,8]{1,0:T(2,128)S(1)}, s32[2,8]{1,0:T(2,128)S(1)}, u32[]{:S(2)}, u32[]{:S(2)}) %collective-permute-start.24) | collective-permute-done | bytes 96 | tf_op jit(solution)/shard_map/ppermute | solution.py:339
  57.7 0.5 collective-permute-start.21
  58.5 0.6 gather_fusion
  59.2 1.0 constant_dynamic-update-slice_fusion.3
  60.3 1.0 constant_dynamic-update-slice_fusion.2.refs_7_
  61.4 0.8 copy-done.24
  62.1 9.6 %project.1.refs_1_ = f32[4,256,128]{2,1,0:T(8,128)} custom-call(s32[16]{0:T(128)} %get-tuple-element.35.idx, s32[16]{0:T(128)} %copy-done.19, s32[16]{0:T(128)} %count.7, bf16[2048,2048]{1,0:T(8,128)(2,1)} %x.4, bf16[2,64,2048]{2,1,0:T(8,128)(2,1)} %refs_0_.3, bf16[2,64,2048]{2,1,0:T(8,128)(2,1)} %collective-permute-done.17.refs_1_, ...), custom_call_target="tpu_custom_call" | custom-call | bytes 1200000 | tf_op jit(solution)/shard_map/project/pallas_call | solution.py:105
  71.8 1.0 copy-done.8
  72.8 0.8 copy-done.9
  73.6 1.0 collective-permute-start.25
  74.6 37.5 %all_to_all.15.refs_1_ = f32[4,256,128]{2,1,0:T(8,128)S(1)} all-to-all(f32[4,256,128]{2,1,0:T(8,128)} %copy-done.9), channel_id=1, replica_groups=mesh['dp'=8,'tsp'=4] {'tsp'}, dimensions={0} | all-to-all | bytes 1048576 | tf_op jit(solution)/shard_map/all_to_all | solution.py:407
  112.1 0.8 broadcast_in_dim.86
  112.9 3.4 %all-to-all-start.1 = ((bf16[4,256,128]{2,1,0:T(8,128)(2,1)}), bf16[4,256,128]{2,1,0:T(8,128)(2,1)S(1)}, u32[]{:S(2)}, u32[]{:S(2)}) async-start(bf16[4,256,128]{2,1,0:T(8,128)(2,1)} %broadcast_in_dim.86), calls=%async_computation.1 | async-start | bytes 524288 | tf_op jit(solution)/shard_map/all_to_all | solution.py:412
  116.4 0.5 collective-permute-start.13
  117.0 0.4 collective-permute-start.15
  117.4 0.7 collective-permute-done.3.refs_1_
  118.1 0.3 collective-permute-done.13.refs_3_
  118.4 0.4 collective-permute-done.14.refs_5_
  118.8 0.4 collective-permute-done.15.refs_7_
  119.2 11.4 %down_sums.1 = (bf16[8,64,2304]{2,1,0:T(8,128)(2,1)}, bf16[2048,64]{1,0:T(8,128)(2,1)}) custom-call(s32[1]{0:T(128)} %bitcast.z, s32[16]{0:T(128)} %get-tuple-element.35.idx, s32[16]{0:T(128)} %copy-done.22, s32[16]{0:T(128)} %copy-done.19, s32[16]{0:T(128)} %count.7, bf16[2048,2048]{1,0:T(8,128)(2,1)} %x.4, bf16[4,2,64,256]{3,2,1,0:T(8,128)(2,1)} %copy-done.26, ...), custom_call_target="tpu_custom_call" | custom-call | bytes 2100000 | tf_op jit(solution)/shard_map/down_sums/pallas_call | solution.py:226
  130.6 0.7 copy-done.17
  131.3 1.2 copy-done.11
  132.5 0.9 copy-done.18
  133.5 0.7 copy-done.23
  134.2 1.9 %up_sums.1 = bf16[8,64,2304]{2,1,0:T(8,128)(2,1)} custom-call(s32[16]{0:T(128)S(1)} %copy-done.23, s32[16]{0:T(128)S(1)} %copy-done.20, s32[16]{0:T(128)S(1)} %copy-done.21, bf16[2048,256]{1,0:T(8,128)(2,1)S(1)} %copy-done.11, bf16[4,256,128]{2,1,0:T(8,128)(2,1)S(1)} %copy-done.18, ...), custom_call_target="tpu_custom_call", output_to_operand_aliasing={{}: (5, {})} | custom-call | bytes 600000 | tf_op jit(solution)/shard_map/up_sums/pallas_call | solution.py:162
  136.1 3.6 %all-to-all-start.2 = ((bf16[8,64,2304]{2,1,0:T(8,128)(2,1)}), bf16[8,64,2304]{2,1,0:T(8,128)(2,1)S(1)}, u32[]{:S(2)}, u32[]{:S(2)}) async-start(bf16[8,64,2304]{2,1,0:T(8,128)(2,1)} %up_sums.1), calls=%async_computation.2 | async-start | bytes 4718592 | tf_op jit(solution)/shard_map/all_to_all | solution.py:418
  139.7 21.2 %token_gradient.1 = bf16[2048,2048]{1,0:T(8,128)(2,1)} custom-call(s32[1]{0:T(128)} %bitcast.z, s32[16]{0:T(128)} %get-tuple-element.35.idx, s32[16]{0:T(128)} %copy-done.19, s32[16]{0:T(128)} %count.7, bf16[2048,1024]{1,0:T(8,128)(2,1)} %weight.1, bf16[2048,64]{1,0:T(8,128)(2,1)} %get-tuple-element.31.pulled, bf16[2,64,2048]{2,1,0:T(8,128)(2,1)} %refs_0_.3, ...), custom_call_target="tpu_custom_call" | custom-call | bytes 4800000 | tf_op jit(solution)/shard_map/token_gradient/pallas_call | solution.py:296
  161.0 8.2 %all-to-all-done.2 = bf16[8,64,2304]{2,1,0:T(8,128)(2,1)S(1)} async-done(((bf16[8,64,2304]{2,1,0:T(8,128)(2,1)}), bf16[8,64,2304]{2,1,0:T(8,128)(2,1)S(1)}, u32[]{:S(2)}, u32[]{:S(2)}) %all-to-all-start.2) | async-done | bytes 2359328 | tf_op jit(solution)/shard_map/all_to_all | solution.py:418
  169.1 0.4 convert_element_type.7
  169.5 0.7 select_reduce_fusion
  170.3 1.1 slice.18
  171.3 0.7 slice.19
  (88 shorter events, 1.7 us)
Async XLA Ops:
  0.6 8.6 %collective-permute-start = (bf16[2,64,256]{2,1,0:T(8,128)(2,1)}, bf16[2,64,256]{2,1,0:T(8,128)(2,1)S(1)}, u32[]{:S(2)}, u32[]{:S(2)}) collective-permute-start(bf16[2,64,256]{2,1,0:T(8,128)(2,1)} %param.12), channel_id=1, source_target_pairs={{0,1},{1,2},{2,3},{3,0},{4,5},{5,6},{6,7},{7,4},{8,9},{9,10},{10,1... | collective-permute-start | bytes 196616 | tf_op jit(solution)/shard_map/ppermute | solution.py:371
  3.7 7.3 %collective-permute-start.1 = (bf16[2,64,256]{2,1,0:T(8,128)(2,1)}, bf16[2,64,256]{2,1,0:T(8,128)(2,1)S(1)}, u32[]{:S(2)}, u32[]{:S(2)}) collective-permute-start(bf16[2,64,256]{2,1,0:T(8,128)(2,1)} %param.12), channel_id=1, source_target_pairs={{0,2},{1,3},{2,0},{3,1},{4,6},{5,7},{6,4},{7,5},{8,10},{9,11},{10,... | collective-permute-start | bytes 196616 | tf_op jit(solution)/shard_map/ppermute | solution.py:371
  6.3 4.9 %collective-permute-start.2 = (bf16[2,64,256]{2,1,0:T(8,128)(2,1)}, bf16[2,64,256]{2,1,0:T(8,128)(2,1)S(1)}, u32[]{:S(2)}, u32[]{:S(2)}) collective-permute-start(bf16[2,64,256]{2,1,0:T(8,128)(2,1)} %param.12), channel_id=1, source_target_pairs={{0,3},{1,0},{2,1},{3,2},{4,7},{5,4},{6,5},{7,6},{8,11},{9,8},{10,9... | collective-permute-start | bytes 196616 | tf_op jit(solution)/shard_map/ppermute | solution.py:371
  9.2 52.1 %copy-start.19 = (s32[16]{0:T(128)}, s32[16]{0:T(128)S(1)}, u32[]{:S(2)}) copy-start(s32[16]{0:T(128)S(1)} %fusion.3.off) | copy-start | bytes 196
  11.2 1.2 copy-start.10
  13.2 58.5 %copy-start = (bf16[2048,256]{1,0:T(8,128)(2,1)}, bf16[2048,256]{1,0:T(8,128)(2,1)S(1)}, u32[]{:S(2)}) copy-start(bf16[2048,256]{1,0:T(8,128)(2,1)S(1)} %pack.1.refs_8_) | copy-start | bytes 3145732
  13.2 26.5 %collective-permute-start.4 = (bf16[2048,256]{1,0:T(8,128)(2,1)S(1)}, bf16[2048,256]{1,0:T(8,128)(2,1)S(1)}, u32[]{:S(2)}, u32[]{:S(2)}) collective-permute-start(bf16[2048,256]{1,0:T(8,128)(2,1)S(1)} %pack.1.refs_8_), channel_id=1, source_target_pairs={{0,1},{1,2},{2,3},{3,0},{4,5},{5,6},{6,7},{7,4},{8,9},{9,10},{10,1... | collective-permute-start | bytes 3145736 | tf_op jit(solution)/shard_map/ppermute | solution.py:335
  14.9 13.7 %collective-permute-start.5 = (bf16[2,64,2048]{2,1,0:T(8,128)(2,1)}, bf16[2,64,2048]{2,1,0:T(8,128)(2,1)S(1)}, u32[]{:S(2)}, u32[]{:S(2)}) collective-permute-start(bf16[2,64,2048]{2,1,0:T(8,128)(2,1)} %refs_0_.3), channel_id=1, source_target_pairs={{0,8},{4,12},{8,0},{12,4},{16,24},{20,28},{24,16},{28,20},{1,9},{5... | collective-permute-start | bytes 1572872 | tf_op jit(solution)/shard_map/ppermute | solution.py:339
  16.3 19.0 %collective-permute-start.6 = (bf16[2,64,2048]{2,1,0:T(8,128)(2,1)}, bf16[2,64,2048]{2,1,0:T(8,128)(2,1)S(1)}, u32[]{:S(2)}, u32[]{:S(2)}) collective-permute-start(bf16[2,64,2048]{2,1,0:T(8,128)(2,1)} %refs_0_.3), channel_id=1, source_target_pairs={{0,16},{4,20},{8,24},{12,28},{16,0},{20,4},{24,8},{28,12},{1,17},{... | collective-permute-start | bytes 1572872 | tf_op jit(solution)/shard_map/ppermute | solution.py:339
  19.2 99.9 %copy-start.22 = (s32[16]{0:T(128)}, s32[16]{0:T(128)S(1)}, u32[]{:S(2)}) copy-start(s32[16]{0:T(128)S(1)} %get-tuple-element.36.owner) | copy-start | bytes 196
  19.4 22.3 %collective-permute-start.12 = (s32[1,8]{1,0:T(1,128)S(1)}, s32[1,8]{1,0:T(1,128)S(1)}, u32[]{:S(2)}, u32[]{:S(2)}) collective-permute-start(s32[1,8]{1,0:T(1,128)S(1)} %bitcast.14), channel_id=1, source_target_pairs={{0,4},{4,0},{8,12},{12,8},{16,20},{20,16},{24,28},{28,24},{1,5},{5... | collective-permute-start | bytes 104 | tf_op jit(solution)/shard_map/ppermute | solution.py:339
  20.3 37.9 %copy-start.26 = (bf16[4,2,64,256]{3,2,1,0:T(8,128)(2,1)}, bf16[4,2,64,256]{3,2,1,0:T(8,128)(2,1)S(1)}, u32[]{:S(2)}) copy-start(bf16[4,2,64,256]{3,2,1,0:T(8,128)(2,1)S(1)} %pad_maximum_fusion.refs_0_) | copy-start | bytes 786436
  20.3 22.9 %collective-permute-start.10 = (bf16[4,2,64,256]{3,2,1,0:T(8,128)(2,1)S(1)}, bf16[4,2,64,256]{3,2,1,0:T(8,128)(2,1)S(1)}, u32[]{:S(2)}, u32[]{:S(2)}) collective-permute-start(bf16[4,2,64,256]{3,2,1,0:T(8,128)(2,1)S(1)} %pad_maximum_fusion.refs_0_), channel_id=1, source_target_pairs={{0,16},{4,20},{8,24},{12,28},{16,0},{20,4},{24,8},{28,12},{1,17},{... | collective-permute-start | bytes 786440 | tf_op jit(solution)/shard_map/ppermute | solution.py:339
  28.6 6.8 %copy-start.4 = (bf16[2,64,2048]{2,1,0:T(8,128)(2,1)}, bf16[2,64,2048]{2,1,0:T(8,128)(2,1)S(1)}, u32[]{:S(2)}) copy-start(bf16[2,64,2048]{2,1,0:T(8,128)(2,1)S(1)} %collective-permute-done.5.refs_1_) | copy-start | bytes 1572868
  28.6 15.4 %collective-permute-start.11 = (bf16[4,2,64,256]{3,2,1,0:T(8,128)(2,1)S(1)}, bf16[4,2,64,256]{3,2,1,0:T(8,128)(2,1)S(1)}, u32[]{:S(2)}, u32[]{:S(2)}) collective-permute-start(bf16[4,2,64,256]{3,2,1,0:T(8,128)(2,1)S(1)} %pad_maximum_fusion.refs_0_), channel_id=1, source_target_pairs={{0,24},{4,28},{8,16},{12,20},{16,8},{20,12},{24,0},{28,4},{1,25},{... | collective-permute-start | bytes 786440 | tf_op jit(solution)/shard_map/ppermute | solution.py:339
  35.3 8.7 %collective-permute-start.9 = (bf16[4,2,64,256]{3,2,1,0:T(8,128)(2,1)S(1)}, bf16[4,2,64,256]{3,2,1,0:T(8,128)(2,1)S(1)}, u32[]{:S(2)}, u32[]{:S(2)}) collective-permute-start(bf16[4,2,64,256]{3,2,1,0:T(8,128)(2,1)S(1)} %pad_maximum_fusion.refs_0_), channel_id=1, source_target_pairs={{0,8},{4,12},{8,0},{12,4},{16,24},{20,28},{24,16},{28,20},{1,9},{5... | collective-permute-start | bytes 786440 | tf_op jit(solution)/shard_map/ppermute | solution.py:339
  39.7 1.0 copy-start.5
  40.8 2.5 %copy-start.6 = (bf16[2,64,2048]{2,1,0:T(8,128)(2,1)}, bf16[2,64,2048]{2,1,0:T(8,128)(2,1)S(1)}, u32[]{:S(2)}) copy-start(bf16[2,64,2048]{2,1,0:T(8,128)(2,1)S(1)} %get-tuple-element.19.refs_2_) | copy-start | bytes 1572868
  40.8 2.5 %copy-start.7 = (bf16[2,64,2048]{2,1,0:T(8,128)(2,1)}, bf16[2,64,2048]{2,1,0:T(8,128)(2,1)S(1)}, u32[]{:S(2)}) copy-start(bf16[2,64,2048]{2,1,0:T(8,128)(2,1)S(1)} %get-tuple-element.20.refs_4_) | copy-start | bytes 1572868
  40.8 31.0 %copy-start.2 = (bf16[2048,256]{1,0:T(8,128)(2,1)}, bf16[2048,256]{1,0:T(8,128)(2,1)S(1)}, u32[]{:S(2)}) copy-start(bf16[2048,256]{1,0:T(8,128)(2,1)S(1)} %get-tuple-element.24.refs_9_) | copy-start | bytes 3145732
  40.8 7.0 %collective-permute-start.7 = (bf16[1,64,2048]{2,1,0:T(8,128)(2,1)S(1)}, bf16[1,64,2048]{2,1,0:T(8,128)(2,1)S(1)}, u32[]{:S(2)}, u32[]{:S(2)}) collective-permute-start(bf16[1,64,2048]{2,1,0:T(8,128)(2,1)S(1)} %slice.12), channel_id=1, source_target_pairs={{0,16},{4,20},{8,24},{12,28},{16,0},{20,4},{24,8},{28,12},{1,17},{... | collective-permute-start | bytes 786440 | tf_op jit(solution)/shard_map/ppermute | solution.py:339
  41.7 6.5 %collective-permute-start.8 = (bf16[1,64,2048]{2,1,0:T(8,128)(2,1)S(1)}, bf16[1,64,2048]{2,1,0:T(8,128)(2,1)}, u32[]{:S(2)}, u32[]{:S(2)}) collective-permute-start(bf16[1,64,2048]{2,1,0:T(8,128)(2,1)S(1)} %slice.13), channel_id=1, source_target_pairs={{0,8},{4,12},{8,0},{12,4},{16,24},{20,28},{24,16},{28,20},{1,9},{5... | collective-permute-start | bytes 786440 | tf_op jit(solution)/shard_map/ppermute | solution.py:339
  43.3 28.5 %collective-permute-start.16 = (bf16[2048,256]{1,0:T(8,128)(2,1)S(1)}, bf16[2048,256]{1,0:T(8,128)(2,1)S(1)}, u32[]{:S(2)}, u32[]{:S(2)}) collective-permute-start(bf16[2048,256]{1,0:T(8,128)(2,1)S(1)} %get-tuple-element.24.refs_9_), channel_id=1, source_target_pairs={{0,1},{1,2},{2,3},{3,0},{4,5},{5,6},{6,7},{7,4},{8,9},{9,10},{10,1... | collective-permute-start | bytes 3145736 | tf_op jit(solution)/shard_map/ppermute | solution.py:335
  44.0 17.4 %collective-permute-start.17 = (bf16[2,64,2048]{2,1,0:T(8,128)(2,1)}, bf16[2,64,2048]{2,1,0:T(8,128)(2,1)}, u32[]{:S(2)}, u32[]{:S(2)}) collective-permute-start(bf16[2,64,2048]{2,1,0:T(8,128)(2,1)} %refs_0_.3), channel_id=1, source_target_pairs={{0,4},{4,0},{8,12},{12,8},{16,20},{20,16},{24,28},{28,24},{1,5},{5... | collective-permute-start | bytes 1572872 | tf_op jit(solution)/shard_map/ppermute | solution.py:339
  48.2 0.7 copy-start.13
  49.0 0.7 copy-start.15
  49.7 67.2 %copy-start.12 = (bf16[4,2,64,256]{3,2,1,0:T(8,128)(2,1)}, bf16[4,2,64,256]{3,2,1,0:T(8,128)(2,1)S(1)}, u32[]{:S(2)}) copy-start(bf16[4,2,64,256]{3,2,1,0:T(8,128)(2,1)S(1)} %get-tuple-element.22.refs_4_) | copy-start | bytes 786436
  49.7 3.6 %collective-permute-start.22 = (s32[2,8]{1,0:T(2,128)S(1)}, s32[2,8]{1,0:T(2,128)S(1)}, u32[]{:S(2)}, u32[]{:S(2)}) collective-permute-start(s32[2,8]{1,0:T(2,128)S(1)} %get-tuple-element.27), channel_id=1, source_target_pairs={{0,8},{4,12},{8,0},{12,4},{16,24},{20,28},{24,16},{28,20},{1,9},{5... | collective-permute-start | bytes 200 | tf_op jit(solution)/shard_map/ppermute | solution.py:339
  51.2 3.6 %collective-permute-start.23 = (s32[2,8]{1,0:T(2,128)S(1)}, s32[2,8]{1,0:T(2,128)S(1)}, u32[]{:S(2)}, u32[]{:S(2)}) collective-permute-start(s32[2,8]{1,0:T(2,128)S(1)} %get-tuple-element.27), channel_id=1, source_target_pairs={{0,16},{4,20},{8,24},{12,28},{16,0},{20,4},{24,8},{28,12},{1,17},{... | collective-permute-start | bytes 200 | tf_op jit(solution)/shard_map/ppermute | solution.py:339
  51.7 6.0 %collective-permute-start.20 = (bf16[1,64,2048]{2,1,0:T(8,128)(2,1)S(1)}, bf16[1,64,2048]{2,1,0:T(8,128)(2,1)S(1)}, u32[]{:S(2)}, u32[]{:S(2)}) collective-permute-start(bf16[1,64,2048]{2,1,0:T(8,128)(2,1)S(1)} %get-tuple-element.25), channel_id=1, source_target_pairs={{0,4},{4,0},{8,12},{12,8},{16,20},{20,16},{24,28},{28,24},{1,5},{5... | collective-permute-start | bytes 786440 | tf_op jit(solution)/shard_map/ppermute | solution.py:339
  52.7 5.6 %copy-start.25 = (bf16[2,64,2048]{2,1,0:T(8,128)(2,1)}, bf16[2,64,2048]{2,1,0:T(8,128)(2,1)S(1)}, u32[]{:S(2)}) copy-start(bf16[2,64,2048]{2,1,0:T(8,128)(2,1)S(1)} %constant_dynamic-update-slice_fusion.refs_6_) | copy-start | bytes 1572868
  53.2 4.5 %collective-permute-start.24 = (s32[2,8]{1,0:T(2,128)S(1)}, s32[2,8]{1,0:T(2,128)S(1)}, u32[]{:S(2)}, u32[]{:S(2)}) collective-permute-start(s32[2,8]{1,0:T(2,128)S(1)} %get-tuple-element.27), channel_id=1, source_target_pairs={{0,24},{4,28},{8,16},{12,20},{16,8},{20,12},{24,0},{28,4},{1,25},{... | collective-permute-start | bytes 200 | tf_op jit(solution)/shard_map/ppermute | solution.py:339
  54.7 6.6 %collective-permute-start.18 = (bf16[2,64,2048]{2,1,0:T(8,128)(2,1)}, bf16[2,64,2048]{2,1,0:T(8,128)(2,1)}, u32[]{:S(2)}, u32[]{:S(2)}) collective-permute-start(bf16[2,64,2048]{2,1,0:T(8,128)(2,1)} %copy-done.6), channel_id=1, source_target_pairs={{0,4},{4,0},{8,12},{12,8},{16,20},{20,16},{24,28},{28,24},{1,5},{5... | collective-permute-start | bytes 1572872 | tf_op jit(solution)/shard_map/ppermute | solution.py:339
  57.7 3.6 %collective-permute-start.19 = (bf16[2,64,2048]{2,1,0:T(8,128)(2,1)}, bf16[2,64,2048]{2,1,0:T(8,128)(2,1)}, u32[]{:S(2)}, u32[]{:S(2)}) collective-permute-start(bf16[2,64,2048]{2,1,0:T(8,128)(2,1)} %copy-done.7), channel_id=1, source_target_pairs={{0,4},{4,0},{8,12},{12,8},{16,20},{20,16},{24,28},{28,24},{1,5},{5... | collective-permute-start | bytes 1572872 | tf_op jit(solution)/shard_map/ppermute | solution.py:339
  57.7 0.7 copy-start.28
  57.7 2.6 %collective-permute-start.21 = (bf16[1,64,2048]{2,1,0:T(8,128)(2,1)}, bf16[1,64,2048]{2,1,0:T(8,128)(2,1)}, u32[]{:S(2)}, u32[]{:S(2)}) collective-permute-start(bf16[1,64,2048]{2,1,0:T(8,128)(2,1)} %get-tuple-element.26), channel_id=1, source_target_pairs={{0,4},{4,0},{8,12},{12,8},{16,20},{20,16},{24,28},{28,24},{1,5},{5... | collective-permute-start | bytes 786440 | tf_op jit(solution)/shard_map/ppermute | solution.py:339
  61.3 0.8 copy-start.24
  71.8 1.0 copy-start.8
  72.8 43.6 %copy-start.16 = (bf16[4,2,64,256]{3,2,1,0:T(8,128)(2,1)S(1)}, bf16[4,2,64,256]{3,2,1,0:T(8,128)(2,1)}, u32[]{:S(2)}) copy-start(bf16[4,2,64,256]{3,2,1,0:T(8,128)(2,1)} %copy-done.15) | copy-start | bytes 786436
  72.8 44.2 %copy-start.14 = (bf16[4,2,64,256]{3,2,1,0:T(8,128)(2,1)S(1)}, bf16[4,2,64,256]{3,2,1,0:T(8,128)(2,1)}, u32[]{:S(2)}) copy-start(bf16[4,2,64,256]{3,2,1,0:T(8,128)(2,1)} %copy-done.13) | copy-start | bytes 786436
  72.8 0.8 copy-start.9
  73.6 45.6 %copy-start.1 = (bf16[2048,256]{1,0:T(8,128)(2,1)}, bf16[2048,256]{1,0:T(8,128)(2,1)S(1)}, u32[]{:S(2)}) copy-start(bf16[2048,256]{1,0:T(8,128)(2,1)S(1)} %get-tuple-element.28.refs_10_) | copy-start | bytes 3145732
  73.6 38.4 %collective-permute-start.25 = (bf16[2048,256]{1,0:T(8,128)(2,1)S(1)}, bf16[2048,256]{1,0:T(8,128)(2,1)S(1)}, u32[]{:S(2)}, u32[]{:S(2)}) collective-permute-start(bf16[2048,256]{1,0:T(8,128)(2,1)S(1)} %get-tuple-element.28.refs_10_), channel_id=1, source_target_pairs={{0,1},{1,2},{2,3},{3,0},{4,5},{5,6},{6,7},{7,4},{8,9},{9,10},{10,1... | collective-permute-start | bytes 3145736 | tf_op jit(solution)/shard_map/ppermute | solution.py:335
  112.1 7.1 %copy-start.3 = (bf16[2048,256]{1,0:T(8,128)(2,1)}, bf16[2048,256]{1,0:T(8,128)(2,1)S(1)}, u32[]{:S(2)}) copy-start(bf16[2048,256]{1,0:T(8,128)(2,1)S(1)} %get-tuple-element.30.refs_11_) | copy-start | bytes 3145732
  112.9 17.7 %all-to-all-start.1 = ((bf16[4,256,128]{2,1,0:T(8,128)(2,1)}), bf16[4,256,128]{2,1,0:T(8,128)(2,1)S(1)}, u32[]{:S(2)}, u32[]{:S(2)}) async-start(bf16[4,256,128]{2,1,0:T(8,128)(2,1)} %broadcast_in_dim.86), calls=%async_computation.1 | async-start | bytes 524288 | tf_op jit(solution)/shard_map/all_to_all | solution.py:412
  116.3 1.8 %collective-permute-start.3 = (bf16[4,2,64,256]{3,2,1,0:T(8,128)(2,1)}, bf16[4,2,64,256]{3,2,1,0:T(8,128)(2,1)S(1)}, u32[]{:S(2)}, u32[]{:S(2)}) collective-permute-start(bf16[4,2,64,256]{3,2,1,0:T(8,128)(2,1)} %copy-done.26), channel_id=1, source_target_pairs={{0,4},{4,0},{8,12},{12,8},{16,20},{20,16},{24,28},{28,24},{1,5},{5... | collective-permute-start | bytes 786440 | tf_op jit(solution)/shard_map/ppermute | solution.py:339
  116.4 2.0 %collective-permute-start.13 = (bf16[4,2,64,256]{3,2,1,0:T(8,128)(2,1)S(1)}, bf16[4,2,64,256]{3,2,1,0:T(8,128)(2,1)}, u32[]{:S(2)}, u32[]{:S(2)}) collective-permute-start(bf16[4,2,64,256]{3,2,1,0:T(8,128)(2,1)S(1)} %copy-done.16), channel_id=1, source_target_pairs={{0,4},{4,0},{8,12},{12,8},{16,20},{20,16},{24,28},{28,24},{1,5},{5... | collective-permute-start | bytes 786440 | tf_op jit(solution)/shard_map/ppermute | solution.py:339
  116.9 1.9 %collective-permute-start.14 = (bf16[4,2,64,256]{3,2,1,0:T(8,128)(2,1)S(1)}, bf16[4,2,64,256]{3,2,1,0:T(8,128)(2,1)}, u32[]{:S(2)}, u32[]{:S(2)}) collective-permute-start(bf16[4,2,64,256]{3,2,1,0:T(8,128)(2,1)S(1)} %get-tuple-element.22.refs_4_), channel_id=1, source_target_pairs={{0,4},{4,0},{8,12},{12,8},{16,20},{20,16},{24,28},{28,24},{1,5},{5... | collective-permute-start | bytes 786440 | tf_op jit(solution)/shard_map/ppermute | solution.py:339
  117.0 2.2 %collective-permute-start.15 = (bf16[4,2,64,256]{3,2,1,0:T(8,128)(2,1)S(1)}, bf16[4,2,64,256]{3,2,1,0:T(8,128)(2,1)}, u32[]{:S(2)}, u32[]{:S(2)}) collective-permute-start(bf16[4,2,64,256]{3,2,1,0:T(8,128)(2,1)S(1)} %copy-done.14), channel_id=1, source_target_pairs={{0,4},{4,0},{8,12},{12,8},{16,20},{20,16},{24,28},{28,24},{1,5},{5... | collective-permute-start | bytes 786440 | tf_op jit(solution)/shard_map/ppermute | solution.py:339
  118.1 1.1 copy-start.27
  119.2 12.1 %copy-start.20 = (s32[16]{0:T(128)S(1)}, s32[16]{0:T(128)}, u32[]{:S(2)}) copy-start(s32[16]{0:T(128)} %copy-done.19) | copy-start | bytes 196
  119.2 12.1 %copy-start.21 = (s32[16]{0:T(128)S(1)}, s32[16]{0:T(128)}, u32[]{:S(2)}) copy-start(s32[16]{0:T(128)} %count.7) | copy-start | bytes 196
  130.6 0.7 copy-start.17
  131.3 1.2 copy-start.11
  132.5 0.9 copy-start.18
  133.5 0.7 copy-start.23
  136.1 33.0 %all-to-all-start.2 = ((bf16[8,64,2304]{2,1,0:T(8,128)(2,1)}), bf16[8,64,2304]{2,1,0:T(8,128)(2,1)S(1)}, u32[]{:S(2)}, u32[]{:S(2)}) async-start(bf16[8,64,2304]{2,1,0:T(8,128)(2,1)} %up_sums.1), calls=%async_computation.2 | async-start | bytes 4718592 | tf_op jit(solution)/shard_map/all_to_all | solution.py:418

commit v3 on v2

v3 whole, which is shorter than its diff:
```python
import functools

import jax
import jax.numpy as jnp
from jax import lax
from jax.experimental import pallas as pl
from jax.experimental.pallas import tpu as pltpu
from jax.sharding import PartitionSpec as P

ADAPTER_SCALE = 2.0
HBM = pl.BlockSpec(memory_space=pltpu.HBM)
SMEM = pl.BlockSpec(memory_space=pltpu.SMEM)
VMEM = pl.BlockSpec(memory_space=pltpu.VMEM)
NT = (((1,), (1,)), ((), ()))
TN = (((0,), (0,)), ((), ()))
NN = (((1,), (0,)), ((), ()))
MIB = 1024 * 1024


def params(mib=60):
    return pltpu.CompilerParams(vmem_limit_bytes=mib * MIB)


def cost(us):
    return pl.CostEstimate(flops=0, bytes_accessed=int(us * 3e5), transcendentals=0)


def map_copies(maps, table, sem):
    copies, first = [], 0
    for i, m in enumerate(maps):
        copies.append(pltpu.make_async_copy(m, table.at[pl.ds(first, m.shape[0])], sem.at[i]))
        first += m.shape[0]
    return copies


def load_all(copies):
    for copy in copies:
        copy.start()
    for copy in copies:
        copy.wait()


def live_mask(count, rows, width):
    return lax.broadcasted_iota(jnp.int32, (rows, width), 0) < count


def plan_kernel(held, cube, me, table, adapter, owner, idx, wanted):
    for k in range(wanted.shape[0]):
        wanted[k] = -1
    for g in range(owner.shape[0]):
        place = table[adapter[g]]
        who = lax.div(place, held)
        owner[g] = who
        wanted[who] = lax.rem(place, held)
        idx[g] = lax.bitwise_xor(who, me[0]) * held + lax.rem(place, held) if cube else place


def plan(me, table, adapter, held, owners, cube):
    whole = lambda length: jax.ShapeDtypeStruct((length,), jnp.int32)
    segs = adapter.shape[0]
    return pl.pallas_call(
        functools.partial(plan_kernel, held, cube),
        out_shape=[whole(segs), whole(segs), whole(owners)],
        in_specs=[SMEM] * 3,
        out_specs=[SMEM] * 3,
        compiler_params=params(),
        cost_estimate=cost(1),
        name="plan",
    )(me, table, adapter)


def project_kernel(n, per, rows, n_maps, idx, count, x, *refs):
    maps, (out, table, buf, sem) = refs[:n_maps], refs[-4:]
    step = pl.program_id(0)

    @pl.when(step == 0)
    def _():
        load_all(map_copies(maps, table, sem))

    for i in range(per):
        g = step * per + i
        term = lax.dot_general(
            table[idx[g]], x[i * rows : (i + 1) * rows, :], NT, preferred_element_type=jnp.float32
        ).T
        term = jnp.where(live_mask(count[g], *term.shape), term, 0.0)
        buf[pl.ds(pl.multiple_of(g * rows, rows), rows), :] = term

    @pl.when(step == pl.num_programs(0) - 1)
    def _():
        half = out.shape[1]
        for j in range(n):
            start = 2 * j * half
            out[j] = jnp.concatenate(
                [buf[start : start + half, :], buf[start + half : start + 2 * half, :]], axis=1
            )


def project(idx, count, x, maps, n, per, us):
    segs = idx.shape[0]
    rows, width = x.shape[0] // segs, x.shape[1]
    ranks = maps[0].shape[1]
    total = sum(m.shape[0] for m in maps)
    shape = (n, x.shape[0] // n // 2, 2 * ranks)
    return pl.pallas_call(
        functools.partial(project_kernel, n, per, rows, len(maps)),
        grid=(segs // per,),
        out_shape=jax.ShapeDtypeStruct(shape, jnp.float32),
        in_specs=[SMEM] * 2 + [pl.BlockSpec((per * rows, width), lambda i: (i, 0))] + [HBM] * len(maps),
        out_specs=pl.BlockSpec(shape, lambda i: (0, 0, 0)),
        scratch_shapes=[
            pltpu.VMEM((total, ranks, width), x.dtype),
            pltpu.VMEM((x.shape[0], ranks), jnp.float32),
            pltpu.SemaphoreType.DMA((len(maps),)),
        ],
        compiler_params=params(),
        cost_estimate=cost(us),
        name="project",
    )(idx, count, x, *maps)


def cot_copies(n, z, cots, cot, sem):
    key = cots[0].shape[1]
    copies = []
    for s in range(n):
        column = pl.multiple_of(lax.rem(z - s + n, n) * key, key)
        copies.append(pltpu.make_async_copy(cots[s], cot.at[:, pl.ds(column, key)], sem.at[s]))
    return copies


def add_terms(total, owner, terms, x):
    total[owner] += lax.dot_general(terms, x, TN, preferred_element_type=jnp.float32)


def up_sums_kernel(n, rows, scale, z, owner, x_hbm, *refs):
    blocks, (out, x, raw, buf, total, sem) = refs[:n], refs[-6:]
    half, ranks = raw.shape[1], raw.shape[2] // 2
    copies = [pltpu.make_async_copy(x_hbm, x, sem.at[n])]
    for s in range(n):
        copies.append(pltpu.make_async_copy(blocks[s], raw.at[lax.rem(z[0] - s + n, n)], sem.at[s]))
    for copy in copies:
        copy.start()
    total[...] = jnp.zeros_like(total)
    for copy in copies:
        copy.wait()
    for j in range(n):
        start = 2 * j * half
        buf[start : start + half, :] = raw[j][:, :ranks]
        buf[start + half : start + 2 * half, :] = raw[j][:, ranks:]
    for g in range(x.shape[0] // rows):
        add_terms(total, owner[g], buf[g * rows : (g + 1) * rows, :], x[g * rows : (g + 1) * rows, :])
    out[...] = (total[...] * scale).astype(out.dtype)


def up_sums(z, owner, x, blocks, owners, us, after=()):
    segs, n = owner.shape[0], len(blocks)
    rows, width = x.shape[0] // segs, x.shape[1]
    ranks = blocks[0].shape[1] // 2
    shape = (owners, ranks, width)
    return pl.pallas_call(
        functools.partial(up_sums_kernel, n, rows, ADAPTER_SCALE / rows),
        out_shape=jax.ShapeDtypeStruct(shape, jnp.bfloat16),
        in_specs=[SMEM] * 2 + [HBM] * (1 + n + len(after)),
        out_specs=VMEM,
        scratch_shapes=[
            pltpu.VMEM(x.shape, x.dtype),
            pltpu.VMEM((n, *blocks[0].shape), jnp.bfloat16),
            pltpu.VMEM((x.shape[0], ranks), jnp.bfloat16),
            pltpu.VMEM(shape, jnp.float32),
            pltpu.SemaphoreType.DMA((n + 1,)),
        ],
        compiler_params=params(),
        cost_estimate=cost(us),
        name="up_sums",
    )(z, owner, x, *blocks, *after)


def down_sums_kernel(n, per, rows, n_maps, scale, z, idx, owner, count, x, *refs):
    maps, refs = refs[:n_maps], refs[n_maps:]
    cots, (out, pulled, table, cot, total, map_sem, cot_sem) = refs[:n], refs[-7:]
    step = pl.program_id(0)

    @pl.when(step == 0)
    def _():
        copies = cot_copies(n, z[0], cots, cot, cot_sem)
        parts, held, _, key = maps[0].shape
        for i, m in enumerate(maps):
            for j in range(parts):
                column = pl.multiple_of(lax.rem(z[0] - j + n, n) * key, key)
                dst = table.at[pl.ds(i * held, held), :, pl.ds(column, key)]
                copies.append(pltpu.make_async_copy(m.at[j], dst, map_sem.at[i * parts + j]))
        for copy in copies:
            copy.start()
        total[...] = jnp.zeros_like(total)
        for copy in copies:
            copy.wait()

    for i in range(per):
        g = step * per + i
        terms = lax.dot_general(
            cot[pl.ds(pl.multiple_of(g * rows, rows), rows), :],
            table[idx[g]],
            NT,
            preferred_element_type=jnp.float32,
        )
        terms = jnp.where(live_mask(count[g], *terms.shape), terms, 0.0).astype(pulled.dtype)
        pulled[i * rows : (i + 1) * rows, :] = terms
        add_terms(total, owner[g], terms, x[i * rows : (i + 1) * rows, :])

    @pl.when(step == pl.num_programs(0) - 1)
    def _():
        out[...] = (total[...] * scale).astype(out.dtype)


def down_sums(z, idx, owner, count, x, maps, cots, owners, n, per, us):
    segs = owner.shape[0]
    rows, width = x.shape[0] // segs, x.shape[1]
    parts, held, ranks, key = maps[0].shape
    shape = (owners, ranks, width)
    return pl.pallas_call(
        functools.partial(down_sums_kernel, n, per, rows, len(maps), ADAPTER_SCALE / rows),
        grid=(segs // per,),
        out_shape=[
            jax.ShapeDtypeStruct(shape, jnp.bfloat16),
            jax.ShapeDtypeStruct((x.shape[0], ranks), jnp.bfloat16),
        ],
        in_specs=[SMEM] * 4
        + [pl.BlockSpec((per * rows, width), lambda i: (i, 0))]
        + [HBM] * (len(maps) + n),
        out_specs=[
            pl.BlockSpec(shape, lambda i: (0, 0, 0)),
            pl.BlockSpec((per * rows, ranks), lambda i: (i, 0)),
        ],
        scratch_shapes=[
            pltpu.VMEM((held * len(maps), ranks, parts * key), jnp.bfloat16),
            pltpu.VMEM((x.shape[0], n * key), jnp.bfloat16),
            pltpu.VMEM(shape, jnp.float32),
            pltpu.SemaphoreType.DMA((parts * len(maps),)),
            pltpu.SemaphoreType.DMA((n,)),
        ],
        compiler_params=params(),
        cost_estimate=cost(us),
        name="down_sums",
    )(z, idx, owner, count, x, *maps, *cots)


def token_kernel(n, per, rows, n_maps, z, idx, count, weight, pulled, *refs):
    maps, refs = refs[:n_maps], refs[n_maps:]
    cots, (out, table, cot, map_sem, cot_sem) = refs[:n], refs[-5:]
    step = pl.program_id(0)

    @pl.when(step == 0)
    def _():
        load_all(cot_copies(n, z[0], cots, cot, cot_sem) + map_copies(maps, table, map_sem))

    width = weight.shape[1]
    tile = min(512, width)
    counts = [count[step * per + i] for i in range(per)]
    x = cot[pl.ds(pl.multiple_of(step * per * rows, per * rows), per * rows), :]
    for d in range(0, width, tile):
        total = lax.dot_general(x, weight[:, d : d + tile], NN, preferred_element_type=jnp.float32)
        for i in range(per):
            adapter = lax.dot_general(
                pulled[i * rows : (i + 1) * rows, :],
                table[idx[step * per + i], :, d : d + tile],
                NN,
                preferred_element_type=jnp.float32,
            )
            both = total[i * rows : (i + 1) * rows, :] + ADAPTER_SCALE * adapter
            both = jnp.where(live_mask(counts[i], rows, tile), both, 0.0)
            out[i * rows : (i + 1) * rows, d : d + tile] = both.astype(out.dtype)


def token_gradients(z, idx, count, weight, pulled, maps, cots, n, rows, per, after=()):
    segs = idx.shape[0]
    keys, width = weight.shape
    ranks = maps[0].shape[1]
    total = sum(m.shape[0] for m in maps)
    return pl.pallas_call(
        functools.partial(token_kernel, n, per, rows, len(maps)),
        grid=(segs // per,),
        out_shape=jax.ShapeDtypeStruct((segs * rows, width), jnp.bfloat16),
        in_specs=[SMEM] * 3
        + [pl.BlockSpec(weight.shape, lambda i: (0, 0), pipeline_mode=pl.Buffered(1))]
        + [pl.BlockSpec((per * rows, ranks), lambda i: (i, 0))]
        + [HBM] * (len(maps) + n + len(after)),
        out_specs=pl.BlockSpec((per * rows, width), lambda i: (i, 0)),
        scratch_shapes=[
            pltpu.VMEM((total, ranks, width), jnp.bfloat16),
            pltpu.VMEM((segs * rows, keys), jnp.bfloat16),
            pltpu.SemaphoreType.DMA((len(maps),)),
            pltpu.SemaphoreType.DMA((n,)),
        ],
        compiler_params=params(),
        cost_estimate=cost(16),
        name="token_gradient",
    )(z, idx, count, weight, pulled, *maps, *cots, *after)


def owned_kernel(asked, got, out):
    for e in range(out.shape[0]):
        total = jnp.zeros(got.shape[1:], jnp.float32)
        for k in range(got.shape[0]):
            total += jnp.where(asked[k] == e, got[k].astype(jnp.float32), 0.0)
        out[e] = total


def owned(asked, got, held, mib):
    peers, ranks, width = got.shape
    per = min(16, ranks)
    return pl.pallas_call(
        owned_kernel,
        grid=(ranks // per,),
        out_shape=jax.ShapeDtypeStruct((held, ranks, width), jnp.float32),
        in_specs=[SMEM, pl.BlockSpec((peers, per, width), lambda i: (0, i, 0))],
        out_specs=pl.BlockSpec((held, per, width), lambda i: (0, i, 0)),
        compiler_params=params(mib),
        cost_estimate=cost(2),
        name="owned",
    )(asked, got)


def gate_kernel(*refs):
    del refs


def gate(*arrays, after=()):
    return pl.pallas_call(
        gate_kernel,
        out_shape=[jax.ShapeDtypeStruct(a.shape, a.dtype) for a in arrays],
        in_specs=[HBM] * (len(arrays) + len(after)),
        out_specs=[HBM] * len(arrays),
        input_output_aliases={i: i for i in range(len(arrays))},
        compiler_params=params(),
        cost_estimate=cost(0),
        name="gate",
    )(*arrays, *after)


def ring(x, n):
    return lax.ppermute(x, "tsp", [(i, (i + 1) % n) for i in range(n)])


def flip(x, n, by):
    return lax.ppermute(x, "dp", [(i, i ^ by) for i in range(n)])


def on_device(
    tokens,
    cotangent,
    frozen_key_weight,
    adapter_down_weight,
    adapter_up_weight,
    adapter_place_table,
    segment_adapter,
    segment_live_count,
):
    n_dp = lax.axis_size("dp")
    n = lax.axis_size("tsp")
    me = lax.axis_index("dp").astype(jnp.int32)
    z = lax.axis_index("tsp").astype(jnp.int32)[None]
    held = adapter_down_weight.shape[0]
    segs = segment_adapter.shape[0]
    rows = tokens.shape[0] // segs
    full = segs * rows
    cube = n_dp == 8 and held == 2

    peers = jnp.arange(n_dp, dtype=jnp.int32)
    count = segment_live_count
    ups, downs = adapter_up_weight, adapter_down_weight

    cots = [cotangent, ring(cotangent, n)]
    owner, idx, wanted = plan(me[None], adapter_place_table, segment_adapter, held, n_dp, cube)
    if cube:
        over_x, over_y = gate(flip(downs, n_dp, 2), flip(downs, n_dp, 4))
        ups = gate(ups, after=[over_x, over_y])[0]
    line = [lax.ppermute(ups, "tsp", [(i, (i + s) % n) for i in range(n)]) for s in range(1, n)]
    weight = frozen_key_weight.T
    if cube:
        cots[1], ups, weight, over_x, over_y, *line = gate(cots[1], ups, weight, over_x, over_y, *line)
        corner = [flip(over_x[:1], n_dp, 4), flip(over_y[1:], n_dp, 2)]
    else:
        cots[1], ups, weight, *line = gate(cots[1], ups, weight, *line)

    while len(cots) < n - 1:
        cots.append(ring(cots[-1], n))
    up_line = jnp.stack([ups, *line])
    if cube:
        same = [downs, over_x, over_y]
        downs_here = [m for d in same for m in (d, flip(d, n_dp, 1))]
        downs_here += corner + [flip(m, n_dp, 1) for m in corner]
    else:
        downs_here = [lax.all_gather(downs, "dp", axis=0, tiled=True)]
    lowered = project(idx, count, tokens, downs_here, n, 4, 4)
    cots[-1], up_line = gate(cots[-1], up_line, after=[lowered])

    cots.append(ring(cots[-1], n))
    if cube:
        same = [up_line] + [flip(up_line, n_dp, k) for k in (2, 4, 6)]
        all_ups = [m for u in same for m in (u, flip(u, n_dp, 1))]
        word = jnp.stack([wanted, flip(wanted, n_dp, 1)])
        words = jnp.concatenate([word] + [flip(word, n_dp, k) for k in (2, 4, 6)])
        asked = jnp.sum(jnp.where(peers[None, :] == me, words, 0), axis=1)[peers ^ me]
    else:
        all_ups = [lax.all_gather(up_line, "dp", axis=1, tiled=True)]
        asked = lax.all_gather(wanted, "dp", axis=0, tiled=False)[:, me]
    cots[-1], lowered = gate(cots[-1], lowered, after=[*all_ups, asked])

    parts = lax.all_to_all(lowered, "tsp", 0, 0, tiled=True)
    sent, pulled = down_sums(z, idx, owner, count, tokens, all_ups, cots, n_dp, n, 4, 7)
    down_got = lax.all_to_all(sent, "dp", 0, 0, tiled=True)
    token_gradient = token_gradients(
        z, idx, count, weight, pulled, downs_here, cots, n, rows, 4, after=[parts]
    )
    parts = gate(parts, after=[token_gradient])[0]
    lowered = jnp.sum(parts, axis=0).astype(jnp.bfloat16)
    lowered = [lowered] + [
        lax.ppermute(lowered, "tsp", [(i, (i + s) % n) for i in range(n)]) for s in range(1, n)
    ]
    sent = up_sums(z, owner, cotangent, lowered, n_dp, 2)
    sent = gate(sent, after=[down_got])[0]
    up_got = lax.all_to_all(sent, "dp", 0, 0, tiled=True)
    return token_gradient, owned(asked, down_got, held, 60), owned(asked, up_got, held, 16)


def solution(mesh):
    placed = (
        P("dp", "tsp"),
        P("dp", "tsp"),
        P("tsp", None),
        P("dp", None, "tsp"),
        P("dp", None, "tsp"),
        P(),
        P("dp"),
        P("dp"),
    )
    return jax.shard_map(
        on_device,
        mesh=mesh,
        in_specs=placed,
        out_specs=(P("dp", "tsp"), P("dp", None, "tsp"), P("dp", None, "tsp")),
        check_vma=False,
    )
```

time: 173 us -> 164 us (0.948)
  blocking collectives: 37.5 us -> 0 us
  waiting for transfers between devices: 36.5 us -> 53.6 us
  starting transfers between devices: 30.7 us -> 36.5 us
  Pallas kernels: 44.9 us -> 50.4 us
  other arithmetic: 5.18 us -> 2.89 us
  local copies, waits for them, and re-layouts: 16.3 us -> 18.5 us
    all_to_all x1 -> x0, blocking collectives: 37.5 us -> none  [main(): parts = lax.all_to_all(lowered, 'tsp', 0, 0, tiled=True)]
    ppermute x20, waiting for transfers between devices: 22 us -> 32.8 us  [flip(): return lax.ppermute(x, 'dp', [(i, i ^ by) for i in range(n)])]
    ppermute x3 -> x6, waiting for transfers between devices: 1.99 us -> 11.4 us  [the longest x3 7.14 us: on_device(): lax.ppermute(lowered, 'tsp', [(i, (i + s) % n) for i in range(n)])]
    pallas_call x5 -> x7, Pallas kernels: 44.9 us -> 50.4 us  [the longest x1 19.1 us: token_gradients(): pl.pallas_call(functools.partial(token_kernel, n, per, rows, len(maps)),...]
    unnamed x60, local copies, waits for them, and re-layouts: 11.1 us -> 15.4 us
    all_to_all x2 -> x3, starting transfers between devices: 7.02 us -> 10.9 us  [the longest x1 3.87 us: on_device(): up_got = lax.all_to_all(sent, 'dp', 0, 0, tiled=True)]
    ppermute x20, starting transfers between devices: 13.4 us -> 15.7 us  [flip(): return lax.ppermute(x, 'dp', [(i, i ^ by) for i in range(n)])]
    concatenate x2 -> x1, local copies, waits for them, and re-layouts: 1.94 us -> 0.02 us  [on_device(): words = jnp.concatenate([word] + [flip(word, n_dp, k) for k in (2, 4, 6)])]
  transfers between devices with their start and end apart: 28 -> 32, of which waited for: 16 -> 16; matrix products, arithmetic and copies ran while one was open for 4% -> 8% of each run, Pallas kernels for 25% -> 30%
where the time goes in v3:
time: 164 us; the launch traced here: 163 us
  waiting for transfers between devices  53.6 us (33%)
  Pallas kernels  50.4 us (31%)
  starting transfers between devices  36.5 us (22%)
  local copies, waits for them, and re-layouts  18.5 us (11%)
  other arithmetic  2.89 us (2%)
    ppermute x20, waiting for transfers between devices, flip(): return lax.ppermute(x, 'dp', [(i, i ^ by) for i in range(n)])  32.8 us
    pallas_call x1, Pallas kernels, token_gradients(): pl.pallas_call(functools.partial(token_kernel, n, per, rows, len(maps)),...  19.1 us
    ppermute x20, starting transfers between devices, flip(): return lax.ppermute(x, 'dp', [(i, i ^ by) for i in range(n)])  15.7 us
    unnamed x60, local copies, waits for them, and re-layouts  15.4 us
    pallas_call x1, Pallas kernels, down_sums(): pl.pallas_call(functools.partial(down_sums_kernel, n, per, rows, len(maps...  11.3 us
    pallas_call x1, Pallas kernels, project(): pl.pallas_call(functools.partial(project_kernel, n, per, rows, len(maps))...  9.57 us
    ppermute x3, waiting for transfers between devices, on_device(): lax.ppermute(lowered, 'tsp', [(i, (i + s) % n) for i in range(n)])  7.14 us
    pallas_call x2, Pallas kernels, owned(): pl.pallas_call(owned_kernel, grid=(ranks // per,), out_shape=jax.ShapeDty...  5.9 us
  transfers between devices with their start and end apart: 32, of which 16 were waited for; matrix products, arithmetic and copies ran while one was open for 8% of the time, Pallas kernels for 30%

profile of v3, /device:TPU:0, one launch (start us, length us, event | category | flops | bytes accessed | tf_op | source)
XLA Modules:
  0.0 162.9 jit_solution(8360515389886529878)
XLA Ops:
  0.6 1.5 copy.48.refs_0_
  2.1 3.0 %collective-permute-start = (bf16[2048,256]{1,0:T(8,128)(2,1)}, bf16[2048,256]{1,0:T(8,128)(2,1)S(1)}, u32[]{:S(2)}, u32[]{:S(2)}) collective-permute-start(bf16[2048,256]{1,0:T(8,128)(2,1)} %x_hbm.1), channel_id=1, source_target_pairs={{0,1},{1,2},{2,3},{3,0},{4,5},{5,6},{6,7},{7,4},{8,9},{9,10},{10,1... | collective-permute-start | bytes 3145736 | tf_op jit(solution)/shard_map/ppermute | solution.py:340
  5.1 1.5 collective-permute-start.2
  6.6 1.5 collective-permute-start.1
  8.1 10.6 %collective-permute-done.2.refs_1_ = bf16[2,64,2048]{2,1,0:T(8,128)(2,1)S(1)} collective-permute-done((bf16[2,64,2048]{2,1,0:T(8,128)(2,1)}, bf16[2,64,2048]{2,1,0:T(8,128)(2,1)S(1)}, u32[]{:S(2)}, u32[]{:S(2)}) %collective-permute-start.2) | collective-permute-done | bytes 524320 | tf_op jit(solution)/shard_map/ppermute | solution.py:344
  18.7 1.2 collective-permute-done.1.refs_0_
  20.0 0.8 copy-done.3
  20.8 2.3 %collective-permute-start.5 = (bf16[2,64,256]{2,1,0:T(8,128)(2,1)}, bf16[2,64,256]{2,1,0:T(8,128)(2,1)S(1)}, u32[]{:S(2)}, u32[]{:S(2)}) collective-permute-start(bf16[2,64,256]{2,1,0:T(8,128)(2,1)} %gate.8.refs_1_), channel_id=1, source_target_pairs={{0,3},{1,0},{2,1},{3,2},{4,7},{5,4},{6,5},{7,6},{8,11},{9,8},{10,9... | collective-permute-start | bytes 196616 | tf_op jit(solution)/shard_map/ppermute | solution.py:376
  23.1 0.7 collective-permute-start.4
  23.8 1.6 collective-permute-start.3
  25.4 6.5 %copy.29 = bf16[2048,1024]{0,1:T(8,128)(2,1)} copy(bf16[2048,1024]{1,0:T(8,128)(2,1)} %param.10) | data formatting | bytes 8388608 | tf_op args[2]
  31.9 4.2 %collective-permute-done.4.refs_6_ = bf16[2,64,256]{2,1,0:T(8,128)(2,1)S(1)} collective-permute-done((bf16[2,64,256]{2,1,0:T(8,128)(2,1)}, bf16[2,64,256]{2,1,0:T(8,128)(2,1)S(1)}, u32[]{:S(2)}, u32[]{:S(2)}) %collective-permute-start.4) | collective-permute-done | bytes 65568 | tf_op jit(solution)/shard_map/ppermute | solution.py:376
  36.2 0.6 copy-done.22
  36.8 0.4 copy-done.5
  37.2 1.0 slice.6
  38.2 1.0 slice.7
  39.2 0.6 collective-permute-start.9
  39.7 1.5 collective-permute-start.11
  41.2 1.5 collective-permute-start.10
  42.8 5.3 %collective-permute-done.11.refs_7_ = bf16[1,64,2048]{2,1,0:T(8,128)(2,1)S(1)} collective-permute-done((bf16[1,64,2048]{2,1,0:T(8,128)(2,1)S(1)}, bf16[1,64,2048]{2,1,0:T(8,128)(2,1)S(1)}, u32[]{:S(2)}, u32[]{:S(2)}) %collective-permute-start.11) | collective-permute-done | bytes 262176 | tf_op jit(solution)/shard_map/ppermute | solution.py:344
  48.0 1.2 collective-permute-done.10.refs_6_
  49.2 1.3 plan.1
  50.5 1.7 %pad_maximum_fusion.refs_1_ = bf16[4,2,64,256]{3,2,1,0:T(8,128)(2,1)} fusion(bf16[1,2,64,256]{3,2,1,0:T(8,128)(2,1)} %bitcast.13, bf16[1,2,64,256]{3,2,1,0:T(8,128)(2,1)} %bitcast.14, bf16[1,2,64,256]{3,2,1,0:T(8,128)(2,1)} %bitcast.15, bf16[1,2,64,256]{3,2,1,0:T(8,128)(2,1)} %bitcast.12), kind=kLoop, calls=%fused_computation.1 | loop fusion | flops 393216 | bytes 524288 | tf_op jit(solution)/shard_map/stack | solution.py:386
  52.3 0.7 copy-done.9
  53.0 0.2 copy-done.10
  53.3 9.6 %project.1.refs_2_.refs_1_ = f32[4,256,128]{2,1,0:T(8,128)} custom-call(s32[16]{0:T(128)} %get-tuple-element.22.idx, s32[16]{0:T(128)} %count.5, bf16[2048,2048]{1,0:T(8,128)(2,1)} %x.3, bf16[2,64,2048]{2,1,0:T(8,128)(2,1)} %refs_0_.4, bf16[2,64,2048]{2,1,0:T(8,128)(2,1)} %copy-done.8, bf16[2,64,2048]{2,1,0:T(8,128)(2,1)} %get-tuple-element.32.refs_2_, ...), custom_call_target="tpu_custom_call" | custom-call | bytes 1200000 | tf_op jit(solution)/shard_map/project/pallas_call | solution.py:104
  62.9 1.4 collective-permute-done.6.refs_0_
  64.2 1.0 copy-done.4
  65.2 2.4 %collective-permute-start.19 = (bf16[4,2,64,256]{3,2,1,0:T(8,128)(2,1)}, bf16[4,2,64,256]{3,2,1,0:T(8,128)(2,1)S(1)}, u32[]{:S(2)}, u32[]{:S(2)}) collective-permute-start(bf16[4,2,64,256]{3,2,1,0:T(8,128)(2,1)} %get-tuple-element.34.refs_2_.refs_0_), channel_id=1, source_target_pairs={{0,24},{4,28},{8,16},{12,20},{16,8},{20,12},{24,0},{28,4},{1,25},{... | collective-permute-start | bytes 786440 | tf_op jit(solution)/shard_map/ppermute | solution.py:344
  67.7 0.5 collective-permute-start.17
  68.2 0.5 collective-permute-start.15
  68.7 1.1 collective-permute-done.22
  69.9 2.5 %collective-permute-start.25 = (s32[2,8]{1,0:T(2,128)S(1)}, s32[2,8]{1,0:T(2,128)S(1)}, u32[]{:S(2)}, u32[]{:S(2)}) collective-permute-start(s32[2,8]{1,0:T(2,128)S(1)} %pad_add_fusion), channel_id=1, source_target_pairs={{0,24},{4,28},{8,16},{12,20},{16,8},{20,12},{24,0},{28,4},{1,25},{... | collective-permute-start | bytes 200 | tf_op jit(solution)/shard_map/ppermute | solution.py:344
  72.4 8.0 %collective-permute-done.25 = s32[2,8]{1,0:T(2,128)S(1)} collective-permute-done((s32[2,8]{1,0:T(2,128)S(1)}, s32[2,8]{1,0:T(2,128)S(1)}, u32[]{:S(2)}, u32[]{:S(2)}) %collective-permute-start.25) | collective-permute-done | bytes 96 | tf_op jit(solution)/shard_map/ppermute | solution.py:344
  80.4 1.5 collective-permute-start.24
  81.9 2.0 %collective-permute-done.24 = s32[2,8]{1,0:T(2,128)S(1)} collective-permute-done((s32[2,8]{1,0:T(2,128)S(1)}, s32[2,8]{1,0:T(2,128)S(1)}, u32[]{:S(2)}, u32[]{:S(2)}) %collective-permute-start.24) | collective-permute-done | bytes 96 | tf_op jit(solution)/shard_map/ppermute | solution.py:344
  83.9 0.5 collective-permute-start.23
  84.5 3.0 %collective-permute-done.23 = s32[2,8]{1,0:T(2,128)S(1)} collective-permute-done((s32[2,8]{1,0:T(2,128)S(1)}, s32[2,8]{1,0:T(2,128)S(1)}, u32[]{:S(2)}, u32[]{:S(2)}) %collective-permute-start.23) | collective-permute-done | bytes 96 | tf_op jit(solution)/shard_map/ppermute | solution.py:344
  87.5 0.5 collective-permute-start.20
  88.0 0.1 collective-permute-start.18
  88.1 0.4 collective-permute-start.16
  88.6 0.1 select_reduce_fusion
  88.7 1.1 gather_fusion
  89.9 0.3 collective-permute-done.16.refs_5_.refs_3_
  90.2 1.6 collective-permute-done.21.refs_0_
  91.8 1.1 copy-done.6
  92.9 3.5 %all-to-all-start = ((f32[4,256,128]{2,1,0:T(8,128)}), f32[4,256,128]{2,1,0:T(8,128)S(1)}, u32[]{:S(2)}, u32[]{:S(2)}) async-start(f32[4,256,128]{2,1,0:T(8,128)} %get-tuple-element.39), calls=%async_computation | async-start | bytes 1048576 | tf_op jit(solution)/shard_map/all_to_all | solution.py:408
  96.3 11.3 %down_sums.1 = (bf16[8,64,2048]{2,1,0:T(8,128)(2,1)}, bf16[2048,64]{1,0:T(8,128)(2,1)}) custom-call(s32[1]{0:T(128)} %bitcast.z, s32[16]{0:T(128)} %get-tuple-element.22.idx, s32[16]{0:T(128)} %get-tuple-element.26.owner, s32[16]{0:T(128)} %count.5, bf16[2048,2048]{1,0:T(8,128)(2,1)} %x.3, bf16[4,2,64,256]{3,2,1,0:T(8,128)(2,1)} %get-tuple-element.34.refs_2_.refs_0_, ...), custom_call_target="tpu_custom_call" | custom-call | bytes 2100000 | tf_op jit(solution)/shard_map/down_sums/pallas_call | solution.py:219
  107.7 3.4 %all-to-all-done.refs_14_.refs_0_ = f32[4,256,128]{2,1,0:T(8,128)S(1)} async-done(((f32[4,256,128]{2,1,0:T(8,128)}), f32[4,256,128]{2,1,0:T(8,128)S(1)}, u32[]{:S(2)}, u32[]{:S(2)}) %all-to-all-start) | async-done | bytes 524320 | tf_op jit(solution)/shard_map/all_to_all | solution.py:408
  111.1 3.6 %all-to-all-start.1 = ((bf16[8,64,2048]{2,1,0:T(8,128)(2,1)}), bf16[8,64,2048]{2,1,0:T(8,128)(2,1)S(1)}, u32[]{:S(2)}, u32[]{:S(2)}) async-start(bf16[8,64,2048]{2,1,0:T(8,128)(2,1)} %get-tuple-element.40), calls=%async_computation.1 | async-start | bytes 4194304 | tf_op jit(solution)/shard_map/all_to_all | solution.py:410
  114.7 19.1 %token_gradient.1.refs_1_ = bf16[2048,2048]{1,0:T(8,128)(2,1)} custom-call(s32[1]{0:T(128)} %bitcast.z, s32[16]{0:T(128)} %get-tuple-element.22.idx, s32[16]{0:T(128)} %count.5, bf16[1024,2048]{1,0:T(8,128)(2,1)} %get-tuple-element.25.weight, bf16[2048,64]{1,0:T(8,128)(2,1)} %get-tuple-element.38.pulled, bf16[2,64,2048]{2,1,0:T(8,128)(2,1)} %refs_0_.4, ...), custom_call_target="tpu_custom_call" | custom-call | bytes 4800000 | tf_op jit(solution)/shard_map/token_gradient/pallas_call | solution.py:278
  133.9 1.1 reduce_sum.19.refs_0_
  135.0 1.5 collective-permute-start.28
  136.5 0.6 collective-permute-start.26
  137.1 2.3 %collective-permute-done.28.refs_3_ = bf16[256,128]{1,0:T(8,128)(2,1)S(1)} collective-permute-done((bf16[256,128]{1,0:T(8,128)(2,1)S(1)}, bf16[256,128]{1,0:T(8,128)(2,1)S(1)}, u32[]{:S(2)}, u32[]{:S(2)}) %collective-permute-start.28) | collective-permute-done | bytes 65568 | tf_op jit(solution)/shard_map/ppermute | solution.py:417
  139.4 4.9 %collective-permute-done.27.refs_2_ = bf16[256,128]{1,0:T(8,128)(2,1)S(1)} collective-permute-done((bf16[256,128]{1,0:T(8,128)(2,1)S(1)}, bf16[256,128]{1,0:T(8,128)(2,1)S(1)}, u32[]{:S(2)}, u32[]{:S(2)}) %collective-permute-start.27) | collective-permute-done | bytes 65568 | tf_op jit(solution)/shard_map/ppermute | solution.py:417
  144.3 0.6 copy-done.26
  144.9 0.6 copy-done.27
  145.5 3.3 %up_sums.1.refs_0_ = bf16[8,64,256]{2,1,0:T(8,128)(2,1)} custom-call(s32[1]{0:T(128)} %bitcast.z, s32[16]{0:T(128)} %get-tuple-element.26.owner, bf16[2048,256]{1,0:T(8,128)(2,1)} %x_hbm.1, bf16[256,128]{1,0:T(8,128)(2,1)} %copy-done.24, bf16[256,128]{1,0:T(8,128)(2,1)} %copy-done.27, bf16[256,128]{1,0:T(8,128)(2,1)} %copy-done.26, bf16[256,128]{1,0:T(8,128)(2,1)} %copy-done.25), custom_call_target="tpu_custom_call" | custom-call | bytes 600000 | tf_op jit(solution)/shard_map/up_sums/pallas_call | solution.py:159
  148.8 1.3 copy-done.1
  150.2 3.9 %all-to-all-start.2 = ((bf16[8,64,256]{2,1,0:T(8,128)(2,1)}), bf16[8,64,256]{2,1,0:T(8,128)(2,1)S(1)}, u32[]{:S(2)}, u32[]{:S(2)}) async-start(bf16[8,64,256]{2,1,0:T(8,128)(2,1)} %gate.13), calls=%async_computation.2 | async-start | bytes 524288 | tf_op jit(solution)/shard_map/all_to_all | solution.py:421
  154.0 4.0 %owned.2 = f32[2,64,2048]{2,1,0:T(8,128)} custom-call(s32[8]{0:T(128)} %gather_fusion, bf16[8,64,2048]{2,1,0:T(8,128)(2,1)} %copy-done.1), custom_call_target="tpu_custom_call" | custom-call | bytes 600000 | tf_op jit(solution)/shard_map/owned/pallas_call | solution.py:310
  158.0 3.0 %all-to-all-done.2.got = bf16[8,64,256]{2,1,0:T(8,128)(2,1)S(1)} async-done(((bf16[8,64,256]{2,1,0:T(8,128)(2,1)}), bf16[8,64,256]{2,1,0:T(8,128)(2,1)S(1)}, u32[]{:S(2)}, u32[]{:S(2)}) %all-to-all-start.2) | async-done | bytes 262176 | tf_op jit(solution)/shard_map/all_to_all | solution.py:421
  161.0 1.9 %owned.3 = f32[2,64,256]{2,1,0:T(8,128)} custom-call(s32[8]{0:T(128)S(1)} %copy-done, bf16[8,64,256]{2,1,0:T(8,128)(2,1)S(1)} %all-to-all-done.2.got), custom_call_target="tpu_custom_call" | custom-call | bytes 600000 | tf_op jit(solution)/shard_map/owned/pallas_call | solution.py:310
  (85 shorter events, 0.4 us)
Async XLA Ops:
  2.1 34.0 %collective-permute-start = (bf16[2048,256]{1,0:T(8,128)(2,1)}, bf16[2048,256]{1,0:T(8,128)(2,1)S(1)}, u32[]{:S(2)}, u32[]{:S(2)}) collective-permute-start(bf16[2048,256]{1,0:T(8,128)(2,1)} %x_hbm.1), channel_id=1, source_target_pairs={{0,1},{1,2},{2,3},{3,0},{4,5},{5,6},{6,7},{7,4},{8,9},{9,10},{10,1... | collective-permute-start | bytes 3145736 | tf_op jit(solution)/shard_map/ppermute | solution.py:340
  5.1 13.6 %collective-permute-start.2 = (bf16[2,64,2048]{2,1,0:T(8,128)(2,1)}, bf16[2,64,2048]{2,1,0:T(8,128)(2,1)S(1)}, u32[]{:S(2)}, u32[]{:S(2)}) collective-permute-start(bf16[2,64,2048]{2,1,0:T(8,128)(2,1)} %refs_0_.4), channel_id=1, source_target_pairs={{0,16},{4,20},{8,24},{12,28},{16,0},{20,4},{24,8},{28,12},{1,17},{... | collective-permute-start | bytes 1572872 | tf_op jit(solution)/shard_map/ppermute | solution.py:344
  6.6 13.3 %collective-permute-start.1 = (bf16[2,64,2048]{2,1,0:T(8,128)(2,1)}, bf16[2,64,2048]{2,1,0:T(8,128)(2,1)S(1)}, u32[]{:S(2)}, u32[]{:S(2)}) collective-permute-start(bf16[2,64,2048]{2,1,0:T(8,128)(2,1)} %refs_0_.4), channel_id=1, source_target_pairs={{0,8},{4,12},{8,0},{12,4},{16,24},{20,28},{24,16},{28,20},{1,9},{5... | collective-permute-start | bytes 1572872 | tf_op jit(solution)/shard_map/ppermute | solution.py:344
  18.7 1.2 copy-start.2
  20.0 0.8 copy-start.3
  20.8 11.1 %collective-permute-start.5 = (bf16[2,64,256]{2,1,0:T(8,128)(2,1)}, bf16[2,64,256]{2,1,0:T(8,128)(2,1)S(1)}, u32[]{:S(2)}, u32[]{:S(2)}) collective-permute-start(bf16[2,64,256]{2,1,0:T(8,128)(2,1)} %gate.8.refs_1_), channel_id=1, source_target_pairs={{0,3},{1,0},{2,1},{3,2},{4,7},{5,4},{6,5},{7,6},{8,11},{9,8},{10,9... | collective-permute-start | bytes 196616 | tf_op jit(solution)/shard_map/ppermute | solution.py:376
  23.1 13.0 %collective-permute-start.4 = (bf16[2,64,256]{2,1,0:T(8,128)(2,1)}, bf16[2,64,256]{2,1,0:T(8,128)(2,1)S(1)}, u32[]{:S(2)}, u32[]{:S(2)}) collective-permute-start(bf16[2,64,256]{2,1,0:T(8,128)(2,1)} %gate.8.refs_1_), channel_id=1, source_target_pairs={{0,2},{1,3},{2,0},{3,1},{4,6},{5,7},{6,4},{7,5},{8,10},{9,11},{10,... | collective-permute-start | bytes 196616 | tf_op jit(solution)/shard_map/ppermute | solution.py:376
  23.8 12.3 %collective-permute-start.3 = (bf16[2,64,256]{2,1,0:T(8,128)(2,1)}, bf16[2,64,256]{2,1,0:T(8,128)(2,1)S(1)}, u32[]{:S(2)}, u32[]{:S(2)}) collective-permute-start(bf16[2,64,256]{2,1,0:T(8,128)(2,1)} %gate.8.refs_1_), channel_id=1, source_target_pairs={{0,1},{1,2},{2,3},{3,0},{4,5},{5,6},{6,7},{7,4},{8,9},{9,10},{10,1... | collective-permute-start | bytes 196616 | tf_op jit(solution)/shard_map/ppermute | solution.py:376
  25.4 15.8 %collective-permute-start.7 = (bf16[2,64,2048]{2,1,0:T(8,128)(2,1)}, bf16[2,64,2048]{2,1,0:T(8,128)(2,1)S(1)}, u32[]{:S(2)}, u32[]{:S(2)}) collective-permute-start(bf16[2,64,2048]{2,1,0:T(8,128)(2,1)} %refs_0_.4), channel_id=1, source_target_pairs={{0,4},{4,0},{8,12},{12,8},{16,20},{20,16},{24,28},{28,24},{1,5},{5... | collective-permute-start | bytes 1572872 | tf_op jit(solution)/shard_map/ppermute | solution.py:344
  31.9 4.2 %copy-start.21 = (bf16[2,64,256]{2,1,0:T(8,128)(2,1)}, bf16[2,64,256]{2,1,0:T(8,128)(2,1)S(1)}, u32[]{:S(2)}) copy-start(bf16[2,64,256]{2,1,0:T(8,128)(2,1)S(1)} %collective-permute-done.5.refs_7_) | copy-start | bytes 196612
  36.1 0.6 copy-start.22
  36.1 0.6 copy-start.23
  36.2 1.0 copy-start.5
  37.2 27.1 %collective-permute-start.6 = (bf16[2048,256]{1,0:T(8,128)(2,1)}, bf16[2048,256]{1,0:T(8,128)(2,1)S(1)}, u32[]{:S(2)}, u32[]{:S(2)}) collective-permute-start(bf16[2048,256]{1,0:T(8,128)(2,1)} %get-tuple-element.27.refs_9_.refs_11_), channel_id=1, source_target_pairs={{0,1},{1,2},{2,3},{3,0},{4,5},{5,6},{6,7},{7,4},{8,9},{9,10},{10,1... | collective-permute-start | bytes 3145736 | tf_op jit(solution)/shard_map/ppermute | solution.py:340
  38.1 14.1 %collective-permute-start.8 = (bf16[2,64,2048]{2,1,0:T(8,128)(2,1)}, bf16[2,64,2048]{2,1,0:T(8,128)(2,1)S(1)}, u32[]{:S(2)}, u32[]{:S(2)}) collective-permute-start(bf16[2,64,2048]{2,1,0:T(8,128)(2,1)} %get-tuple-element.32.refs_2_), channel_id=1, source_target_pairs={{0,4},{4,0},{8,12},{12,8},{16,20},{20,16},{24,28},{28,24},{1,5},{5... | collective-permute-start | bytes 1572872 | tf_op jit(solution)/shard_map/ppermute | solution.py:344
  39.2 13.0 %collective-permute-start.9 = (bf16[2,64,2048]{2,1,0:T(8,128)(2,1)}, bf16[2,64,2048]{2,1,0:T(8,128)(2,1)S(1)}, u32[]{:S(2)}, u32[]{:S(2)}) collective-permute-start(bf16[2,64,2048]{2,1,0:T(8,128)(2,1)} %get-tuple-element.33.refs_4_), channel_id=1, source_target_pairs={{0,4},{4,0},{8,12},{12,8},{16,20},{20,16},{24,28},{28,24},{1,5},{5... | collective-permute-start | bytes 1572872 | tf_op jit(solution)/shard_map/ppermute | solution.py:344
  39.7 8.3 %collective-permute-start.11 = (bf16[1,64,2048]{2,1,0:T(8,128)(2,1)S(1)}, bf16[1,64,2048]{2,1,0:T(8,128)(2,1)S(1)}, u32[]{:S(2)}, u32[]{:S(2)}) collective-permute-start(bf16[1,64,2048]{2,1,0:T(8,128)(2,1)S(1)} %slice.7), channel_id=1, source_target_pairs={{0,8},{4,12},{8,0},{12,4},{16,24},{20,28},{24,16},{28,20},{1,9},{5... | collective-permute-start | bytes 786440 | tf_op jit(solution)/shard_map/ppermute | solution.py:344
  41.2 11.0 %copy-start.8 = (bf16[2,64,2048]{2,1,0:T(8,128)(2,1)}, bf16[2,64,2048]{2,1,0:T(8,128)(2,1)S(1)}, u32[]{:S(2)}) copy-start(bf16[2,64,2048]{2,1,0:T(8,128)(2,1)S(1)} %collective-permute-done.7.refs_1_) | copy-start | bytes 1572868
  41.2 8.0 %collective-permute-start.10 = (bf16[1,64,2048]{2,1,0:T(8,128)(2,1)S(1)}, bf16[1,64,2048]{2,1,0:T(8,128)(2,1)S(1)}, u32[]{:S(2)}, u32[]{:S(2)}) collective-permute-start(bf16[1,64,2048]{2,1,0:T(8,128)(2,1)S(1)} %slice.6), channel_id=1, source_target_pairs={{0,16},{4,20},{8,24},{12,28},{16,0},{20,4},{24,8},{28,12},{1,17},{... | collective-permute-start | bytes 786440 | tf_op jit(solution)/shard_map/ppermute | solution.py:344
  48.0 4.3 %copy-start.18 = (bf16[1,64,2048]{2,1,0:T(8,128)(2,1)}, bf16[1,64,2048]{2,1,0:T(8,128)(2,1)S(1)}, u32[]{:S(2)}) copy-start(bf16[1,64,2048]{2,1,0:T(8,128)(2,1)S(1)} %collective-permute-done.11.refs_7_) | copy-start | bytes 786436
  48.0 4.2 %collective-permute-start.13 = (bf16[1,64,2048]{2,1,0:T(8,128)(2,1)S(1)}, bf16[1,64,2048]{2,1,0:T(8,128)(2,1)S(1)}, u32[]{:S(2)}, u32[]{:S(2)}) collective-permute-start(bf16[1,64,2048]{2,1,0:T(8,128)(2,1)S(1)} %collective-permute-done.11.refs_7_), channel_id=1, source_target_pairs={{0,4},{4,0},{8,12},{12,8},{16,20},{20,16},{24,28},{28,24},{1,5},{5... | collective-permute-start | bytes 786440 | tf_op jit(solution)/shard_map/ppermute | solution.py:344
  49.2 3.0 %copy-start.19 = (bf16[1,64,2048]{2,1,0:T(8,128)(2,1)}, bf16[1,64,2048]{2,1,0:T(8,128)(2,1)S(1)}, u32[]{:S(2)}) copy-start(bf16[1,64,2048]{2,1,0:T(8,128)(2,1)S(1)} %collective-permute-done.10.refs_6_) | copy-start | bytes 786436
  49.2 3.0 %collective-permute-start.12 = (bf16[1,64,2048]{2,1,0:T(8,128)(2,1)S(1)}, bf16[1,64,2048]{2,1,0:T(8,128)(2,1)}, u32[]{:S(2)}, u32[]{:S(2)}) collective-permute-start(bf16[1,64,2048]{2,1,0:T(8,128)(2,1)S(1)} %collective-permute-done.10.refs_6_), channel_id=1, source_target_pairs={{0,4},{4,0},{8,12},{12,8},{16,20},{20,16},{24,28},{28,24},{1,5},{5... | collective-permute-start | bytes 786440 | tf_op jit(solution)/shard_map/ppermute | solution.py:344
  52.2 0.8 copy-start.9
  52.2 1.0 copy-start.10
  52.2 1.0 copy-start.20
  53.3 15.4 %copy-start.28 = (s32[8]{0:T(128)S(1)}, s32[8]{0:T(128)}, u32[]{:S(2)}) copy-start(s32[8]{0:T(128)} %get-tuple-element.36) | copy-start | bytes 100
  64.2 1.0 copy-start.4
  65.2 26.5 %collective-permute-start.21 = (bf16[2048,256]{1,0:T(8,128)(2,1)}, bf16[2048,256]{1,0:T(8,128)(2,1)S(1)}, u32[]{:S(2)}, u32[]{:S(2)}) collective-permute-start(bf16[2048,256]{1,0:T(8,128)(2,1)} %get-tuple-element.35.refs_10_.refs_12_), channel_id=1, source_target_pairs={{0,1},{1,2},{2,3},{3,0},{4,5},{5,6},{6,7},{7,4},{8,9},{9,10},{10,1... | collective-permute-start | bytes 3145736 | tf_op jit(solution)/shard_map/ppermute | solution.py:340
  65.2 22.3 %collective-permute-start.19 = (bf16[4,2,64,256]{3,2,1,0:T(8,128)(2,1)}, bf16[4,2,64,256]{3,2,1,0:T(8,128)(2,1)S(1)}, u32[]{:S(2)}, u32[]{:S(2)}) collective-permute-start(bf16[4,2,64,256]{3,2,1,0:T(8,128)(2,1)} %get-tuple-element.34.refs_2_.refs_0_), channel_id=1, source_target_pairs={{0,24},{4,28},{8,16},{12,20},{16,8},{20,12},{24,0},{28,4},{1,25},{... | collective-permute-start | bytes 786440 | tf_op jit(solution)/shard_map/ppermute | solution.py:344
  67.7 20.3 %collective-permute-start.17 = (bf16[4,2,64,256]{3,2,1,0:T(8,128)(2,1)}, bf16[4,2,64,256]{3,2,1,0:T(8,128)(2,1)S(1)}, u32[]{:S(2)}, u32[]{:S(2)}) collective-permute-start(bf16[4,2,64,256]{3,2,1,0:T(8,128)(2,1)} %get-tuple-element.34.refs_2_.refs_0_), channel_id=1, source_target_pairs={{0,16},{4,20},{8,24},{12,28},{16,0},{20,4},{24,8},{28,12},{1,17},{... | collective-permute-start | bytes 786440 | tf_op jit(solution)/shard_map/ppermute | solution.py:344
  68.2 19.9 %collective-permute-start.15 = (bf16[4,2,64,256]{3,2,1,0:T(8,128)(2,1)}, bf16[4,2,64,256]{3,2,1,0:T(8,128)(2,1)S(1)}, u32[]{:S(2)}, u32[]{:S(2)}) collective-permute-start(bf16[4,2,64,256]{3,2,1,0:T(8,128)(2,1)} %get-tuple-element.34.refs_2_.refs_0_), channel_id=1, source_target_pairs={{0,8},{4,12},{8,0},{12,4},{16,24},{20,28},{24,16},{28,20},{1,9},{5... | collective-permute-start | bytes 786440 | tf_op jit(solution)/shard_map/ppermute | solution.py:344
  68.7 1.1 collective-permute-start.22
  69.9 10.5 %collective-permute-start.25 = (s32[2,8]{1,0:T(2,128)S(1)}, s32[2,8]{1,0:T(2,128)S(1)}, u32[]{:S(2)}, u32[]{:S(2)}) collective-permute-start(s32[2,8]{1,0:T(2,128)S(1)} %pad_add_fusion), channel_id=1, source_target_pairs={{0,24},{4,28},{8,16},{12,20},{16,8},{20,12},{24,0},{28,4},{1,25},{... | collective-permute-start | bytes 200 | tf_op jit(solution)/shard_map/ppermute | solution.py:344
  80.4 3.6 %collective-permute-start.24 = (s32[2,8]{1,0:T(2,128)S(1)}, s32[2,8]{1,0:T(2,128)S(1)}, u32[]{:S(2)}, u32[]{:S(2)}) collective-permute-start(s32[2,8]{1,0:T(2,128)S(1)} %pad_add_fusion), channel_id=1, source_target_pairs={{0,16},{4,20},{8,24},{12,28},{16,0},{20,4},{24,8},{28,12},{1,17},{... | collective-permute-start | bytes 200 | tf_op jit(solution)/shard_map/ppermute | solution.py:344
  83.9 3.6 %collective-permute-start.23 = (s32[2,8]{1,0:T(2,128)S(1)}, s32[2,8]{1,0:T(2,128)S(1)}, u32[]{:S(2)}, u32[]{:S(2)}) collective-permute-start(s32[2,8]{1,0:T(2,128)S(1)} %pad_add_fusion), channel_id=1, source_target_pairs={{0,8},{4,12},{8,0},{12,4},{16,24},{20,28},{24,16},{28,20},{1,9},{5... | collective-permute-start | bytes 200 | tf_op jit(solution)/shard_map/ppermute | solution.py:344
  87.5 2.3 %collective-permute-start.14 = (bf16[4,2,64,256]{3,2,1,0:T(8,128)(2,1)}, bf16[4,2,64,256]{3,2,1,0:T(8,128)(2,1)S(1)}, u32[]{:S(2)}, u32[]{:S(2)}) collective-permute-start(bf16[4,2,64,256]{3,2,1,0:T(8,128)(2,1)} %get-tuple-element.34.refs_2_.refs_0_), channel_id=1, source_target_pairs={{0,4},{4,0},{8,12},{12,8},{16,20},{20,16},{24,28},{28,24},{1,5},{5... | collective-permute-start | bytes 786440 | tf_op jit(solution)/shard_map/ppermute | solution.py:344
  87.5 4.2 %copy-start.11 = (bf16[4,2,64,256]{3,2,1,0:T(8,128)(2,1)}, bf16[4,2,64,256]{3,2,1,0:T(8,128)(2,1)S(1)}, u32[]{:S(2)}) copy-start(bf16[4,2,64,256]{3,2,1,0:T(8,128)(2,1)S(1)} %collective-permute-done.19.refs_8_.refs_6_) | copy-start | bytes 786436
  87.5 2.3 %collective-permute-start.20 = (bf16[4,2,64,256]{3,2,1,0:T(8,128)(2,1)S(1)}, bf16[4,2,64,256]{3,2,1,0:T(8,128)(2,1)S(1)}, u32[]{:S(2)}, u32[]{:S(2)}) collective-permute-start(bf16[4,2,64,256]{3,2,1,0:T(8,128)(2,1)S(1)} %collective-permute-done.19.refs_8_.refs_6_), channel_id=1, source_target_pairs={{0,4},{4,0},{8,12},{12,8},{16,20},{20,16},{24,28},{28,24},{1,5},{5... | collective-permute-start | bytes 786440 | tf_op jit(solution)/shard_map/ppermute | solution.py:344
  88.0 3.7 %copy-start.12 = (bf16[4,2,64,256]{3,2,1,0:T(8,128)(2,1)}, bf16[4,2,64,256]{3,2,1,0:T(8,128)(2,1)S(1)}, u32[]{:S(2)}) copy-start(bf16[4,2,64,256]{3,2,1,0:T(8,128)(2,1)S(1)} %collective-permute-done.17.refs_6_.refs_4_) | copy-start | bytes 786436
  88.0 1.8 %collective-permute-start.18 = (bf16[4,2,64,256]{3,2,1,0:T(8,128)(2,1)S(1)}, bf16[4,2,64,256]{3,2,1,0:T(8,128)(2,1)S(1)}, u32[]{:S(2)}, u32[]{:S(2)}) collective-permute-start(bf16[4,2,64,256]{3,2,1,0:T(8,128)(2,1)S(1)} %collective-permute-done.17.refs_6_.refs_4_), channel_id=1, source_target_pairs={{0,4},{4,0},{8,12},{12,8},{16,20},{20,16},{24,28},{28,24},{1,5},{5... | collective-permute-start | bytes 786440 | tf_op jit(solution)/shard_map/ppermute | solution.py:344
  88.1 3.6 %copy-start.13 = (bf16[4,2,64,256]{3,2,1,0:T(8,128)(2,1)}, bf16[4,2,64,256]{3,2,1,0:T(8,128)(2,1)S(1)}, u32[]{:S(2)}) copy-start(bf16[4,2,64,256]{3,2,1,0:T(8,128)(2,1)S(1)} %collective-permute-done.15.refs_4_.refs_2_) | copy-start | bytes 786436
  88.1 2.0 %collective-permute-start.16 = (bf16[4,2,64,256]{3,2,1,0:T(8,128)(2,1)S(1)}, bf16[4,2,64,256]{3,2,1,0:T(8,128)(2,1)S(1)}, u32[]{:S(2)}, u32[]{:S(2)}) collective-permute-start(bf16[4,2,64,256]{3,2,1,0:T(8,128)(2,1)S(1)} %collective-permute-done.15.refs_4_.refs_2_), channel_id=1, source_target_pairs={{0,4},{4,0},{8,12},{12,8},{16,20},{20,16},{24,28},{28,24},{1,5},{5... | collective-permute-start | bytes 786440 | tf_op jit(solution)/shard_map/ppermute | solution.py:344
  89.8 1.9 %copy-start.14 = (bf16[4,2,64,256]{3,2,1,0:T(8,128)(2,1)}, bf16[4,2,64,256]{3,2,1,0:T(8,128)(2,1)S(1)}, u32[]{:S(2)}) copy-start(bf16[4,2,64,256]{3,2,1,0:T(8,128)(2,1)S(1)} %collective-permute-done.14.refs_3_.refs_1_) | copy-start | bytes 786436
  89.8 1.9 %copy-start.15 = (bf16[4,2,64,256]{3,2,1,0:T(8,128)(2,1)}, bf16[4,2,64,256]{3,2,1,0:T(8,128)(2,1)S(1)}, u32[]{:S(2)}) copy-start(bf16[4,2,64,256]{3,2,1,0:T(8,128)(2,1)S(1)} %collective-permute-done.20.refs_9_.refs_7_) | copy-start | bytes 786436
  89.9 1.9 %copy-start.16 = (bf16[4,2,64,256]{3,2,1,0:T(8,128)(2,1)}, bf16[4,2,64,256]{3,2,1,0:T(8,128)(2,1)S(1)}, u32[]{:S(2)}) copy-start(bf16[4,2,64,256]{3,2,1,0:T(8,128)(2,1)S(1)} %collective-permute-done.18.refs_7_.refs_5_) | copy-start | bytes 786436
  90.2 1.6 copy-start.17
  91.8 1.1 copy-start.6
  92.9 18.3 %all-to-all-start = ((f32[4,256,128]{2,1,0:T(8,128)}), f32[4,256,128]{2,1,0:T(8,128)S(1)}, u32[]{:S(2)}, u32[]{:S(2)}) async-start(f32[4,256,128]{2,1,0:T(8,128)} %get-tuple-element.39), calls=%async_computation | async-start | bytes 1048576 | tf_op jit(solution)/shard_map/all_to_all | solution.py:408
  111.1 3.6 %copy-start.7 = (f32[4,256,128]{2,1,0:T(8,128)}, f32[4,256,128]{2,1,0:T(8,128)S(1)}, u32[]{:S(2)}) copy-start(f32[4,256,128]{2,1,0:T(8,128)S(1)} %all-to-all-done.refs_14_.refs_0_) | copy-start | bytes 1572868
  111.1 37.7 %all-to-all-start.1 = ((bf16[8,64,2048]{2,1,0:T(8,128)(2,1)}), bf16[8,64,2048]{2,1,0:T(8,128)(2,1)S(1)}, u32[]{:S(2)}, u32[]{:S(2)}) async-start(bf16[8,64,2048]{2,1,0:T(8,128)(2,1)} %get-tuple-element.40), calls=%async_computation.1 | async-start | bytes 4194304 | tf_op jit(solution)/shard_map/all_to_all | solution.py:410
  133.9 27.1 %copy-start = (s32[8]{0:T(128)S(1)}, s32[8]{0:T(128)}, u32[]{:S(2)}) copy-start(s32[8]{0:T(128)} %gather_fusion) | copy-start | bytes 100
  134.9 9.3 %copy-start.24 = (bf16[256,128]{1,0:T(8,128)(2,1)}, bf16[256,128]{1,0:T(8,128)(2,1)S(1)}, u32[]{:S(2)}) copy-start(bf16[256,128]{1,0:T(8,128)(2,1)S(1)} %reduce_sum.19.refs_0_) | copy-start | bytes 196612
  135.0 4.4 %collective-permute-start.28 = (bf16[256,128]{1,0:T(8,128)(2,1)S(1)}, bf16[256,128]{1,0:T(8,128)(2,1)S(1)}, u32[]{:S(2)}, u32[]{:S(2)}) collective-permute-start(bf16[256,128]{1,0:T(8,128)(2,1)S(1)} %reduce_sum.19.refs_0_), channel_id=1, source_target_pairs={{0,3},{1,0},{2,1},{3,2},{4,7},{5,4},{6,5},{7,6},{8,11},{9,8},{10,9... | collective-permute-start | bytes 196616 | tf_op jit(solution)/shard_map/ppermute | solution.py:417
  136.5 7.8 %collective-permute-start.27 = (bf16[256,128]{1,0:T(8,128)(2,1)S(1)}, bf16[256,128]{1,0:T(8,128)(2,1)S(1)}, u32[]{:S(2)}, u32[]{:S(2)}) collective-permute-start(bf16[256,128]{1,0:T(8,128)(2,1)S(1)} %reduce_sum.19.refs_0_), channel_id=1, source_target_pairs={{0,2},{1,3},{2,0},{3,1},{4,6},{5,7},{6,4},{7,5},{8,10},{9,11},{10,... | collective-permute-start | bytes 196616 | tf_op jit(solution)/shard_map/ppermute | solution.py:417
  136.5 7.8 %collective-permute-start.26 = (bf16[256,128]{1,0:T(8,128)(2,1)S(1)}, bf16[256,128]{1,0:T(8,128)(2,1)S(1)}, u32[]{:S(2)}, u32[]{:S(2)}) collective-permute-start(bf16[256,128]{1,0:T(8,128)(2,1)S(1)} %reduce_sum.19.refs_0_), channel_id=1, source_target_pairs={{0,1},{1,2},{2,3},{3,0},{4,5},{5,6},{6,7},{7,4},{8,9},{9,10},{10,1... | collective-permute-start | bytes 196616 | tf_op jit(solution)/shard_map/ppermute | solution.py:417
  139.4 4.9 %copy-start.25 = (bf16[256,128]{1,0:T(8,128)(2,1)}, bf16[256,128]{1,0:T(8,128)(2,1)S(1)}, u32[]{:S(2)}) copy-start(bf16[256,128]{1,0:T(8,128)(2,1)S(1)} %collective-permute-done.28.refs_3_) | copy-start | bytes 196612
  144.3 0.6 copy-start.26
  144.9 0.6 copy-start.27
  148.8 1.3 copy-start.1
  150.2 10.8 %all-to-all-start.2 = ((bf16[8,64,256]{2,1,0:T(8,128)(2,1)}), bf16[8,64,256]{2,1,0:T(8,128)(2,1)S(1)}, u32[]{:S(2)}, u32[]{:S(2)}) async-start(bf16[8,64,256]{2,1,0:T(8,128)(2,1)} %gate.13), calls=%async_computation.2 | async-start | bytes 524288 | tf_op jit(solution)/shard_map/all_to_all | solution.py:421

commit v4 on v3

--- a/solution.py
+++ b/solution.py
@@ -69,8 +69,8 @@
     )(me, table, adapter)
 
 
-def project_kernel(n, per, rows, n_maps, idx, count, x, *refs):
-    maps, (out, table, buf, sem) = refs[:n_maps], refs[-4:]
+def project_kernel(n, per, rows, n_maps, z, idx, count, x, *refs):
+    maps, outs, (table, buf, sem) = refs[:n_maps], refs[n_maps : n_maps + n], refs[-3:]
     step = pl.program_id(0)
 
     @pl.when(step == 0)
@@ -87,26 +87,26 @@
 
     @pl.when(step == pl.num_programs(0) - 1)
     def _():
-        half = out.shape[1]
-        for j in range(n):
-            start = 2 * j * half
-            out[j] = jnp.concatenate(
-                [buf[start : start + half, :], buf[start + half : start + 2 * half, :]], axis=1
+        half = outs[0].shape[0]
+        for s in range(n):
+            start = pl.multiple_of(lax.rem(z[0] + s, n) * 2 * half, 2 * half)
+            outs[s][...] = jnp.concatenate(
+                [buf[pl.ds(start, half), :], buf[pl.ds(start + half, half), :]], axis=1
             )
 
 
-def project(idx, count, x, maps, n, per, us):
+def project(z, idx, count, x, maps, n, per, us):
     segs = idx.shape[0]
     rows, width = x.shape[0] // segs, x.shape[1]
     ranks = maps[0].shape[1]
     total = sum(m.shape[0] for m in maps)
-    shape = (n, x.shape[0] // n // 2, 2 * ranks)
+    shape = (x.shape[0] // n // 2, 2 * ranks)
     return pl.pallas_call(
         functools.partial(project_kernel, n, per, rows, len(maps)),
         grid=(segs // per,),
-        out_shape=jax.ShapeDtypeStruct(shape, jnp.float32),
-        in_specs=[SMEM] * 2 + [pl.BlockSpec((per * rows, width), lambda i: (i, 0))] + [HBM] * len(maps),
-        out_specs=pl.BlockSpec(shape, lambda i: (0, 0, 0)),
+        out_shape=[jax.ShapeDtypeStruct(shape, jnp.float32)] * n,
+        in_specs=[SMEM] * 3 + [pl.BlockSpec((per * rows, width), lambda i: (i, 0))] + [HBM] * len(maps),
+        out_specs=[pl.BlockSpec(shape, lambda i: (0, 0))] * n,
         scratch_shapes=[
             pltpu.VMEM((total, ranks, width), x.dtype),
             pltpu.VMEM((x.shape[0], ranks), jnp.float32),
@@ -115,7 +115,7 @@
         compiler_params=params(),
         cost_estimate=cost(us),
         name="project",
-    )(idx, count, x, *maps)
+    )(z, idx, count, x, *maps)
 
 
 def cot_copies(n, z, cots, cot, sem):
@@ -174,20 +174,63 @@
     )(z, owner, x, *blocks, *after)
 
 
-def down_sums_kernel(n, per, rows, n_maps, scale, z, idx, owner, count, x, *refs):
-    maps, refs = refs[:n_maps], refs[n_maps:]
-    cots, (out, pulled, table, cot, total, map_sem, cot_sem) = refs[:n], refs[-7:]
+def up_copies(maps, size, distances, table, sem):
+    key = maps[0].shape[1]
+    copies = []
+    for i, m in enumerate(maps):
+        for k, j in enumerate(distances):
+            dst = table.at[pl.ds(i * size, size), pl.ds(k * key, key)]
+            copies.append(pltpu.make_async_copy(m.at[pl.ds(j * size, size)], dst, sem.at[i * len(distances) + k]))
+    return copies
+
+
+def pick(place, ranks):
+    return pl.ds(pl.multiple_of(place * ranks, ranks), ranks)
+
+
+def pulled_part_kernel(n, per, rows, ranks, size, n_maps, idx, *refs):
+    cots, maps, (out, table, sem) = refs[: n - 1], refs[n - 1 : n - 1 + n_maps], refs[-3:]
     step = pl.program_id(0)
 
     @pl.when(step == 0)
     def _():
-        copies = cot_copies(n, z[0], cots, cot, cot_sem)
-        parts, held, _, key = maps[0].shape
-        for i, m in enumerate(maps):
-            for j in range(parts):
-                column = pl.multiple_of(lax.rem(z[0] - j + n, n) * key, key)
-                dst = table.at[pl.ds(i * held, held), :, pl.ds(column, key)]
-                copies.append(pltpu.make_async_copy(m.at[j], dst, map_sem.at[i * parts + j]))
+        load_all(up_copies(maps, size, range(n - 1), table, sem))
+
+    for i in range(per):
+        x = jnp.concatenate([cot[i * rows : (i + 1) * rows, :] for cot in cots], axis=1)
+        out[i * rows : (i + 1) * rows, :] = lax.dot_general(
+            x, table[pick(idx[step * per + i], ranks), :], NT, preferred_element_type=jnp.float32
+        )
+
+
+def pulled_part(idx, maps, cots, ranks, size, per, us):
+    segs, n = idx.shape[0], len(cots) + 1
+    rows, key = cots[0].shape[0] // segs, cots[0].shape[1]
+    return pl.pallas_call(
+        functools.partial(pulled_part_kernel, n, per, rows, ranks, size, len(maps)),
+        grid=(segs // per,),
+        out_shape=jax.ShapeDtypeStruct((segs * rows, ranks), jnp.float32),
+        in_specs=[SMEM]
+        + [pl.BlockSpec((per * rows, key), lambda i: (i, 0))] * (n - 1)
+        + [HBM] * len(maps),
+        out_specs=pl.BlockSpec((per * rows, ranks), lambda i: (i, 0)),
+        scratch_shapes=[
+            pltpu.VMEM((size * len(maps), (n - 1) * key), jnp.bfloat16),
+            pltpu.SemaphoreType.DMA(((n - 1) * len(maps),)),
+        ],
+        compiler_params=params(),
+        cost_estimate=cost(us),
+        name="pulled_part",
+    )(idx, *cots, *maps)
+
+
+def down_sums_kernel(n, per, rows, ranks, size, n_maps, scale, idx, owner, count, x, part, cot, *refs):
+    maps, (out, pulled, table, total, sem) = refs[:n_maps], refs[-5:]
+    step = pl.program_id(0)
+
+    @pl.when(step == 0)
+    def _():
+        copies = up_copies(maps, size, [n - 1], table, sem)
         for copy in copies:
             copy.start()
         total[...] = jnp.zeros_like(total)
@@ -196,11 +239,8 @@
 
     for i in range(per):
         g = step * per + i
-        terms = lax.dot_general(
-            cot[pl.ds(pl.multiple_of(g * rows, rows), rows), :],
-            table[idx[g]],
-            NT,
-            preferred_element_type=jnp.float32,
+        terms = part[i * rows : (i + 1) * rows, :] + lax.dot_general(
+            cot[i * rows : (i + 1) * rows, :], table[pick(idx[g], ranks), :], NT, preferred_element_type=jnp.float32
         )
         terms = jnp.where(live_mask(count[g], *terms.shape), terms, 0.0).astype(pulled.dtype)
         pulled[i * rows : (i + 1) * rows, :] = terms
@@ -211,36 +251,30 @@
         out[...] = (total[...] * scale).astype(out.dtype)
 
 
-def down_sums(z, idx, owner, count, x, maps, cots, owners, n, per, us):
+def down_sums(idx, owner, count, x, part, cot, maps, size, owners, n, per, us):
     segs = owner.shape[0]
     rows, width = x.shape[0] // segs, x.shape[1]
-    parts, held, ranks, key = maps[0].shape
+    ranks, key = part.shape[1], cot.shape[1]
     shape = (owners, ranks, width)
-    return pl.pallas_call(
-        functools.partial(down_sums_kernel, n, per, rows, len(maps), ADAPTER_SCALE / rows),
+    by_rows = lambda columns: pl.BlockSpec((per * rows, columns), lambda i: (i, 0))
+    return pl.pallas_call(
+        functools.partial(down_sums_kernel, n, per, rows, ranks, size, len(maps), ADAPTER_SCALE / rows),
         grid=(segs // per,),
         out_shape=[
             jax.ShapeDtypeStruct(shape, jnp.bfloat16),
             jax.ShapeDtypeStruct((x.shape[0], ranks), jnp.bfloat16),
         ],
-        in_specs=[SMEM] * 4
-        + [pl.BlockSpec((per * rows, width), lambda i: (i, 0))]
-        + [HBM] * (len(maps) + n),
-        out_specs=[
-            pl.BlockSpec(shape, lambda i: (0, 0, 0)),
-            pl.BlockSpec((per * rows, ranks), lambda i: (i, 0)),
-        ],
+        in_specs=[SMEM] * 3 + [by_rows(width), by_rows(ranks), by_rows(key)] + [HBM] * len(maps),
+        out_specs=[pl.BlockSpec(shape, lambda i: (0, 0, 0)), by_rows(ranks)],
         scratch_shapes=[
-            pltpu.VMEM((held * len(maps), ranks, parts * key), jnp.bfloat16),
-            pltpu.VMEM((x.shape[0], n * key), jnp.bfloat16),
+            pltpu.VMEM((size * len(maps), key), jnp.bfloat16),
             pltpu.VMEM(shape, jnp.float32),
-            pltpu.SemaphoreType.DMA((parts * len(maps),)),
-            pltpu.SemaphoreType.DMA((n,)),
+            pltpu.SemaphoreType.DMA((len(maps),)),
         ],
         compiler_params=params(),
         cost_estimate=cost(us),
         name="down_sums",
-    )(z, idx, owner, count, x, *maps, *cots)
+    )(idx, owner, count, x, part, cot, *maps)
 
 
 def token_kernel(n, per, rows, n_maps, z, idx, count, weight, pulled, *refs):
@@ -296,27 +330,54 @@
     )(z, idx, count, weight, pulled, *maps, *cots, *after)
 
 
-def owned_kernel(asked, got, out):
+def told_kernel(row, me, *refs):
+    arrays, (out, raw, sem) = refs[:-3], refs[-3:]
+    load_all([pltpu.make_async_copy(m.at[pl.ds(row, 16)], raw.at[i], sem.at[i]) for i, m in enumerate(arrays)])
+    for i in range(len(arrays)):
+        codes = raw[i][:8, :].astype(jnp.float32)
+        mine = lax.broadcasted_iota(jnp.int32, codes.shape, 1) == me[0]
+        code = jnp.sum(jnp.where(mine, codes, 0.0), axis=1, keepdims=True)
+        out[i : i + 1, :] = jnp.broadcast_to(code, (codes.shape[0], out.shape[1]))[:1, :]
+
+
+def told(me, arrays, row):
+    return pl.pallas_call(
+        functools.partial(told_kernel, row),
+        out_shape=jax.ShapeDtypeStruct((len(arrays), 128), jnp.float32),
+        in_specs=[SMEM] + [HBM] * len(arrays),
+        out_specs=VMEM,
+        scratch_shapes=[
+            pltpu.VMEM((len(arrays), 16, arrays[0].shape[1]), arrays[0].dtype),
+            pltpu.SemaphoreType.DMA((len(arrays),)),
+        ],
+        compiler_params=params(),
+        cost_estimate=cost(1),
+        name="told",
+    )(me, *arrays)
+
+
+def owned_kernel(first, asked, got, out):
     for e in range(out.shape[0]):
         total = jnp.zeros(got.shape[1:], jnp.float32)
         for k in range(got.shape[0]):
-            total += jnp.where(asked[k] == e, got[k].astype(jnp.float32), 0.0)
+            code = asked[pl.ds(lax.bitwise_xor(first[0], k), 1), :1]
+            total += jnp.where(code == jnp.float32(e), got[k].astype(jnp.float32), 0.0)
         out[e] = total
 
 
-def owned(asked, got, held, mib):
+def owned(first, asked, got, held, mib):
     peers, ranks, width = got.shape
     per = min(16, ranks)
     return pl.pallas_call(
         owned_kernel,
         grid=(ranks // per,),
         out_shape=jax.ShapeDtypeStruct((held, ranks, width), jnp.float32),
-        in_specs=[SMEM, pl.BlockSpec((peers, per, width), lambda i: (0, i, 0))],
+        in_specs=[SMEM, VMEM, pl.BlockSpec((peers, per, width), lambda i: (0, i, 0))],
         out_specs=pl.BlockSpec((held, per, width), lambda i: (0, i, 0)),
         compiler_params=params(mib),
         cost_estimate=cost(2),
         name="owned",
-    )(asked, got)
+    )(first, asked, got)
 
 
 def gate_kernel(*refs):
@@ -334,6 +395,24 @@
         cost_estimate=cost(0),
         name="gate",
     )(*arrays, *after)
+
+
+def late_kernel(x, *refs):
+    out, sem = refs[-2:]
+    load_all([pltpu.make_async_copy(x, out, sem)])
+
+
+def late(x, after):
+    return pl.pallas_call(
+        late_kernel,
+        out_shape=jax.ShapeDtypeStruct(x.shape, x.dtype),
+        in_specs=[HBM] * (1 + len(after)),
+        out_specs=HBM,
+        scratch_shapes=[pltpu.SemaphoreType.DMA(())],
+        compiler_params=params(),
+        cost_estimate=cost(0),
+        name="late",
+    )(x, *after)
 
 
 def ring(x, n):
@@ -372,7 +451,7 @@
     owner, idx, wanted = plan(me[None], adapter_place_table, segment_adapter, held, n_dp, cube)
     if cube:
         over_x, over_y = gate(flip(downs, n_dp, 2), flip(downs, n_dp, 4))
-        ups = gate(ups, after=[over_x, over_y])[0]
+        ups = late(ups, [over_x, over_y])
     line = [lax.ppermute(ups, "tsp", [(i, (i + s) % n) for i in range(n)]) for s in range(1, n)]
     weight = frozen_key_weight.T
     if cube:
@@ -383,43 +462,46 @@
 
     while len(cots) < n - 1:
         cots.append(ring(cots[-1], n))
-    up_line = jnp.stack([ups, *line])
+    ranks = ups.shape[1]
+    size = held * ranks
+    info = jnp.zeros((16, ups.shape[2]), ups.dtype).at[0, :n_dp].set(wanted.astype(ups.dtype))
+    up_line = jnp.concatenate([u.reshape(size, -1) for u in [ups, *line]] + [info])
     if cube:
         same = [downs, over_x, over_y]
         downs_here = [m for d in same for m in (d, flip(d, n_dp, 1))]
         downs_here += corner + [flip(m, n_dp, 1) for m in corner]
     else:
         downs_here = [lax.all_gather(downs, "dp", axis=0, tiled=True)]
-    lowered = project(idx, count, tokens, downs_here, n, 4, 4)
-    cots[-1], up_line = gate(cots[-1], up_line, after=[lowered])
+    lowered = project(z, idx, count, tokens, downs_here, n, 4, 4)
+    cots[-1], up_line = gate(cots[-1], up_line, after=[lowered[0]])
 
     cots.append(ring(cots[-1], n))
     if cube:
         same = [up_line] + [flip(up_line, n_dp, k) for k in (2, 4, 6)]
         all_ups = [m for u in same for m in (u, flip(u, n_dp, 1))]
-        word = jnp.stack([wanted, flip(wanted, n_dp, 1)])
-        words = jnp.concatenate([word] + [flip(word, n_dp, k) for k in (2, 4, 6)])
-        asked = jnp.sum(jnp.where(peers[None, :] == me, words, 0), axis=1)[peers ^ me]
+        origin = me[None]
     else:
-        all_ups = [lax.all_gather(up_line, "dp", axis=1, tiled=True)]
-        asked = lax.all_gather(wanted, "dp", axis=0, tiled=False)[:, me]
-    cots[-1], lowered = gate(cots[-1], lowered, after=[*all_ups, asked])
-
-    parts = lax.all_to_all(lowered, "tsp", 0, 0, tiled=True)
-    sent, pulled = down_sums(z, idx, owner, count, tokens, all_ups, cots, n_dp, n, 4, 7)
+        all_ups = [lax.all_gather(up_line, "dp", axis=0, tiled=False)[k] for k in range(n_dp)]
+        origin = jnp.zeros((1,), jnp.int32)
+    asked = told(me[None], all_ups, n * size)
+    part = pulled_part(idx, all_ups, cots[:-1], ranks, size, 4, 5)
+    cots[-1], *lowered = gate(cots[-1], *lowered, after=[part])
+
+    shift = lambda x, s: lax.ppermute(x, "tsp", [(i, (i + s) % n) for i in range(n)]) if s else x
+    parts = [shift(block, s) for s, block in enumerate(lowered)]
+    sent, pulled = down_sums(idx, owner, count, tokens, part, cots[-1], all_ups, size, n_dp, n, 4, 7)
+    sent = gate(sent, after=parts)[0]
     down_got = lax.all_to_all(sent, "dp", 0, 0, tiled=True)
     token_gradient = token_gradients(
-        z, idx, count, weight, pulled, downs_here, cots, n, rows, 4, after=[parts]
+        z, idx, count, weight, pulled, downs_here, cots, n, rows, 4
     )
-    parts = gate(parts, after=[token_gradient])[0]
-    lowered = jnp.sum(parts, axis=0).astype(jnp.bfloat16)
-    lowered = [lowered] + [
-        lax.ppermute(lowered, "tsp", [(i, (i + s) % n) for i in range(n)]) for s in range(1, n)
-    ]
+    parts = gate(*parts, after=[token_gradient])
+    lowered = functools.reduce(jnp.add, parts).astype(jnp.bfloat16)
+    lowered = [shift(lowered, s) for s in range(n)]
     sent = up_sums(z, owner, cotangent, lowered, n_dp, 2)
     sent = gate(sent, after=[down_got])[0]
     up_got = lax.all_to_all(sent, "dp", 0, 0, tiled=True)
-    return token_gradient, owned(asked, down_got, held, 60), owned(asked, up_got, held, 16)
+    return token_gradient, owned(origin, asked, down_got, held, 60), owned(origin, asked, up_got, held, 16)
 
 
 def solution(mesh):

time: 164 us -> 159 us (0.970)
  waiting for transfers between devices: 53.6 us -> 40.2 us
  Pallas kernels: 50.4 us -> 59.4 us
  local copies, waits for them, and re-layouts: 18.5 us -> 21.8 us
  starting transfers between devices: 36.5 us -> 33.8 us
    pallas_call x1 -> x4, Pallas kernels: 11.3 us -> 20.8 us  [the longest x1 10.1 us: down_sums(): pl.pallas_call(functools.partial(down_sums_kernel, n, per, rows, ranks, s...]
    ppermute x3 -> x6, starting transfers between devices: 2.17 us -> 7.92 us  [on_device(): lax.ppermute(x, 'tsp', [(i, (i + s) % n) for i in range(n)])]
    ppermute x20 -> x16, starting transfers between devices: 15.7 us -> 10.4 us  [flip(): return lax.ppermute(x, 'dp', [(i, i ^ by) for i in range(n)])]
    ppermute x20 -> x16, waiting for transfers between devices: 32.8 us -> 28.2 us  [flip(): return lax.ppermute(x, 'dp', [(i, i ^ by) for i in range(n)])]
    unnamed x60 -> x69, local copies, waits for them, and re-layouts: 15.4 us -> 19.8 us
    all_to_all x1 -> x0, starting transfers between devices: 3.47 us -> none  [on_device(): parts = lax.all_to_all(lowered, 'tsp', 0, 0, tiled=True)]
    all_to_all x1 -> x0, waiting for transfers between devices: 3.43 us -> none  [on_device(): parts = lax.all_to_all(lowered, 'tsp', 0, 0, tiled=True)]
    ppermute x3, waiting for transfers between devices: 4.26 us -> 1.15 us  [on_device(): lax.ppermute(ups, 'tsp', [(i, (i + s) % n) for i in range(n)])]
  transfers between devices with their start and end apart: 32 -> 30, of which waited for: 16 -> 15; matrix products, arithmetic and copies ran while one was open for 8% -> 9% of each run, Pallas kernels for 30% -> 37%
where the time goes in v4:
time: 159 us; the launch traced here: 158 us
  Pallas kernels  59.4 us (37%)
  waiting for transfers between devices  40.2 us (25%)
  starting transfers between devices  33.8 us (21%)
  local copies, waits for them, and re-layouts  21.8 us (14%)
  other arithmetic  1.72 us (1%)
    ppermute x16, waiting for transfers between devices, flip(): return lax.ppermute(x, 'dp', [(i, i ^ by) for i in range(n)])  28.2 us
    unnamed x69, local copies, waits for them, and re-layouts  19.8 us
    pallas_call x1, Pallas kernels, token_gradients(): pl.pallas_call(functools.partial(token_kernel, n, per, rows, len(maps)),...  19.1 us
    ppermute x16, starting transfers between devices, flip(): return lax.ppermute(x, 'dp', [(i, i ^ by) for i in range(n)])  10.4 us
    pallas_call x1, Pallas kernels, down_sums(): pl.pallas_call(functools.partial(down_sums_kernel, n, per, rows, ranks, s...  10.1 us
    pallas_call x1, Pallas kernels, project(): pl.pallas_call(functools.partial(project_kernel, n, per, rows, len(maps))...  9.55 us
    ppermute x6, starting transfers between devices, on_device(): lax.ppermute(x, 'tsp', [(i, (i + s) % n) for i in range(n)])  7.92 us
    pallas_call x1, Pallas kernels, pulled_part(): pl.pallas_call(functools.partial(pulled_part_kernel, n, per, rows, ranks,...  6.01 us
  transfers between devices with their start and end apart: 30, of which 15 were waited for; matrix products, arithmetic and copies ran while one was open for 9% of the time, Pallas kernels for 37%

profile of v4, /device:TPU:0, one launch (start us, length us, event | category | flops | bytes accessed | tf_op | source)
XLA Modules:
  0.0 157.9 jit_solution(14781960663271783384)
XLA Ops:
  0.6 3.1 %collective-permute-start = (bf16[2048,256]{1,0:T(8,128)(2,1)}, bf16[2048,256]{1,0:T(8,128)(2,1)S(1)}, u32[]{:S(2)}, u32[]{:S(2)}) collective-permute-start(bf16[2048,256]{1,0:T(8,128)(2,1)} %x_hbm.1), channel_id=1, source_target_pairs={{0,1},{1,2},{2,3},{3,0},{4,5},{5,6},{6,7},{7,4},{8,9},{9,10},{10,1... | collective-permute-start | bytes 3145736 | tf_op jit(solution)/shard_map/ppermute | solution.py:419
  3.7 1.5 collective-permute-start.2
  5.2 1.5 collective-permute-start.1
  6.7 10.6 %collective-permute-done.2.refs_1_ = bf16[2,64,2048]{2,1,0:T(8,128)(2,1)S(1)} collective-permute-done((bf16[2,64,2048]{2,1,0:T(8,128)(2,1)}, bf16[2,64,2048]{2,1,0:T(8,128)(2,1)S(1)}, u32[]{:S(2)}, u32[]{:S(2)}) %collective-permute-start.2) | collective-permute-done | bytes 524320 | tf_op jit(solution)/shard_map/ppermute | solution.py:423
  17.3 1.2 collective-permute-done.1.refs_0_
  18.5 0.8 copy-done.3
  19.3 3.1 %late.1.refs_1_ = bf16[2,64,256]{2,1,0:T(8,128)(2,1)} custom-call(bf16[2,64,256]{2,1,0:T(8,128)(2,1)} %x.5, bf16[2,64,2048]{2,1,0:T(8,128)(2,1)} %get-tuple-element.46.refs_0_.refs_3_, bf16[2,64,2048]{2,1,0:T(8,128)(2,1)} %get-tuple-element.47.refs_1_.refs_4_), custom_call_target="tpu_custom_call" | custom-call | tf_op jit(solution)/shard_map/late/pallas_call | solution.py:406
  22.4 2.4 %collective-permute-start.5 = (bf16[2,64,256]{2,1,0:T(8,128)(2,1)}, bf16[2,64,256]{2,1,0:T(8,128)(2,1)S(1)}, u32[]{:S(2)}, u32[]{:S(2)}) collective-permute-start(bf16[2,64,256]{2,1,0:T(8,128)(2,1)} %late.1.refs_1_), channel_id=1, source_target_pairs={{0,3},{1,0},{2,1},{3,2},{4,7},{5,4},{6,5},{7,6},{8,11},{9,8},{10,9... | collective-permute-start | bytes 196616 | tf_op jit(solution)/shard_map/ppermute | solution.py:455
  24.9 0.7 collective-permute-start.4
  25.5 1.6 collective-permute-start.3
  27.1 6.5 %copy.34 = bf16[2048,1024]{0,1:T(8,128)(2,1)} copy(bf16[2048,1024]{1,0:T(8,128)(2,1)} %param.12) | data formatting | bytes 8388608 | tf_op args[2]
  33.6 1.1 collective-permute-done.4.refs_6_
  34.8 0.6 copy-done.26
  35.9 1.3 plan.1
  37.2 1.0 slice.22
  38.1 1.0 slice.23
  39.1 1.6 collective-permute-start.11
  40.7 1.4 collective-permute-start.10
  42.0 0.6 convert_bitcast_fusion
  42.7 0.5 collective-permute-start.9
  43.2 0.8 constant_dynamic-update-slice_fusion.4
  44.0 0.8 constant_dynamic-update-slice_fusion.3
  44.9 2.8 %collective-permute-done.11.refs_7_ = bf16[1,64,2048]{2,1,0:T(8,128)(2,1)S(1)} collective-permute-done((bf16[1,64,2048]{2,1,0:T(8,128)(2,1)S(1)}, bf16[1,64,2048]{2,1,0:T(8,128)(2,1)S(1)}, u32[]{:S(2)}, u32[]{:S(2)}) %collective-permute-start.11) | collective-permute-done | bytes 262176 | tf_op jit(solution)/shard_map/ppermute | solution.py:423
  47.6 1.2 collective-permute-done.10.refs_6_
  48.8 0.9 constant_dynamic-update-slice_fusion.2
  49.7 0.8 constant_dynamic-update-slice_fusion.1
  50.7 0.7 copy-done.16
  51.8 9.6 %project.1 = (f32[256,128]{1,0:T(8,128)}, f32[256,128]{1,0:T(8,128)}, f32[256,128]{1,0:T(8,128)}, f32[256,128]{1,0:T(8,128)}) custom-call(s32[1]{0:T(128)} %bitcast.z, s32[16]{0:T(128)} %get-tuple-element.45.idx, s32[16]{0:T(128)} %count.5, bf16[2048,2048]{1,0:T(8,128)(2,1)} %x.7, bf16[2,64,2048]{2,1,0:T(8,128)(2,1)} %refs_0_.5, ...), custom_call_target="tpu_custom_call" | custom-call | bytes 1200000 | tf_op jit(solution)/shard_map/project/pallas_call | solution.py:104
  61.4 1.4 collective-permute-done.6.refs_0_
  62.8 1.0 copy-done.5
  63.9 2.4 %collective-permute-start.19 = (bf16[528,256]{1,0:T(8,128)(2,1)}, bf16[528,256]{1,0:T(8,128)(2,1)S(1)}, u32[]{:S(2)}, u32[]{:S(2)}) collective-permute-start(bf16[528,256]{1,0:T(8,128)(2,1)} %get-tuple-element.60.refs_3_.refs_0_), channel_id=1, source_target_pairs={{0,24},{4,28},{8,16},{12,20},{16,8},{20,12},{24,0},{28,4},{1,25},{... | collective-permute-start | bytes 811016 | tf_op jit(solution)/shard_map/ppermute | solution.py:423
  66.3 0.5 collective-permute-start.17
  66.8 0.5 collective-permute-start.15
  67.4 7.1 %collective-permute-done.19.refs_9_.refs_6_ = bf16[528,256]{1,0:T(8,128)(2,1)S(1)} collective-permute-done((bf16[528,256]{1,0:T(8,128)(2,1)}, bf16[528,256]{1,0:T(8,128)(2,1)S(1)}, u32[]{:S(2)}, u32[]{:S(2)}) %collective-permute-start.19) | collective-permute-done | bytes 270368 | tf_op jit(solution)/shard_map/ppermute | solution.py:423
  74.5 3.9 %collective-permute-done.17.refs_7_.refs_4_ = bf16[528,256]{1,0:T(8,128)(2,1)S(1)} collective-permute-done((bf16[528,256]{1,0:T(8,128)(2,1)}, bf16[528,256]{1,0:T(8,128)(2,1)S(1)}, u32[]{:S(2)}, u32[]{:S(2)}) %collective-permute-start.17) | collective-permute-done | bytes 270368 | tf_op jit(solution)/shard_map/ppermute | solution.py:423
  78.4 0.4 collective-permute-start.16
  78.9 1.0 collective-permute-done.18.refs_8_.refs_5_
  79.9 0.4 collective-permute-done.16.refs_6_.refs_3_
  80.6 0.7 copy-done.14
  81.3 6.0 %pulled_part.1.refs_5_.part = f32[2048,64]{1,0:T(8,128)} custom-call(s32[16]{0:T(128)} %get-tuple-element.45.idx, bf16[2048,256]{1,0:T(8,128)(2,1)} %x_hbm.1, bf16[2048,256]{1,0:T(8,128)(2,1)} %get-tuple-element.50.refs_1_.refs_11_, bf16[2048,256]{1,0:T(8,128)(2,1)} %get-tuple-element.59.refs_2_.refs_12_, ...), custom_call_target="tpu_custom_call" | custom-call | bytes 1500000 | tf_op jit(solution)/shard_map/pulled_part/pallas_call | solution.py:209
  87.3 2.8 %collective-permute-done.21.refs_0_ = bf16[2048,256]{1,0:T(8,128)(2,1)S(1)} collective-permute-done((bf16[2048,256]{1,0:T(8,128)(2,1)}, bf16[2048,256]{1,0:T(8,128)(2,1)S(1)}, u32[]{:S(2)}, u32[]{:S(2)}) %collective-permute-start.21) | collective-permute-done | bytes 1048608 | tf_op jit(solution)/shard_map/ppermute | solution.py:419
  90.1 1.0 copy-done.6
  91.1 1.8 %collective-permute-start.23 = (f32[256,128]{1,0:T(8,128)}, f32[256,128]{1,0:T(8,128)S(1)}, u32[]{:S(2)}, u32[]{:S(2)}) collective-permute-start(f32[256,128]{1,0:T(8,128)} %get-tuple-element.69), channel_id=1, source_target_pairs={{0,2},{1,3},{2,0},{3,1},{4,6},{5,7},{6,4},{7,5},{8,10},{9,11},{10,... | collective-permute-start | bytes 393224 | tf_op jit(solution)/shard_map/ppermute | solution.py:490
  92.9 2.0 %collective-permute-start.24 = (f32[256,128]{1,0:T(8,128)}, f32[256,128]{1,0:T(8,128)S(1)}, u32[]{:S(2)}, u32[]{:S(2)}) collective-permute-start(f32[256,128]{1,0:T(8,128)} %get-tuple-element.70), channel_id=1, source_target_pairs={{0,3},{1,0},{2,1},{3,2},{4,7},{5,4},{6,5},{7,6},{8,11},{9,8},{10,9... | collective-permute-start | bytes 393224 | tf_op jit(solution)/shard_map/ppermute | solution.py:490
  94.9 10.1 %down_sums.1 = (bf16[8,64,2048]{2,1,0:T(8,128)(2,1)}, bf16[2048,64]{1,0:T(8,128)(2,1)}) custom-call(s32[16]{0:T(128)} %get-tuple-element.45.idx, s32[16]{0:T(128)} %get-tuple-element.49.owner, s32[16]{0:T(128)} %count.5, bf16[2048,2048]{1,0:T(8,128)(2,1)} %x.7, f32[2048,64]{1,0:T(8,128)} %pulled_part.1.refs_5_.part, ...), custom_call_target="tpu_custom_call" | custom-call | bytes 2100000 | tf_op jit(solution)/shard_map/down_sums/pallas_call | solution.py:260
  105.1 0.6 copy-done.18
  105.8 3.7 %all-to-all-start = ((bf16[8,64,2048]{2,1,0:T(8,128)(2,1)}), bf16[8,64,2048]{2,1,0:T(8,128)(2,1)S(1)}, u32[]{:S(2)}, u32[]{:S(2)}) async-start(bf16[8,64,2048]{2,1,0:T(8,128)(2,1)} %gate.11), calls=%async_computation | async-start | bytes 4194304 | tf_op jit(solution)/shard_map/all_to_all | solution.py:494
  109.6 19.1 %token_gradient.1.refs_4_ = bf16[2048,2048]{1,0:T(8,128)(2,1)} custom-call(s32[1]{0:T(128)} %bitcast.z, s32[16]{0:T(128)} %get-tuple-element.45.idx, s32[16]{0:T(128)} %count.5, bf16[1024,2048]{1,0:T(8,128)(2,1)} %get-tuple-element.48.weight, bf16[2048,64]{1,0:T(8,128)(2,1)} %get-tuple-element.65.pulled, bf16[2,64,2048]{2,1,0:T(8,128)(2,1)} %refs_0_.5, ...), custom_call_target="tpu_custom_call" | custom-call | bytes 4800000 | tf_op jit(solution)/shard_map/token_gradient/pallas_call | solution.py:312
  128.6 1.1 add_convert_fusion.refs_0_
  129.8 1.6 %collective-permute-start.27 = (bf16[256,128]{1,0:T(8,128)(2,1)S(1)}, bf16[256,128]{1,0:T(8,128)(2,1)S(1)}, u32[]{:S(2)}, u32[]{:S(2)}) collective-permute-start(bf16[256,128]{1,0:T(8,128)(2,1)S(1)} %add_convert_fusion.refs_0_), channel_id=1, source_target_pairs={{0,3},{1,0},{2,1},{3,2},{4,7},{5,4},{6,5},{7,6},{8,11},{9,8},{10,9... | collective-permute-start | bytes 196616 | tf_op jit(solution)/shard_map/ppermute | solution.py:490
  131.4 0.6 collective-permute-start.26
  131.9 1.9 %collective-permute-start.25 = (bf16[256,128]{1,0:T(8,128)(2,1)S(1)}, bf16[256,128]{1,0:T(8,128)(2,1)S(1)}, u32[]{:S(2)}, u32[]{:S(2)}) collective-permute-start(bf16[256,128]{1,0:T(8,128)(2,1)S(1)} %add_convert_fusion.refs_0_), channel_id=1, source_target_pairs={{0,1},{1,2},{2,3},{3,0},{4,5},{5,6},{6,7},{7,4},{8,9},{9,10},{10,1... | collective-permute-start | bytes 196616 | tf_op jit(solution)/shard_map/ppermute | solution.py:490
  133.9 0.4 collective-permute-done.27.refs_3_
  134.3 4.8 %collective-permute-done.26.refs_2_ = bf16[256,128]{1,0:T(8,128)(2,1)S(1)} collective-permute-done((bf16[256,128]{1,0:T(8,128)(2,1)S(1)}, bf16[256,128]{1,0:T(8,128)(2,1)S(1)}, u32[]{:S(2)}, u32[]{:S(2)}) %collective-permute-start.26) | collective-permute-done | bytes 65568 | tf_op jit(solution)/shard_map/ppermute | solution.py:490
  139.2 0.6 copy-done.30
  139.8 0.6 copy-done.31
  140.4 3.2 %up_sums.1.refs_0_ = bf16[8,64,256]{2,1,0:T(8,128)(2,1)} custom-call(s32[1]{0:T(128)} %bitcast.z, s32[16]{0:T(128)} %get-tuple-element.49.owner, bf16[2048,256]{1,0:T(8,128)(2,1)} %x_hbm.1, bf16[256,128]{1,0:T(8,128)(2,1)} %copy-done.28, bf16[256,128]{1,0:T(8,128)(2,1)} %copy-done.31, bf16[256,128]{1,0:T(8,128)(2,1)} %copy-done.30, bf16[256,128]{1,0:T(8,128)(2,1)} %copy-done.29), custom_call_target="tpu_custom_call" | custom-call | bytes 600000 | tf_op jit(solution)/shard_map/up_sums/pallas_call | solution.py:159
  143.7 1.3 copy-done.1
  145.0 3.9 %all-to-all-start.1 = ((bf16[8,64,256]{2,1,0:T(8,128)(2,1)}), bf16[8,64,256]{2,1,0:T(8,128)(2,1)S(1)}, u32[]{:S(2)}, u32[]{:S(2)}) async-start(bf16[8,64,256]{2,1,0:T(8,128)(2,1)} %gate.13), calls=%async_computation.1 | async-start | bytes 524288 | tf_op jit(solution)/shard_map/all_to_all | solution.py:503
  148.9 1.6 told.1.asked
  150.4 4.0 %owned.2 = f32[2,64,2048]{2,1,0:T(8,128)} custom-call(s32[1]{0:T(128)} %bitcast.1.me.first, f32[8,128]{1,0:T(8,128)} %told.1.asked, bf16[8,64,2048]{2,1,0:T(8,128)(2,1)} %copy-done.1), custom_call_target="tpu_custom_call" | custom-call | bytes 600000 | tf_op jit(solution)/shard_map/owned/pallas_call | solution.py:371
  154.5 1.3 all-to-all-done.1.got
  155.8 0.7 copy-done
  156.5 1.5 owned.3
  (87 shorter events, 1.6 us)
Async XLA Ops:
  0.6 34.1 %collective-permute-start = (bf16[2048,256]{1,0:T(8,128)(2,1)}, bf16[2048,256]{1,0:T(8,128)(2,1)S(1)}, u32[]{:S(2)}, u32[]{:S(2)}) collective-permute-start(bf16[2048,256]{1,0:T(8,128)(2,1)} %x_hbm.1), channel_id=1, source_target_pairs={{0,1},{1,2},{2,3},{3,0},{4,5},{5,6},{6,7},{7,4},{8,9},{9,10},{10,1... | collective-permute-start | bytes 3145736 | tf_op jit(solution)/shard_map/ppermute | solution.py:419
  3.7 13.6 %collective-permute-start.2 = (bf16[2,64,2048]{2,1,0:T(8,128)(2,1)}, bf16[2,64,2048]{2,1,0:T(8,128)(2,1)S(1)}, u32[]{:S(2)}, u32[]{:S(2)}) collective-permute-start(bf16[2,64,2048]{2,1,0:T(8,128)(2,1)} %refs_0_.5), channel_id=1, source_target_pairs={{0,16},{4,20},{8,24},{12,28},{16,0},{20,4},{24,8},{28,12},{1,17},{... | collective-permute-start | bytes 1572872 | tf_op jit(solution)/shard_map/ppermute | solution.py:423
  5.2 13.3 %collective-permute-start.1 = (bf16[2,64,2048]{2,1,0:T(8,128)(2,1)}, bf16[2,64,2048]{2,1,0:T(8,128)(2,1)S(1)}, u32[]{:S(2)}, u32[]{:S(2)}) collective-permute-start(bf16[2,64,2048]{2,1,0:T(8,128)(2,1)} %refs_0_.5), channel_id=1, source_target_pairs={{0,8},{4,12},{8,0},{12,4},{16,24},{20,28},{24,16},{28,20},{1,9},{5... | collective-permute-start | bytes 1572872 | tf_op jit(solution)/shard_map/ppermute | solution.py:423
  17.3 1.2 copy-start.2
  18.5 0.8 copy-start.3
  22.4 11.1 %collective-permute-start.5 = (bf16[2,64,256]{2,1,0:T(8,128)(2,1)}, bf16[2,64,256]{2,1,0:T(8,128)(2,1)S(1)}, u32[]{:S(2)}, u32[]{:S(2)}) collective-permute-start(bf16[2,64,256]{2,1,0:T(8,128)(2,1)} %late.1.refs_1_), channel_id=1, source_target_pairs={{0,3},{1,0},{2,1},{3,2},{4,7},{5,4},{6,5},{7,6},{8,11},{9,8},{10,9... | collective-permute-start | bytes 196616 | tf_op jit(solution)/shard_map/ppermute | solution.py:455
  24.9 9.8 %collective-permute-start.4 = (bf16[2,64,256]{2,1,0:T(8,128)(2,1)}, bf16[2,64,256]{2,1,0:T(8,128)(2,1)S(1)}, u32[]{:S(2)}, u32[]{:S(2)}) collective-permute-start(bf16[2,64,256]{2,1,0:T(8,128)(2,1)} %late.1.refs_1_), channel_id=1, source_target_pairs={{0,2},{1,3},{2,0},{3,1},{4,6},{5,7},{6,4},{7,5},{8,10},{9,11},{10,... | collective-permute-start | bytes 196616 | tf_op jit(solution)/shard_map/ppermute | solution.py:455
  25.5 9.2 %collective-permute-start.3 = (bf16[2,64,256]{2,1,0:T(8,128)(2,1)}, bf16[2,64,256]{2,1,0:T(8,128)(2,1)S(1)}, u32[]{:S(2)}, u32[]{:S(2)}) collective-permute-start(bf16[2,64,256]{2,1,0:T(8,128)(2,1)} %late.1.refs_1_), channel_id=1, source_target_pairs={{0,1},{1,2},{2,3},{3,0},{4,5},{5,6},{6,7},{7,4},{8,9},{9,10},{10,1... | collective-permute-start | bytes 196616 | tf_op jit(solution)/shard_map/ppermute | solution.py:455
  27.1 15.6 %collective-permute-start.7 = (bf16[2,64,2048]{2,1,0:T(8,128)(2,1)}, bf16[2,64,2048]{2,1,0:T(8,128)(2,1)S(1)}, u32[]{:S(2)}, u32[]{:S(2)}) collective-permute-start(bf16[2,64,2048]{2,1,0:T(8,128)(2,1)} %refs_0_.5), channel_id=1, source_target_pairs={{0,4},{4,0},{8,12},{12,8},{16,20},{20,16},{24,28},{28,24},{1,5},{5... | collective-permute-start | bytes 1572872 | tf_op jit(solution)/shard_map/ppermute | solution.py:423
  33.6 1.2 copy-start.25
  34.7 0.6 copy-start.26
  34.7 0.6 copy-start.27
  34.7 1.0 copy-start.4
  35.7 27.1 %collective-permute-start.6 = (bf16[2048,256]{1,0:T(8,128)(2,1)}, bf16[2048,256]{1,0:T(8,128)(2,1)S(1)}, u32[]{:S(2)}, u32[]{:S(2)}) collective-permute-start(bf16[2048,256]{1,0:T(8,128)(2,1)} %get-tuple-element.50.refs_1_.refs_11_), channel_id=1, source_target_pairs={{0,1},{1,2},{2,3},{3,0},{4,5},{5,6},{6,7},{7,4},{8,9},{9,10},{10,1... | collective-permute-start | bytes 3145736 | tf_op jit(solution)/shard_map/ppermute | solution.py:419
  39.1 8.5 %collective-permute-start.11 = (bf16[1,64,2048]{2,1,0:T(8,128)(2,1)S(1)}, bf16[1,64,2048]{2,1,0:T(8,128)(2,1)S(1)}, u32[]{:S(2)}, u32[]{:S(2)}) collective-permute-start(bf16[1,64,2048]{2,1,0:T(8,128)(2,1)S(1)} %slice.23), channel_id=1, source_target_pairs={{0,8},{4,12},{8,0},{12,4},{16,24},{20,28},{24,16},{28,20},{1,9},{5... | collective-permute-start | bytes 786440 | tf_op jit(solution)/shard_map/ppermute | solution.py:423
  40.7 8.2 %collective-permute-start.10 = (bf16[1,64,2048]{2,1,0:T(8,128)(2,1)S(1)}, bf16[1,64,2048]{2,1,0:T(8,128)(2,1)S(1)}, u32[]{:S(2)}, u32[]{:S(2)}) collective-permute-start(bf16[1,64,2048]{2,1,0:T(8,128)(2,1)S(1)} %slice.22), channel_id=1, source_target_pairs={{0,16},{4,20},{8,24},{12,28},{16,0},{20,4},{24,8},{28,12},{1,17},{... | collective-permute-start | bytes 786440 | tf_op jit(solution)/shard_map/ppermute | solution.py:423
  42.6 7.9 %collective-permute-start.8 = (bf16[2,64,2048]{2,1,0:T(8,128)(2,1)}, bf16[2,64,2048]{2,1,0:T(8,128)(2,1)S(1)}, u32[]{:S(2)}, u32[]{:S(2)}) collective-permute-start(bf16[2,64,2048]{2,1,0:T(8,128)(2,1)} %get-tuple-element.56.refs_2_), channel_id=1, source_target_pairs={{0,4},{4,0},{8,12},{12,8},{16,20},{20,16},{24,28},{28,24},{1,5},{5... | collective-permute-start | bytes 1572872 | tf_op jit(solution)/shard_map/ppermute | solution.py:423
  42.7 8.0 %copy-start.15 = (bf16[2,64,2048]{2,1,0:T(8,128)(2,1)}, bf16[2,64,2048]{2,1,0:T(8,128)(2,1)S(1)}, u32[]{:S(2)}) copy-start(bf16[2,64,2048]{2,1,0:T(8,128)(2,1)S(1)} %collective-permute-done.7.refs_1_) | copy-start | bytes 1572868
  42.7 7.9 %collective-permute-start.9 = (bf16[2,64,2048]{2,1,0:T(8,128)(2,1)}, bf16[2,64,2048]{2,1,0:T(8,128)(2,1)S(1)}, u32[]{:S(2)}, u32[]{:S(2)}) collective-permute-start(bf16[2,64,2048]{2,1,0:T(8,128)(2,1)} %get-tuple-element.57.refs_4_), channel_id=1, source_target_pairs={{0,4},{4,0},{8,12},{12,8},{16,20},{20,16},{24,28},{28,24},{1,5},{5... | collective-permute-start | bytes 1572872 | tf_op jit(solution)/shard_map/ppermute | solution.py:423
  47.6 3.1 %copy-start.21 = (bf16[1,64,2048]{2,1,0:T(8,128)(2,1)}, bf16[1,64,2048]{2,1,0:T(8,128)(2,1)S(1)}, u32[]{:S(2)}) copy-start(bf16[1,64,2048]{2,1,0:T(8,128)(2,1)S(1)} %collective-permute-done.11.refs_7_) | copy-start | bytes 786436
  47.6 3.0 %collective-permute-start.13 = (bf16[1,64,2048]{2,1,0:T(8,128)(2,1)S(1)}, bf16[1,64,2048]{2,1,0:T(8,128)(2,1)S(1)}, u32[]{:S(2)}, u32[]{:S(2)}) collective-permute-start(bf16[1,64,2048]{2,1,0:T(8,128)(2,1)S(1)} %collective-permute-done.11.refs_7_), channel_id=1, source_target_pairs={{0,4},{4,0},{8,12},{12,8},{16,20},{20,16},{24,28},{28,24},{1,5},{5... | collective-permute-start | bytes 786440 | tf_op jit(solution)/shard_map/ppermute | solution.py:423
  48.8 1.9 %copy-start.22 = (bf16[1,64,2048]{2,1,0:T(8,128)(2,1)}, bf16[1,64,2048]{2,1,0:T(8,128)(2,1)S(1)}, u32[]{:S(2)}) copy-start(bf16[1,64,2048]{2,1,0:T(8,128)(2,1)S(1)} %collective-permute-done.10.refs_6_) | copy-start | bytes 786436
  48.8 1.8 %collective-permute-start.12 = (bf16[1,64,2048]{2,1,0:T(8,128)(2,1)S(1)}, bf16[1,64,2048]{2,1,0:T(8,128)(2,1)S(1)}, u32[]{:S(2)}, u32[]{:S(2)}) collective-permute-start(bf16[1,64,2048]{2,1,0:T(8,128)(2,1)S(1)} %collective-permute-done.10.refs_6_), channel_id=1, source_target_pairs={{0,4},{4,0},{8,12},{12,8},{16,20},{20,16},{24,28},{28,24},{1,5},{5... | collective-permute-start | bytes 786440 | tf_op jit(solution)/shard_map/ppermute | solution.py:423
  50.6 10.8 %copy-start.7 = (bf16[528,256]{1,0:T(8,128)(2,1)}, bf16[528,256]{1,0:T(8,128)(2,1)S(1)}, u32[]{:S(2)}) copy-start(bf16[528,256]{1,0:T(8,128)(2,1)S(1)} %constant_dynamic-update-slice_fusion.refs_1_) | copy-start | bytes 811012
  50.6 0.8 copy-start.16
  50.6 1.0 copy-start.17
  50.6 1.1 copy-start.23
  50.6 1.2 copy-start.24
  62.8 1.0 copy-start.5
  63.9 26.2 %collective-permute-start.21 = (bf16[2048,256]{1,0:T(8,128)(2,1)}, bf16[2048,256]{1,0:T(8,128)(2,1)S(1)}, u32[]{:S(2)}, u32[]{:S(2)}) collective-permute-start(bf16[2048,256]{1,0:T(8,128)(2,1)} %get-tuple-element.59.refs_2_.refs_12_), channel_id=1, source_target_pairs={{0,1},{1,2},{2,3},{3,0},{4,5},{5,6},{6,7},{7,4},{8,9},{9,10},{10,1... | collective-permute-start | bytes 3145736 | tf_op jit(solution)/shard_map/ppermute | solution.py:419
  63.9 10.6 %collective-permute-start.19 = (bf16[528,256]{1,0:T(8,128)(2,1)}, bf16[528,256]{1,0:T(8,128)(2,1)S(1)}, u32[]{:S(2)}, u32[]{:S(2)}) collective-permute-start(bf16[528,256]{1,0:T(8,128)(2,1)} %get-tuple-element.60.refs_3_.refs_0_), channel_id=1, source_target_pairs={{0,24},{4,28},{8,16},{12,20},{16,8},{20,12},{24,0},{28,4},{1,25},{... | collective-permute-start | bytes 811016 | tf_op jit(solution)/shard_map/ppermute | solution.py:423
  66.3 12.0 %collective-permute-start.17 = (bf16[528,256]{1,0:T(8,128)(2,1)}, bf16[528,256]{1,0:T(8,128)(2,1)S(1)}, u32[]{:S(2)}, u32[]{:S(2)}) collective-permute-start(bf16[528,256]{1,0:T(8,128)(2,1)} %get-tuple-element.60.refs_3_.refs_0_), channel_id=1, source_target_pairs={{0,16},{4,20},{8,24},{12,28},{16,0},{20,4},{24,8},{28,12},{1,17},{... | collective-permute-start | bytes 811016 | tf_op jit(solution)/shard_map/ppermute | solution.py:423
  66.8 11.6 %collective-permute-start.15 = (bf16[528,256]{1,0:T(8,128)(2,1)}, bf16[528,256]{1,0:T(8,128)(2,1)S(1)}, u32[]{:S(2)}, u32[]{:S(2)}) collective-permute-start(bf16[528,256]{1,0:T(8,128)(2,1)} %get-tuple-element.60.refs_3_.refs_0_), channel_id=1, source_target_pairs={{0,8},{4,12},{8,0},{12,4},{16,24},{20,28},{24,16},{28,20},{1,9},{5... | collective-permute-start | bytes 811016 | tf_op jit(solution)/shard_map/ppermute | solution.py:423
  67.4 11.5 %collective-permute-start.14 = (bf16[528,256]{1,0:T(8,128)(2,1)}, bf16[528,256]{1,0:T(8,128)(2,1)S(1)}, u32[]{:S(2)}, u32[]{:S(2)}) collective-permute-start(bf16[528,256]{1,0:T(8,128)(2,1)} %get-tuple-element.60.refs_3_.refs_0_), channel_id=1, source_target_pairs={{0,4},{4,0},{8,12},{12,8},{16,20},{20,16},{24,28},{28,24},{1,5},{5... | collective-permute-start | bytes 811016 | tf_op jit(solution)/shard_map/ppermute | solution.py:423
  74.4 5.8 %copy-start.8 = (bf16[528,256]{1,0:T(8,128)(2,1)}, bf16[528,256]{1,0:T(8,128)(2,1)S(1)}, u32[]{:S(2)}) copy-start(bf16[528,256]{1,0:T(8,128)(2,1)S(1)} %collective-permute-done.19.refs_9_.refs_6_) | copy-start | bytes 811012
  74.4 4.4 %collective-permute-start.20 = (bf16[528,256]{1,0:T(8,128)(2,1)S(1)}, bf16[528,256]{1,0:T(8,128)(2,1)S(1)}, u32[]{:S(2)}, u32[]{:S(2)}) collective-permute-start(bf16[528,256]{1,0:T(8,128)(2,1)S(1)} %collective-permute-done.19.refs_9_.refs_6_), channel_id=1, source_target_pairs={{0,4},{4,0},{8,12},{12,8},{16,20},{20,16},{24,28},{28,24},{1,5},{5... | collective-permute-start | bytes 811016 | tf_op jit(solution)/shard_map/ppermute | solution.py:423
  78.3 1.9 %copy-start.9 = (bf16[528,256]{1,0:T(8,128)(2,1)}, bf16[528,256]{1,0:T(8,128)(2,1)S(1)}, u32[]{:S(2)}) copy-start(bf16[528,256]{1,0:T(8,128)(2,1)S(1)} %collective-permute-done.17.refs_7_.refs_4_) | copy-start | bytes 811012
  78.3 1.5 collective-permute-start.18
  78.4 1.8 %copy-start.10 = (bf16[528,256]{1,0:T(8,128)(2,1)}, bf16[528,256]{1,0:T(8,128)(2,1)S(1)}, u32[]{:S(2)}) copy-start(bf16[528,256]{1,0:T(8,128)(2,1)S(1)} %collective-permute-done.15.refs_5_.refs_2_) | copy-start | bytes 811012
  78.4 1.8 %collective-permute-start.16 = (bf16[528,256]{1,0:T(8,128)(2,1)S(1)}, bf16[528,256]{1,0:T(8,128)(2,1)S(1)}, u32[]{:S(2)}, u32[]{:S(2)}) collective-permute-start(bf16[528,256]{1,0:T(8,128)(2,1)S(1)} %collective-permute-done.15.refs_5_.refs_2_), channel_id=1, source_target_pairs={{0,4},{4,0},{8,12},{12,8},{16,20},{20,16},{24,28},{28,24},{1,5},{5... | collective-permute-start | bytes 811016 | tf_op jit(solution)/shard_map/ppermute | solution.py:423
  78.9 1.4 copy-start.11
  78.9 1.4 copy-start.12
  79.9 0.7 copy-start.13
  80.6 0.7 copy-start.14
  90.1 1.0 copy-start.6
  91.1 13.9 %collective-permute-start.22 = (f32[256,128]{1,0:T(8,128)}, f32[256,128]{1,0:T(8,128)S(1)}, u32[]{:S(2)}, u32[]{:S(2)}) collective-permute-start(f32[256,128]{1,0:T(8,128)} %get-tuple-element.68), channel_id=1, source_target_pairs={{0,1},{1,2},{2,3},{3,0},{4,5},{5,6},{6,7},{7,4},{8,9},{9,10},{10,1... | collective-permute-start | bytes 393224 | tf_op jit(solution)/shard_map/ppermute | solution.py:490
  91.1 14.0 %collective-permute-start.23 = (f32[256,128]{1,0:T(8,128)}, f32[256,128]{1,0:T(8,128)S(1)}, u32[]{:S(2)}, u32[]{:S(2)}) collective-permute-start(f32[256,128]{1,0:T(8,128)} %get-tuple-element.69), channel_id=1, source_target_pairs={{0,2},{1,3},{2,0},{3,1},{4,6},{5,7},{6,4},{7,5},{8,10},{9,11},{10,... | collective-permute-start | bytes 393224 | tf_op jit(solution)/shard_map/ppermute | solution.py:490
  92.9 12.2 %collective-permute-start.24 = (f32[256,128]{1,0:T(8,128)}, f32[256,128]{1,0:T(8,128)S(1)}, u32[]{:S(2)}, u32[]{:S(2)}) collective-permute-start(f32[256,128]{1,0:T(8,128)} %get-tuple-element.70), channel_id=1, source_target_pairs={{0,3},{1,0},{2,1},{3,2},{4,7},{5,4},{6,5},{7,6},{8,11},{9,8},{10,9... | collective-permute-start | bytes 393224 | tf_op jit(solution)/shard_map/ppermute | solution.py:490
  105.1 0.7 copy-start.18
  105.1 0.7 copy-start.19
  105.1 0.7 copy-start.20
  105.8 37.8 %all-to-all-start = ((bf16[8,64,2048]{2,1,0:T(8,128)(2,1)}), bf16[8,64,2048]{2,1,0:T(8,128)(2,1)S(1)}, u32[]{:S(2)}, u32[]{:S(2)}) async-start(bf16[8,64,2048]{2,1,0:T(8,128)(2,1)} %gate.11), calls=%async_computation | async-start | bytes 4194304 | tf_op jit(solution)/shard_map/all_to_all | solution.py:494
  129.8 9.4 %copy-start.28 = (bf16[256,128]{1,0:T(8,128)(2,1)}, bf16[256,128]{1,0:T(8,128)(2,1)S(1)}, u32[]{:S(2)}) copy-start(bf16[256,128]{1,0:T(8,128)(2,1)S(1)} %add_convert_fusion.refs_0_) | copy-start | bytes 196612
  129.8 4.5 %collective-permute-start.27 = (bf16[256,128]{1,0:T(8,128)(2,1)S(1)}, bf16[256,128]{1,0:T(8,128)(2,1)S(1)}, u32[]{:S(2)}, u32[]{:S(2)}) collective-permute-start(bf16[256,128]{1,0:T(8,128)(2,1)S(1)} %add_convert_fusion.refs_0_), channel_id=1, source_target_pairs={{0,3},{1,0},{2,1},{3,2},{4,7},{5,4},{6,5},{7,6},{8,11},{9,8},{10,9... | collective-permute-start | bytes 196616 | tf_op jit(solution)/shard_map/ppermute | solution.py:490
  131.4 7.8 %collective-permute-start.26 = (bf16[256,128]{1,0:T(8,128)(2,1)S(1)}, bf16[256,128]{1,0:T(8,128)(2,1)S(1)}, u32[]{:S(2)}, u32[]{:S(2)}) collective-permute-start(bf16[256,128]{1,0:T(8,128)(2,1)S(1)} %add_convert_fusion.refs_0_), channel_id=1, source_target_pairs={{0,2},{1,3},{2,0},{3,1},{4,6},{5,7},{6,4},{7,5},{8,10},{9,11},{10,... | collective-permute-start | bytes 196616 | tf_op jit(solution)/shard_map/ppermute | solution.py:490
  131.9 7.2 %collective-permute-start.25 = (bf16[256,128]{1,0:T(8,128)(2,1)S(1)}, bf16[256,128]{1,0:T(8,128)(2,1)S(1)}, u32[]{:S(2)}, u32[]{:S(2)}) collective-permute-start(bf16[256,128]{1,0:T(8,128)(2,1)S(1)} %add_convert_fusion.refs_0_), channel_id=1, source_target_pairs={{0,1},{1,2},{2,3},{3,0},{4,5},{5,6},{6,7},{7,4},{8,9},{9,10},{10,1... | collective-permute-start | bytes 196616 | tf_op jit(solution)/shard_map/ppermute | solution.py:490
  134.3 4.8 %copy-start.29 = (bf16[256,128]{1,0:T(8,128)(2,1)}, bf16[256,128]{1,0:T(8,128)(2,1)S(1)}, u32[]{:S(2)}) copy-start(bf16[256,128]{1,0:T(8,128)(2,1)S(1)} %collective-permute-done.27.refs_3_) | copy-start | bytes 196612
  139.2 0.6 copy-start.30
  139.8 0.6 copy-start.31
  143.6 1.3 copy-start.1
  145.0 10.8 %all-to-all-start.1 = ((bf16[8,64,256]{2,1,0:T(8,128)(2,1)}), bf16[8,64,256]{2,1,0:T(8,128)(2,1)S(1)}, u32[]{:S(2)}, u32[]{:S(2)}) async-start(bf16[8,64,256]{2,1,0:T(8,128)(2,1)} %gate.13), calls=%async_computation.1 | async-start | bytes 524288 | tf_op jit(solution)/shard_map/all_to_all | solution.py:503
  155.8 0.7 copy-start

commit v5 on v4

--- a/solution.py
+++ b/solution.py
@@ -131,8 +131,8 @@
     total[owner] += lax.dot_general(terms, x, TN, preferred_element_type=jnp.float32)
 
 
-def up_sums_kernel(n, rows, scale, z, owner, x_hbm, *refs):
-    blocks, (out, x, raw, buf, total, sem) = refs[:n], refs[-6:]
+def up_sums_kernel(n, owners, rows, scale, z, origin, owner, x_hbm, *refs):
+    blocks, outs, (x, raw, buf, total, sem) = refs[:n], refs[n : n + owners], refs[-5:]
     half, ranks = raw.shape[1], raw.shape[2] // 2
     copies = [pltpu.make_async_copy(x_hbm, x, sem.at[n])]
     for s in range(n):
@@ -148,19 +148,20 @@
         buf[start + half : start + 2 * half, :] = raw[j][:, ranks:]
     for g in range(x.shape[0] // rows):
         add_terms(total, owner[g], buf[g * rows : (g + 1) * rows, :], x[g * rows : (g + 1) * rows, :])
-    out[...] = (total[...] * scale).astype(out.dtype)
-
-
-def up_sums(z, owner, x, blocks, owners, us, after=()):
+    for k, out in enumerate(outs):
+        out[...] = (total[lax.bitwise_xor(origin[0], k)] * scale).astype(out.dtype)
+
+
+def up_sums(z, origin, owner, x, blocks, owners, us):
     segs, n = owner.shape[0], len(blocks)
     rows, width = x.shape[0] // segs, x.shape[1]
     ranks = blocks[0].shape[1] // 2
     shape = (owners, ranks, width)
     return pl.pallas_call(
-        functools.partial(up_sums_kernel, n, rows, ADAPTER_SCALE / rows),
-        out_shape=jax.ShapeDtypeStruct(shape, jnp.bfloat16),
-        in_specs=[SMEM] * 2 + [HBM] * (1 + n + len(after)),
-        out_specs=VMEM,
+        functools.partial(up_sums_kernel, n, owners, rows, ADAPTER_SCALE / rows),
+        out_shape=[jax.ShapeDtypeStruct(shape[1:], jnp.bfloat16)] * owners,
+        in_specs=[SMEM] * 3 + [HBM] * (1 + n),
+        out_specs=[VMEM] * owners,
         scratch_shapes=[
             pltpu.VMEM(x.shape, x.dtype),
             pltpu.VMEM((n, *blocks[0].shape), jnp.bfloat16),
@@ -171,7 +172,7 @@
         compiler_params=params(),
         cost_estimate=cost(us),
         name="up_sums",
-    )(z, owner, x, *blocks, *after)
+    )(z, origin, owner, x, *blocks)
 
 
 def up_copies(maps, size, distances, table, sem):
@@ -378,6 +379,27 @@
         cost_estimate=cost(2),
         name="owned",
     )(first, asked, got)
+
+
+def owned_each_kernel(asked, *refs):
+    got, out = refs[:-1], refs[-1]
+    for e in range(out.shape[0]):
+        total = jnp.zeros(got[0].shape, jnp.float32)
+        for k, term in enumerate(got):
+            total += jnp.where(asked[k : k + 1, :1] == jnp.float32(e), term[...].astype(jnp.float32), 0.0)
+        out[e] = total
+
+
+def owned_each(asked, got, held):
+    return pl.pallas_call(
+        owned_each_kernel,
+        out_shape=jax.ShapeDtypeStruct((held, *got[0].shape), jnp.float32),
+        in_specs=[VMEM] * (1 + len(got)),
+        out_specs=VMEM,
+        compiler_params=params(16),
+        cost_estimate=cost(2),
+        name="owned_each",
+    )(asked, *got)
 
 
 def gate_kernel(*refs):
@@ -449,16 +471,16 @@
 
     cots = [cotangent, ring(cotangent, n)]
     owner, idx, wanted = plan(me[None], adapter_place_table, segment_adapter, held, n_dp, cube)
+    weight = frozen_key_weight.T
     if cube:
-        over_x, over_y = gate(flip(downs, n_dp, 2), flip(downs, n_dp, 4))
+        over_x, over_y, weight = gate(flip(downs, n_dp, 2), flip(downs, n_dp, 4), weight)
         ups = late(ups, [over_x, over_y])
     line = [lax.ppermute(ups, "tsp", [(i, (i + s) % n) for i in range(n)]) for s in range(1, n)]
-    weight = frozen_key_weight.T
     if cube:
-        cots[1], ups, weight, over_x, over_y, *line = gate(cots[1], ups, weight, over_x, over_y, *line)
+        cots[1], ups, over_x, over_y, *line = gate(cots[1], ups, over_x, over_y, *line)
         corner = [flip(over_x[:1], n_dp, 4), flip(over_y[1:], n_dp, 2)]
     else:
-        cots[1], ups, weight, *line = gate(cots[1], ups, weight, *line)
+        cots[1], ups, *line = gate(cots[1], ups, *line)
 
     while len(cots) < n - 1:
         cots.append(ring(cots[-1], n))
@@ -485,23 +507,27 @@
         origin = jnp.zeros((1,), jnp.int32)
     asked = told(me[None], all_ups, n * size)
     part = pulled_part(idx, all_ups, cots[:-1], ranks, size, 4, 5)
-    cots[-1], *lowered = gate(cots[-1], *lowered, after=[part])
+    cots[-1], *lowered = gate(cots[-1], *lowered, after=[part, asked])
 
     shift = lambda x, s: lax.ppermute(x, "tsp", [(i, (i + s) % n) for i in range(n)]) if s else x
     parts = [shift(block, s) for s, block in enumerate(lowered)]
     sent, pulled = down_sums(idx, owner, count, tokens, part, cots[-1], all_ups, size, n_dp, n, 4, 7)
-    sent = gate(sent, after=parts)[0]
+    sent, *parts = gate(sent, *parts)
     down_got = lax.all_to_all(sent, "dp", 0, 0, tiled=True)
-    token_gradient = token_gradients(
-        z, idx, count, weight, pulled, downs_here, cots, n, rows, 4
-    )
-    parts = gate(*parts, after=[token_gradient])
     lowered = functools.reduce(jnp.add, parts).astype(jnp.bfloat16)
     lowered = [shift(lowered, s) for s in range(n)]
-    sent = up_sums(z, owner, cotangent, lowered, n_dp, 2)
-    sent = gate(sent, after=[down_got])[0]
-    up_got = lax.all_to_all(sent, "dp", 0, 0, tiled=True)
-    return token_gradient, owned(origin, asked, down_got, held, 60), owned(origin, asked, up_got, held, 16)
+    token_gradient = token_gradients(
+        z, idx, count, weight, pulled, downs_here, cots, n, rows, 4, after=lowered[:1]
+    )
+    lowered[0] = gate(lowered[0], after=[token_gradient])[0]
+    got = up_sums(z, origin, owner, cotangent, lowered, n_dp, 2)
+    if cube:
+        got = [flip(term, n_dp, k) if k else term for k, term in enumerate(got)]
+    else:
+        got = lax.all_to_all(jnp.stack(got), "dp", 0, 0, tiled=True)
+        got = [got[k] for k in range(n_dp)]
+    down_grad = owned(origin, asked, down_got, held, 16)
+    return token_gradient, down_grad, owned_each(asked, got, held)
 
 
 def solution(mesh):

time: 159 us -> 153 us (0.962)
  waiting for transfers between devices: 40.2 us -> 36.3 us
  starting transfers between devices: 33.8 us -> 36.7 us
  Pallas kernels: 59.4 us -> 57 us
    ppermute x16 -> x23, starting transfers between devices: 10.4 us -> 17.2 us  [flip(): return lax.ppermute(x, 'dp', [(i, i ^ by) for i in range(n)])]
    ppermute x3, waiting for transfers between devices: 1.15 us -> 7.6 us  [on_device(): lax.ppermute(ups, 'tsp', [(i, (i + s) % n) for i in range(n)])]
    ppermute x6, waiting for transfers between devices: 5.27 us -> 0.02 us  [on_device(): lax.ppermute(x, 'tsp', [(i, (i + s) % n) for i in range(n)])]
    all_to_all x1 -> x0, starting transfers between devices: 3.87 us -> none  [on_device(): up_got = lax.all_to_all(sent, 'dp', 0, 0, tiled=True)]
    pallas_call x2 -> x1, Pallas kernels: 5.49 us -> 2.28 us  [owned(): pl.pallas_call(owned_kernel, grid=(ranks // per,), out_shape=jax.ShapeDty...]
    ppermute x16 -> x23, waiting for transfers between devices: 28.2 us -> 25.7 us  [flip(): return lax.ppermute(x, 'dp', [(i, i ^ by) for i in range(n)])]
    unnamed x69 -> x79, local copies, waits for them, and re-layouts: 19.8 us -> 18.6 us
    pallas_call x1 -> x2, Pallas kernels: 3.24 us -> 4.04 us  [the longest x1 3.25 us: up_sums(): pl.pallas_call(functools.partial(up_sums_kernel, n, owners, rows, ADAPTER...]
  transfers between devices with their start and end apart: 30 -> 36, of which waited for: 15 -> 16; matrix products, arithmetic and copies ran while one was open for 9% -> 8% of each run, Pallas kernels for 37% -> 36%
where the time goes in v5:
time: 153 us; the launch traced here: 152 us
  Pallas kernels  57 us (37%)
  starting transfers between devices  36.7 us (24%)
  waiting for transfers between devices  36.3 us (24%)
  local copies, waits for them, and re-layouts  20.6 us (13%)
    ppermute x23, waiting for transfers between devices, flip(): return lax.ppermute(x, 'dp', [(i, i ^ by) for i in range(n)])  25.7 us
    pallas_call x1, Pallas kernels, token_gradients(): pl.pallas_call(functools.partial(token_kernel, n, per, rows, len(maps)),...  19.1 us
    unnamed x79, local copies, waits for them, and re-layouts  18.6 us
    ppermute x23, starting transfers between devices, flip(): return lax.ppermute(x, 'dp', [(i, i ^ by) for i in range(n)])  17.2 us
    pallas_call x1, Pallas kernels, down_sums(): pl.pallas_call(functools.partial(down_sums_kernel, n, per, rows, ranks, s...  10.1 us
    pallas_call x1, Pallas kernels, project(): pl.pallas_call(functools.partial(project_kernel, n, per, rows, len(maps))...  9.56 us
    ppermute x6, starting transfers between devices, on_device(): lax.ppermute(x, 'tsp', [(i, (i + s) % n) for i in range(n)])  8.04 us
    ppermute x3, waiting for transfers between devices, on_device(): lax.ppermute(ups, 'tsp', [(i, (i + s) % n) for i in range(n)])  7.6 us
  transfers between devices with their start and end apart: 36, of which 16 were waited for; matrix products, arithmetic and copies ran while one was open for 8% of the time, Pallas kernels for 36%

profile of v5, /device:TPU:0, one launch (start us, length us, event | category | flops | bytes accessed | tf_op | source)
XLA Modules:
  0.0 152.4 jit_solution(7774016273696581572)
XLA Ops:
  0.6 3.1 %collective-permute-start.2 = (bf16[2048,256]{1,0:T(8,128)(2,1)}, bf16[2048,256]{1,0:T(8,128)(2,1)S(1)}, u32[]{:S(2)}, u32[]{:S(2)}) collective-permute-start(bf16[2048,256]{1,0:T(8,128)(2,1)} %x_hbm.1), channel_id=1, source_target_pairs={{0,1},{1,2},{2,3},{3,0},{4,5},{5,6},{6,7},{7,4},{8,9},{9,10},{10,1... | collective-permute-start | bytes 3145736 | tf_op jit(solution)/shard_map/ppermute | solution.py:441
  3.7 1.5 collective-permute-start.1
  5.2 1.5 collective-permute-start
  6.7 6.5 %copy.34 = bf16[2048,1024]{0,1:T(8,128)(2,1)} copy(bf16[2048,1024]{1,0:T(8,128)(2,1)} %param.12) | data formatting | bytes 8388608 | tf_op args[2]
  13.2 4.1 %collective-permute-done.1.refs_1_ = bf16[2,64,2048]{2,1,0:T(8,128)(2,1)S(1)} collective-permute-done((bf16[2,64,2048]{2,1,0:T(8,128)(2,1)}, bf16[2,64,2048]{2,1,0:T(8,128)(2,1)S(1)}, u32[]{:S(2)}, u32[]{:S(2)}) %collective-permute-start.1) | collective-permute-done | bytes 524320 | tf_op jit(solution)/shard_map/ppermute | solution.py:445
  17.3 1.2 collective-permute-done.refs_0_
  18.5 0.8 copy-done.3
  19.3 3.1 %late.1.refs_1_ = bf16[2,64,256]{2,1,0:T(8,128)(2,1)} custom-call(bf16[2,64,256]{2,1,0:T(8,128)(2,1)} %x.5, bf16[2,64,2048]{2,1,0:T(8,128)(2,1)} %get-tuple-element.57.refs_0_.refs_2_, bf16[2,64,2048]{2,1,0:T(8,128)(2,1)} %get-tuple-element.58.refs_1_.refs_3_), custom_call_target="tpu_custom_call" | custom-call | tf_op jit(solution)/shard_map/late/pallas_call | solution.py:428
  22.4 2.4 %collective-permute-start.5 = (bf16[2,64,256]{2,1,0:T(8,128)(2,1)}, bf16[2,64,256]{2,1,0:T(8,128)(2,1)S(1)}, u32[]{:S(2)}, u32[]{:S(2)}) collective-permute-start(bf16[2,64,256]{2,1,0:T(8,128)(2,1)} %late.1.refs_1_), channel_id=1, source_target_pairs={{0,3},{1,0},{2,1},{3,2},{4,7},{5,4},{6,5},{7,6},{8,11},{9,8},{10,9... | collective-permute-start | bytes 196616 | tf_op jit(solution)/shard_map/ppermute | solution.py:478
  24.9 0.7 collective-permute-start.4
  25.5 1.6 %collective-permute-start.3 = (bf16[2,64,256]{2,1,0:T(8,128)(2,1)}, bf16[2,64,256]{2,1,0:T(8,128)(2,1)S(1)}, u32[]{:S(2)}, u32[]{:S(2)}) collective-permute-start(bf16[2,64,256]{2,1,0:T(8,128)(2,1)} %late.1.refs_1_), channel_id=1, source_target_pairs={{0,1},{1,2},{2,3},{3,0},{4,5},{5,6},{6,7},{7,4},{8,9},{9,10},{10,1... | collective-permute-start | bytes 196616 | tf_op jit(solution)/shard_map/ppermute | solution.py:478
  27.1 3.4 %collective-permute-done.5.refs_6_ = bf16[2,64,256]{2,1,0:T(8,128)(2,1)S(1)} collective-permute-done((bf16[2,64,256]{2,1,0:T(8,128)(2,1)}, bf16[2,64,256]{2,1,0:T(8,128)(2,1)S(1)}, u32[]{:S(2)}, u32[]{:S(2)}) %collective-permute-start.5) | collective-permute-done | bytes 65568 | tf_op jit(solution)/shard_map/ppermute | solution.py:478
  30.5 4.2 %collective-permute-done.4.refs_5_ = bf16[2,64,256]{2,1,0:T(8,128)(2,1)S(1)} collective-permute-done((bf16[2,64,256]{2,1,0:T(8,128)(2,1)}, bf16[2,64,256]{2,1,0:T(8,128)(2,1)S(1)}, u32[]{:S(2)}, u32[]{:S(2)}) %collective-permute-start.4) | collective-permute-done | bytes 65568 | tf_op jit(solution)/shard_map/ppermute | solution.py:478
  34.7 0.6 copy-done.32
  35.4 1.0 copy-done.6
  36.3 1.3 plan.1
  37.6 1.0 slice.22
  38.6 1.0 slice.23
  39.6 1.6 %collective-permute-start.11 = (bf16[1,64,2048]{2,1,0:T(8,128)(2,1)S(1)}, bf16[1,64,2048]{2,1,0:T(8,128)(2,1)S(1)}, u32[]{:S(2)}, u32[]{:S(2)}) collective-permute-start(bf16[1,64,2048]{2,1,0:T(8,128)(2,1)S(1)} %slice.23), channel_id=1, source_target_pairs={{0,8},{4,12},{8,0},{12,4},{16,24},{20,28},{24,16},{28,20},{1,9},{5... | collective-permute-start | bytes 786440 | tf_op jit(solution)/shard_map/ppermute | solution.py:445
  41.1 1.5 collective-permute-start.10
  42.7 0.7 convert_bitcast_fusion
  43.3 0.5 collective-permute-start.9
  43.8 0.8 constant_dynamic-update-slice_fusion.4
  44.7 0.8 constant_dynamic-update-slice_fusion.3
  45.5 2.3 %collective-permute-done.11.refs_7_ = bf16[1,64,2048]{2,1,0:T(8,128)(2,1)S(1)} collective-permute-done((bf16[1,64,2048]{2,1,0:T(8,128)(2,1)S(1)}, bf16[1,64,2048]{2,1,0:T(8,128)(2,1)S(1)}, u32[]{:S(2)}, u32[]{:S(2)}) %collective-permute-start.11) | collective-permute-done | bytes 262176 | tf_op jit(solution)/shard_map/ppermute | solution.py:445
  47.9 1.2 collective-permute-done.10.refs_6_
  49.1 0.9 constant_dynamic-update-slice_fusion.2
  50.0 0.8 constant_dynamic-update-slice_fusion.1
  51.0 0.7 copy-done.17
  52.0 9.6 %project.1 = (f32[256,128]{1,0:T(8,128)}, f32[256,128]{1,0:T(8,128)}, f32[256,128]{1,0:T(8,128)}, f32[256,128]{1,0:T(8,128)}) custom-call(s32[1]{0:T(128)} %bitcast.z, s32[16]{0:T(128)} %get-tuple-element.54.idx, s32[16]{0:T(128)} %count.5, bf16[2048,2048]{1,0:T(8,128)(2,1)} %x.7, bf16[2,64,2048]{2,1,0:T(8,128)(2,1)} %refs_0_.5, ...), custom_call_target="tpu_custom_call" | custom-call | bytes 1200000 | tf_op jit(solution)/shard_map/project/pallas_call | solution.py:104
  61.6 1.8 %collective-permute-done.6.refs_0_ = bf16[2048,256]{1,0:T(8,128)(2,1)S(1)} collective-permute-done((bf16[2048,256]{1,0:T(8,128)(2,1)}, bf16[2048,256]{1,0:T(8,128)(2,1)S(1)}, u32[]{:S(2)}, u32[]{:S(2)}) %collective-permute-start.6) | collective-permute-done | bytes 1048608 | tf_op jit(solution)/shard_map/ppermute | solution.py:441
  63.4 1.0 copy-done.5
  64.5 2.4 %collective-permute-start.19 = (bf16[528,256]{1,0:T(8,128)(2,1)}, bf16[528,256]{1,0:T(8,128)(2,1)S(1)}, u32[]{:S(2)}, u32[]{:S(2)}) collective-permute-start(bf16[528,256]{1,0:T(8,128)(2,1)} %get-tuple-element.69.refs_3_.refs_0_), channel_id=1, source_target_pairs={{0,24},{4,28},{8,16},{12,20},{16,8},{20,12},{24,0},{28,4},{1,25},{... | collective-permute-start | bytes 811016 | tf_op jit(solution)/shard_map/ppermute | solution.py:445
  66.9 0.5 collective-permute-start.17
  67.4 0.5 collective-permute-start.15
  68.0 7.1 %collective-permute-done.19.refs_9_.refs_6_ = bf16[528,256]{1,0:T(8,128)(2,1)S(1)} collective-permute-done((bf16[528,256]{1,0:T(8,128)(2,1)}, bf16[528,256]{1,0:T(8,128)(2,1)S(1)}, u32[]{:S(2)}, u32[]{:S(2)}) %collective-permute-start.19) | collective-permute-done | bytes 270368 | tf_op jit(solution)/shard_map/ppermute | solution.py:445
  75.1 3.9 %collective-permute-done.17.refs_7_.refs_4_ = bf16[528,256]{1,0:T(8,128)(2,1)S(1)} collective-permute-done((bf16[528,256]{1,0:T(8,128)(2,1)}, bf16[528,256]{1,0:T(8,128)(2,1)S(1)}, u32[]{:S(2)}, u32[]{:S(2)}) %collective-permute-start.17) | collective-permute-done | bytes 270368 | tf_op jit(solution)/shard_map/ppermute | solution.py:445
  79.0 0.4 collective-permute-start.16
  79.5 1.0 collective-permute-done.18.refs_8_.refs_5_
  80.5 0.4 collective-permute-done.16.refs_6_.refs_3_
  81.2 0.7 copy-done.14
  81.9 1.6 %told.1.refs_6_.asked = f32[8,128]{1,0:T(8,128)} custom-call(s32[1]{0:T(128)} %bitcast.1.me.first.origin, bf16[528,256]{1,0:T(8,128)(2,1)} %get-tuple-element.69.refs_3_.refs_0_, bf16[528,256]{1,0:T(8,128)(2,1)} %copy-done.11, bf16[528,256]{1,0:T(8,128)(2,1)} %copy-done.10, bf16[528,256]{1,0:T(8,128)(2,1)} %copy-done.14, bf16[528,256]{1,0:T(8,128)(2,1)} %copy-done.9, ...), custom_call_target="tpu_custom_call" | custom-call | bytes 300000 | tf_op jit(solution)/shard_map/told/pallas_call | solution.py:345
  83.5 6.0 %pulled_part.1.refs_5_.part = f32[2048,64]{1,0:T(8,128)} custom-call(s32[16]{0:T(128)} %get-tuple-element.54.idx, bf16[2048,256]{1,0:T(8,128)(2,1)} %x_hbm.1, bf16[2048,256]{1,0:T(8,128)(2,1)} %get-tuple-element.59.refs_1_.refs_11_, bf16[2048,256]{1,0:T(8,128)(2,1)} %get-tuple-element.68.refs_2_.refs_12_, ...), custom_call_target="tpu_custom_call" | custom-call | bytes 1500000 | tf_op jit(solution)/shard_map/pulled_part/pallas_call | solution.py:210
  89.5 1.2 collective-permute-done.21.refs_0_
  90.7 1.0 copy-done.4
  91.8 2.9 %collective-permute-start.23 = (f32[256,128]{1,0:T(8,128)}, f32[256,128]{1,0:T(8,128)S(1)}, u32[]{:S(2)}, u32[]{:S(2)}) collective-permute-start(f32[256,128]{1,0:T(8,128)} %get-tuple-element.78), channel_id=1, source_target_pairs={{0,2},{1,3},{2,0},{3,1},{4,6},{5,7},{6,4},{7,5},{8,10},{9,11},{10,... | collective-permute-start | bytes 393224 | tf_op jit(solution)/shard_map/ppermute | solution.py:512
  94.7 2.1 %collective-permute-start.24 = (f32[256,128]{1,0:T(8,128)}, f32[256,128]{1,0:T(8,128)S(1)}, u32[]{:S(2)}, u32[]{:S(2)}) collective-permute-start(f32[256,128]{1,0:T(8,128)} %get-tuple-element.79), channel_id=1, source_target_pairs={{0,3},{1,0},{2,1},{3,2},{4,7},{5,4},{6,5},{7,6},{8,11},{9,8},{10,9... | collective-permute-start | bytes 393224 | tf_op jit(solution)/shard_map/ppermute | solution.py:512
  96.8 10.1 %down_sums.1 = (bf16[8,64,2048]{2,1,0:T(8,128)(2,1)}, bf16[2048,64]{1,0:T(8,128)(2,1)}) custom-call(s32[16]{0:T(128)} %get-tuple-element.54.idx, s32[16]{0:T(128)} %get-tuple-element.56.owner, s32[16]{0:T(128)} %count.5, bf16[2048,2048]{1,0:T(8,128)(2,1)} %x.7, f32[2048,64]{1,0:T(8,128)} %pulled_part.1.refs_5_.part, ...), custom_call_target="tpu_custom_call" | custom-call | bytes 2100000 | tf_op jit(solution)/shard_map/down_sums/pallas_call | solution.py:261
  107.0 0.6 copy-done.25
  107.7 3.7 %all-to-all-start = ((bf16[8,64,2048]{2,1,0:T(8,128)(2,1)}), bf16[8,64,2048]{2,1,0:T(8,128)(2,1)S(1)}, u32[]{:S(2)}, u32[]{:S(2)}) async-start(bf16[8,64,2048]{2,1,0:T(8,128)(2,1)} %get-tuple-element.84), calls=%async_computation | async-start | bytes 4194304 | tf_op jit(solution)/shard_map/all_to_all | solution.py:516
  111.6 2.0 %collective-permute-start.27 = (bf16[256,128]{1,0:T(8,128)(2,1)S(1)}, bf16[256,128]{1,0:T(8,128)(2,1)S(1)}, u32[]{:S(2)}, u32[]{:S(2)}) collective-permute-start(bf16[256,128]{1,0:T(8,128)(2,1)S(1)} %add_convert_fusion.refs_14_.refs_0_), channel_id=1, source_target_pairs={{0,3},{1,0},{2,1},{3,2},{4,7},{5,4},{6,5},{7,6},{8,11},{9,8},{10,9... | collective-permute-start | bytes 196616 | tf_op jit(solution)/shard_map/ppermute | solution.py:512
  113.6 0.9 collective-permute-start.25
  114.5 19.1 %token_gradient.1.refs_1_ = bf16[2048,2048]{1,0:T(8,128)(2,1)} custom-call(s32[1]{0:T(128)} %bitcast.z, s32[16]{0:T(128)} %get-tuple-element.54.idx, s32[16]{0:T(128)} %count.5, bf16[1024,2048]{1,0:T(8,128)(2,1)} %get-tuple-element.55.weight, bf16[2048,64]{1,0:T(8,128)(2,1)} %get-tuple-element.74.pulled, bf16[2,64,2048]{2,1,0:T(8,128)(2,1)} %refs_0_.5, ...), custom_call_target="tpu_custom_call" | custom-call | bytes 4800000 | tf_op jit(solution)/shard_map/token_gradient/pallas_call | solution.py:313
  133.7 0.6 copy-done.34
  134.3 3.2 %up_sums.1 = (bf16[64,256]{1,0:T(8,128)(2,1)}, bf16[64,256]{1,0:T(8,128)(2,1)}, bf16[64,256]{1,0:T(8,128)(2,1)}, bf16[64,256]{1,0:T(8,128)(2,1)}, bf16[64,256]{1...) custom-call(s32[1]{0:T(128)} %bitcast.z, s32[1]{0:T(128)} %bitcast.1.me.first.origin, ...), custom_call_target="tpu_custom_call" | custom-call | bytes 600000 | tf_op jit(solution)/shard_map/up_sums/pallas_call | solution.py:160
  137.6 2.1 %collective-permute-start.29 = (bf16[64,256]{1,0:T(8,128)(2,1)}, bf16[64,256]{1,0:T(8,128)(2,1)S(1)}, u32[]{:S(2)}, u32[]{:S(2)}) collective-permute-start(bf16[64,256]{1,0:T(8,128)(2,1)} %get-tuple-element.87), channel_id=1, source_target_pairs={{0,8},{4,12},{8,0},{12,4},{16,24},{20,28},{24,16},{28,20},{1,9},{5... | collective-permute-start | bytes 98312 | tf_op jit(solution)/shard_map/ppermute | solution.py:445
  139.8 1.7 %collective-permute-start.31 = (bf16[64,256]{1,0:T(8,128)(2,1)}, bf16[64,256]{1,0:T(8,128)(2,1)S(1)}, u32[]{:S(2)}, u32[]{:S(2)}) collective-permute-start(bf16[64,256]{1,0:T(8,128)(2,1)} %get-tuple-element.89), channel_id=1, source_target_pairs={{0,16},{4,20},{8,24},{12,28},{16,0},{20,4},{24,8},{28,12},{1,17},{... | collective-permute-start | bytes 98312 | tf_op jit(solution)/shard_map/ppermute | solution.py:445
  141.5 2.6 %collective-permute-start.33 = (bf16[64,256]{1,0:T(8,128)(2,1)}, bf16[64,256]{1,0:T(8,128)(2,1)S(1)}, u32[]{:S(2)}, u32[]{:S(2)}) collective-permute-start(bf16[64,256]{1,0:T(8,128)(2,1)} %get-tuple-element.91), channel_id=1, source_target_pairs={{0,24},{4,28},{8,16},{12,20},{16,8},{20,12},{24,0},{28,4},{1,25},{... | collective-permute-start | bytes 98312 | tf_op jit(solution)/shard_map/ppermute | solution.py:445
  144.3 1.0 collective-permute-done.32.refs_5_
  145.2 1.4 collective-permute-done.33.refs_6_
  146.6 2.0 %collective-permute-done.34.refs_7_ = bf16[64,256]{1,0:T(8,128)(2,1)S(1)} collective-permute-done((bf16[64,256]{1,0:T(8,128)(2,1)}, bf16[64,256]{1,0:T(8,128)(2,1)S(1)}, u32[]{:S(2)}, u32[]{:S(2)}) %collective-permute-start.34) | collective-permute-done | bytes 32800 | tf_op jit(solution)/shard_map/ppermute | solution.py:445
  148.6 0.8 copy-done.1
  149.3 0.8 owned_each.1
  150.1 2.3 %owned.1 = f32[2,64,2048]{2,1,0:T(8,128)} custom-call(s32[1]{0:T(128)} %bitcast.1.me.first.origin, f32[8,128]{1,0:T(8,128)S(1)} %copy-done, bf16[8,64,2048]{2,1,0:T(8,128)(2,1)S(1)} %all-to-all-done.got), custom_call_target="tpu_custom_call" | custom-call | bytes 600000 | tf_op jit(solution)/shard_map/owned/pallas_call | solution.py:372
  (108 shorter events, 1.4 us)
Async XLA Ops:
  0.6 34.1 %collective-permute-start.2 = (bf16[2048,256]{1,0:T(8,128)(2,1)}, bf16[2048,256]{1,0:T(8,128)(2,1)S(1)}, u32[]{:S(2)}, u32[]{:S(2)}) collective-permute-start(bf16[2048,256]{1,0:T(8,128)(2,1)} %x_hbm.1), channel_id=1, source_target_pairs={{0,1},{1,2},{2,3},{3,0},{4,5},{5,6},{6,7},{7,4},{8,9},{9,10},{10,1... | collective-permute-start | bytes 3145736 | tf_op jit(solution)/shard_map/ppermute | solution.py:441
  3.7 13.6 %collective-permute-start.1 = (bf16[2,64,2048]{2,1,0:T(8,128)(2,1)}, bf16[2,64,2048]{2,1,0:T(8,128)(2,1)S(1)}, u32[]{:S(2)}, u32[]{:S(2)}) collective-permute-start(bf16[2,64,2048]{2,1,0:T(8,128)(2,1)} %refs_0_.5), channel_id=1, source_target_pairs={{0,16},{4,20},{8,24},{12,28},{16,0},{20,4},{24,8},{28,12},{1,17},{... | collective-permute-start | bytes 1572872 | tf_op jit(solution)/shard_map/ppermute | solution.py:445
  5.2 13.3 %collective-permute-start = (bf16[2,64,2048]{2,1,0:T(8,128)(2,1)}, bf16[2,64,2048]{2,1,0:T(8,128)(2,1)S(1)}, u32[]{:S(2)}, u32[]{:S(2)}) collective-permute-start(bf16[2,64,2048]{2,1,0:T(8,128)(2,1)} %refs_0_.5), channel_id=1, source_target_pairs={{0,8},{4,12},{8,0},{12,4},{16,24},{20,28},{24,16},{28,20},{1,9},{5... | collective-permute-start | bytes 1572872 | tf_op jit(solution)/shard_map/ppermute | solution.py:445
  13.2 13.9 %copy-start.15 = (bf16[2,64,2048]{2,1,0:T(8,128)(2,1)S(1)}, bf16[2,64,2048]{2,1,0:T(8,128)(2,1)}, u32[]{:S(2)}) copy-start(bf16[2,64,2048]{2,1,0:T(8,128)(2,1)} %refs_0_.5) | copy-start | bytes 1572868
  17.3 1.2 copy-start.2
  18.5 0.8 copy-start.3
  22.4 8.1 %collective-permute-start.5 = (bf16[2,64,256]{2,1,0:T(8,128)(2,1)}, bf16[2,64,256]{2,1,0:T(8,128)(2,1)S(1)}, u32[]{:S(2)}, u32[]{:S(2)}) collective-permute-start(bf16[2,64,256]{2,1,0:T(8,128)(2,1)} %late.1.refs_1_), channel_id=1, source_target_pairs={{0,3},{1,0},{2,1},{3,2},{4,7},{5,4},{6,5},{7,6},{8,11},{9,8},{10,9... | collective-permute-start | bytes 196616 | tf_op jit(solution)/shard_map/ppermute | solution.py:478
  24.9 9.8 %collective-permute-start.4 = (bf16[2,64,256]{2,1,0:T(8,128)(2,1)}, bf16[2,64,256]{2,1,0:T(8,128)(2,1)S(1)}, u32[]{:S(2)}, u32[]{:S(2)}) collective-permute-start(bf16[2,64,256]{2,1,0:T(8,128)(2,1)} %late.1.refs_1_), channel_id=1, source_target_pairs={{0,2},{1,3},{2,0},{3,1},{4,6},{5,7},{6,4},{7,5},{8,10},{9,11},{10,... | collective-permute-start | bytes 196616 | tf_op jit(solution)/shard_map/ppermute | solution.py:478
  25.5 9.2 %collective-permute-start.3 = (bf16[2,64,256]{2,1,0:T(8,128)(2,1)}, bf16[2,64,256]{2,1,0:T(8,128)(2,1)S(1)}, u32[]{:S(2)}, u32[]{:S(2)}) collective-permute-start(bf16[2,64,256]{2,1,0:T(8,128)(2,1)} %late.1.refs_1_), channel_id=1, source_target_pairs={{0,1},{1,2},{2,3},{3,0},{4,5},{5,6},{6,7},{7,4},{8,9},{9,10},{10,1... | collective-permute-start | bytes 196616 | tf_op jit(solution)/shard_map/ppermute | solution.py:478
  27.1 16.2 %collective-permute-start.7 = (bf16[2,64,2048]{2,1,0:T(8,128)(2,1)S(1)}, bf16[2,64,2048]{2,1,0:T(8,128)(2,1)S(1)}, u32[]{:S(2)}, u32[]{:S(2)}) collective-permute-start(bf16[2,64,2048]{2,1,0:T(8,128)(2,1)S(1)} %copy-done.15), channel_id=1, source_target_pairs={{0,4},{4,0},{8,12},{12,8},{16,20},{20,16},{24,28},{28,24},{1,5},{5... | collective-permute-start | bytes 1572872 | tf_op jit(solution)/shard_map/ppermute | solution.py:445
  30.5 4.2 %copy-start.31 = (bf16[2,64,256]{2,1,0:T(8,128)(2,1)}, bf16[2,64,256]{2,1,0:T(8,128)(2,1)S(1)}, u32[]{:S(2)}) copy-start(bf16[2,64,256]{2,1,0:T(8,128)(2,1)S(1)} %collective-permute-done.5.refs_6_) | copy-start | bytes 196612
  35.4 1.0 copy-start.6
  36.3 27.1 %collective-permute-start.6 = (bf16[2048,256]{1,0:T(8,128)(2,1)}, bf16[2048,256]{1,0:T(8,128)(2,1)S(1)}, u32[]{:S(2)}, u32[]{:S(2)}) collective-permute-start(bf16[2048,256]{1,0:T(8,128)(2,1)} %get-tuple-element.59.refs_1_.refs_11_), channel_id=1, source_target_pairs={{0,1},{1,2},{2,3},{3,0},{4,5},{5,6},{6,7},{7,4},{8,9},{9,10},{10,1... | collective-permute-start | bytes 3145736 | tf_op jit(solution)/shard_map/ppermute | solution.py:441
  39.6 8.3 %collective-permute-start.11 = (bf16[1,64,2048]{2,1,0:T(8,128)(2,1)S(1)}, bf16[1,64,2048]{2,1,0:T(8,128)(2,1)S(1)}, u32[]{:S(2)}, u32[]{:S(2)}) collective-permute-start(bf16[1,64,2048]{2,1,0:T(8,128)(2,1)S(1)} %slice.23), channel_id=1, source_target_pairs={{0,8},{4,12},{8,0},{12,4},{16,24},{20,28},{24,16},{28,20},{1,9},{5... | collective-permute-start | bytes 786440 | tf_op jit(solution)/shard_map/ppermute | solution.py:445
  41.1 7.9 %collective-permute-start.10 = (bf16[1,64,2048]{2,1,0:T(8,128)(2,1)S(1)}, bf16[1,64,2048]{2,1,0:T(8,128)(2,1)S(1)}, u32[]{:S(2)}, u32[]{:S(2)}) collective-permute-start(bf16[1,64,2048]{2,1,0:T(8,128)(2,1)S(1)} %slice.22), channel_id=1, source_target_pairs={{0,16},{4,20},{8,24},{12,28},{16,0},{20,4},{24,8},{28,12},{1,17},{... | collective-permute-start | bytes 786440 | tf_op jit(solution)/shard_map/ppermute | solution.py:445
  43.3 7.5 %collective-permute-start.8 = (bf16[2,64,2048]{2,1,0:T(8,128)(2,1)}, bf16[2,64,2048]{2,1,0:T(8,128)(2,1)S(1)}, u32[]{:S(2)}, u32[]{:S(2)}) collective-permute-start(bf16[2,64,2048]{2,1,0:T(8,128)(2,1)} %get-tuple-element.65.refs_2_), channel_id=1, source_target_pairs={{0,4},{4,0},{8,12},{12,8},{16,20},{20,16},{24,28},{28,24},{1,5},{5... | collective-permute-start | bytes 1572872 | tf_op jit(solution)/shard_map/ppermute | solution.py:445
  43.3 7.6 %copy-start.16 = (bf16[2,64,2048]{2,1,0:T(8,128)(2,1)}, bf16[2,64,2048]{2,1,0:T(8,128)(2,1)S(1)}, u32[]{:S(2)}) copy-start(bf16[2,64,2048]{2,1,0:T(8,128)(2,1)S(1)} %collective-permute-done.7.refs_1_) | copy-start | bytes 1572868
  43.3 7.5 %collective-permute-start.9 = (bf16[2,64,2048]{2,1,0:T(8,128)(2,1)}, bf16[2,64,2048]{2,1,0:T(8,128)(2,1)S(1)}, u32[]{:S(2)}, u32[]{:S(2)}) collective-permute-start(bf16[2,64,2048]{2,1,0:T(8,128)(2,1)} %get-tuple-element.66.refs_4_), channel_id=1, source_target_pairs={{0,4},{4,0},{8,12},{12,8},{16,20},{20,16},{24,28},{28,24},{1,5},{5... | collective-permute-start | bytes 1572872 | tf_op jit(solution)/shard_map/ppermute | solution.py:445
  47.9 3.1 %copy-start.20 = (bf16[1,64,2048]{2,1,0:T(8,128)(2,1)}, bf16[1,64,2048]{2,1,0:T(8,128)(2,1)S(1)}, u32[]{:S(2)}) copy-start(bf16[1,64,2048]{2,1,0:T(8,128)(2,1)S(1)} %collective-permute-done.11.refs_7_) | copy-start | bytes 786436
  47.9 3.0 %collective-permute-start.13 = (bf16[1,64,2048]{2,1,0:T(8,128)(2,1)S(1)}, bf16[1,64,2048]{2,1,0:T(8,128)(2,1)S(1)}, u32[]{:S(2)}, u32[]{:S(2)}) collective-permute-start(bf16[1,64,2048]{2,1,0:T(8,128)(2,1)S(1)} %collective-permute-done.11.refs_7_), channel_id=1, source_target_pairs={{0,4},{4,0},{8,12},{12,8},{16,20},{20,16},{24,28},{28,24},{1,5},{5... | collective-permute-start | bytes 786440 | tf_op jit(solution)/shard_map/ppermute | solution.py:445
  49.1 1.9 %copy-start.21 = (bf16[1,64,2048]{2,1,0:T(8,128)(2,1)}, bf16[1,64,2048]{2,1,0:T(8,128)(2,1)S(1)}, u32[]{:S(2)}) copy-start(bf16[1,64,2048]{2,1,0:T(8,128)(2,1)S(1)} %collective-permute-done.10.refs_6_) | copy-start | bytes 786436
  49.1 1.8 %collective-permute-start.12 = (bf16[1,64,2048]{2,1,0:T(8,128)(2,1)S(1)}, bf16[1,64,2048]{2,1,0:T(8,128)(2,1)S(1)}, u32[]{:S(2)}, u32[]{:S(2)}) collective-permute-start(bf16[1,64,2048]{2,1,0:T(8,128)(2,1)S(1)} %collective-permute-done.10.refs_6_), channel_id=1, source_target_pairs={{0,4},{4,0},{8,12},{12,8},{16,20},{20,16},{24,28},{28,24},{1,5},{5... | collective-permute-start | bytes 786440 | tf_op jit(solution)/shard_map/ppermute | solution.py:445
  50.8 10.8 %copy-start.7 = (bf16[528,256]{1,0:T(8,128)(2,1)}, bf16[528,256]{1,0:T(8,128)(2,1)S(1)}, u32[]{:S(2)}) copy-start(bf16[528,256]{1,0:T(8,128)(2,1)S(1)} %constant_dynamic-update-slice_fusion.refs_1_) | copy-start | bytes 811012
  50.9 0.8 copy-start.17
  50.9 1.0 copy-start.18
  50.9 1.0 copy-start.22
  50.9 1.1 copy-start.23
  63.4 1.0 copy-start.5
  64.5 26.2 %collective-permute-start.21 = (bf16[2048,256]{1,0:T(8,128)(2,1)}, bf16[2048,256]{1,0:T(8,128)(2,1)S(1)}, u32[]{:S(2)}, u32[]{:S(2)}) collective-permute-start(bf16[2048,256]{1,0:T(8,128)(2,1)} %get-tuple-element.68.refs_2_.refs_12_), channel_id=1, source_target_pairs={{0,1},{1,2},{2,3},{3,0},{4,5},{5,6},{6,7},{7,4},{8,9},{9,10},{10,1... | collective-permute-start | bytes 3145736 | tf_op jit(solution)/shard_map/ppermute | solution.py:441
  64.5 10.6 %collective-permute-start.19 = (bf16[528,256]{1,0:T(8,128)(2,1)}, bf16[528,256]{1,0:T(8,128)(2,1)S(1)}, u32[]{:S(2)}, u32[]{:S(2)}) collective-permute-start(bf16[528,256]{1,0:T(8,128)(2,1)} %get-tuple-element.69.refs_3_.refs_0_), channel_id=1, source_target_pairs={{0,24},{4,28},{8,16},{12,20},{16,8},{20,12},{24,0},{28,4},{1,25},{... | collective-permute-start | bytes 811016 | tf_op jit(solution)/shard_map/ppermute | solution.py:445
  66.9 12.0 %collective-permute-start.17 = (bf16[528,256]{1,0:T(8,128)(2,1)}, bf16[528,256]{1,0:T(8,128)(2,1)S(1)}, u32[]{:S(2)}, u32[]{:S(2)}) collective-permute-start(bf16[528,256]{1,0:T(8,128)(2,1)} %get-tuple-element.69.refs_3_.refs_0_), channel_id=1, source_target_pairs={{0,16},{4,20},{8,24},{12,28},{16,0},{20,4},{24,8},{28,12},{1,17},{... | collective-permute-start | bytes 811016 | tf_op jit(solution)/shard_map/ppermute | solution.py:445
  67.4 11.6 %collective-permute-start.15 = (bf16[528,256]{1,0:T(8,128)(2,1)}, bf16[528,256]{1,0:T(8,128)(2,1)S(1)}, u32[]{:S(2)}, u32[]{:S(2)}) collective-permute-start(bf16[528,256]{1,0:T(8,128)(2,1)} %get-tuple-element.69.refs_3_.refs_0_), channel_id=1, source_target_pairs={{0,8},{4,12},{8,0},{12,4},{16,24},{20,28},{24,16},{28,20},{1,9},{5... | collective-permute-start | bytes 811016 | tf_op jit(solution)/shard_map/ppermute | solution.py:445
  68.0 11.5 %collective-permute-start.14 = (bf16[528,256]{1,0:T(8,128)(2,1)}, bf16[528,256]{1,0:T(8,128)(2,1)S(1)}, u32[]{:S(2)}, u32[]{:S(2)}) collective-permute-start(bf16[528,256]{1,0:T(8,128)(2,1)} %get-tuple-element.69.refs_3_.refs_0_), channel_id=1, source_target_pairs={{0,4},{4,0},{8,12},{12,8},{16,20},{20,16},{24,28},{28,24},{1,5},{5... | collective-permute-start | bytes 811016 | tf_op jit(solution)/shard_map/ppermute | solution.py:445
  75.1 5.8 %copy-start.8 = (bf16[528,256]{1,0:T(8,128)(2,1)}, bf16[528,256]{1,0:T(8,128)(2,1)S(1)}, u32[]{:S(2)}) copy-start(bf16[528,256]{1,0:T(8,128)(2,1)S(1)} %collective-permute-done.19.refs_9_.refs_6_) | copy-start | bytes 811012
  75.1 4.4 %collective-permute-start.20 = (bf16[528,256]{1,0:T(8,128)(2,1)S(1)}, bf16[528,256]{1,0:T(8,128)(2,1)S(1)}, u32[]{:S(2)}, u32[]{:S(2)}) collective-permute-start(bf16[528,256]{1,0:T(8,128)(2,1)S(1)} %collective-permute-done.19.refs_9_.refs_6_), channel_id=1, source_target_pairs={{0,4},{4,0},{8,12},{12,8},{16,20},{20,16},{24,28},{28,24},{1,5},{5... | collective-permute-start | bytes 811016 | tf_op jit(solution)/shard_map/ppermute | solution.py:445
  78.9 1.9 %copy-start.9 = (bf16[528,256]{1,0:T(8,128)(2,1)}, bf16[528,256]{1,0:T(8,128)(2,1)S(1)}, u32[]{:S(2)}) copy-start(bf16[528,256]{1,0:T(8,128)(2,1)S(1)} %collective-permute-done.17.refs_7_.refs_4_) | copy-start | bytes 811012
  78.9 1.5 %collective-permute-start.18 = (bf16[528,256]{1,0:T(8,128)(2,1)S(1)}, bf16[528,256]{1,0:T(8,128)(2,1)S(1)}, u32[]{:S(2)}, u32[]{:S(2)}) collective-permute-start(bf16[528,256]{1,0:T(8,128)(2,1)S(1)} %collective-permute-done.17.refs_7_.refs_4_), channel_id=1, source_target_pairs={{0,4},{4,0},{8,12},{12,8},{16,20},{20,16},{24,28},{28,24},{1,5},{5... | collective-permute-start | bytes 811016 | tf_op jit(solution)/shard_map/ppermute | solution.py:445
  79.0 1.8 %copy-start.10 = (bf16[528,256]{1,0:T(8,128)(2,1)}, bf16[528,256]{1,0:T(8,128)(2,1)S(1)}, u32[]{:S(2)}) copy-start(bf16[528,256]{1,0:T(8,128)(2,1)S(1)} %collective-permute-done.15.refs_5_.refs_2_) | copy-start | bytes 811012
  79.0 1.8 %collective-permute-start.16 = (bf16[528,256]{1,0:T(8,128)(2,1)S(1)}, bf16[528,256]{1,0:T(8,128)(2,1)S(1)}, u32[]{:S(2)}, u32[]{:S(2)}) collective-permute-start(bf16[528,256]{1,0:T(8,128)(2,1)S(1)} %collective-permute-done.15.refs_5_.refs_2_), channel_id=1, source_target_pairs={{0,4},{4,0},{8,12},{12,8},{16,20},{20,16},{24,28},{28,24},{1,5},{5... | collective-permute-start | bytes 811016 | tf_op jit(solution)/shard_map/ppermute | solution.py:445
  79.5 1.4 copy-start.11
  79.5 1.4 copy-start.12
  81.2 0.7 copy-start.14
  90.7 1.0 copy-start.4
  91.8 15.2 %collective-permute-start.22 = (f32[256,128]{1,0:T(8,128)}, f32[256,128]{1,0:T(8,128)S(1)}, u32[]{:S(2)}, u32[]{:S(2)}) collective-permute-start(f32[256,128]{1,0:T(8,128)} %get-tuple-element.77), channel_id=1, source_target_pairs={{0,1},{1,2},{2,3},{3,0},{4,5},{5,6},{6,7},{7,4},{8,9},{9,10},{10,1... | collective-permute-start | bytes 393224 | tf_op jit(solution)/shard_map/ppermute | solution.py:512
  91.8 15.2 %collective-permute-start.23 = (f32[256,128]{1,0:T(8,128)}, f32[256,128]{1,0:T(8,128)S(1)}, u32[]{:S(2)}, u32[]{:S(2)}) collective-permute-start(f32[256,128]{1,0:T(8,128)} %get-tuple-element.78), channel_id=1, source_target_pairs={{0,2},{1,3},{2,0},{3,1},{4,6},{5,7},{6,4},{7,5},{8,10},{9,11},{10,... | collective-permute-start | bytes 393224 | tf_op jit(solution)/shard_map/ppermute | solution.py:512
  94.7 12.3 %collective-permute-start.24 = (f32[256,128]{1,0:T(8,128)}, f32[256,128]{1,0:T(8,128)S(1)}, u32[]{:S(2)}, u32[]{:S(2)}) collective-permute-start(f32[256,128]{1,0:T(8,128)} %get-tuple-element.79), channel_id=1, source_target_pairs={{0,3},{1,0},{2,1},{3,2},{4,7},{5,4},{6,5},{7,6},{8,11},{9,8},{10,9... | collective-permute-start | bytes 393224 | tf_op jit(solution)/shard_map/ppermute | solution.py:512
  107.7 3.8 %copy-start.19 = (f32[256,128]{1,0:T(8,128)S(1)}, f32[256,128]{1,0:T(8,128)}, u32[]{:S(2)}) copy-start(f32[256,128]{1,0:T(8,128)} %get-tuple-element.80) | copy-start | bytes 393220
  107.7 3.8 %copy-start.26 = (f32[256,128]{1,0:T(8,128)S(1)}, f32[256,128]{1,0:T(8,128)}, u32[]{:S(2)}) copy-start(f32[256,128]{1,0:T(8,128)} %get-tuple-element.81) | copy-start | bytes 393220
  107.7 3.8 %copy-start.28 = (f32[256,128]{1,0:T(8,128)S(1)}, f32[256,128]{1,0:T(8,128)}, u32[]{:S(2)}) copy-start(f32[256,128]{1,0:T(8,128)} %get-tuple-element.82) | copy-start | bytes 393220
  107.7 3.8 %copy-start.30 = (f32[256,128]{1,0:T(8,128)S(1)}, f32[256,128]{1,0:T(8,128)}, u32[]{:S(2)}) copy-start(f32[256,128]{1,0:T(8,128)} %get-tuple-element.83) | copy-start | bytes 393220
  107.7 42.4 %all-to-all-start = ((bf16[8,64,2048]{2,1,0:T(8,128)(2,1)}), bf16[8,64,2048]{2,1,0:T(8,128)(2,1)S(1)}, u32[]{:S(2)}, u32[]{:S(2)}) async-start(bf16[8,64,2048]{2,1,0:T(8,128)(2,1)} %get-tuple-element.84), calls=%async_computation | async-start | bytes 4194304 | tf_op jit(solution)/shard_map/all_to_all | solution.py:516
  111.6 3.0 %copy-start.24 = (bf16[256,128]{1,0:T(8,128)(2,1)}, bf16[256,128]{1,0:T(8,128)(2,1)S(1)}, u32[]{:S(2)}) copy-start(bf16[256,128]{1,0:T(8,128)(2,1)S(1)} %add_convert_fusion.refs_14_.refs_0_) | copy-start | bytes 196612
  111.6 22.1 %collective-permute-start.27 = (bf16[256,128]{1,0:T(8,128)(2,1)S(1)}, bf16[256,128]{1,0:T(8,128)(2,1)S(1)}, u32[]{:S(2)}, u32[]{:S(2)}) collective-permute-start(bf16[256,128]{1,0:T(8,128)(2,1)S(1)} %add_convert_fusion.refs_14_.refs_0_), channel_id=1, source_target_pairs={{0,3},{1,0},{2,1},{3,2},{4,7},{5,4},{6,5},{7,6},{8,11},{9,8},{10,9... | collective-permute-start | bytes 196616 | tf_op jit(solution)/shard_map/ppermute | solution.py:512
  113.6 20.0 %collective-permute-start.26 = (bf16[256,128]{1,0:T(8,128)(2,1)S(1)}, bf16[256,128]{1,0:T(8,128)(2,1)S(1)}, u32[]{:S(2)}, u32[]{:S(2)}) collective-permute-start(bf16[256,128]{1,0:T(8,128)(2,1)S(1)} %add_convert_fusion.refs_14_.refs_0_), channel_id=1, source_target_pairs={{0,2},{1,3},{2,0},{3,1},{4,6},{5,7},{6,4},{7,5},{8,10},{9,11},{10,... | collective-permute-start | bytes 196616 | tf_op jit(solution)/shard_map/ppermute | solution.py:512
  113.6 20.1 %collective-permute-start.25 = (bf16[256,128]{1,0:T(8,128)(2,1)S(1)}, bf16[256,128]{1,0:T(8,128)(2,1)S(1)}, u32[]{:S(2)}, u32[]{:S(2)}) collective-permute-start(bf16[256,128]{1,0:T(8,128)(2,1)S(1)} %add_convert_fusion.refs_14_.refs_0_), channel_id=1, source_target_pairs={{0,1},{1,2},{2,3},{3,0},{4,5},{5,6},{6,7},{7,4},{8,9},{9,10},{10,1... | collective-permute-start | bytes 196616 | tf_op jit(solution)/shard_map/ppermute | solution.py:512
  133.6 15.0 %copy-start = (f32[8,128]{1,0:T(8,128)S(1)}, f32[8,128]{1,0:T(8,128)}, u32[]{:S(2)}) copy-start(f32[8,128]{1,0:T(8,128)} %told.1.refs_6_.asked) | copy-start | bytes 12292
  137.6 4.0 %collective-permute-start.28 = (bf16[64,256]{1,0:T(8,128)(2,1)}, bf16[64,256]{1,0:T(8,128)(2,1)S(1)}, u32[]{:S(2)}, u32[]{:S(2)}) collective-permute-start(bf16[64,256]{1,0:T(8,128)(2,1)} %get-tuple-element.86), channel_id=1, source_target_pairs={{0,4},{4,0},{8,12},{12,8},{16,20},{20,16},{24,28},{28,24},{1,5},{5... | collective-permute-start | bytes 98312 | tf_op jit(solution)/shard_map/ppermute | solution.py:445
  137.6 6.5 %collective-permute-start.29 = (bf16[64,256]{1,0:T(8,128)(2,1)}, bf16[64,256]{1,0:T(8,128)(2,1)S(1)}, u32[]{:S(2)}, u32[]{:S(2)}) collective-permute-start(bf16[64,256]{1,0:T(8,128)(2,1)} %get-tuple-element.87), channel_id=1, source_target_pairs={{0,8},{4,12},{8,0},{12,4},{16,24},{20,28},{24,16},{28,20},{1,9},{5... | collective-permute-start | bytes 98312 | tf_op jit(solution)/shard_map/ppermute | solution.py:445
  139.7 4.5 %collective-permute-start.30 = (bf16[64,256]{1,0:T(8,128)(2,1)}, bf16[64,256]{1,0:T(8,128)(2,1)S(1)}, u32[]{:S(2)}, u32[]{:S(2)}) collective-permute-start(bf16[64,256]{1,0:T(8,128)(2,1)} %get-tuple-element.88), channel_id=1, source_target_pairs={{0,12},{4,8},{8,4},{12,0},{16,28},{20,24},{24,20},{28,16},{1,13},{... | collective-permute-start | bytes 98312 | tf_op jit(solution)/shard_map/ppermute | solution.py:445
  139.8 4.5 %collective-permute-start.31 = (bf16[64,256]{1,0:T(8,128)(2,1)}, bf16[64,256]{1,0:T(8,128)(2,1)S(1)}, u32[]{:S(2)}, u32[]{:S(2)}) collective-permute-start(bf16[64,256]{1,0:T(8,128)(2,1)} %get-tuple-element.89), channel_id=1, source_target_pairs={{0,16},{4,20},{8,24},{12,28},{16,0},{20,4},{24,8},{28,12},{1,17},{... | collective-permute-start | bytes 98312 | tf_op jit(solution)/shard_map/ppermute | solution.py:445
  141.5 3.7 %collective-permute-start.32 = (bf16[64,256]{1,0:T(8,128)(2,1)}, bf16[64,256]{1,0:T(8,128)(2,1)S(1)}, u32[]{:S(2)}, u32[]{:S(2)}) collective-permute-start(bf16[64,256]{1,0:T(8,128)(2,1)} %get-tuple-element.90), channel_id=1, source_target_pairs={{0,20},{4,16},{8,28},{12,24},{16,4},{20,0},{24,12},{28,8},{1,21},{... | collective-permute-start | bytes 98312 | tf_op jit(solution)/shard_map/ppermute | solution.py:445
  141.5 5.0 %collective-permute-start.33 = (bf16[64,256]{1,0:T(8,128)(2,1)}, bf16[64,256]{1,0:T(8,128)(2,1)S(1)}, u32[]{:S(2)}, u32[]{:S(2)}) collective-permute-start(bf16[64,256]{1,0:T(8,128)(2,1)} %get-tuple-element.91), channel_id=1, source_target_pairs={{0,24},{4,28},{8,16},{12,20},{16,8},{20,12},{24,0},{28,4},{1,25},{... | collective-permute-start | bytes 98312 | tf_op jit(solution)/shard_map/ppermute | solution.py:445
  144.1 4.5 %collective-permute-start.34 = (bf16[64,256]{1,0:T(8,128)(2,1)}, bf16[64,256]{1,0:T(8,128)(2,1)S(1)}, u32[]{:S(2)}, u32[]{:S(2)}) collective-permute-start(bf16[64,256]{1,0:T(8,128)(2,1)} %get-tuple-element.92), channel_id=1, source_target_pairs={{0,28},{4,24},{8,20},{12,16},{16,12},{20,8},{24,4},{28,0},{1,29},{... | collective-permute-start | bytes 98312 | tf_op jit(solution)/shard_map/ppermute | solution.py:445
  148.6 0.8 copy-start.1
  (9 other events, 5.9 us)

commit v6 on v5

--- a/solution.py
+++ b/solution.py
@@ -382,7 +382,7 @@
 
 
 def owned_each_kernel(asked, *refs):
-    got, out = refs[:-1], refs[-1]
+    got, out = refs[:-2], refs[-1]
     for e in range(out.shape[0]):
         total = jnp.zeros(got[0].shape, jnp.float32)
         for k, term in enumerate(got):
@@ -390,16 +390,16 @@
         out[e] = total
 
 
-def owned_each(asked, got, held):
+def owned_each(asked, got, held, after):
     return pl.pallas_call(
         owned_each_kernel,
         out_shape=jax.ShapeDtypeStruct((held, *got[0].shape), jnp.float32),
-        in_specs=[VMEM] * (1 + len(got)),
+        in_specs=[VMEM] * (1 + len(got)) + [HBM],
         out_specs=VMEM,
-        compiler_params=params(16),
+        compiler_params=params(),
         cost_estimate=cost(2),
         name="owned_each",
-    )(asked, *got)
+    )(asked, *got, after)
 
 
 def gate_kernel(*refs):
@@ -527,7 +527,7 @@
         got = lax.all_to_all(jnp.stack(got), "dp", 0, 0, tiled=True)
         got = [got[k] for k in range(n_dp)]
     down_grad = owned(origin, asked, down_got, held, 16)
-    return token_gradient, down_grad, owned_each(asked, got, held)
+    return token_gradient, down_grad, owned_each(asked, got, held, down_grad)
 
 
 def solution(mesh):

time: 153 us -> 152 us (level)
  waiting for transfers between devices: 36.3 us -> 34 us
    ppermute x23, waiting for transfers between devices: 25.7 us -> 23.3 us  [flip(): return lax.ppermute(x, 'dp', [(i, i ^ by) for i in range(n)])]
    unnamed x79 -> x91, local copies, waits for them, and re-layouts: 18.6 us -> 18.5 us
  transfers between devices with their start and end apart: 36 -> 36, of which waited for: 16 -> 14; matrix products, arithmetic and copies ran while one was open for 8% -> 8% of each run, Pallas kernels for 36% -> 37%
where the time goes in v6:
time: 152 us; the launch traced here: 151 us
  Pallas kernels  57.9 us (38%)
  starting transfers between devices  36.7 us (24%)
  waiting for transfers between devices  34 us (22%)
  local copies, waits for them, and re-layouts  20.4 us (13%)
    ppermute x23, waiting for transfers between devices, flip(): return lax.ppermute(x, 'dp', [(i, i ^ by) for i in range(n)])  23.3 us
    pallas_call x1, Pallas kernels, token_gradients(): pl.pallas_call(functools.partial(token_kernel, n, per, rows, len(maps)),...  19.1 us
    unnamed x91, local copies, waits for them, and re-layouts  18.5 us
    ppermute x23, starting transfers between devices, flip(): return lax.ppermute(x, 'dp', [(i, i ^ by) for i in range(n)])  17.2 us
    pallas_call x1, Pallas kernels, down_sums(): pl.pallas_call(functools.partial(down_sums_kernel, n, per, rows, ranks, s...  10.1 us
    pallas_call x1, Pallas kernels, project(): pl.pallas_call(functools.partial(project_kernel, n, per, rows, len(maps))...  9.57 us
    ppermute x6, starting transfers between devices, on_device(): lax.ppermute(x, 'tsp', [(i, (i + s) % n) for i in range(n)])  8.03 us
    ppermute x3, waiting for transfers between devices, on_device(): lax.ppermute(ups, 'tsp', [(i, (i + s) % n) for i in range(n)])  7.61 us
  transfers between devices with their start and end apart: 36, of which 14 were waited for; matrix products, arithmetic and copies ran while one was open for 8% of the time, Pallas kernels for 37%

profile of v6, /device:TPU:0, one launch (start us, length us, event | category | flops | bytes accessed | tf_op | source)
XLA Modules:
  0.0 150.9 jit_solution(387947147160023987)
XLA Ops:
  0.6 3.1 %collective-permute-start.2 = (bf16[2048,256]{1,0:T(8,128)(2,1)}, bf16[2048,256]{1,0:T(8,128)(2,1)S(1)}, u32[]{:S(2)}, u32[]{:S(2)}) collective-permute-start(bf16[2048,256]{1,0:T(8,128)(2,1)} %x_hbm.1), channel_id=1, source_target_pairs={{0,1},{1,2},{2,3},{3,0},{4,5},{5,6},{6,7},{7,4},{8,9},{9,10},{10,1... | collective-permute-start | bytes 3145736 | tf_op jit(solution)/shard_map/ppermute | solution.py:441
  3.7 1.5 %collective-permute-start.1 = (bf16[2,64,2048]{2,1,0:T(8,128)(2,1)}, bf16[2,64,2048]{2,1,0:T(8,128)(2,1)S(1)}, u32[]{:S(2)}, u32[]{:S(2)}) collective-permute-start(bf16[2,64,2048]{2,1,0:T(8,128)(2,1)} %refs_0_.5), channel_id=1, source_target_pairs={{0,16},{4,20},{8,24},{12,28},{16,0},{20,4},{24,8},{28,12},{1,17},{... | collective-permute-start | bytes 1572872 | tf_op jit(solution)/shard_map/ppermute | solution.py:445
  5.2 1.5 collective-permute-start
  6.7 6.5 %copy.34 = bf16[2048,1024]{0,1:T(8,128)(2,1)} copy(bf16[2048,1024]{1,0:T(8,128)(2,1)} %param.12) | data formatting | bytes 8388608 | tf_op args[2]
  13.2 4.1 %collective-permute-done.1.refs_1_ = bf16[2,64,2048]{2,1,0:T(8,128)(2,1)S(1)} collective-permute-done((bf16[2,64,2048]{2,1,0:T(8,128)(2,1)}, bf16[2,64,2048]{2,1,0:T(8,128)(2,1)S(1)}, u32[]{:S(2)}, u32[]{:S(2)}) %collective-permute-start.1) | collective-permute-done | bytes 524320 | tf_op jit(solution)/shard_map/ppermute | solution.py:445
  17.3 1.2 collective-permute-done.refs_0_
  18.5 0.8 copy-done.2
  19.3 3.1 %late.1.refs_1_ = bf16[2,64,256]{2,1,0:T(8,128)(2,1)} custom-call(bf16[2,64,256]{2,1,0:T(8,128)(2,1)} %x.5, bf16[2,64,2048]{2,1,0:T(8,128)(2,1)} %get-tuple-element.57.refs_0_.refs_2_, bf16[2,64,2048]{2,1,0:T(8,128)(2,1)} %get-tuple-element.58.refs_1_.refs_3_), custom_call_target="tpu_custom_call" | custom-call | tf_op jit(solution)/shard_map/late/pallas_call | solution.py:428
  22.4 2.4 %collective-permute-start.5 = (bf16[2,64,256]{2,1,0:T(8,128)(2,1)}, bf16[2,64,256]{2,1,0:T(8,128)(2,1)S(1)}, u32[]{:S(2)}, u32[]{:S(2)}) collective-permute-start(bf16[2,64,256]{2,1,0:T(8,128)(2,1)} %late.1.refs_1_), channel_id=1, source_target_pairs={{0,3},{1,0},{2,1},{3,2},{4,7},{5,4},{6,5},{7,6},{8,11},{9,8},{10,9... | collective-permute-start | bytes 196616 | tf_op jit(solution)/shard_map/ppermute | solution.py:478
  24.9 0.7 collective-permute-start.4
  25.5 1.6 %collective-permute-start.3 = (bf16[2,64,256]{2,1,0:T(8,128)(2,1)}, bf16[2,64,256]{2,1,0:T(8,128)(2,1)S(1)}, u32[]{:S(2)}, u32[]{:S(2)}) collective-permute-start(bf16[2,64,256]{2,1,0:T(8,128)(2,1)} %late.1.refs_1_), channel_id=1, source_target_pairs={{0,1},{1,2},{2,3},{3,0},{4,5},{5,6},{6,7},{7,4},{8,9},{9,10},{10,1... | collective-permute-start | bytes 196616 | tf_op jit(solution)/shard_map/ppermute | solution.py:478
  27.1 3.4 %collective-permute-done.5.refs_6_ = bf16[2,64,256]{2,1,0:T(8,128)(2,1)S(1)} collective-permute-done((bf16[2,64,256]{2,1,0:T(8,128)(2,1)}, bf16[2,64,256]{2,1,0:T(8,128)(2,1)S(1)}, u32[]{:S(2)}, u32[]{:S(2)}) %collective-permute-start.5) | collective-permute-done | bytes 65568 | tf_op jit(solution)/shard_map/ppermute | solution.py:478
  30.5 4.2 %collective-permute-done.4.refs_5_ = bf16[2,64,256]{2,1,0:T(8,128)(2,1)S(1)} collective-permute-done((bf16[2,64,256]{2,1,0:T(8,128)(2,1)}, bf16[2,64,256]{2,1,0:T(8,128)(2,1)S(1)}, u32[]{:S(2)}, u32[]{:S(2)}) %collective-permute-start.4) | collective-permute-done | bytes 65568 | tf_op jit(solution)/shard_map/ppermute | solution.py:478
  34.7 0.6 copy-done.31
  35.4 1.0 copy-done.5
  36.3 1.3 plan.1
  37.6 1.0 slice.22
  38.6 1.0 slice.23
  39.6 1.6 %collective-permute-start.11 = (bf16[1,64,2048]{2,1,0:T(8,128)(2,1)S(1)}, bf16[1,64,2048]{2,1,0:T(8,128)(2,1)S(1)}, u32[]{:S(2)}, u32[]{:S(2)}) collective-permute-start(bf16[1,64,2048]{2,1,0:T(8,128)(2,1)S(1)} %slice.23), channel_id=1, source_target_pairs={{0,8},{4,12},{8,0},{12,4},{16,24},{20,28},{24,16},{28,20},{1,9},{5... | collective-permute-start | bytes 786440 | tf_op jit(solution)/shard_map/ppermute | solution.py:445
  41.1 1.5 %collective-permute-start.10 = (bf16[1,64,2048]{2,1,0:T(8,128)(2,1)S(1)}, bf16[1,64,2048]{2,1,0:T(8,128)(2,1)S(1)}, u32[]{:S(2)}, u32[]{:S(2)}) collective-permute-start(bf16[1,64,2048]{2,1,0:T(8,128)(2,1)S(1)} %slice.22), channel_id=1, source_target_pairs={{0,16},{4,20},{8,24},{12,28},{16,0},{20,4},{24,8},{28,12},{1,17},{... | collective-permute-start | bytes 786440 | tf_op jit(solution)/shard_map/ppermute | solution.py:445
  42.7 0.7 convert_bitcast_fusion
  43.3 0.5 collective-permute-start.9
  43.8 0.8 constant_dynamic-update-slice_fusion.4
  44.7 0.8 constant_dynamic-update-slice_fusion.3
  45.5 2.3 %collective-permute-done.11.refs_7_ = bf16[1,64,2048]{2,1,0:T(8,128)(2,1)S(1)} collective-permute-done((bf16[1,64,2048]{2,1,0:T(8,128)(2,1)S(1)}, bf16[1,64,2048]{2,1,0:T(8,128)(2,1)S(1)}, u32[]{:S(2)}, u32[]{:S(2)}) %collective-permute-start.11) | collective-permute-done | bytes 262176 | tf_op jit(solution)/shard_map/ppermute | solution.py:445
  47.9 1.2 collective-permute-done.10.refs_6_
  49.1 0.9 constant_dynamic-update-slice_fusion.2
  50.0 0.8 constant_dynamic-update-slice_fusion.1
  51.0 0.8 copy-done.16
  51.7 0.1 copy-done.17
  52.0 9.6 %project.1 = (f32[256,128]{1,0:T(8,128)}, f32[256,128]{1,0:T(8,128)}, f32[256,128]{1,0:T(8,128)}, f32[256,128]{1,0:T(8,128)}) custom-call(s32[1]{0:T(128)} %bitcast.z, s32[16]{0:T(128)} %get-tuple-element.54.idx, s32[16]{0:T(128)} %count.5, bf16[2048,2048]{1,0:T(8,128)(2,1)} %x.7, bf16[2,64,2048]{2,1,0:T(8,128)(2,1)} %refs_0_.5, ...), custom_call_target="tpu_custom_call" | custom-call | bytes 1200000 | tf_op jit(solution)/shard_map/project/pallas_call | solution.py:104
  61.6 1.8 %collective-permute-done.6.refs_0_ = bf16[2048,256]{1,0:T(8,128)(2,1)S(1)} collective-permute-done((bf16[2048,256]{1,0:T(8,128)(2,1)}, bf16[2048,256]{1,0:T(8,128)(2,1)S(1)}, u32[]{:S(2)}, u32[]{:S(2)}) %collective-permute-start.6) | collective-permute-done | bytes 1048608 | tf_op jit(solution)/shard_map/ppermute | solution.py:441
  63.4 1.0 copy-done.4
  64.5 2.4 %collective-permute-start.19 = (bf16[528,256]{1,0:T(8,128)(2,1)}, bf16[528,256]{1,0:T(8,128)(2,1)S(1)}, u32[]{:S(2)}, u32[]{:S(2)}) collective-permute-start(bf16[528,256]{1,0:T(8,128)(2,1)} %get-tuple-element.69.refs_3_.refs_0_), channel_id=1, source_target_pairs={{0,24},{4,28},{8,16},{12,20},{16,8},{20,12},{24,0},{28,4},{1,25},{... | collective-permute-start | bytes 811016 | tf_op jit(solution)/shard_map/ppermute | solution.py:445
  66.9 0.5 collective-permute-start.17
  67.4 0.5 collective-permute-start.15
  68.0 7.1 %collective-permute-done.19.refs_9_.refs_6_ = bf16[528,256]{1,0:T(8,128)(2,1)S(1)} collective-permute-done((bf16[528,256]{1,0:T(8,128)(2,1)}, bf16[528,256]{1,0:T(8,128)(2,1)S(1)}, u32[]{:S(2)}, u32[]{:S(2)}) %collective-permute-start.19) | collective-permute-done | bytes 270368 | tf_op jit(solution)/shard_map/ppermute | solution.py:445
  75.1 3.9 %collective-permute-done.17.refs_7_.refs_4_ = bf16[528,256]{1,0:T(8,128)(2,1)S(1)} collective-permute-done((bf16[528,256]{1,0:T(8,128)(2,1)}, bf16[528,256]{1,0:T(8,128)(2,1)S(1)}, u32[]{:S(2)}, u32[]{:S(2)}) %collective-permute-start.17) | collective-permute-done | bytes 270368 | tf_op jit(solution)/shard_map/ppermute | solution.py:445
  79.0 0.4 collective-permute-start.16
  79.5 1.0 collective-permute-done.18.refs_8_.refs_5_
  80.5 0.4 collective-permute-done.16.refs_6_.refs_3_
  80.9 0.3 copy-done.12
  81.2 0.7 copy-done.13
  81.9 1.6 %told.1.refs_6_.asked = f32[8,128]{1,0:T(8,128)} custom-call(s32[1]{0:T(128)} %bitcast.1.me.first.origin, bf16[528,256]{1,0:T(8,128)(2,1)} %get-tuple-element.69.refs_3_.refs_0_, bf16[528,256]{1,0:T(8,128)(2,1)} %copy-done.10, bf16[528,256]{1,0:T(8,128)(2,1)} %copy-done.9, bf16[528,256]{1,0:T(8,128)(2,1)} %copy-done.13, bf16[528,256]{1,0:T(8,128)(2,1)} %copy-done.8, ...), custom_call_target="tpu_custom_call" | custom-call | bytes 300000 | tf_op jit(solution)/shard_map/told/pallas_call | solution.py:345
  83.5 6.0 %pulled_part.1.refs_5_.part = f32[2048,64]{1,0:T(8,128)} custom-call(s32[16]{0:T(128)} %get-tuple-element.54.idx, bf16[2048,256]{1,0:T(8,128)(2,1)} %x_hbm.1, bf16[2048,256]{1,0:T(8,128)(2,1)} %get-tuple-element.59.refs_1_.refs_11_, bf16[2048,256]{1,0:T(8,128)(2,1)} %get-tuple-element.68.refs_2_.refs_12_, ...), custom_call_target="tpu_custom_call" | custom-call | bytes 1500000 | tf_op jit(solution)/shard_map/pulled_part/pallas_call | solution.py:210
  89.5 1.2 collective-permute-done.21.refs_0_
  90.7 1.1 copy-done.3
  91.8 2.9 %collective-permute-start.23 = (f32[256,128]{1,0:T(8,128)}, f32[256,128]{1,0:T(8,128)S(1)}, u32[]{:S(2)}, u32[]{:S(2)}) collective-permute-start(f32[256,128]{1,0:T(8,128)} %get-tuple-element.78), channel_id=1, source_target_pairs={{0,2},{1,3},{2,0},{3,1},{4,6},{5,7},{6,4},{7,5},{8,10},{9,11},{10,... | collective-permute-start | bytes 393224 | tf_op jit(solution)/shard_map/ppermute | solution.py:512
  94.7 2.1 %collective-permute-start.24 = (f32[256,128]{1,0:T(8,128)}, f32[256,128]{1,0:T(8,128)S(1)}, u32[]{:S(2)}, u32[]{:S(2)}) collective-permute-start(f32[256,128]{1,0:T(8,128)} %get-tuple-element.79), channel_id=1, source_target_pairs={{0,3},{1,0},{2,1},{3,2},{4,7},{5,4},{6,5},{7,6},{8,11},{9,8},{10,9... | collective-permute-start | bytes 393224 | tf_op jit(solution)/shard_map/ppermute | solution.py:512
  96.8 10.1 %down_sums.1 = (bf16[8,64,2048]{2,1,0:T(8,128)(2,1)}, bf16[2048,64]{1,0:T(8,128)(2,1)}) custom-call(s32[16]{0:T(128)} %get-tuple-element.54.idx, s32[16]{0:T(128)} %get-tuple-element.56.owner, s32[16]{0:T(128)} %count.5, bf16[2048,2048]{1,0:T(8,128)(2,1)} %x.7, f32[2048,64]{1,0:T(8,128)} %pulled_part.1.refs_5_.part, ...), custom_call_target="tpu_custom_call" | custom-call | bytes 2100000 | tf_op jit(solution)/shard_map/down_sums/pallas_call | solution.py:261
  107.0 0.6 copy-done.24
  107.7 3.7 %all-to-all-start = ((bf16[8,64,2048]{2,1,0:T(8,128)(2,1)}), bf16[8,64,2048]{2,1,0:T(8,128)(2,1)S(1)}, u32[]{:S(2)}, u32[]{:S(2)}) async-start(bf16[8,64,2048]{2,1,0:T(8,128)(2,1)} %get-tuple-element.84), calls=%async_computation | async-start | bytes 4194304 | tf_op jit(solution)/shard_map/all_to_all | solution.py:516
  111.6 2.0 %collective-permute-start.27 = (bf16[256,128]{1,0:T(8,128)(2,1)S(1)}, bf16[256,128]{1,0:T(8,128)(2,1)S(1)}, u32[]{:S(2)}, u32[]{:S(2)}) collective-permute-start(bf16[256,128]{1,0:T(8,128)(2,1)S(1)} %add_convert_fusion.refs_14_.refs_0_), channel_id=1, source_target_pairs={{0,3},{1,0},{2,1},{3,2},{4,7},{5,4},{6,5},{7,6},{8,11},{9,8},{10,9... | collective-permute-start | bytes 196616 | tf_op jit(solution)/shard_map/ppermute | solution.py:512
  113.6 1.0 collective-permute-start.25
  114.6 19.1 %token_gradient.1.refs_1_ = bf16[2048,2048]{1,0:T(8,128)(2,1)} custom-call(s32[1]{0:T(128)} %bitcast.z, s32[16]{0:T(128)} %get-tuple-element.54.idx, s32[16]{0:T(128)} %count.5, bf16[1024,2048]{1,0:T(8,128)(2,1)} %get-tuple-element.55.weight, bf16[2048,64]{1,0:T(8,128)(2,1)} %get-tuple-element.74.pulled, bf16[2,64,2048]{2,1,0:T(8,128)(2,1)} %refs_0_.5, ...), custom_call_target="tpu_custom_call" | custom-call | bytes 4800000 | tf_op jit(solution)/shard_map/token_gradient/pallas_call | solution.py:313
  133.7 0.6 copy-done.33
  134.4 3.2 %up_sums.1 = (bf16[64,256]{1,0:T(8,128)(2,1)}, bf16[64,256]{1,0:T(8,128)(2,1)}, bf16[64,256]{1,0:T(8,128)(2,1)}, bf16[64,256]{1,0:T(8,128)(2,1)}, bf16[64,256]{1...) custom-call(s32[1]{0:T(128)} %bitcast.z, s32[1]{0:T(128)} %bitcast.1.me.first.origin, ...), custom_call_target="tpu_custom_call" | custom-call | bytes 600000 | tf_op jit(solution)/shard_map/up_sums/pallas_call | solution.py:160
  137.7 2.1 %collective-permute-start.29 = (bf16[64,256]{1,0:T(8,128)(2,1)}, bf16[64,256]{1,0:T(8,128)(2,1)S(1)}, u32[]{:S(2)}, u32[]{:S(2)}) collective-permute-start(bf16[64,256]{1,0:T(8,128)(2,1)} %get-tuple-element.87), channel_id=1, source_target_pairs={{0,8},{4,12},{8,0},{12,4},{16,24},{20,28},{24,16},{28,20},{1,9},{5... | collective-permute-start | bytes 98312 | tf_op jit(solution)/shard_map/ppermute | solution.py:445
  139.8 1.7 %collective-permute-start.31 = (bf16[64,256]{1,0:T(8,128)(2,1)}, bf16[64,256]{1,0:T(8,128)(2,1)S(1)}, u32[]{:S(2)}, u32[]{:S(2)}) collective-permute-start(bf16[64,256]{1,0:T(8,128)(2,1)} %get-tuple-element.89), channel_id=1, source_target_pairs={{0,16},{4,20},{8,24},{12,28},{16,0},{20,4},{24,8},{28,12},{1,17},{... | collective-permute-start | bytes 98312 | tf_op jit(solution)/shard_map/ppermute | solution.py:445
  141.6 2.6 %collective-permute-start.33 = (bf16[64,256]{1,0:T(8,128)(2,1)}, bf16[64,256]{1,0:T(8,128)(2,1)S(1)}, u32[]{:S(2)}, u32[]{:S(2)}) collective-permute-start(bf16[64,256]{1,0:T(8,128)(2,1)} %get-tuple-element.91), channel_id=1, source_target_pairs={{0,24},{4,28},{8,16},{12,20},{16,8},{20,12},{24,0},{28,4},{1,25},{... | collective-permute-start | bytes 98312 | tf_op jit(solution)/shard_map/ppermute | solution.py:445
  144.3 2.3 %owned.1.refs_8_ = f32[2,64,2048]{2,1,0:T(8,128)} custom-call(s32[1]{0:T(128)} %bitcast.1.me.first.origin, f32[8,128]{1,0:T(8,128)S(1)} %copy-done, bf16[8,64,2048]{2,1,0:T(8,128)(2,1)S(1)} %all-to-all-done.got), custom_call_target="tpu_custom_call" | custom-call | bytes 600000 | tf_op jit(solution)/shard_map/owned/pallas_call | solution.py:372
  146.7 1.9 %collective-permute-done.34.refs_7_ = bf16[64,256]{1,0:T(8,128)(2,1)S(1)} collective-permute-done((bf16[64,256]{1,0:T(8,128)(2,1)}, bf16[64,256]{1,0:T(8,128)(2,1)S(1)}, u32[]{:S(2)}, u32[]{:S(2)}) %collective-permute-start.34) | collective-permute-done | bytes 32800 | tf_op jit(solution)/shard_map/ppermute | solution.py:445
  148.6 0.6 copy-done.42
  149.2 1.7 %owned_each.1 = f32[2,64,256]{2,1,0:T(8,128)} custom-call(f32[8,128]{1,0:T(8,128)} %told.1.refs_6_.asked, bf16[64,256]{1,0:T(8,128)(2,1)} %get-tuple-element.85.refs_0_, bf16[64,256]{1,0:T(8,128)(2,1)} %copy-done.36, bf16[64,256]{1,0:T(8,128)(2,1)} %copy-done.37, bf16[64,256]{1,0:T(8,128)(2,1)} %copy-done.38, bf16[64,256]{1,0:T(8,128)(2,1)} %copy-done.39, ...), custom_call_target="tpu_custom_call" | custom-call | bytes 600000 | tf_op jit(solution)/shard_map/owned_each/pallas_call | solution.py:394
  (120 shorter events, 1.0 us)
Async XLA Ops:
  0.6 34.1 %collective-permute-start.2 = (bf16[2048,256]{1,0:T(8,128)(2,1)}, bf16[2048,256]{1,0:T(8,128)(2,1)S(1)}, u32[]{:S(2)}, u32[]{:S(2)}) collective-permute-start(bf16[2048,256]{1,0:T(8,128)(2,1)} %x_hbm.1), channel_id=1, source_target_pairs={{0,1},{1,2},{2,3},{3,0},{4,5},{5,6},{6,7},{7,4},{8,9},{9,10},{10,1... | collective-permute-start | bytes 3145736 | tf_op jit(solution)/shard_map/ppermute | solution.py:441
  3.7 13.6 %collective-permute-start.1 = (bf16[2,64,2048]{2,1,0:T(8,128)(2,1)}, bf16[2,64,2048]{2,1,0:T(8,128)(2,1)S(1)}, u32[]{:S(2)}, u32[]{:S(2)}) collective-permute-start(bf16[2,64,2048]{2,1,0:T(8,128)(2,1)} %refs_0_.5), channel_id=1, source_target_pairs={{0,16},{4,20},{8,24},{12,28},{16,0},{20,4},{24,8},{28,12},{1,17},{... | collective-permute-start | bytes 1572872 | tf_op jit(solution)/shard_map/ppermute | solution.py:445
  5.2 13.3 %collective-permute-start = (bf16[2,64,2048]{2,1,0:T(8,128)(2,1)}, bf16[2,64,2048]{2,1,0:T(8,128)(2,1)S(1)}, u32[]{:S(2)}, u32[]{:S(2)}) collective-permute-start(bf16[2,64,2048]{2,1,0:T(8,128)(2,1)} %refs_0_.5), channel_id=1, source_target_pairs={{0,8},{4,12},{8,0},{12,4},{16,24},{20,28},{24,16},{28,20},{1,9},{5... | collective-permute-start | bytes 1572872 | tf_op jit(solution)/shard_map/ppermute | solution.py:445
  13.2 13.9 %copy-start.14 = (bf16[2,64,2048]{2,1,0:T(8,128)(2,1)S(1)}, bf16[2,64,2048]{2,1,0:T(8,128)(2,1)}, u32[]{:S(2)}) copy-start(bf16[2,64,2048]{2,1,0:T(8,128)(2,1)} %refs_0_.5) | copy-start | bytes 1572868
  17.3 1.2 copy-start.1
  22.4 8.1 %collective-permute-start.5 = (bf16[2,64,256]{2,1,0:T(8,128)(2,1)}, bf16[2,64,256]{2,1,0:T(8,128)(2,1)S(1)}, u32[]{:S(2)}, u32[]{:S(2)}) collective-permute-start(bf16[2,64,256]{2,1,0:T(8,128)(2,1)} %late.1.refs_1_), channel_id=1, source_target_pairs={{0,3},{1,0},{2,1},{3,2},{4,7},{5,4},{6,5},{7,6},{8,11},{9,8},{10,9... | collective-permute-start | bytes 196616 | tf_op jit(solution)/shard_map/ppermute | solution.py:478
  24.9 9.8 %collective-permute-start.4 = (bf16[2,64,256]{2,1,0:T(8,128)(2,1)}, bf16[2,64,256]{2,1,0:T(8,128)(2,1)S(1)}, u32[]{:S(2)}, u32[]{:S(2)}) collective-permute-start(bf16[2,64,256]{2,1,0:T(8,128)(2,1)} %late.1.refs_1_), channel_id=1, source_target_pairs={{0,2},{1,3},{2,0},{3,1},{4,6},{5,7},{6,4},{7,5},{8,10},{9,11},{10,... | collective-permute-start | bytes 196616 | tf_op jit(solution)/shard_map/ppermute | solution.py:478
  25.5 9.2 %collective-permute-start.3 = (bf16[2,64,256]{2,1,0:T(8,128)(2,1)}, bf16[2,64,256]{2,1,0:T(8,128)(2,1)S(1)}, u32[]{:S(2)}, u32[]{:S(2)}) collective-permute-start(bf16[2,64,256]{2,1,0:T(8,128)(2,1)} %late.1.refs_1_), channel_id=1, source_target_pairs={{0,1},{1,2},{2,3},{3,0},{4,5},{5,6},{6,7},{7,4},{8,9},{9,10},{10,1... | collective-permute-start | bytes 196616 | tf_op jit(solution)/shard_map/ppermute | solution.py:478
  27.1 16.2 %collective-permute-start.7 = (bf16[2,64,2048]{2,1,0:T(8,128)(2,1)S(1)}, bf16[2,64,2048]{2,1,0:T(8,128)(2,1)S(1)}, u32[]{:S(2)}, u32[]{:S(2)}) collective-permute-start(bf16[2,64,2048]{2,1,0:T(8,128)(2,1)S(1)} %copy-done.14), channel_id=1, source_target_pairs={{0,4},{4,0},{8,12},{12,8},{16,20},{20,16},{24,28},{28,24},{1,5},{5... | collective-permute-start | bytes 1572872 | tf_op jit(solution)/shard_map/ppermute | solution.py:445
  30.5 4.2 %copy-start.30 = (bf16[2,64,256]{2,1,0:T(8,128)(2,1)}, bf16[2,64,256]{2,1,0:T(8,128)(2,1)S(1)}, u32[]{:S(2)}) copy-start(bf16[2,64,256]{2,1,0:T(8,128)(2,1)S(1)} %collective-permute-done.5.refs_6_) | copy-start | bytes 196612
  36.3 27.1 %collective-permute-start.6 = (bf16[2048,256]{1,0:T(8,128)(2,1)}, bf16[2048,256]{1,0:T(8,128)(2,1)S(1)}, u32[]{:S(2)}, u32[]{:S(2)}) collective-permute-start(bf16[2048,256]{1,0:T(8,128)(2,1)} %get-tuple-element.59.refs_1_.refs_11_), channel_id=1, source_target_pairs={{0,1},{1,2},{2,3},{3,0},{4,5},{5,6},{6,7},{7,4},{8,9},{9,10},{10,1... | collective-permute-start | bytes 3145736 | tf_op jit(solution)/shard_map/ppermute | solution.py:441
  39.6 8.3 %collective-permute-start.11 = (bf16[1,64,2048]{2,1,0:T(8,128)(2,1)S(1)}, bf16[1,64,2048]{2,1,0:T(8,128)(2,1)S(1)}, u32[]{:S(2)}, u32[]{:S(2)}) collective-permute-start(bf16[1,64,2048]{2,1,0:T(8,128)(2,1)S(1)} %slice.23), channel_id=1, source_target_pairs={{0,8},{4,12},{8,0},{12,4},{16,24},{20,28},{24,16},{28,20},{1,9},{5... | collective-permute-start | bytes 786440 | tf_op jit(solution)/shard_map/ppermute | solution.py:445
  41.1 7.9 %collective-permute-start.10 = (bf16[1,64,2048]{2,1,0:T(8,128)(2,1)S(1)}, bf16[1,64,2048]{2,1,0:T(8,128)(2,1)S(1)}, u32[]{:S(2)}, u32[]{:S(2)}) collective-permute-start(bf16[1,64,2048]{2,1,0:T(8,128)(2,1)S(1)} %slice.22), channel_id=1, source_target_pairs={{0,16},{4,20},{8,24},{12,28},{16,0},{20,4},{24,8},{28,12},{1,17},{... | collective-permute-start | bytes 786440 | tf_op jit(solution)/shard_map/ppermute | solution.py:445
  43.3 7.5 %collective-permute-start.8 = (bf16[2,64,2048]{2,1,0:T(8,128)(2,1)}, bf16[2,64,2048]{2,1,0:T(8,128)(2,1)S(1)}, u32[]{:S(2)}, u32[]{:S(2)}) collective-permute-start(bf16[2,64,2048]{2,1,0:T(8,128)(2,1)} %get-tuple-element.65.refs_2_), channel_id=1, source_target_pairs={{0,4},{4,0},{8,12},{12,8},{16,20},{20,16},{24,28},{28,24},{1,5},{5... | collective-permute-start | bytes 1572872 | tf_op jit(solution)/shard_map/ppermute | solution.py:445
  43.3 7.6 %copy-start.15 = (bf16[2,64,2048]{2,1,0:T(8,128)(2,1)}, bf16[2,64,2048]{2,1,0:T(8,128)(2,1)S(1)}, u32[]{:S(2)}) copy-start(bf16[2,64,2048]{2,1,0:T(8,128)(2,1)S(1)} %collective-permute-done.7.refs_1_) | copy-start | bytes 1572868
  43.3 7.5 %collective-permute-start.9 = (bf16[2,64,2048]{2,1,0:T(8,128)(2,1)}, bf16[2,64,2048]{2,1,0:T(8,128)(2,1)S(1)}, u32[]{:S(2)}, u32[]{:S(2)}) collective-permute-start(bf16[2,64,2048]{2,1,0:T(8,128)(2,1)} %get-tuple-element.66.refs_4_), channel_id=1, source_target_pairs={{0,4},{4,0},{8,12},{12,8},{16,20},{20,16},{24,28},{28,24},{1,5},{5... | collective-permute-start | bytes 1572872 | tf_op jit(solution)/shard_map/ppermute | solution.py:445
  47.9 3.1 %copy-start.19 = (bf16[1,64,2048]{2,1,0:T(8,128)(2,1)}, bf16[1,64,2048]{2,1,0:T(8,128)(2,1)S(1)}, u32[]{:S(2)}) copy-start(bf16[1,64,2048]{2,1,0:T(8,128)(2,1)S(1)} %collective-permute-done.11.refs_7_) | copy-start | bytes 786436
  47.9 3.0 %collective-permute-start.13 = (bf16[1,64,2048]{2,1,0:T(8,128)(2,1)S(1)}, bf16[1,64,2048]{2,1,0:T(8,128)(2,1)S(1)}, u32[]{:S(2)}, u32[]{:S(2)}) collective-permute-start(bf16[1,64,2048]{2,1,0:T(8,128)(2,1)S(1)} %collective-permute-done.11.refs_7_), channel_id=1, source_target_pairs={{0,4},{4,0},{8,12},{12,8},{16,20},{20,16},{24,28},{28,24},{1,5},{5... | collective-permute-start | bytes 786440 | tf_op jit(solution)/shard_map/ppermute | solution.py:445
  49.1 1.9 %copy-start.20 = (bf16[1,64,2048]{2,1,0:T(8,128)(2,1)}, bf16[1,64,2048]{2,1,0:T(8,128)(2,1)S(1)}, u32[]{:S(2)}) copy-start(bf16[1,64,2048]{2,1,0:T(8,128)(2,1)S(1)} %collective-permute-done.10.refs_6_) | copy-start | bytes 786436
  49.1 1.8 %collective-permute-start.12 = (bf16[1,64,2048]{2,1,0:T(8,128)(2,1)S(1)}, bf16[1,64,2048]{2,1,0:T(8,128)(2,1)S(1)}, u32[]{:S(2)}, u32[]{:S(2)}) collective-permute-start(bf16[1,64,2048]{2,1,0:T(8,128)(2,1)S(1)} %collective-permute-done.10.refs_6_), channel_id=1, source_target_pairs={{0,4},{4,0},{8,12},{12,8},{16,20},{20,16},{24,28},{28,24},{1,5},{5... | collective-permute-start | bytes 786440 | tf_op jit(solution)/shard_map/ppermute | solution.py:445
  50.8 10.8 %copy-start.6 = (bf16[528,256]{1,0:T(8,128)(2,1)}, bf16[528,256]{1,0:T(8,128)(2,1)S(1)}, u32[]{:S(2)}) copy-start(bf16[528,256]{1,0:T(8,128)(2,1)S(1)} %constant_dynamic-update-slice_fusion.refs_1_) | copy-start | bytes 811012
  50.9 1.1 copy-start.21
  50.9 1.1 copy-start.22
  63.4 1.0 copy-start.4
  64.5 26.2 %collective-permute-start.21 = (bf16[2048,256]{1,0:T(8,128)(2,1)}, bf16[2048,256]{1,0:T(8,128)(2,1)S(1)}, u32[]{:S(2)}, u32[]{:S(2)}) collective-permute-start(bf16[2048,256]{1,0:T(8,128)(2,1)} %get-tuple-element.68.refs_2_.refs_12_), channel_id=1, source_target_pairs={{0,1},{1,2},{2,3},{3,0},{4,5},{5,6},{6,7},{7,4},{8,9},{9,10},{10,1... | collective-permute-start | bytes 3145736 | tf_op jit(solution)/shard_map/ppermute | solution.py:441
  64.5 10.6 %collective-permute-start.19 = (bf16[528,256]{1,0:T(8,128)(2,1)}, bf16[528,256]{1,0:T(8,128)(2,1)S(1)}, u32[]{:S(2)}, u32[]{:S(2)}) collective-permute-start(bf16[528,256]{1,0:T(8,128)(2,1)} %get-tuple-element.69.refs_3_.refs_0_), channel_id=1, source_target_pairs={{0,24},{4,28},{8,16},{12,20},{16,8},{20,12},{24,0},{28,4},{1,25},{... | collective-permute-start | bytes 811016 | tf_op jit(solution)/shard_map/ppermute | solution.py:445
  66.9 12.0 %collective-permute-start.17 = (bf16[528,256]{1,0:T(8,128)(2,1)}, bf16[528,256]{1,0:T(8,128)(2,1)S(1)}, u32[]{:S(2)}, u32[]{:S(2)}) collective-permute-start(bf16[528,256]{1,0:T(8,128)(2,1)} %get-tuple-element.69.refs_3_.refs_0_), channel_id=1, source_target_pairs={{0,16},{4,20},{8,24},{12,28},{16,0},{20,4},{24,8},{28,12},{1,17},{... | collective-permute-start | bytes 811016 | tf_op jit(solution)/shard_map/ppermute | solution.py:445
  67.4 11.6 %collective-permute-start.15 = (bf16[528,256]{1,0:T(8,128)(2,1)}, bf16[528,256]{1,0:T(8,128)(2,1)S(1)}, u32[]{:S(2)}, u32[]{:S(2)}) collective-permute-start(bf16[528,256]{1,0:T(8,128)(2,1)} %get-tuple-element.69.refs_3_.refs_0_), channel_id=1, source_target_pairs={{0,8},{4,12},{8,0},{12,4},{16,24},{20,28},{24,16},{28,20},{1,9},{5... | collective-permute-start | bytes 811016 | tf_op jit(solution)/shard_map/ppermute | solution.py:445
  68.0 11.5 %collective-permute-start.14 = (bf16[528,256]{1,0:T(8,128)(2,1)}, bf16[528,256]{1,0:T(8,128)(2,1)S(1)}, u32[]{:S(2)}, u32[]{:S(2)}) collective-permute-start(bf16[528,256]{1,0:T(8,128)(2,1)} %get-tuple-element.69.refs_3_.refs_0_), channel_id=1, source_target_pairs={{0,4},{4,0},{8,12},{12,8},{16,20},{20,16},{24,28},{28,24},{1,5},{5... | collective-permute-start | bytes 811016 | tf_op jit(solution)/shard_map/ppermute | solution.py:445
  75.1 5.8 %copy-start.7 = (bf16[528,256]{1,0:T(8,128)(2,1)}, bf16[528,256]{1,0:T(8,128)(2,1)S(1)}, u32[]{:S(2)}) copy-start(bf16[528,256]{1,0:T(8,128)(2,1)S(1)} %collective-permute-done.19.refs_9_.refs_6_) | copy-start | bytes 811012
  75.1 4.4 %collective-permute-start.20 = (bf16[528,256]{1,0:T(8,128)(2,1)S(1)}, bf16[528,256]{1,0:T(8,128)(2,1)S(1)}, u32[]{:S(2)}, u32[]{:S(2)}) collective-permute-start(bf16[528,256]{1,0:T(8,128)(2,1)S(1)} %collective-permute-done.19.refs_9_.refs_6_), channel_id=1, source_target_pairs={{0,4},{4,0},{8,12},{12,8},{16,20},{20,16},{24,28},{28,24},{1,5},{5... | collective-permute-start | bytes 811016 | tf_op jit(solution)/shard_map/ppermute | solution.py:445
  78.9 1.9 %copy-start.8 = (bf16[528,256]{1,0:T(8,128)(2,1)}, bf16[528,256]{1,0:T(8,128)(2,1)S(1)}, u32[]{:S(2)}) copy-start(bf16[528,256]{1,0:T(8,128)(2,1)S(1)} %collective-permute-done.17.refs_7_.refs_4_) | copy-start | bytes 811012
  78.9 1.5 %collective-permute-start.18 = (bf16[528,256]{1,0:T(8,128)(2,1)S(1)}, bf16[528,256]{1,0:T(8,128)(2,1)S(1)}, u32[]{:S(2)}, u32[]{:S(2)}) collective-permute-start(bf16[528,256]{1,0:T(8,128)(2,1)S(1)} %collective-permute-done.17.refs_7_.refs_4_), channel_id=1, source_target_pairs={{0,4},{4,0},{8,12},{12,8},{16,20},{20,16},{24,28},{28,24},{1,5},{5... | collective-permute-start | bytes 811016 | tf_op jit(solution)/shard_map/ppermute | solution.py:445
  79.0 1.8 %copy-start.9 = (bf16[528,256]{1,0:T(8,128)(2,1)}, bf16[528,256]{1,0:T(8,128)(2,1)S(1)}, u32[]{:S(2)}) copy-start(bf16[528,256]{1,0:T(8,128)(2,1)S(1)} %collective-permute-done.15.refs_5_.refs_2_) | copy-start | bytes 811012
  79.0 1.8 %collective-permute-start.16 = (bf16[528,256]{1,0:T(8,128)(2,1)S(1)}, bf16[528,256]{1,0:T(8,128)(2,1)S(1)}, u32[]{:S(2)}, u32[]{:S(2)}) collective-permute-start(bf16[528,256]{1,0:T(8,128)(2,1)S(1)} %collective-permute-done.15.refs_5_.refs_2_), channel_id=1, source_target_pairs={{0,4},{4,0},{8,12},{12,8},{16,20},{20,16},{24,28},{28,24},{1,5},{5... | collective-permute-start | bytes 811016 | tf_op jit(solution)/shard_map/ppermute | solution.py:445
  79.5 1.4 copy-start.10
  79.5 1.4 copy-start.11
  90.7 1.1 copy-start.3
  91.8 15.2 %collective-permute-start.22 = (f32[256,128]{1,0:T(8,128)}, f32[256,128]{1,0:T(8,128)S(1)}, u32[]{:S(2)}, u32[]{:S(2)}) collective-permute-start(f32[256,128]{1,0:T(8,128)} %get-tuple-element.77), channel_id=1, source_target_pairs={{0,1},{1,2},{2,3},{3,0},{4,5},{5,6},{6,7},{7,4},{8,9},{9,10},{10,1... | collective-permute-start | bytes 393224 | tf_op jit(solution)/shard_map/ppermute | solution.py:512
  91.8 15.2 %collective-permute-start.23 = (f32[256,128]{1,0:T(8,128)}, f32[256,128]{1,0:T(8,128)S(1)}, u32[]{:S(2)}, u32[]{:S(2)}) collective-permute-start(f32[256,128]{1,0:T(8,128)} %get-tuple-element.78), channel_id=1, source_target_pairs={{0,2},{1,3},{2,0},{3,1},{4,6},{5,7},{6,4},{7,5},{8,10},{9,11},{10,... | collective-permute-start | bytes 393224 | tf_op jit(solution)/shard_map/ppermute | solution.py:512
  94.7 12.3 %collective-permute-start.24 = (f32[256,128]{1,0:T(8,128)}, f32[256,128]{1,0:T(8,128)S(1)}, u32[]{:S(2)}, u32[]{:S(2)}) collective-permute-start(f32[256,128]{1,0:T(8,128)} %get-tuple-element.79), channel_id=1, source_target_pairs={{0,3},{1,0},{2,1},{3,2},{4,7},{5,4},{6,5},{7,6},{8,11},{9,8},{10,9... | collective-permute-start | bytes 393224 | tf_op jit(solution)/shard_map/ppermute | solution.py:512
  107.7 3.8 %copy-start.18 = (f32[256,128]{1,0:T(8,128)S(1)}, f32[256,128]{1,0:T(8,128)}, u32[]{:S(2)}) copy-start(f32[256,128]{1,0:T(8,128)} %get-tuple-element.80) | copy-start | bytes 393220
  107.7 3.8 %copy-start.25 = (f32[256,128]{1,0:T(8,128)S(1)}, f32[256,128]{1,0:T(8,128)}, u32[]{:S(2)}) copy-start(f32[256,128]{1,0:T(8,128)} %get-tuple-element.81) | copy-start | bytes 393220
  107.7 3.8 %copy-start.27 = (f32[256,128]{1,0:T(8,128)S(1)}, f32[256,128]{1,0:T(8,128)}, u32[]{:S(2)}) copy-start(f32[256,128]{1,0:T(8,128)} %get-tuple-element.82) | copy-start | bytes 393220
  107.7 3.8 %copy-start.29 = (f32[256,128]{1,0:T(8,128)S(1)}, f32[256,128]{1,0:T(8,128)}, u32[]{:S(2)}) copy-start(f32[256,128]{1,0:T(8,128)} %get-tuple-element.83) | copy-start | bytes 393220
  107.7 36.6 %all-to-all-start = ((bf16[8,64,2048]{2,1,0:T(8,128)(2,1)}), bf16[8,64,2048]{2,1,0:T(8,128)(2,1)S(1)}, u32[]{:S(2)}, u32[]{:S(2)}) async-start(bf16[8,64,2048]{2,1,0:T(8,128)(2,1)} %get-tuple-element.84), calls=%async_computation | async-start | bytes 4194304 | tf_op jit(solution)/shard_map/all_to_all | solution.py:516
  111.5 3.0 %copy-start.23 = (bf16[256,128]{1,0:T(8,128)(2,1)}, bf16[256,128]{1,0:T(8,128)(2,1)S(1)}, u32[]{:S(2)}) copy-start(bf16[256,128]{1,0:T(8,128)(2,1)S(1)} %add_convert_fusion.refs_14_.refs_0_) | copy-start | bytes 196612
  111.6 22.1 %collective-permute-start.27 = (bf16[256,128]{1,0:T(8,128)(2,1)S(1)}, bf16[256,128]{1,0:T(8,128)(2,1)S(1)}, u32[]{:S(2)}, u32[]{:S(2)}) collective-permute-start(bf16[256,128]{1,0:T(8,128)(2,1)S(1)} %add_convert_fusion.refs_14_.refs_0_), channel_id=1, source_target_pairs={{0,3},{1,0},{2,1},{3,2},{4,7},{5,4},{6,5},{7,6},{8,11},{9,8},{10,9... | collective-permute-start | bytes 196616 | tf_op jit(solution)/shard_map/ppermute | solution.py:512
  113.6 20.1 %collective-permute-start.26 = (bf16[256,128]{1,0:T(8,128)(2,1)S(1)}, bf16[256,128]{1,0:T(8,128)(2,1)S(1)}, u32[]{:S(2)}, u32[]{:S(2)}) collective-permute-start(bf16[256,128]{1,0:T(8,128)(2,1)S(1)} %add_convert_fusion.refs_14_.refs_0_), channel_id=1, source_target_pairs={{0,2},{1,3},{2,0},{3,1},{4,6},{5,7},{6,4},{7,5},{8,10},{9,11},{10,... | collective-permute-start | bytes 196616 | tf_op jit(solution)/shard_map/ppermute | solution.py:512
  113.6 20.1 %collective-permute-start.25 = (bf16[256,128]{1,0:T(8,128)(2,1)S(1)}, bf16[256,128]{1,0:T(8,128)(2,1)S(1)}, u32[]{:S(2)}, u32[]{:S(2)}) collective-permute-start(bf16[256,128]{1,0:T(8,128)(2,1)S(1)} %add_convert_fusion.refs_14_.refs_0_), channel_id=1, source_target_pairs={{0,1},{1,2},{2,3},{3,0},{4,5},{5,6},{6,7},{7,4},{8,9},{9,10},{10,1... | collective-permute-start | bytes 196616 | tf_op jit(solution)/shard_map/ppermute | solution.py:512
  133.7 10.6 %copy-start = (f32[8,128]{1,0:T(8,128)S(1)}, f32[8,128]{1,0:T(8,128)}, u32[]{:S(2)}) copy-start(f32[8,128]{1,0:T(8,128)} %told.1.refs_6_.asked) | copy-start | bytes 12292
  137.6 4.0 %collective-permute-start.28 = (bf16[64,256]{1,0:T(8,128)(2,1)}, bf16[64,256]{1,0:T(8,128)(2,1)S(1)}, u32[]{:S(2)}, u32[]{:S(2)}) collective-permute-start(bf16[64,256]{1,0:T(8,128)(2,1)} %get-tuple-element.86), channel_id=1, source_target_pairs={{0,4},{4,0},{8,12},{12,8},{16,20},{20,16},{24,28},{28,24},{1,5},{5... | collective-permute-start | bytes 98312 | tf_op jit(solution)/shard_map/ppermute | solution.py:445
  137.7 6.5 %collective-permute-start.29 = (bf16[64,256]{1,0:T(8,128)(2,1)}, bf16[64,256]{1,0:T(8,128)(2,1)S(1)}, u32[]{:S(2)}, u32[]{:S(2)}) collective-permute-start(bf16[64,256]{1,0:T(8,128)(2,1)} %get-tuple-element.87), channel_id=1, source_target_pairs={{0,8},{4,12},{8,0},{12,4},{16,24},{20,28},{24,16},{28,20},{1,9},{5... | collective-permute-start | bytes 98312 | tf_op jit(solution)/shard_map/ppermute | solution.py:445
  139.7 6.8 %collective-permute-start.30 = (bf16[64,256]{1,0:T(8,128)(2,1)}, bf16[64,256]{1,0:T(8,128)(2,1)S(1)}, u32[]{:S(2)}, u32[]{:S(2)}) collective-permute-start(bf16[64,256]{1,0:T(8,128)(2,1)} %get-tuple-element.88), channel_id=1, source_target_pairs={{0,12},{4,8},{8,4},{12,0},{16,28},{20,24},{24,20},{28,16},{1,13},{... | collective-permute-start | bytes 98312 | tf_op jit(solution)/shard_map/ppermute | solution.py:445
  139.8 6.8 %collective-permute-start.31 = (bf16[64,256]{1,0:T(8,128)(2,1)}, bf16[64,256]{1,0:T(8,128)(2,1)S(1)}, u32[]{:S(2)}, u32[]{:S(2)}) collective-permute-start(bf16[64,256]{1,0:T(8,128)(2,1)} %get-tuple-element.89), channel_id=1, source_target_pairs={{0,16},{4,20},{8,24},{12,28},{16,0},{20,4},{24,8},{28,12},{1,17},{... | collective-permute-start | bytes 98312 | tf_op jit(solution)/shard_map/ppermute | solution.py:445
  141.6 5.0 %collective-permute-start.32 = (bf16[64,256]{1,0:T(8,128)(2,1)}, bf16[64,256]{1,0:T(8,128)(2,1)S(1)}, u32[]{:S(2)}, u32[]{:S(2)}) collective-permute-start(bf16[64,256]{1,0:T(8,128)(2,1)} %get-tuple-element.90), channel_id=1, source_target_pairs={{0,20},{4,16},{8,28},{12,24},{16,4},{20,0},{24,12},{28,8},{1,21},{... | collective-permute-start | bytes 98312 | tf_op jit(solution)/shard_map/ppermute | solution.py:445
  141.6 7.0 %copy-start.36 = (bf16[64,256]{1,0:T(8,128)(2,1)}, bf16[64,256]{1,0:T(8,128)(2,1)S(1)}, u32[]{:S(2)}) copy-start(bf16[64,256]{1,0:T(8,128)(2,1)S(1)} %collective-permute-done.28.refs_1_) | copy-start | bytes 98308
  141.6 5.1 %collective-permute-start.33 = (bf16[64,256]{1,0:T(8,128)(2,1)}, bf16[64,256]{1,0:T(8,128)(2,1)S(1)}, u32[]{:S(2)}, u32[]{:S(2)}) collective-permute-start(bf16[64,256]{1,0:T(8,128)(2,1)} %get-tuple-element.91), channel_id=1, source_target_pairs={{0,24},{4,28},{8,16},{12,20},{16,8},{20,12},{24,0},{28,4},{1,25},{... | collective-permute-start | bytes 98312 | tf_op jit(solution)/shard_map/ppermute | solution.py:445
  144.1 4.5 %copy-start.37 = (bf16[64,256]{1,0:T(8,128)(2,1)}, bf16[64,256]{1,0:T(8,128)(2,1)S(1)}, u32[]{:S(2)}) copy-start(bf16[64,256]{1,0:T(8,128)(2,1)S(1)} %collective-permute-done.29.refs_2_) | copy-start | bytes 98308
  144.1 4.5 %collective-permute-start.34 = (bf16[64,256]{1,0:T(8,128)(2,1)}, bf16[64,256]{1,0:T(8,128)(2,1)S(1)}, u32[]{:S(2)}, u32[]{:S(2)}) collective-permute-start(bf16[64,256]{1,0:T(8,128)(2,1)} %get-tuple-element.92), channel_id=1, source_target_pairs={{0,28},{4,24},{8,20},{12,16},{16,12},{20,8},{24,4},{28,0},{1,29},{... | collective-permute-start | bytes 98312 | tf_op jit(solution)/shard_map/ppermute | solution.py:445
  146.6 2.0 %copy-start.38 = (bf16[64,256]{1,0:T(8,128)(2,1)}, bf16[64,256]{1,0:T(8,128)(2,1)S(1)}, u32[]{:S(2)}) copy-start(bf16[64,256]{1,0:T(8,128)(2,1)S(1)} %collective-permute-done.30.refs_3_) | copy-start | bytes 98308
  146.6 2.0 %copy-start.39 = (bf16[64,256]{1,0:T(8,128)(2,1)}, bf16[64,256]{1,0:T(8,128)(2,1)S(1)}, u32[]{:S(2)}) copy-start(bf16[64,256]{1,0:T(8,128)(2,1)S(1)} %collective-permute-done.31.refs_4_) | copy-start | bytes 98308
  146.6 2.0 %copy-start.40 = (bf16[64,256]{1,0:T(8,128)(2,1)}, bf16[64,256]{1,0:T(8,128)(2,1)S(1)}, u32[]{:S(2)}) copy-start(bf16[64,256]{1,0:T(8,128)(2,1)S(1)} %collective-permute-done.32.refs_5_) | copy-start | bytes 98308
  146.7 2.0 %copy-start.41 = (bf16[64,256]{1,0:T(8,128)(2,1)}, bf16[64,256]{1,0:T(8,128)(2,1)S(1)}, u32[]{:S(2)}) copy-start(bf16[64,256]{1,0:T(8,128)(2,1)S(1)} %collective-permute-done.33.refs_6_) | copy-start | bytes 98308
  (15 other events, 10.8 us)

commit v7 on v6

--- a/solution.py
+++ b/solution.py
@@ -118,12 +118,13 @@
     )(z, idx, count, x, *maps)
 
 
-def cot_copies(n, z, cots, cot, sem):
+def cot_copies(n, z, cots, cot, first, size, sem, at):
     key = cots[0].shape[1]
     copies = []
     for s in range(n):
         column = pl.multiple_of(lax.rem(z - s + n, n) * key, key)
-        copies.append(pltpu.make_async_copy(cots[s], cot.at[:, pl.ds(column, key)], sem.at[s]))
+        dst = cot.at[pl.ds(first, size), pl.ds(column, key)]
+        copies.append(pltpu.make_async_copy(cots[s].at[pl.ds(first, size)], dst, sem.at[at + s]))
     return copies
 
 
@@ -282,17 +283,32 @@
     maps, refs = refs[:n_maps], refs[n_maps:]
     cots, (out, table, cot, map_sem, cot_sem) = refs[:n], refs[-5:]
     step = pl.program_id(0)
+    block = per * rows
 
     @pl.when(step == 0)
     def _():
-        load_all(cot_copies(n, z[0], cots, cot, cot_sem) + map_copies(maps, table, map_sem))
-
+        for k in range(cot.shape[0] // block):
+            for copy in cot_copies(n, z[0], cots, cot, k * block, block, cot_sem, k * n):
+                copy.start()
+        for copy in map_copies(maps, table, map_sem):
+            copy.start()
+
+    begin = pl.multiple_of(step * block, block)
+    for copy in cot_copies(n, z[0], cots, cot, begin, block, cot_sem, step * n):
+        copy.wait()
     width = weight.shape[1]
     tile = min(512, width)
     counts = [count[step * per + i] for i in range(per)]
-    x = cot[pl.ds(pl.multiple_of(step * per * rows, per * rows), per * rows), :]
+    x = cot[pl.ds(begin, block), :]
     for d in range(0, width, tile):
         total = lax.dot_general(x, weight[:, d : d + tile], NN, preferred_element_type=jnp.float32)
+        if d == 0:
+
+            @pl.when(step == 0)
+            def _():
+                for copy in map_copies(maps, table, map_sem):
+                    copy.wait()
+
         for i in range(per):
             adapter = lax.dot_general(
                 pulled[i * rows : (i + 1) * rows, :],
@@ -323,7 +339,7 @@
             pltpu.VMEM((total, ranks, width), jnp.bfloat16),
             pltpu.VMEM((segs * rows, keys), jnp.bfloat16),
             pltpu.SemaphoreType.DMA((len(maps),)),
-            pltpu.SemaphoreType.DMA((n,)),
+            pltpu.SemaphoreType.DMA((n * segs // per,)),
         ],
         compiler_params=params(),
         cost_estimate=cost(16),

time: 152 us -> 152 us (level)
  no operation moved by 1% of the time
where the time goes in v7:
time: 152 us; the launch traced here: 151 us
  Pallas kernels  57.8 us (38%)
  starting transfers between devices  36.7 us (24%)
  waiting for transfers between devices  34 us (22%)
  local copies, waits for them, and re-layouts  20.4 us (13%)
    ppermute x23, waiting for transfers between devices, flip(): return lax.ppermute(x, 'dp', [(i, i ^ by) for i in range(n)])  23.3 us
    pallas_call x1, Pallas kernels, token_gradients(): pl.pallas_call(functools.partial(token_kernel, n, per, rows, len(maps)),...  18.9 us
    unnamed x91, local copies, waits for them, and re-layouts  18.5 us
    ppermute x23, starting transfers between devices, flip(): return lax.ppermute(x, 'dp', [(i, i ^ by) for i in range(n)])  17.2 us
    pallas_call x1, Pallas kernels, down_sums(): pl.pallas_call(functools.partial(down_sums_kernel, n, per, rows, ranks, s...  10.1 us
    pallas_call x1, Pallas kernels, project(): pl.pallas_call(functools.partial(project_kernel, n, per, rows, len(maps))...  9.57 us
    ppermute x6, starting transfers between devices, on_device(): lax.ppermute(x, 'tsp', [(i, (i + s) % n) for i in range(n)])  8.03 us
    ppermute x3, waiting for transfers between devices, on_device(): lax.ppermute(ups, 'tsp', [(i, (i + s) % n) for i in range(n)])  7.61 us
  transfers between devices with their start and end apart: 36, of which 14 were waited for; matrix products, arithmetic and copies ran while one was open for 8% of the time, Pallas kernels for 37%

profile of v7, /device:TPU:0, one launch (start us, length us, event | category | flops | bytes accessed | tf_op | source)
XLA Modules:
  0.0 150.7 jit_solution(3155162178113007821)
XLA Ops:
  0.6 3.1 %collective-permute-start.2 = (bf16[2048,256]{1,0:T(8,128)(2,1)}, bf16[2048,256]{1,0:T(8,128)(2,1)S(1)}, u32[]{:S(2)}, u32[]{:S(2)}) collective-permute-start(bf16[2048,256]{1,0:T(8,128)(2,1)} %x_hbm.1), channel_id=1, source_target_pairs={{0,1},{1,2},{2,3},{3,0},{4,5},{5,6},{6,7},{7,4},{8,9},{9,10},{10,1... | collective-permute-start | bytes 3145736 | tf_op jit(solution)/shard_map/ppermute | solution.py:457
  3.7 1.5 %collective-permute-start.1 = (bf16[2,64,2048]{2,1,0:T(8,128)(2,1)}, bf16[2,64,2048]{2,1,0:T(8,128)(2,1)S(1)}, u32[]{:S(2)}, u32[]{:S(2)}) collective-permute-start(bf16[2,64,2048]{2,1,0:T(8,128)(2,1)} %refs_0_.5), channel_id=1, source_target_pairs={{0,16},{4,20},{8,24},{12,28},{16,0},{20,4},{24,8},{28,12},{1,17},{... | collective-permute-start | bytes 1572872 | tf_op jit(solution)/shard_map/ppermute | solution.py:461
  5.2 1.5 collective-permute-start
  6.7 6.5 %copy.34 = bf16[2048,1024]{0,1:T(8,128)(2,1)} copy(bf16[2048,1024]{1,0:T(8,128)(2,1)} %param.12) | data formatting | bytes 8388608 | tf_op args[2]
  13.2 4.1 %collective-permute-done.1.refs_1_ = bf16[2,64,2048]{2,1,0:T(8,128)(2,1)S(1)} collective-permute-done((bf16[2,64,2048]{2,1,0:T(8,128)(2,1)}, bf16[2,64,2048]{2,1,0:T(8,128)(2,1)S(1)}, u32[]{:S(2)}, u32[]{:S(2)}) %collective-permute-start.1) | collective-permute-done | bytes 524320 | tf_op jit(solution)/shard_map/ppermute | solution.py:461
  17.3 1.2 collective-permute-done.refs_0_
  18.5 0.8 copy-done.2
  19.3 3.1 %late.1.refs_1_ = bf16[2,64,256]{2,1,0:T(8,128)(2,1)} custom-call(bf16[2,64,256]{2,1,0:T(8,128)(2,1)} %x.5, bf16[2,64,2048]{2,1,0:T(8,128)(2,1)} %get-tuple-element.57.refs_0_.refs_2_, bf16[2,64,2048]{2,1,0:T(8,128)(2,1)} %get-tuple-element.58.refs_1_.refs_3_), custom_call_target="tpu_custom_call" | custom-call | tf_op jit(solution)/shard_map/late/pallas_call | solution.py:444
  22.4 2.4 %collective-permute-start.5 = (bf16[2,64,256]{2,1,0:T(8,128)(2,1)}, bf16[2,64,256]{2,1,0:T(8,128)(2,1)S(1)}, u32[]{:S(2)}, u32[]{:S(2)}) collective-permute-start(bf16[2,64,256]{2,1,0:T(8,128)(2,1)} %late.1.refs_1_), channel_id=1, source_target_pairs={{0,3},{1,0},{2,1},{3,2},{4,7},{5,4},{6,5},{7,6},{8,11},{9,8},{10,9... | collective-permute-start | bytes 196616 | tf_op jit(solution)/shard_map/ppermute | solution.py:494
  24.9 0.7 collective-permute-start.4
  25.5 1.6 %collective-permute-start.3 = (bf16[2,64,256]{2,1,0:T(8,128)(2,1)}, bf16[2,64,256]{2,1,0:T(8,128)(2,1)S(1)}, u32[]{:S(2)}, u32[]{:S(2)}) collective-permute-start(bf16[2,64,256]{2,1,0:T(8,128)(2,1)} %late.1.refs_1_), channel_id=1, source_target_pairs={{0,1},{1,2},{2,3},{3,0},{4,5},{5,6},{6,7},{7,4},{8,9},{9,10},{10,1... | collective-permute-start | bytes 196616 | tf_op jit(solution)/shard_map/ppermute | solution.py:494
  27.1 3.4 %collective-permute-done.5.refs_6_ = bf16[2,64,256]{2,1,0:T(8,128)(2,1)S(1)} collective-permute-done((bf16[2,64,256]{2,1,0:T(8,128)(2,1)}, bf16[2,64,256]{2,1,0:T(8,128)(2,1)S(1)}, u32[]{:S(2)}, u32[]{:S(2)}) %collective-permute-start.5) | collective-permute-done | bytes 65568 | tf_op jit(solution)/shard_map/ppermute | solution.py:494
  30.5 4.2 %collective-permute-done.4.refs_5_ = bf16[2,64,256]{2,1,0:T(8,128)(2,1)S(1)} collective-permute-done((bf16[2,64,256]{2,1,0:T(8,128)(2,1)}, bf16[2,64,256]{2,1,0:T(8,128)(2,1)S(1)}, u32[]{:S(2)}, u32[]{:S(2)}) %collective-permute-start.4) | collective-permute-done | bytes 65568 | tf_op jit(solution)/shard_map/ppermute | solution.py:494
  34.7 0.6 copy-done.31
  35.4 1.0 copy-done.5
  36.3 1.3 plan.1
  37.6 1.0 slice.22
  38.6 1.0 slice.23
  39.6 1.6 %collective-permute-start.11 = (bf16[1,64,2048]{2,1,0:T(8,128)(2,1)S(1)}, bf16[1,64,2048]{2,1,0:T(8,128)(2,1)S(1)}, u32[]{:S(2)}, u32[]{:S(2)}) collective-permute-start(bf16[1,64,2048]{2,1,0:T(8,128)(2,1)S(1)} %slice.23), channel_id=1, source_target_pairs={{0,8},{4,12},{8,0},{12,4},{16,24},{20,28},{24,16},{28,20},{1,9},{5... | collective-permute-start | bytes 786440 | tf_op jit(solution)/shard_map/ppermute | solution.py:461
  41.1 1.5 %collective-permute-start.10 = (bf16[1,64,2048]{2,1,0:T(8,128)(2,1)S(1)}, bf16[1,64,2048]{2,1,0:T(8,128)(2,1)S(1)}, u32[]{:S(2)}, u32[]{:S(2)}) collective-permute-start(bf16[1,64,2048]{2,1,0:T(8,128)(2,1)S(1)} %slice.22), channel_id=1, source_target_pairs={{0,16},{4,20},{8,24},{12,28},{16,0},{20,4},{24,8},{28,12},{1,17},{... | collective-permute-start | bytes 786440 | tf_op jit(solution)/shard_map/ppermute | solution.py:461
  42.7 0.7 convert_bitcast_fusion
  43.3 0.5 collective-permute-start.9
  43.8 0.8 constant_dynamic-update-slice_fusion.4
  44.7 0.8 constant_dynamic-update-slice_fusion.3
  45.5 2.3 %collective-permute-done.11.refs_7_ = bf16[1,64,2048]{2,1,0:T(8,128)(2,1)S(1)} collective-permute-done((bf16[1,64,2048]{2,1,0:T(8,128)(2,1)S(1)}, bf16[1,64,2048]{2,1,0:T(8,128)(2,1)S(1)}, u32[]{:S(2)}, u32[]{:S(2)}) %collective-permute-start.11) | collective-permute-done | bytes 262176 | tf_op jit(solution)/shard_map/ppermute | solution.py:461
  47.9 1.2 collective-permute-done.10.refs_6_
  49.1 0.9 constant_dynamic-update-slice_fusion.2
  50.0 0.8 constant_dynamic-update-slice_fusion.1
  51.0 0.8 copy-done.16
  51.7 0.1 copy-done.17
  52.0 9.6 %project.1 = (f32[256,128]{1,0:T(8,128)}, f32[256,128]{1,0:T(8,128)}, f32[256,128]{1,0:T(8,128)}, f32[256,128]{1,0:T(8,128)}) custom-call(s32[1]{0:T(128)} %bitcast.z, s32[16]{0:T(128)} %get-tuple-element.54.idx, s32[16]{0:T(128)} %count.5, bf16[2048,2048]{1,0:T(8,128)(2,1)} %x.7, bf16[2,64,2048]{2,1,0:T(8,128)(2,1)} %refs_0_.5, ...), custom_call_target="tpu_custom_call" | custom-call | bytes 1200000 | tf_op jit(solution)/shard_map/project/pallas_call | solution.py:104
  61.6 1.8 %collective-permute-done.6.refs_0_ = bf16[2048,256]{1,0:T(8,128)(2,1)S(1)} collective-permute-done((bf16[2048,256]{1,0:T(8,128)(2,1)}, bf16[2048,256]{1,0:T(8,128)(2,1)S(1)}, u32[]{:S(2)}, u32[]{:S(2)}) %collective-permute-start.6) | collective-permute-done | bytes 1048608 | tf_op jit(solution)/shard_map/ppermute | solution.py:457
  63.4 1.0 copy-done.4
  64.5 2.4 %collective-permute-start.19 = (bf16[528,256]{1,0:T(8,128)(2,1)}, bf16[528,256]{1,0:T(8,128)(2,1)S(1)}, u32[]{:S(2)}, u32[]{:S(2)}) collective-permute-start(bf16[528,256]{1,0:T(8,128)(2,1)} %get-tuple-element.69.refs_3_.refs_0_), channel_id=1, source_target_pairs={{0,24},{4,28},{8,16},{12,20},{16,8},{20,12},{24,0},{28,4},{1,25},{... | collective-permute-start | bytes 811016 | tf_op jit(solution)/shard_map/ppermute | solution.py:461
  66.9 0.5 collective-permute-start.17
  67.4 0.5 collective-permute-start.15
  68.0 7.1 %collective-permute-done.19.refs_9_.refs_6_ = bf16[528,256]{1,0:T(8,128)(2,1)S(1)} collective-permute-done((bf16[528,256]{1,0:T(8,128)(2,1)}, bf16[528,256]{1,0:T(8,128)(2,1)S(1)}, u32[]{:S(2)}, u32[]{:S(2)}) %collective-permute-start.19) | collective-permute-done | bytes 270368 | tf_op jit(solution)/shard_map/ppermute | solution.py:461
  75.1 3.9 %collective-permute-done.17.refs_7_.refs_4_ = bf16[528,256]{1,0:T(8,128)(2,1)S(1)} collective-permute-done((bf16[528,256]{1,0:T(8,128)(2,1)}, bf16[528,256]{1,0:T(8,128)(2,1)S(1)}, u32[]{:S(2)}, u32[]{:S(2)}) %collective-permute-start.17) | collective-permute-done | bytes 270368 | tf_op jit(solution)/shard_map/ppermute | solution.py:461
  79.0 0.4 collective-permute-start.16
  79.5 1.0 collective-permute-done.18.refs_8_.refs_5_
  80.5 0.4 collective-permute-done.16.refs_6_.refs_3_
  80.9 0.3 copy-done.12
  81.2 0.7 copy-done.13
  81.9 1.6 %told.1.refs_6_.asked = f32[8,128]{1,0:T(8,128)} custom-call(s32[1]{0:T(128)} %bitcast.1.me.first.origin, bf16[528,256]{1,0:T(8,128)(2,1)} %get-tuple-element.69.refs_3_.refs_0_, bf16[528,256]{1,0:T(8,128)(2,1)} %copy-done.10, bf16[528,256]{1,0:T(8,128)(2,1)} %copy-done.9, bf16[528,256]{1,0:T(8,128)(2,1)} %copy-done.13, bf16[528,256]{1,0:T(8,128)(2,1)} %copy-done.8, ...), custom_call_target="tpu_custom_call" | custom-call | bytes 300000 | tf_op jit(solution)/shard_map/told/pallas_call | solution.py:361
  83.5 6.0 %pulled_part.1.refs_5_.part = f32[2048,64]{1,0:T(8,128)} custom-call(s32[16]{0:T(128)} %get-tuple-element.54.idx, bf16[2048,256]{1,0:T(8,128)(2,1)} %x_hbm.1, bf16[2048,256]{1,0:T(8,128)(2,1)} %get-tuple-element.59.refs_1_.refs_11_, bf16[2048,256]{1,0:T(8,128)(2,1)} %get-tuple-element.68.refs_2_.refs_12_, ...), custom_call_target="tpu_custom_call" | custom-call | bytes 1500000 | tf_op jit(solution)/shard_map/pulled_part/pallas_call | solution.py:211
  89.5 1.2 collective-permute-done.21.refs_0_
  90.7 1.1 copy-done.3
  91.8 2.9 %collective-permute-start.23 = (f32[256,128]{1,0:T(8,128)}, f32[256,128]{1,0:T(8,128)S(1)}, u32[]{:S(2)}, u32[]{:S(2)}) collective-permute-start(f32[256,128]{1,0:T(8,128)} %get-tuple-element.78), channel_id=1, source_target_pairs={{0,2},{1,3},{2,0},{3,1},{4,6},{5,7},{6,4},{7,5},{8,10},{9,11},{10,... | collective-permute-start | bytes 393224 | tf_op jit(solution)/shard_map/ppermute | solution.py:528
  94.7 2.1 %collective-permute-start.24 = (f32[256,128]{1,0:T(8,128)}, f32[256,128]{1,0:T(8,128)S(1)}, u32[]{:S(2)}, u32[]{:S(2)}) collective-permute-start(f32[256,128]{1,0:T(8,128)} %get-tuple-element.79), channel_id=1, source_target_pairs={{0,3},{1,0},{2,1},{3,2},{4,7},{5,4},{6,5},{7,6},{8,11},{9,8},{10,9... | collective-permute-start | bytes 393224 | tf_op jit(solution)/shard_map/ppermute | solution.py:528
  96.8 10.1 %down_sums.1 = (bf16[8,64,2048]{2,1,0:T(8,128)(2,1)}, bf16[2048,64]{1,0:T(8,128)(2,1)}) custom-call(s32[16]{0:T(128)} %get-tuple-element.54.idx, s32[16]{0:T(128)} %get-tuple-element.56.owner, s32[16]{0:T(128)} %count.5, bf16[2048,2048]{1,0:T(8,128)(2,1)} %x.7, f32[2048,64]{1,0:T(8,128)} %pulled_part.1.refs_5_.part, ...), custom_call_target="tpu_custom_call" | custom-call | bytes 2100000 | tf_op jit(solution)/shard_map/down_sums/pallas_call | solution.py:262
  107.0 0.6 copy-done.24
  107.7 3.7 %all-to-all-start = ((bf16[8,64,2048]{2,1,0:T(8,128)(2,1)}), bf16[8,64,2048]{2,1,0:T(8,128)(2,1)S(1)}, u32[]{:S(2)}, u32[]{:S(2)}) async-start(bf16[8,64,2048]{2,1,0:T(8,128)(2,1)} %get-tuple-element.84), calls=%async_computation | async-start | bytes 4194304 | tf_op jit(solution)/shard_map/all_to_all | solution.py:532
  111.6 2.0 %collective-permute-start.27 = (bf16[256,128]{1,0:T(8,128)(2,1)S(1)}, bf16[256,128]{1,0:T(8,128)(2,1)S(1)}, u32[]{:S(2)}, u32[]{:S(2)}) collective-permute-start(bf16[256,128]{1,0:T(8,128)(2,1)S(1)} %add_convert_fusion.refs_14_.refs_0_), channel_id=1, source_target_pairs={{0,3},{1,0},{2,1},{3,2},{4,7},{5,4},{6,5},{7,6},{8,11},{9,8},{10,9... | collective-permute-start | bytes 196616 | tf_op jit(solution)/shard_map/ppermute | solution.py:528
  113.6 1.0 collective-permute-start.25
  114.6 18.9 %token_gradient.1.refs_1_ = bf16[2048,2048]{1,0:T(8,128)(2,1)} custom-call(s32[1]{0:T(128)} %bitcast.z, s32[16]{0:T(128)} %get-tuple-element.54.idx, s32[16]{0:T(128)} %count.5, bf16[1024,2048]{1,0:T(8,128)(2,1)} %get-tuple-element.55.weight, bf16[2048,64]{1,0:T(8,128)(2,1)} %get-tuple-element.74.pulled, bf16[2,64,2048]{2,1,0:T(8,128)(2,1)} %refs_0_.5, ...), custom_call_target="tpu_custom_call" | custom-call | bytes 4800000 | tf_op jit(solution)/shard_map/token_gradient/pallas_call | solution.py:329
  133.6 0.6 copy-done.33
  134.2 3.2 %up_sums.1 = (bf16[64,256]{1,0:T(8,128)(2,1)}, bf16[64,256]{1,0:T(8,128)(2,1)}, bf16[64,256]{1,0:T(8,128)(2,1)}, bf16[64,256]{1,0:T(8,128)(2,1)}, bf16[64,256]{1...) custom-call(s32[1]{0:T(128)} %bitcast.z, s32[1]{0:T(128)} %bitcast.1.me.first.origin, ...), custom_call_target="tpu_custom_call" | custom-call | bytes 600000 | tf_op jit(solution)/shard_map/up_sums/pallas_call | solution.py:161
  137.5 2.1 %collective-permute-start.29 = (bf16[64,256]{1,0:T(8,128)(2,1)}, bf16[64,256]{1,0:T(8,128)(2,1)S(1)}, u32[]{:S(2)}, u32[]{:S(2)}) collective-permute-start(bf16[64,256]{1,0:T(8,128)(2,1)} %get-tuple-element.87), channel_id=1, source_target_pairs={{0,8},{4,12},{8,0},{12,4},{16,24},{20,28},{24,16},{28,20},{1,9},{5... | collective-permute-start | bytes 98312 | tf_op jit(solution)/shard_map/ppermute | solution.py:461
  139.7 1.8 %collective-permute-start.31 = (bf16[64,256]{1,0:T(8,128)(2,1)}, bf16[64,256]{1,0:T(8,128)(2,1)S(1)}, u32[]{:S(2)}, u32[]{:S(2)}) collective-permute-start(bf16[64,256]{1,0:T(8,128)(2,1)} %get-tuple-element.89), channel_id=1, source_target_pairs={{0,16},{4,20},{8,24},{12,28},{16,0},{20,4},{24,8},{28,12},{1,17},{... | collective-permute-start | bytes 98312 | tf_op jit(solution)/shard_map/ppermute | solution.py:461
  141.4 2.6 %collective-permute-start.33 = (bf16[64,256]{1,0:T(8,128)(2,1)}, bf16[64,256]{1,0:T(8,128)(2,1)S(1)}, u32[]{:S(2)}, u32[]{:S(2)}) collective-permute-start(bf16[64,256]{1,0:T(8,128)(2,1)} %get-tuple-element.91), channel_id=1, source_target_pairs={{0,24},{4,28},{8,16},{12,20},{16,8},{20,12},{24,0},{28,4},{1,25},{... | collective-permute-start | bytes 98312 | tf_op jit(solution)/shard_map/ppermute | solution.py:461
  144.1 2.3 %owned.1.refs_8_ = f32[2,64,2048]{2,1,0:T(8,128)} custom-call(s32[1]{0:T(128)} %bitcast.1.me.first.origin, f32[8,128]{1,0:T(8,128)S(1)} %copy-done, bf16[8,64,2048]{2,1,0:T(8,128)(2,1)S(1)} %all-to-all-done.got), custom_call_target="tpu_custom_call" | custom-call | bytes 600000 | tf_op jit(solution)/shard_map/owned/pallas_call | solution.py:388
  146.5 1.9 %collective-permute-done.34.refs_7_ = bf16[64,256]{1,0:T(8,128)(2,1)S(1)} collective-permute-done((bf16[64,256]{1,0:T(8,128)(2,1)}, bf16[64,256]{1,0:T(8,128)(2,1)S(1)}, u32[]{:S(2)}, u32[]{:S(2)}) %collective-permute-start.34) | collective-permute-done | bytes 32800 | tf_op jit(solution)/shard_map/ppermute | solution.py:461
  148.5 0.6 copy-done.42
  149.1 1.7 %owned_each.1 = f32[2,64,256]{2,1,0:T(8,128)} custom-call(f32[8,128]{1,0:T(8,128)} %told.1.refs_6_.asked, bf16[64,256]{1,0:T(8,128)(2,1)} %get-tuple-element.85.refs_0_, bf16[64,256]{1,0:T(8,128)(2,1)} %copy-done.36, bf16[64,256]{1,0:T(8,128)(2,1)} %copy-done.37, bf16[64,256]{1,0:T(8,128)(2,1)} %copy-done.38, bf16[64,256]{1,0:T(8,128)(2,1)} %copy-done.39, ...), custom_call_target="tpu_custom_call" | custom-call | bytes 600000 | tf_op jit(solution)/shard_map/owned_each/pallas_call | solution.py:410
  (120 shorter events, 1.0 us)
Async XLA Ops:
  0.6 34.1 %collective-permute-start.2 = (bf16[2048,256]{1,0:T(8,128)(2,1)}, bf16[2048,256]{1,0:T(8,128)(2,1)S(1)}, u32[]{:S(2)}, u32[]{:S(2)}) collective-permute-start(bf16[2048,256]{1,0:T(8,128)(2,1)} %x_hbm.1), channel_id=1, source_target_pairs={{0,1},{1,2},{2,3},{3,0},{4,5},{5,6},{6,7},{7,4},{8,9},{9,10},{10,1... | collective-permute-start | bytes 3145736 | tf_op jit(solution)/shard_map/ppermute | solution.py:457
  3.7 13.6 %collective-permute-start.1 = (bf16[2,64,2048]{2,1,0:T(8,128)(2,1)}, bf16[2,64,2048]{2,1,0:T(8,128)(2,1)S(1)}, u32[]{:S(2)}, u32[]{:S(2)}) collective-permute-start(bf16[2,64,2048]{2,1,0:T(8,128)(2,1)} %refs_0_.5), channel_id=1, source_target_pairs={{0,16},{4,20},{8,24},{12,28},{16,0},{20,4},{24,8},{28,12},{1,17},{... | collective-permute-start | bytes 1572872 | tf_op jit(solution)/shard_map/ppermute | solution.py:461
  5.2 13.3 %collective-permute-start = (bf16[2,64,2048]{2,1,0:T(8,128)(2,1)}, bf16[2,64,2048]{2,1,0:T(8,128)(2,1)S(1)}, u32[]{:S(2)}, u32[]{:S(2)}) collective-permute-start(bf16[2,64,2048]{2,1,0:T(8,128)(2,1)} %refs_0_.5), channel_id=1, source_target_pairs={{0,8},{4,12},{8,0},{12,4},{16,24},{20,28},{24,16},{28,20},{1,9},{5... | collective-permute-start | bytes 1572872 | tf_op jit(solution)/shard_map/ppermute | solution.py:461
  13.2 13.9 %copy-start.14 = (bf16[2,64,2048]{2,1,0:T(8,128)(2,1)S(1)}, bf16[2,64,2048]{2,1,0:T(8,128)(2,1)}, u32[]{:S(2)}) copy-start(bf16[2,64,2048]{2,1,0:T(8,128)(2,1)} %refs_0_.5) | copy-start | bytes 1572868
  17.3 1.2 copy-start.1
  22.4 8.1 %collective-permute-start.5 = (bf16[2,64,256]{2,1,0:T(8,128)(2,1)}, bf16[2,64,256]{2,1,0:T(8,128)(2,1)S(1)}, u32[]{:S(2)}, u32[]{:S(2)}) collective-permute-start(bf16[2,64,256]{2,1,0:T(8,128)(2,1)} %late.1.refs_1_), channel_id=1, source_target_pairs={{0,3},{1,0},{2,1},{3,2},{4,7},{5,4},{6,5},{7,6},{8,11},{9,8},{10,9... | collective-permute-start | bytes 196616 | tf_op jit(solution)/shard_map/ppermute | solution.py:494
  24.9 9.8 %collective-permute-start.4 = (bf16[2,64,256]{2,1,0:T(8,128)(2,1)}, bf16[2,64,256]{2,1,0:T(8,128)(2,1)S(1)}, u32[]{:S(2)}, u32[]{:S(2)}) collective-permute-start(bf16[2,64,256]{2,1,0:T(8,128)(2,1)} %late.1.refs_1_), channel_id=1, source_target_pairs={{0,2},{1,3},{2,0},{3,1},{4,6},{5,7},{6,4},{7,5},{8,10},{9,11},{10,... | collective-permute-start | bytes 196616 | tf_op jit(solution)/shard_map/ppermute | solution.py:494
  25.5 9.2 %collective-permute-start.3 = (bf16[2,64,256]{2,1,0:T(8,128)(2,1)}, bf16[2,64,256]{2,1,0:T(8,128)(2,1)S(1)}, u32[]{:S(2)}, u32[]{:S(2)}) collective-permute-start(bf16[2,64,256]{2,1,0:T(8,128)(2,1)} %late.1.refs_1_), channel_id=1, source_target_pairs={{0,1},{1,2},{2,3},{3,0},{4,5},{5,6},{6,7},{7,4},{8,9},{9,10},{10,1... | collective-permute-start | bytes 196616 | tf_op jit(solution)/shard_map/ppermute | solution.py:494
  27.1 16.2 %collective-permute-start.7 = (bf16[2,64,2048]{2,1,0:T(8,128)(2,1)S(1)}, bf16[2,64,2048]{2,1,0:T(8,128)(2,1)S(1)}, u32[]{:S(2)}, u32[]{:S(2)}) collective-permute-start(bf16[2,64,2048]{2,1,0:T(8,128)(2,1)S(1)} %copy-done.14), channel_id=1, source_target_pairs={{0,4},{4,0},{8,12},{12,8},{16,20},{20,16},{24,28},{28,24},{1,5},{5... | collective-permute-start | bytes 1572872 | tf_op jit(solution)/shard_map/ppermute | solution.py:461
  30.5 4.2 %copy-start.30 = (bf16[2,64,256]{2,1,0:T(8,128)(2,1)}, bf16[2,64,256]{2,1,0:T(8,128)(2,1)S(1)}, u32[]{:S(2)}) copy-start(bf16[2,64,256]{2,1,0:T(8,128)(2,1)S(1)} %collective-permute-done.5.refs_6_) | copy-start | bytes 196612
  36.3 27.1 %collective-permute-start.6 = (bf16[2048,256]{1,0:T(8,128)(2,1)}, bf16[2048,256]{1,0:T(8,128)(2,1)S(1)}, u32[]{:S(2)}, u32[]{:S(2)}) collective-permute-start(bf16[2048,256]{1,0:T(8,128)(2,1)} %get-tuple-element.59.refs_1_.refs_11_), channel_id=1, source_target_pairs={{0,1},{1,2},{2,3},{3,0},{4,5},{5,6},{6,7},{7,4},{8,9},{9,10},{10,1... | collective-permute-start | bytes 3145736 | tf_op jit(solution)/shard_map/ppermute | solution.py:457
  39.6 8.3 %collective-permute-start.11 = (bf16[1,64,2048]{2,1,0:T(8,128)(2,1)S(1)}, bf16[1,64,2048]{2,1,0:T(8,128)(2,1)S(1)}, u32[]{:S(2)}, u32[]{:S(2)}) collective-permute-start(bf16[1,64,2048]{2,1,0:T(8,128)(2,1)S(1)} %slice.23), channel_id=1, source_target_pairs={{0,8},{4,12},{8,0},{12,4},{16,24},{20,28},{24,16},{28,20},{1,9},{5... | collective-permute-start | bytes 786440 | tf_op jit(solution)/shard_map/ppermute | solution.py:461
  41.1 7.9 %collective-permute-start.10 = (bf16[1,64,2048]{2,1,0:T(8,128)(2,1)S(1)}, bf16[1,64,2048]{2,1,0:T(8,128)(2,1)S(1)}, u32[]{:S(2)}, u32[]{:S(2)}) collective-permute-start(bf16[1,64,2048]{2,1,0:T(8,128)(2,1)S(1)} %slice.22), channel_id=1, source_target_pairs={{0,16},{4,20},{8,24},{12,28},{16,0},{20,4},{24,8},{28,12},{1,17},{... | collective-permute-start | bytes 786440 | tf_op jit(solution)/shard_map/ppermute | solution.py:461
  43.3 7.5 %collective-permute-start.8 = (bf16[2,64,2048]{2,1,0:T(8,128)(2,1)}, bf16[2,64,2048]{2,1,0:T(8,128)(2,1)S(1)}, u32[]{:S(2)}, u32[]{:S(2)}) collective-permute-start(bf16[2,64,2048]{2,1,0:T(8,128)(2,1)} %get-tuple-element.65.refs_2_), channel_id=1, source_target_pairs={{0,4},{4,0},{8,12},{12,8},{16,20},{20,16},{24,28},{28,24},{1,5},{5... | collective-permute-start | bytes 1572872 | tf_op jit(solution)/shard_map/ppermute | solution.py:461
  43.3 7.6 %copy-start.15 = (bf16[2,64,2048]{2,1,0:T(8,128)(2,1)}, bf16[2,64,2048]{2,1,0:T(8,128)(2,1)S(1)}, u32[]{:S(2)}) copy-start(bf16[2,64,2048]{2,1,0:T(8,128)(2,1)S(1)} %collective-permute-done.7.refs_1_) | copy-start | bytes 1572868
  43.3 7.5 %collective-permute-start.9 = (bf16[2,64,2048]{2,1,0:T(8,128)(2,1)}, bf16[2,64,2048]{2,1,0:T(8,128)(2,1)S(1)}, u32[]{:S(2)}, u32[]{:S(2)}) collective-permute-start(bf16[2,64,2048]{2,1,0:T(8,128)(2,1)} %get-tuple-element.66.refs_4_), channel_id=1, source_target_pairs={{0,4},{4,0},{8,12},{12,8},{16,20},{20,16},{24,28},{28,24},{1,5},{5... | collective-permute-start | bytes 1572872 | tf_op jit(solution)/shard_map/ppermute | solution.py:461
  47.9 3.1 %copy-start.19 = (bf16[1,64,2048]{2,1,0:T(8,128)(2,1)}, bf16[1,64,2048]{2,1,0:T(8,128)(2,1)S(1)}, u32[]{:S(2)}) copy-start(bf16[1,64,2048]{2,1,0:T(8,128)(2,1)S(1)} %collective-permute-done.11.refs_7_) | copy-start | bytes 786436
  47.9 3.0 %collective-permute-start.13 = (bf16[1,64,2048]{2,1,0:T(8,128)(2,1)S(1)}, bf16[1,64,2048]{2,1,0:T(8,128)(2,1)S(1)}, u32[]{:S(2)}, u32[]{:S(2)}) collective-permute-start(bf16[1,64,2048]{2,1,0:T(8,128)(2,1)S(1)} %collective-permute-done.11.refs_7_), channel_id=1, source_target_pairs={{0,4},{4,0},{8,12},{12,8},{16,20},{20,16},{24,28},{28,24},{1,5},{5... | collective-permute-start | bytes 786440 | tf_op jit(solution)/shard_map/ppermute | solution.py:461
  49.1 1.9 %copy-start.20 = (bf16[1,64,2048]{2,1,0:T(8,128)(2,1)}, bf16[1,64,2048]{2,1,0:T(8,128)(2,1)S(1)}, u32[]{:S(2)}) copy-start(bf16[1,64,2048]{2,1,0:T(8,128)(2,1)S(1)} %collective-permute-done.10.refs_6_) | copy-start | bytes 786436
  49.1 1.8 %collective-permute-start.12 = (bf16[1,64,2048]{2,1,0:T(8,128)(2,1)S(1)}, bf16[1,64,2048]{2,1,0:T(8,128)(2,1)S(1)}, u32[]{:S(2)}, u32[]{:S(2)}) collective-permute-start(bf16[1,64,2048]{2,1,0:T(8,128)(2,1)S(1)} %collective-permute-done.10.refs_6_), channel_id=1, source_target_pairs={{0,4},{4,0},{8,12},{12,8},{16,20},{20,16},{24,28},{28,24},{1,5},{5... | collective-permute-start | bytes 786440 | tf_op jit(solution)/shard_map/ppermute | solution.py:461
  50.8 10.8 %copy-start.6 = (bf16[528,256]{1,0:T(8,128)(2,1)}, bf16[528,256]{1,0:T(8,128)(2,1)S(1)}, u32[]{:S(2)}) copy-start(bf16[528,256]{1,0:T(8,128)(2,1)S(1)} %constant_dynamic-update-slice_fusion.refs_1_) | copy-start | bytes 811012
  50.9 1.1 copy-start.21
  50.9 1.1 copy-start.22
  63.4 1.0 copy-start.4
  64.5 26.2 %collective-permute-start.21 = (bf16[2048,256]{1,0:T(8,128)(2,1)}, bf16[2048,256]{1,0:T(8,128)(2,1)S(1)}, u32[]{:S(2)}, u32[]{:S(2)}) collective-permute-start(bf16[2048,256]{1,0:T(8,128)(2,1)} %get-tuple-element.68.refs_2_.refs_12_), channel_id=1, source_target_pairs={{0,1},{1,2},{2,3},{3,0},{4,5},{5,6},{6,7},{7,4},{8,9},{9,10},{10,1... | collective-permute-start | bytes 3145736 | tf_op jit(solution)/shard_map/ppermute | solution.py:457
  64.5 10.6 %collective-permute-start.19 = (bf16[528,256]{1,0:T(8,128)(2,1)}, bf16[528,256]{1,0:T(8,128)(2,1)S(1)}, u32[]{:S(2)}, u32[]{:S(2)}) collective-permute-start(bf16[528,256]{1,0:T(8,128)(2,1)} %get-tuple-element.69.refs_3_.refs_0_), channel_id=1, source_target_pairs={{0,24},{4,28},{8,16},{12,20},{16,8},{20,12},{24,0},{28,4},{1,25},{... | collective-permute-start | bytes 811016 | tf_op jit(solution)/shard_map/ppermute | solution.py:461
  66.9 12.0 %collective-permute-start.17 = (bf16[528,256]{1,0:T(8,128)(2,1)}, bf16[528,256]{1,0:T(8,128)(2,1)S(1)}, u32[]{:S(2)}, u32[]{:S(2)}) collective-permute-start(bf16[528,256]{1,0:T(8,128)(2,1)} %get-tuple-element.69.refs_3_.refs_0_), channel_id=1, source_target_pairs={{0,16},{4,20},{8,24},{12,28},{16,0},{20,4},{24,8},{28,12},{1,17},{... | collective-permute-start | bytes 811016 | tf_op jit(solution)/shard_map/ppermute | solution.py:461
  67.4 11.6 %collective-permute-start.15 = (bf16[528,256]{1,0:T(8,128)(2,1)}, bf16[528,256]{1,0:T(8,128)(2,1)S(1)}, u32[]{:S(2)}, u32[]{:S(2)}) collective-permute-start(bf16[528,256]{1,0:T(8,128)(2,1)} %get-tuple-element.69.refs_3_.refs_0_), channel_id=1, source_target_pairs={{0,8},{4,12},{8,0},{12,4},{16,24},{20,28},{24,16},{28,20},{1,9},{5... | collective-permute-start | bytes 811016 | tf_op jit(solution)/shard_map/ppermute | solution.py:461
  68.0 11.5 %collective-permute-start.14 = (bf16[528,256]{1,0:T(8,128)(2,1)}, bf16[528,256]{1,0:T(8,128)(2,1)S(1)}, u32[]{:S(2)}, u32[]{:S(2)}) collective-permute-start(bf16[528,256]{1,0:T(8,128)(2,1)} %get-tuple-element.69.refs_3_.refs_0_), channel_id=1, source_target_pairs={{0,4},{4,0},{8,12},{12,8},{16,20},{20,16},{24,28},{28,24},{1,5},{5... | collective-permute-start | bytes 811016 | tf_op jit(solution)/shard_map/ppermute | solution.py:461
  75.1 5.8 %copy-start.7 = (bf16[528,256]{1,0:T(8,128)(2,1)}, bf16[528,256]{1,0:T(8,128)(2,1)S(1)}, u32[]{:S(2)}) copy-start(bf16[528,256]{1,0:T(8,128)(2,1)S(1)} %collective-permute-done.19.refs_9_.refs_6_) | copy-start | bytes 811012
  75.1 4.4 %collective-permute-start.20 = (bf16[528,256]{1,0:T(8,128)(2,1)S(1)}, bf16[528,256]{1,0:T(8,128)(2,1)S(1)}, u32[]{:S(2)}, u32[]{:S(2)}) collective-permute-start(bf16[528,256]{1,0:T(8,128)(2,1)S(1)} %collective-permute-done.19.refs_9_.refs_6_), channel_id=1, source_target_pairs={{0,4},{4,0},{8,12},{12,8},{16,20},{20,16},{24,28},{28,24},{1,5},{5... | collective-permute-start | bytes 811016 | tf_op jit(solution)/shard_map/ppermute | solution.py:461
  78.9 1.9 %copy-start.8 = (bf16[528,256]{1,0:T(8,128)(2,1)}, bf16[528,256]{1,0:T(8,128)(2,1)S(1)}, u32[]{:S(2)}) copy-start(bf16[528,256]{1,0:T(8,128)(2,1)S(1)} %collective-permute-done.17.refs_7_.refs_4_) | copy-start | bytes 811012
  78.9 1.5 %collective-permute-start.18 = (bf16[528,256]{1,0:T(8,128)(2,1)S(1)}, bf16[528,256]{1,0:T(8,128)(2,1)S(1)}, u32[]{:S(2)}, u32[]{:S(2)}) collective-permute-start(bf16[528,256]{1,0:T(8,128)(2,1)S(1)} %collective-permute-done.17.refs_7_.refs_4_), channel_id=1, source_target_pairs={{0,4},{4,0},{8,12},{12,8},{16,20},{20,16},{24,28},{28,24},{1,5},{5... | collective-permute-start | bytes 811016 | tf_op jit(solution)/shard_map/ppermute | solution.py:461
  79.0 1.8 %copy-start.9 = (bf16[528,256]{1,0:T(8,128)(2,1)}, bf16[528,256]{1,0:T(8,128)(2,1)S(1)}, u32[]{:S(2)}) copy-start(bf16[528,256]{1,0:T(8,128)(2,1)S(1)} %collective-permute-done.15.refs_5_.refs_2_) | copy-start | bytes 811012
  79.0 1.8 %collective-permute-start.16 = (bf16[528,256]{1,0:T(8,128)(2,1)S(1)}, bf16[528,256]{1,0:T(8,128)(2,1)S(1)}, u32[]{:S(2)}, u32[]{:S(2)}) collective-permute-start(bf16[528,256]{1,0:T(8,128)(2,1)S(1)} %collective-permute-done.15.refs_5_.refs_2_), channel_id=1, source_target_pairs={{0,4},{4,0},{8,12},{12,8},{16,20},{20,16},{24,28},{28,24},{1,5},{5... | collective-permute-start | bytes 811016 | tf_op jit(solution)/shard_map/ppermute | solution.py:461
  79.5 1.4 copy-start.10
  79.5 1.4 copy-start.11
  90.7 1.1 copy-start.3
  91.8 15.2 %collective-permute-start.22 = (f32[256,128]{1,0:T(8,128)}, f32[256,128]{1,0:T(8,128)S(1)}, u32[]{:S(2)}, u32[]{:S(2)}) collective-permute-start(f32[256,128]{1,0:T(8,128)} %get-tuple-element.77), channel_id=1, source_target_pairs={{0,1},{1,2},{2,3},{3,0},{4,5},{5,6},{6,7},{7,4},{8,9},{9,10},{10,1... | collective-permute-start | bytes 393224 | tf_op jit(solution)/shard_map/ppermute | solution.py:528
  91.8 15.2 %collective-permute-start.23 = (f32[256,128]{1,0:T(8,128)}, f32[256,128]{1,0:T(8,128)S(1)}, u32[]{:S(2)}, u32[]{:S(2)}) collective-permute-start(f32[256,128]{1,0:T(8,128)} %get-tuple-element.78), channel_id=1, source_target_pairs={{0,2},{1,3},{2,0},{3,1},{4,6},{5,7},{6,4},{7,5},{8,10},{9,11},{10,... | collective-permute-start | bytes 393224 | tf_op jit(solution)/shard_map/ppermute | solution.py:528
  94.7 12.3 %collective-permute-start.24 = (f32[256,128]{1,0:T(8,128)}, f32[256,128]{1,0:T(8,128)S(1)}, u32[]{:S(2)}, u32[]{:S(2)}) collective-permute-start(f32[256,128]{1,0:T(8,128)} %get-tuple-element.79), channel_id=1, source_target_pairs={{0,3},{1,0},{2,1},{3,2},{4,7},{5,4},{6,5},{7,6},{8,11},{9,8},{10,9... | collective-permute-start | bytes 393224 | tf_op jit(solution)/shard_map/ppermute | solution.py:528
  107.7 3.8 %copy-start.18 = (f32[256,128]{1,0:T(8,128)S(1)}, f32[256,128]{1,0:T(8,128)}, u32[]{:S(2)}) copy-start(f32[256,128]{1,0:T(8,128)} %get-tuple-element.80) | copy-start | bytes 393220
  107.7 3.8 %copy-start.25 = (f32[256,128]{1,0:T(8,128)S(1)}, f32[256,128]{1,0:T(8,128)}, u32[]{:S(2)}) copy-start(f32[256,128]{1,0:T(8,128)} %get-tuple-element.81) | copy-start | bytes 393220
  107.7 3.8 %copy-start.27 = (f32[256,128]{1,0:T(8,128)S(1)}, f32[256,128]{1,0:T(8,128)}, u32[]{:S(2)}) copy-start(f32[256,128]{1,0:T(8,128)} %get-tuple-element.82) | copy-start | bytes 393220
  107.7 3.8 %copy-start.29 = (f32[256,128]{1,0:T(8,128)S(1)}, f32[256,128]{1,0:T(8,128)}, u32[]{:S(2)}) copy-start(f32[256,128]{1,0:T(8,128)} %get-tuple-element.83) | copy-start | bytes 393220
  107.7 36.4 %all-to-all-start = ((bf16[8,64,2048]{2,1,0:T(8,128)(2,1)}), bf16[8,64,2048]{2,1,0:T(8,128)(2,1)S(1)}, u32[]{:S(2)}, u32[]{:S(2)}) async-start(bf16[8,64,2048]{2,1,0:T(8,128)(2,1)} %get-tuple-element.84), calls=%async_computation | async-start | bytes 4194304 | tf_op jit(solution)/shard_map/all_to_all | solution.py:532
  111.5 3.0 %copy-start.23 = (bf16[256,128]{1,0:T(8,128)(2,1)}, bf16[256,128]{1,0:T(8,128)(2,1)S(1)}, u32[]{:S(2)}) copy-start(bf16[256,128]{1,0:T(8,128)(2,1)S(1)} %add_convert_fusion.refs_14_.refs_0_) | copy-start | bytes 196612
  111.6 22.0 %collective-permute-start.27 = (bf16[256,128]{1,0:T(8,128)(2,1)S(1)}, bf16[256,128]{1,0:T(8,128)(2,1)S(1)}, u32[]{:S(2)}, u32[]{:S(2)}) collective-permute-start(bf16[256,128]{1,0:T(8,128)(2,1)S(1)} %add_convert_fusion.refs_14_.refs_0_), channel_id=1, source_target_pairs={{0,3},{1,0},{2,1},{3,2},{4,7},{5,4},{6,5},{7,6},{8,11},{9,8},{10,9... | collective-permute-start | bytes 196616 | tf_op jit(solution)/shard_map/ppermute | solution.py:528
  113.6 19.9 %collective-permute-start.26 = (bf16[256,128]{1,0:T(8,128)(2,1)S(1)}, bf16[256,128]{1,0:T(8,128)(2,1)S(1)}, u32[]{:S(2)}, u32[]{:S(2)}) collective-permute-start(bf16[256,128]{1,0:T(8,128)(2,1)S(1)} %add_convert_fusion.refs_14_.refs_0_), channel_id=1, source_target_pairs={{0,2},{1,3},{2,0},{3,1},{4,6},{5,7},{6,4},{7,5},{8,10},{9,11},{10,... | collective-permute-start | bytes 196616 | tf_op jit(solution)/shard_map/ppermute | solution.py:528
  113.6 20.0 %collective-permute-start.25 = (bf16[256,128]{1,0:T(8,128)(2,1)S(1)}, bf16[256,128]{1,0:T(8,128)(2,1)S(1)}, u32[]{:S(2)}, u32[]{:S(2)}) collective-permute-start(bf16[256,128]{1,0:T(8,128)(2,1)S(1)} %add_convert_fusion.refs_14_.refs_0_), channel_id=1, source_target_pairs={{0,1},{1,2},{2,3},{3,0},{4,5},{5,6},{6,7},{7,4},{8,9},{9,10},{10,1... | collective-permute-start | bytes 196616 | tf_op jit(solution)/shard_map/ppermute | solution.py:528
  133.5 10.6 %copy-start = (f32[8,128]{1,0:T(8,128)S(1)}, f32[8,128]{1,0:T(8,128)}, u32[]{:S(2)}) copy-start(f32[8,128]{1,0:T(8,128)} %told.1.refs_6_.asked) | copy-start | bytes 12292
  137.4 4.0 %collective-permute-start.28 = (bf16[64,256]{1,0:T(8,128)(2,1)}, bf16[64,256]{1,0:T(8,128)(2,1)S(1)}, u32[]{:S(2)}, u32[]{:S(2)}) collective-permute-start(bf16[64,256]{1,0:T(8,128)(2,1)} %get-tuple-element.86), channel_id=1, source_target_pairs={{0,4},{4,0},{8,12},{12,8},{16,20},{20,16},{24,28},{28,24},{1,5},{5... | collective-permute-start | bytes 98312 | tf_op jit(solution)/shard_map/ppermute | solution.py:461
  137.5 6.5 %collective-permute-start.29 = (bf16[64,256]{1,0:T(8,128)(2,1)}, bf16[64,256]{1,0:T(8,128)(2,1)S(1)}, u32[]{:S(2)}, u32[]{:S(2)}) collective-permute-start(bf16[64,256]{1,0:T(8,128)(2,1)} %get-tuple-element.87), channel_id=1, source_target_pairs={{0,8},{4,12},{8,0},{12,4},{16,24},{20,28},{24,16},{28,20},{1,9},{5... | collective-permute-start | bytes 98312 | tf_op jit(solution)/shard_map/ppermute | solution.py:461
  139.6 6.8 %collective-permute-start.30 = (bf16[64,256]{1,0:T(8,128)(2,1)}, bf16[64,256]{1,0:T(8,128)(2,1)S(1)}, u32[]{:S(2)}, u32[]{:S(2)}) collective-permute-start(bf16[64,256]{1,0:T(8,128)(2,1)} %get-tuple-element.88), channel_id=1, source_target_pairs={{0,12},{4,8},{8,4},{12,0},{16,28},{20,24},{24,20},{28,16},{1,13},{... | collective-permute-start | bytes 98312 | tf_op jit(solution)/shard_map/ppermute | solution.py:461
  139.7 6.8 %collective-permute-start.31 = (bf16[64,256]{1,0:T(8,128)(2,1)}, bf16[64,256]{1,0:T(8,128)(2,1)S(1)}, u32[]{:S(2)}, u32[]{:S(2)}) collective-permute-start(bf16[64,256]{1,0:T(8,128)(2,1)} %get-tuple-element.89), channel_id=1, source_target_pairs={{0,16},{4,20},{8,24},{12,28},{16,0},{20,4},{24,8},{28,12},{1,17},{... | collective-permute-start | bytes 98312 | tf_op jit(solution)/shard_map/ppermute | solution.py:461
  141.4 5.0 %collective-permute-start.32 = (bf16[64,256]{1,0:T(8,128)(2,1)}, bf16[64,256]{1,0:T(8,128)(2,1)S(1)}, u32[]{:S(2)}, u32[]{:S(2)}) collective-permute-start(bf16[64,256]{1,0:T(8,128)(2,1)} %get-tuple-element.90), channel_id=1, source_target_pairs={{0,20},{4,16},{8,28},{12,24},{16,4},{20,0},{24,12},{28,8},{1,21},{... | collective-permute-start | bytes 98312 | tf_op jit(solution)/shard_map/ppermute | solution.py:461
  141.4 7.0 %copy-start.36 = (bf16[64,256]{1,0:T(8,128)(2,1)}, bf16[64,256]{1,0:T(8,128)(2,1)S(1)}, u32[]{:S(2)}) copy-start(bf16[64,256]{1,0:T(8,128)(2,1)S(1)} %collective-permute-done.28.refs_1_) | copy-start | bytes 98308
  141.4 5.1 %collective-permute-start.33 = (bf16[64,256]{1,0:T(8,128)(2,1)}, bf16[64,256]{1,0:T(8,128)(2,1)S(1)}, u32[]{:S(2)}, u32[]{:S(2)}) collective-permute-start(bf16[64,256]{1,0:T(8,128)(2,1)} %get-tuple-element.91), channel_id=1, source_target_pairs={{0,24},{4,28},{8,16},{12,20},{16,8},{20,12},{24,0},{28,4},{1,25},{... | collective-permute-start | bytes 98312 | tf_op jit(solution)/shard_map/ppermute | solution.py:461
  144.0 4.5 %copy-start.37 = (bf16[64,256]{1,0:T(8,128)(2,1)}, bf16[64,256]{1,0:T(8,128)(2,1)S(1)}, u32[]{:S(2)}) copy-start(bf16[64,256]{1,0:T(8,128)(2,1)S(1)} %collective-permute-done.29.refs_2_) | copy-start | bytes 98308
  144.0 4.5 %collective-permute-start.34 = (bf16[64,256]{1,0:T(8,128)(2,1)}, bf16[64,256]{1,0:T(8,128)(2,1)S(1)}, u32[]{:S(2)}, u32[]{:S(2)}) collective-permute-start(bf16[64,256]{1,0:T(8,128)(2,1)} %get-tuple-element.92), channel_id=1, source_target_pairs={{0,28},{4,24},{8,20},{12,16},{16,12},{20,8},{24,4},{28,0},{1,29},{... | collective-permute-start | bytes 98312 | tf_op jit(solution)/shard_map/ppermute | solution.py:461
  146.4 2.0 %copy-start.38 = (bf16[64,256]{1,0:T(8,128)(2,1)}, bf16[64,256]{1,0:T(8,128)(2,1)S(1)}, u32[]{:S(2)}) copy-start(bf16[64,256]{1,0:T(8,128)(2,1)S(1)} %collective-permute-done.30.refs_3_) | copy-start | bytes 98308
  146.4 2.0 %copy-start.39 = (bf16[64,256]{1,0:T(8,128)(2,1)}, bf16[64,256]{1,0:T(8,128)(2,1)S(1)}, u32[]{:S(2)}) copy-start(bf16[64,256]{1,0:T(8,128)(2,1)S(1)} %collective-permute-done.31.refs_4_) | copy-start | bytes 98308
  146.5 2.0 %copy-start.40 = (bf16[64,256]{1,0:T(8,128)(2,1)}, bf16[64,256]{1,0:T(8,128)(2,1)S(1)}, u32[]{:S(2)}) copy-start(bf16[64,256]{1,0:T(8,128)(2,1)S(1)} %collective-permute-done.32.refs_5_) | copy-start | bytes 98308
  146.5 2.0 %copy-start.41 = (bf16[64,256]{1,0:T(8,128)(2,1)}, bf16[64,256]{1,0:T(8,128)(2,1)S(1)}, u32[]{:S(2)}) copy-start(bf16[64,256]{1,0:T(8,128)(2,1)S(1)} %collective-permute-done.33.refs_6_) | copy-start | bytes 98308
  (15 other events, 10.8 us)
